TPU v7x, 256 devices: a whole 4x4x8 slice. The times are simulated.
256 devices in a mesh: layer: 4 (over x), row: 8 (over y, core), col: 8 (over z).
Axes of the slice: x: 4, y: 4, z: 8, core: 2. Of those that a mesh axis runs over, the one named last changes fastest.
Arguments:
- blocks: bfloat16 [13, 512, 128, 128], P(None, ('row', 'col'), 'layer'), may hold values from -0.29882812 to 0.29882812
- presence: int32 [13, 512], P(None, ('row', 'col')), may hold values from 0 to 1, as said below
Outputs:
- purified: bfloat16 [13, 512, 128, 128], P(None, ('row', 'col'), 'layer')
Inputs may be any that keep to these rules, and one draw needn't show every extreme that they name: `presence`: the tile on offset 0 is present in every block row.
All inputs are finite; a program needn't handle non-finite values.
Results may differ from a plain program's by a relative error of at most 0.01.
Values may be sent and summed in bfloat16 or wider, within the bound.
No kernel may reach another device: no remote copies, remote signals or barrier semaphores. Data moves between devices by JAX's collectives and lax.ppermute only.
A program may use at most 128 MiB of HBM per device.

v0:
```python
import jax
import jax.numpy as jnp
import numpy as np
from jax import lax
from jax.sharding import PartitionSpec as P

NBG = 512
BAND = 3
FAR = 160


def passed_along(block, axis, distance):
    devices = range(lax.axis_size(axis))
    route = [((i - distance) % len(devices), i) for i in devices]
    return lax.ppermute(block, axis, route)


def with_halo(block, sides, width):
    for axis, dim in sides:
        count = lax.axis_size(axis)
        forward = [(i, i + 1) for i in range(count - 1)]
        forward.append((count - 1, 0))
        backward = [(target, source) for source, target in forward]
        low = lax.ppermute(
            lax.slice_in_dim(block, block.shape[dim] - width, None, axis=dim), axis, forward
        )
        high = lax.ppermute(lax.slice_in_dim(block, 0, width, axis=dim), axis, backward)
        block = jnp.concatenate([low, block, high], axis=dim)
    return block


def offset_table():
    values = list(range(-BAND, BAND + 1))
    values = values + [FAR - 1, FAR, FAR + 1, -FAR - 1, -FAR, -FAR + 1]
    return [value % NBG for value in values]


def pair_table(offsets):
    by_target = []
    for target_index in range(len(offsets)):
        entries = []
        for left_index in range(len(offsets)):
            for right_index in range(len(offsets)):
                if (offsets[left_index] + offsets[right_index]) % NBG == offsets[target_index]:
                    entries.append((left_index, right_index))
        by_target.append(entries)
    return by_target


def fetch_far(source, offset, groups, local_rows):
    whole_steps, remainder = divmod(offset, local_rows)
    upper = passed_along(source[:, remainder:], ("row", "col"), -whole_steps % groups)
    if remainder == 0:
        return upper
    lower = passed_along(source[:, :remainder], ("row", "col"), (-whole_steps - 1) % groups)
    return jnp.concatenate([upper, lower], axis=1)


def per_device(blocks, presence):
    groups = lax.axis_size(("row", "col"))
    local_rows = blocks.shape[1]
    offsets = offset_table()
    by_target = pair_table(offsets)
    weight_mask = presence.astype(jnp.float32)[:, :, None, None]
    masked = blocks * presence.astype(jnp.bfloat16)[:, :, None, None]
    source = lax.all_gather(masked, "layer", axis=2, tiled=True)
    padded = with_halo(source, ((("row", "col"), 1),), BAND)
    far_windows = {}
    for left_index in range(2 * BAND + 1, len(offsets)):
        needed = sorted(
            set(
                (
                    entry[1]
                    for target_list in by_target
                    for entry in target_list
                    if entry[0] == left_index
                )
            )
        )
        picked = jnp.take(source, np.array(needed), axis=0)
        far_windows[left_index] = (
            fetch_far(picked, offsets[left_index], groups, local_rows),
            needed,
        )

    def right_piece(left_index, right_index):
        if left_index <= 2 * BAND:
            return padded[right_index, left_index : left_index + local_rows]
        window, needed = far_windows[left_index]
        return window[needed.index(right_index)]

    def product(left_tiles):
        totals = []
        for target_index in range(len(offsets)):
            pairs = by_target[target_index]
            lefts = jnp.concatenate(
                [left_tiles[left_index] for left_index, right_index in pairs], axis=2
            )
            rights = jnp.concatenate(
                [right_piece(left_index, right_index) for left_index, right_index in pairs], axis=1
            )
            totals.append(
                jnp.einsum("ixk,iky->ixy", lefts, rights, preferred_element_type=jnp.float32)
            )
        return jnp.stack(totals)

    second = (product(masked) * weight_mask).astype(jnp.bfloat16)
    third = product(second) * weight_mask
    return (3.0 * second.astype(jnp.float32) - 2.0 * third).astype(jnp.bfloat16)


def solution(mesh):
    placed = (P(None, ("row", "col"), "layer", None), P(None, ("row", "col")))
    return jax.shard_map(
        per_device,
        mesh=mesh,
        in_specs=placed,
        out_specs=P(None, ("row", "col"), "layer", None),
        check_vma=False,
    )
```

profile of v0, /device:TPU:1, one launch (start us, length us, event | category | flops | bytes accessed | tf_op | source)
XLA Modules:
  0.0 541.5 jit_solution(15222158619149315212)
XLA Ops:
  6.5 0.8 fusion.59
  7.4 2.2 broadcast_multiply_fusion
  9.7 0.9 constant_dynamic-update-slice_fusion.135
  10.6 0.9 constant_dynamic-update-slice_fusion.134
  11.5 0.9 constant_dynamic-update-slice_fusion.133
  12.6 0.8 constant_dynamic-update-slice_fusion.167
  13.5 0.7 constant_dynamic-update-slice_fusion.166
  14.2 0.8 copy-done.20
  16.5 0.7 constant_dynamic-update-slice_fusion.155
  17.2 0.8 constant_dynamic-update-slice_fusion.154
  18.0 0.7 constant_dynamic-update-slice_fusion.95
  19.3 0.7 constant_dynamic-update-slice_fusion.93
  20.0 0.7 constant_dynamic-update-slice_fusion.24
  20.7 0.7 constant_dynamic-update-slice_fusion.92
  21.4 0.7 constant_dynamic-update-slice_fusion.75
  23.5 0.9 copy-done.18
  24.4 33.5 %all-gather.2.cloned.1.call-done = bf16[13,8,128,128]{3,2,1,0:T(8,128)(2,1)} async-done(((bf16[13,8,32,128]{3,2,1,0:T(8,128)(2,1)}), bf16[13,8,128,128]{3,2,1,0:T(8,128)(2,1)}) %all-gather.2.cloned.1.call-update) | async-done | bytes 3407888 | tf_op jit(solution)/shard_map/all_gather | solution.py:66
  57.8 3.7 fusion.58
  61.6 1.3 collective-permute-start
  63.4 0.7 constant_dynamic-update-slice_fusion.72
  64.8 0.7 slice_bitcast_fusion.112
  65.5 2.1 gather_fusion
  67.6 1.6 slice.827
  69.2 6.8 %collective-permute-start.2 = (bf16[6,1,128,128]{3,2,1,0:T(8,128)(2,1)}, bf16[6,1,128,128]{3,2,1,0:T(8,128)(2,1)}, u32[]{:S(2)}, u32[]{:S(2)}) collective-permute-start(bf16[6,1,128,128]{3,2,1,0:T(8,128)(2,1)} %slice.827), channel_id=1, source_target_pairs={{19,0},{20,1},{21,2},{22,3},{23,4},{24,5},{25,6},{26,7},{27,8},{28... | collective-permute-start | bytes 589832 | tf_op jit(solution)/shard_map/ppermute | solution.py:15
  76.0 2.1 gather_fusion.1
  78.1 1.6 slice.830
  79.7 0.8 slice_bitcast_fusion.39
  80.5 2.6 slice.828
  83.1 2.1 gather_fusion.4
  85.2 2.8 slice.858
  88.0 1.6 slice.859
  89.6 1.2 slice.831
  90.8 2.1 gather_fusion.5
  92.9 2.6 slice.863
  95.4 1.6 slice.864
  97.0 1.4 collective-permute-start.1
  98.4 7.0 %collective-permute-start.3 = (bf16[6,7,128,128]{3,2,1,0:T(8,128)(2,1)}, bf16[6,7,128,128]{3,2,1,0:T(8,128)(2,1)}, u32[]{:S(2)}, u32[]{:S(2)}) collective-permute-start(bf16[6,7,128,128]{3,2,1,0:T(8,128)(2,1)} %slice.828), channel_id=1, source_target_pairs={{20,0},{21,1},{22,2},{23,3},{24,4},{25,5},{26,6},{27,7},{28,8},{29... | collective-permute-start | bytes 4128776 | tf_op jit(solution)/shard_map/ppermute | solution.py:15
  105.4 1.9 gather_fusion.2
  107.3 2.0 gather_fusion.3
  109.3 2.0 collective-permute-start.6
  111.2 0.9 constant_dynamic-update-slice_fusion.12
  112.2 3.4 collective-permute-start.8
  115.6 0.9 constant_dynamic-update-slice_fusion.14
  116.5 3.2 collective-permute-start.5
  119.7 1.4 constant_dynamic-update-slice_fusion.1
  121.1 1.1 constant_dynamic-update-slice_fusion.10
  122.8 252.4 %collective-permute-done.1 = bf16[13,3,128,128]{3,2,1,0:T(8,128)(2,1)} collective-permute-done((bf16[13,3,128,128]{3,2,1,0:T(8,128)(2,1)}, bf16[13,3,128,128]{3,2,1,0:T(8,128)(2,1)}, u32[]{:S(2)}, u32[]{:S(2)}) %collective-permute-start.1) | collective-permute-done | bytes 1277984 | tf_op jit(solution)/shard_map/ppermute | solution.py:27
  375.2 1.5 constant_dynamic-update-slice_fusion.9
  377.8 0.7 copy-done.28
  379.1 0.7 constant_dynamic-update-slice_fusion.175
  380.0 9.9 %collective-permute-start.9 = (bf16[6,1,128,128]{3,2,1,0:T(8,128)(2,1)S(1)}, bf16[6,1,128,128]{3,2,1,0:T(8,128)(2,1)S(1)}, u32[]{:S(2)}, u32[]{:S(2)}) collective-permute-start(bf16[6,1,128,128]{3,2,1,0:T(8,128)(2,1)S(1)} %copy-done.36), channel_id=1, source_target_pairs={{21,0},{22,1},{23,2},{24,3},{25,4},{26,5},{27,6},{28,7},{29,8},{30... | collective-permute-start | bytes 589832 | tf_op jit(solution)/shard_map/ppermute | solution.py:15
  390.1 22.5 %collective-permute-done.10 = bf16[6,7,128,128]{3,2,1,0:T(8,128)(2,1)S(1)} collective-permute-done((bf16[6,7,128,128]{3,2,1,0:T(8,128)(2,1)S(1)}, bf16[6,7,128,128]{3,2,1,0:T(8,128)(2,1)S(1)}, u32[]{:S(2)}, u32[]{:S(2)}) %collective-permute-start.10) | collective-permute-done | bytes 1376288 | tf_op jit(solution)/shard_map/ppermute | solution.py:15
  412.6 7.0 %collective-permute-start.7 = (bf16[6,8,128,128]{3,2,1,0:T(8,128)(2,1)S(1)}, bf16[6,8,128,128]{3,2,1,0:T(8,128)(2,1)S(1)}, u32[]{:S(2)}, u32[]{:S(2)}) collective-permute-start(bf16[6,8,128,128]{3,2,1,0:T(8,128)(2,1)S(1)} %copy-done.16), channel_id=1, source_target_pairs={{44,0},{45,1},{46,2},{47,3},{48,4},{49,5},{50,6},{51,7},{52,8},{53... | collective-permute-start | bytes 4718600 | tf_op jit(solution)/shard_map/ppermute | solution.py:15
  419.6 5.8 %collective-permute-done.9 = bf16[6,1,128,128]{3,2,1,0:T(8,128)(2,1)S(1)} collective-permute-done((bf16[6,1,128,128]{3,2,1,0:T(8,128)(2,1)S(1)}, bf16[6,1,128,128]{3,2,1,0:T(8,128)(2,1)S(1)}, u32[]{:S(2)}, u32[]{:S(2)}) %collective-permute-start.9) | collective-permute-done | bytes 196640 | tf_op jit(solution)/shard_map/ppermute | solution.py:15
  425.4 17.5 %collective-permute-start.11 = (bf16[6,1,128,128]{3,2,1,0:T(8,128)(2,1)S(1)}, bf16[6,1,128,128]{3,2,1,0:T(8,128)(2,1)S(1)}, u32[]{:S(2)}, u32[]{:S(2)}) collective-permute-start(bf16[6,1,128,128]{3,2,1,0:T(8,128)(2,1)S(1)} %copy-done.35), channel_id=1, source_target_pairs={{45,0},{46,1},{47,2},{48,3},{49,4},{50,5},{51,6},{52,7},{53,8},{54... | collective-permute-start | bytes 589832 | tf_op jit(solution)/shard_map/ppermute | solution.py:15
  442.9 1.6 constant_dynamic-update-slice_fusion.11
  444.5 69.3 %collective-permute-done.11 = bf16[6,1,128,128]{3,2,1,0:T(8,128)(2,1)S(1)} collective-permute-done((bf16[6,1,128,128]{3,2,1,0:T(8,128)(2,1)S(1)}, bf16[6,1,128,128]{3,2,1,0:T(8,128)(2,1)S(1)}, u32[]{:S(2)}, u32[]{:S(2)}) %collective-permute-start.11) | collective-permute-done | bytes 196640 | tf_op jit(solution)/shard_map/ppermute | solution.py:15
  514.9 0.8 copy-done.26
  516.4 0.9 copy-done.21
  518.0 0.9 copy-done.19
  519.0 0.7 fusion.25
  521.9 0.7 copy-done.13
  529.1 0.7 fusion.18
  533.3 1.3 subtract_convert_fusion
  (197 shorter events, 21.8 us)
Async XLA Ops:
  6.5 51.3 %all-gather.2.cloned.1.call-start = ((), (), s32[]{:S(2)}) async-start(), calls=%async_computation | async-start | bytes 4259840 | tf_op jit(solution)/shard_map/all_gather | solution.py:66
  9.6 2.7 copy-start.1
  12.5 3.2 copy-start.47
  12.5 3.2 copy-start.48
  12.5 3.8 copy-start.45
  12.6 3.8 copy-start.46
  14.2 0.9 copy-start.20
  14.2 1.0 copy-start.6
  14.2 1.1 copy-start.14
  14.2 1.3 copy-start.22
  14.2 1.4 copy-start.25
  18.0 5.4 copy-start.4
  18.0 5.4 copy-start.8
  18.0 5.4 %copy-start.10 = (bf16[8,32,768]{2,1,0:T(8,128)(2,1)}, bf16[8,32,768]{2,1,0:T(8,128)(2,1)S(1)}, u32[]{:S(2)}) copy-start(bf16[8,32,768]{2,1,0:T(8,128)(2,1)S(1)} %get-tuple-element.201) | copy-start | bytes 1179652
  18.0 5.4 %copy-start.12 = (bf16[8,32,768]{2,1,0:T(8,128)(2,1)}, bf16[8,32,768]{2,1,0:T(8,128)(2,1)S(1)}, u32[]{:S(2)}) copy-start(bf16[8,32,768]{2,1,0:T(8,128)(2,1)S(1)} %get-tuple-element.200) | copy-start | bytes 1179652
  23.4 0.9 copy-start.18
  24.3 38.5 %copy-start.43 = (s32[6]{0:T(128)S(1)}, s32[6]{0:T(128)}, u32[]{:S(2)}) copy-start(s32[6]{0:T(128)} %constant.92) | copy-start | bytes 76
  24.3 38.5 %copy-start.44 = (s32[6]{0:T(128)S(1)}, s32[6]{0:T(128)}, u32[]{:S(2)}) copy-start(s32[6]{0:T(128)} %constant.93) | copy-start | bytes 76
  57.8 5.6 %copy-start.2 = (bf16[13,8,32,128]{3,2,1,0:T(8,128)(2,1)S(1)}, bf16[13,8,32,128]{3,2,1,0:T(8,128)(2,1)}, u32[]{:S(2)}) copy-start(bf16[13,8,32,128]{3,2,1,0:T(8,128)(2,1)} %broadcast_multiply_fusion) | copy-start | bytes 2555908
  57.8 7.7 %copy-start = (bf16[13,8,128,128]{3,2,1,0:T(8,128)(2,1)S(1)}, bf16[13,8,128,128]{3,2,1,0:T(8,128)(2,1)}, u32[]{:S(2)}) copy-start(bf16[13,8,128,128]{3,2,1,0:T(8,128)(2,1)} %all-gather.2.cloned.1.call-done) | copy-start | bytes 10223620
  61.6 55.0 %collective-permute-start = (bf16[13,3,128,128]{3,2,1,0:T(8,128)(2,1)}, bf16[13,3,128,128]{3,2,1,0:T(8,128)(2,1)}, u32[]{:S(2)}, u32[]{:S(2)}) collective-permute-start(bf16[13,3,128,128]{3,2,1,0:T(8,128)(2,1)} %get-tuple-element.61), channel_id=1, source_target_pairs={{0,1},{1,2},{2,3},{3,4},{4,5},{5,6},{6,7},{7,8},{8,9},{9,10},{10,1... | collective-permute-start | bytes 3833864 | tf_op jit(solution)/shard_map/ppermute | solution.py:24
  69.2 40.0 %collective-permute-start.2 = (bf16[6,1,128,128]{3,2,1,0:T(8,128)(2,1)}, bf16[6,1,128,128]{3,2,1,0:T(8,128)(2,1)}, u32[]{:S(2)}, u32[]{:S(2)}) collective-permute-start(bf16[6,1,128,128]{3,2,1,0:T(8,128)(2,1)} %slice.827), channel_id=1, source_target_pairs={{19,0},{20,1},{21,2},{22,3},{23,4},{24,5},{25,6},{26,7},{27,8},{28... | collective-permute-start | bytes 589832 | tf_op jit(solution)/shard_map/ppermute | solution.py:15
  79.7 32.5 %collective-permute-start.4 = (bf16[6,1,128,128]{3,2,1,0:T(8,128)(2,1)}, bf16[6,1,128,128]{3,2,1,0:T(8,128)(2,1)}, u32[]{:S(2)}, u32[]{:S(2)}) collective-permute-start(bf16[6,1,128,128]{3,2,1,0:T(8,128)(2,1)} %slice.830), channel_id=1, source_target_pairs={{43,0},{44,1},{45,2},{46,3},{47,4},{48,5},{49,6},{50,7},{51,8},{52... | collective-permute-start | bytes 589832 | tf_op jit(solution)/shard_map/ppermute | solution.py:15
  85.2 4.4 copy-start.3
  97.0 278.1 %collective-permute-start.1 = (bf16[13,3,128,128]{3,2,1,0:T(8,128)(2,1)}, bf16[13,3,128,128]{3,2,1,0:T(8,128)(2,1)}, u32[]{:S(2)}, u32[]{:S(2)}) collective-permute-start(bf16[13,3,128,128]{3,2,1,0:T(8,128)(2,1)} %get-tuple-element.60), channel_id=1, source_target_pairs={{1,0},{2,1},{3,2},{4,3},{5,4},{6,5},{7,6},{8,7},{9,8},{10,9},{11,1... | collective-permute-start | bytes 3833864 | tf_op jit(solution)/shard_map/ppermute | solution.py:27
  98.4 344.5 %collective-permute-start.3 = (bf16[6,7,128,128]{3,2,1,0:T(8,128)(2,1)}, bf16[6,7,128,128]{3,2,1,0:T(8,128)(2,1)}, u32[]{:S(2)}, u32[]{:S(2)}) collective-permute-start(bf16[6,7,128,128]{3,2,1,0:T(8,128)(2,1)} %slice.828), channel_id=1, source_target_pairs={{20,0},{21,1},{22,2},{23,3},{24,4},{25,5},{26,6},{27,7},{28,8},{29... | collective-permute-start | bytes 4128776 | tf_op jit(solution)/shard_map/ppermute | solution.py:15
  109.3 405.0 %collective-permute-start.6 = (bf16[6,8,128,128]{3,2,1,0:T(8,128)(2,1)}, bf16[6,8,128,128]{3,2,1,0:T(8,128)(2,1)S(1)}, u32[]{:S(2)}, u32[]{:S(2)}) collective-permute-start(bf16[6,8,128,128]{3,2,1,0:T(8,128)(2,1)} %gather_fusion.2), channel_id=1, source_target_pairs={{20,0},{21,1},{22,2},{23,3},{24,4},{25,5},{26,6},{27,7},{28,8},{29... | collective-permute-start | bytes 4718600 | tf_op jit(solution)/shard_map/ppermute | solution.py:15
  112.2 267.6 %collective-permute-start.8 = (bf16[6,7,128,128]{3,2,1,0:T(8,128)(2,1)}, bf16[6,7,128,128]{3,2,1,0:T(8,128)(2,1)S(1)}, u32[]{:S(2)}, u32[]{:S(2)}) collective-permute-start(bf16[6,7,128,128]{3,2,1,0:T(8,128)(2,1)} %slice.858), channel_id=1, source_target_pairs={{20,0},{21,1},{22,2},{23,3},{24,4},{25,5},{26,6},{27,7},{28,8},{29... | collective-permute-start | bytes 4128776 | tf_op jit(solution)/shard_map/ppermute | solution.py:15
  116.5 397.3 %collective-permute-start.5 = (bf16[6,7,128,128]{3,2,1,0:T(8,128)(2,1)}, bf16[6,7,128,128]{3,2,1,0:T(8,128)(2,1)S(1)}, u32[]{:S(2)}, u32[]{:S(2)}) collective-permute-start(bf16[6,7,128,128]{3,2,1,0:T(8,128)(2,1)} %slice.831), channel_id=1, source_target_pairs={{44,0},{45,1},{46,2},{47,3},{48,4},{49,5},{50,6},{51,7},{52,8},{53... | collective-permute-start | bytes 4128776 | tf_op jit(solution)/shard_map/ppermute | solution.py:15
  122.5 252.7 %copy-start.17 = (bf16[6,7,128,128]{3,2,1,0:T(8,128)(2,1)S(1)}, bf16[6,7,128,128]{3,2,1,0:T(8,128)(2,1)}, u32[]{:S(2)}) copy-start(bf16[6,7,128,128]{3,2,1,0:T(8,128)(2,1)} %slice.863) | copy-start | bytes 4128772
  375.2 37.4 %collective-permute-start.10 = (bf16[6,7,128,128]{3,2,1,0:T(8,128)(2,1)S(1)}, bf16[6,7,128,128]{3,2,1,0:T(8,128)(2,1)S(1)}, u32[]{:S(2)}, u32[]{:S(2)}) collective-permute-start(bf16[6,7,128,128]{3,2,1,0:T(8,128)(2,1)S(1)} %copy-done.17), channel_id=1, source_target_pairs={{44,0},{45,1},{46,2},{47,3},{48,4},{49,5},{50,6},{51,7},{52,8},{53... | collective-permute-start | bytes 4128776 | tf_op jit(solution)/shard_map/ppermute | solution.py:15
  377.5 1.0 copy-start.28
  377.5 0.9 copy-start.38
  377.6 1.0 copy-start.40
  377.6 1.0 copy-start.41
  377.6 1.2 copy-start.42
  377.6 1.4 copy-start.29
  377.7 1.4 copy-start.31
  377.7 1.4 copy-start.33
  379.1 0.9 copy-start.36
  379.8 32.8 %copy-start.16 = (bf16[6,8,128,128]{3,2,1,0:T(8,128)(2,1)S(1)}, bf16[6,8,128,128]{3,2,1,0:T(8,128)(2,1)}, u32[]{:S(2)}) copy-start(bf16[6,8,128,128]{3,2,1,0:T(8,128)(2,1)} %gather_fusion.3) | copy-start | bytes 4718596
  380.0 45.3 %collective-permute-start.9 = (bf16[6,1,128,128]{3,2,1,0:T(8,128)(2,1)S(1)}, bf16[6,1,128,128]{3,2,1,0:T(8,128)(2,1)S(1)}, u32[]{:S(2)}, u32[]{:S(2)}) collective-permute-start(bf16[6,1,128,128]{3,2,1,0:T(8,128)(2,1)S(1)} %copy-done.36), channel_id=1, source_target_pairs={{21,0},{22,1},{23,2},{24,3},{25,4},{26,5},{27,6},{28,7},{29,8},{30... | collective-permute-start | bytes 589832 | tf_op jit(solution)/shard_map/ppermute | solution.py:15
  390.1 35.3 %copy-start.35 = (bf16[6,1,128,128]{3,2,1,0:T(8,128)(2,1)S(1)}, bf16[6,1,128,128]{3,2,1,0:T(8,128)(2,1)}, u32[]{:S(2)}) copy-start(bf16[6,1,128,128]{3,2,1,0:T(8,128)(2,1)} %slice.864) | copy-start | bytes 589828
  412.6 103.6 %collective-permute-start.7 = (bf16[6,8,128,128]{3,2,1,0:T(8,128)(2,1)S(1)}, bf16[6,8,128,128]{3,2,1,0:T(8,128)(2,1)S(1)}, u32[]{:S(2)}, u32[]{:S(2)}) collective-permute-start(bf16[6,8,128,128]{3,2,1,0:T(8,128)(2,1)S(1)} %copy-done.16), channel_id=1, source_target_pairs={{44,0},{45,1},{46,2},{47,3},{48,4},{49,5},{50,6},{51,7},{52,8},{53... | collective-permute-start | bytes 4718600 | tf_op jit(solution)/shard_map/ppermute | solution.py:15
  425.4 88.4 %collective-permute-start.11 = (bf16[6,1,128,128]{3,2,1,0:T(8,128)(2,1)S(1)}, bf16[6,1,128,128]{3,2,1,0:T(8,128)(2,1)S(1)}, u32[]{:S(2)}, u32[]{:S(2)}) collective-permute-start(bf16[6,1,128,128]{3,2,1,0:T(8,128)(2,1)S(1)} %copy-done.35), channel_id=1, source_target_pairs={{45,0},{46,1},{47,2},{48,3},{49,4},{50,5},{51,6},{52,7},{53,8},{54... | collective-permute-start | bytes 589832 | tf_op jit(solution)/shard_map/ppermute | solution.py:15
  514.7 1.0 copy-start.26
  516.2 1.1 copy-start.21
  517.8 1.2 copy-start.19
  519.0 1.1 copy-start.23
  520.1 1.0 copy-start.24
  520.6 1.0 copy-start.27
  520.6 1.0 copy-start.37
  520.6 1.0 copy-start.39
  521.6 1.0 copy-start.13
  521.9 1.1 copy-start.11
  522.6 1.0 copy-start.7
  523.0 1.0 copy-start.9
  523.6 1.0 copy-start.5
  524.0 1.0 copy-start.15
  526.7 1.0 copy-start.30
  526.7 1.0 copy-start.32
  526.7 1.1 copy-start.34
Sparse Core Ops, SparseCore 0:
  9.8 48.0 all-gather.1
where the time goes:
time: 546 us; the launch traced here: 541 us
  waiting for transfers between devices  383 us (70%)
  local copies, waits for them, and re-layouts  67.7 us (12%)
  starting transfers between devices  59.3 us (11%)
  between operations  14.5 us (3%)
  matrix products  10.8 us (2%)
  other arithmetic  5.74 us (1%)
    ppermute x1, waiting for transfers between devices, with_halo(): lax.ppermute(lax.slice_in_dim(block, 0, width, axis=dim), axis, backward)  252 us
    ppermute x10, waiting for transfers between devices, passed_along(): return lax.ppermute(block, axis, route)  97.6 us
    ppermute x10, starting transfers between devices, passed_along(): return lax.ppermute(block, axis, route)  56.7 us
    all_gather x1, waiting for transfers between devices, per_device(): source = lax.all_gather(masked, 'layer', axis=2, tiled=True)  33.5 us
    unnamed x162, local copies, waits for them, and re-layouts  26.4 us
    gather x6, local copies, waits for them, and re-layouts, per_device(): picked = jnp.take(source, np.array(needed), axis=0)  12.1 us
  transfers between devices with their start and end apart: 13, of which 5 were waited for; matrix products, arithmetic and copies ran while one was open for 10% of the time, Pallas kernels for 0%

commit v1 on v0

v1 whole, which is shorter than its diff:
```python
import jax
import jax.numpy as jnp
from jax import lax
from jax.experimental import pallas as pl
from jax.experimental.pallas import tpu as pltpu
from jax.sharding import PartitionSpec as P

NBG = 512
BAND = 3
FAR = 160
BS = 128
LAYERS = 4
PAIRS = NBG // 2
FAR_PAIRS = FAR // 2
AXES = ("layer", "row", "col")
OFFSETS = list(range(-BAND, BAND + 1)) + [
    FAR - 1, FAR, FAR + 1, -FAR - 1, -FAR, -FAR + 1,
]
DIAGS = len(OFFSETS)
OFFSET_SET = {value % NBG for value in OFFSETS}

REACH = (
    list(range(-BAND, BAND + 2))
    + list(range(FAR - 1, FAR + 3))
    + list(range(-FAR - 1, -FAR + 3))
)
SLOT = {value % NBG: index for index, value in enumerate(REACH)}
NEAR_END = 8 * BS
PLUS_END = 12 * BS
WIDTH = 16 * BS


def needed(j):
    found = set()
    for i in range(2):
        for left in OFFSETS:
            if (i + left - j) % NBG == 0:
                for b, right in enumerate(OFFSETS):
                    if (left + right) % NBG in OFFSET_SET:
                        found.add(b)
    return sorted(found)


def tiles_of(rows):
    return [
        (t, b)
        for t in range(2)
        for b in sorted(set().union(*(needed(j) for j in rows[t])))
    ]


LOW = (-1, tiles_of(([-2], [-1])))
HIGH = (1, tiles_of(([2], [3])))
LOWER = (-2, tiles_of(([], [-3])))
HIGHER = (2, tiles_of(([4], [])))
PLUS = (FAR_PAIRS, tiles_of(([FAR, FAR + 2], [FAR + 1, FAR - 1])))
MINUS = (-FAR_PAIRS, tiles_of(([-FAR, -FAR + 2], [-FAR + 1, -FAR - 1])))
DIRECT = [PLUS, MINUS, LOW, HIGH, LOWER, HIGHER]
FAR_LOW = [(0, 1, b) for b in needed(FAR - 1)] + [(1, 1, b) for b in needed(-FAR - 1)]
FAR_HIGH = [(0, 0, b) for b in needed(FAR + 2)] + [(1, 0, b) for b in needed(-FAR + 2)]


def place_of(p):
    return p % LAYERS * (PAIRS // LAYERS) + p // LAYERS


def moved(x, source_of):
    route = [(place_of(source_of(p)), place_of(p)) for p in range(PAIRS)]
    return lax.ppermute(x, AXES, route)


def from_pair(x, distance):
    return moved(x, lambda p: (p + distance) % PAIRS)


def from_layer(x, distance):
    return moved(x, lambda p: p - p % LAYERS + (p + distance) % LAYERS)


def bf16(*shape):
    return jax.ShapeDtypeStruct(shape, jnp.bfloat16)


def call(body, out_shape, n_smem, n_vmem, scratch=(), flops=0, traffic=1 << 22):
    in_specs = [pl.BlockSpec(memory_space=pltpu.SMEM)] * n_smem
    in_specs += [pl.BlockSpec(memory_space=pltpu.VMEM)] * n_vmem
    return pl.pallas_call(
        body,
        out_shape=out_shape,
        in_specs=in_specs,
        out_specs=jax.tree.map(
            lambda _: pl.BlockSpec(memory_space=pltpu.VMEM), out_shape
        ),
        scratch_shapes=list(scratch),
        compiler_params=pltpu.CompilerParams(vmem_limit_bytes=48 << 20),
        cost_estimate=pl.CostEstimate(
            flops=flops, bytes_accessed=traffic, transcendentals=0
        ),
    )


def split_body(me_ref, presence_ref, blocks_ref, *out_refs):
    me = me_ref[0]
    for s, out_ref in enumerate(out_refs):
        other = lax.rem(me - s + LAYERS, LAYERS)
        for t in range(2):
            row = 2 * other + t
            for d in range(DIAGS):
                tile = blocks_ref[d, row]
                present = presence_ref[d, row] != 0
                out_ref[d, t] = jnp.where(present, tile, jnp.zeros_like(tile))


def pack_body(me_ref, *refs):
    me = me_ref[0]
    pieces, own_ref, out_refs = refs[:LAYERS], refs[LAYERS], refs[LAYERS + 1 :]
    for s, piece in enumerate(pieces):
        other = lax.rem(me + s, LAYERS)
        start = pl.multiple_of(other * (BS // LAYERS), BS // LAYERS)
        own_ref[:, :, pl.ds(start, BS // LAYERS), :] = piece[...]
    for (_, tiles), out_ref in zip(DIRECT, out_refs):
        for k, (t, b) in enumerate(tiles):
            out_ref[k] = own_ref[b, t]


def far_body(plus_ref, minus_ref, low_ref, high_ref):
    sources = ((plus_ref, PLUS[1]), (minus_ref, MINUS[1]))
    for message, out_ref in ((FAR_LOW, low_ref), (FAR_HIGH, high_ref)):
        for k, (which, t, b) in enumerate(message):
            ref, tiles = sources[which]
            out_ref[k] = ref[tiles.index((t, b))]


def placements():
    found = {}

    def place(operand, index, j, b):
        row, column = SLOT[j % NBG], SLOT[(j + OFFSETS[b]) % NBG]
        found[row, column] = (operand, index)

    for t in range(2):
        for b in range(DIAGS):
            place(0, (b, t), t, b)
    for operand, (distance, tiles) in enumerate(DIRECT):
        for k, (t, b) in enumerate(tiles):
            j = 2 * distance + t
            if b in needed(j):
                place(1 + operand, k, j, b)
    for operand, message, rows in (
        (7, FAR_LOW, (FAR - 1, -FAR - 1)),
        (8, FAR_HIGH, (FAR + 2, -FAR + 2)),
    ):
        for k, (which, t, b) in enumerate(message):
            place(operand, k, rows[which], b)
    return found


def purify_body(me_ref, presence_ref, *refs):
    sources, outs = refs[:9], refs[9:13]
    right_ref, left_ref, result_ref = refs[13:]
    me = me_ref[0]
    own_ref = sources[0]
    placed = placements()
    zero = jnp.zeros((BS, BS), jnp.bfloat16)
    for row in range(16):
        for column in range(16):
            where = (pl.ds(row * BS, BS), pl.ds(column * BS, BS))
            if (row, column) in placed:
                operand, index = placed[row, column]
                right_ref[where] = sources[operand][index]
            else:
                right_ref[where] = zero
    targets = {
        (i, SLOT[(i + offset) % NBG]): d
        for i in range(2)
        for d, offset in enumerate(OFFSETS)
    }
    for i in range(2):
        for column in range(16):
            where = (pl.ds(i * BS, BS), pl.ds(column * BS, BS))
            d = targets.get((i, column))
            left_ref[where] = zero if d is None else own_ref[d, i]

    def dot(left, right):
        return jnp.dot(left, right, preferred_element_type=jnp.float32)

    def product(columns):
        start = columns[0] * BS
        wide = pl.ds(start, len(columns) * BS)
        if start < NEAR_END:
            return dot(left_ref[...], right_ref[:, wide])
        if start < PLUS_END:
            return dot(left_ref[:, :PLUS_END], right_ref[:PLUS_END, wide])
        return dot(left_ref[:, :NEAR_END], right_ref[:NEAR_END, wide]) + dot(
            left_ref[:, PLUS_END:], right_ref[PLUS_END:, wide]
        )

    def each(columns, total, use):
        for at, column in enumerate(columns):
            for i in range(2):
                d = targets.get((i, column))
                if d is not None:
                    tile = total[i * BS : (i + 1) * BS, at * BS : (at + 1) * BS]
                    use(i, column, d, presence_ref[d, 2 * me + i] != 0, tile)

    groups = [[c, c + 1] for c in range(0, 16, 2)]

    def keep_second(i, column, d, present, tile):
        second = jnp.where(present, tile, jnp.zeros_like(tile)).astype(jnp.bfloat16)
        result_ref[d, i] = second

    for columns in groups:
        each(columns, product(columns), keep_second)
    for (i, column), d in targets.items():
        left_ref[pl.ds(i * BS, BS), pl.ds(column * BS, BS)] = result_ref[d, i]

    def keep_result(i, column, d, present, tile):
        third = jnp.where(present, tile, jnp.zeros_like(tile))
        second = result_ref[d, i].astype(jnp.float32)
        result_ref[d, i] = (3.0 * second - 2.0 * third).astype(jnp.bfloat16)

    for columns in groups:
        each(columns, product(columns), keep_result)
    for s, out_ref in enumerate(outs):
        other = lax.rem(me - s + LAYERS, LAYERS)
        start = pl.multiple_of(other * (BS // LAYERS), BS // LAYERS)
        out_ref[...] = result_ref[:, :, pl.ds(start, BS // LAYERS), :]


def join_body(me_ref, *refs):
    me = me_ref[0]
    out_ref = refs[LAYERS]
    for s in range(LAYERS):
        row = 2 * lax.rem(me + s, LAYERS)
        for t in range(2):
            for d in range(DIAGS):
                out_ref[d, row + t] = refs[s][d, t]


def per_device(blocks, presence):
    me = lax.axis_index("layer").astype(jnp.int32).reshape(1)
    quarter = bf16(DIAGS, 2, BS // LAYERS, BS)
    tiles = [bf16(len(message), BS, BS) for _, message in DIRECT]

    pieces = call(split_body, [quarter] * LAYERS, 2, 1)(me, presence, blocks)
    pieces = [pieces[0]] + [from_layer(pieces[s], s) for s in range(1, LAYERS)]
    own, *messages = call(
        pack_body, [bf16(DIAGS, 2, BS, BS)] + tiles, 1, LAYERS
    )(me, *pieces)
    arrived = [
        from_pair(message, distance)
        for message, (distance, _) in zip(messages, DIRECT)
    ]
    far_low, far_high = call(
        far_body, [bf16(len(FAR_LOW), BS, BS), bf16(len(FAR_HIGH), BS, BS)], 0, 2
    )(arrived[0], arrived[1])
    far_low, far_high = from_pair(far_low, -1), from_pair(far_high, 1)
    results = call(
        purify_body,
        [quarter] * LAYERS,
        2,
        9,
        scratch=[
            pltpu.VMEM((WIDTH, WIDTH), jnp.bfloat16),
            pltpu.VMEM((2 * BS, WIDTH), jnp.bfloat16),
            pltpu.VMEM((DIAGS, 2, BS, BS), jnp.bfloat16),
        ],
        flops=4 * 224 * 2 * BS**3,
    )(me, presence, own, *arrived, far_low, far_high)
    results = [results[0]] + [from_layer(results[s], s) for s in range(1, LAYERS)]
    return call(join_body, bf16(DIAGS, 2 * LAYERS, BS // LAYERS, BS), 1, LAYERS)(
        me, *results
    )


def solution(mesh):
    placed = (P(None, ("row", "col"), "layer", None), P(None, ("row", "col")))
    return jax.shard_map(
        per_device,
        mesh=mesh,
        in_specs=placed,
        out_specs=P(None, ("row", "col"), "layer", None),
        check_vma=False,
    )
```

time: 546 us -> 132 us (0.24)
  waiting for transfers between devices: 383 us -> 84.6 us
  local copies, waits for them, and re-layouts: 67.7 us -> 1.92 us
  starting transfers between devices: 59.3 us -> 36.8 us
  between operations: 14.5 us -> 0.06 us
  matrix products: 10.8 us -> 0 us
  Pallas kernels: 0 us -> 7.97 us
  other arithmetic: 5.74 us -> 0 us
    ppermute x12 -> x14, waiting for transfers between devices: 350 us -> 84.6 us  [moved(): return lax.ppermute(x, AXES, route)]
    all_gather x1 -> x0, waiting for transfers between devices: 33.5 us -> none  [per_device(): source = lax.all_gather(masked, 'layer', axis=2, tiled=True)]
    unnamed x162 -> x5, local copies, waits for them, and re-layouts: 26.4 us -> 1.92 us
    ppermute x12 -> x14, starting transfers between devices: 59.3 us -> 36.8 us  [moved(): return lax.ppermute(x, AXES, route)]
    slice x9 -> x0, local copies, waits for them, and re-layouts: 19.3 us -> none  [the longest x4 8.59 us: fetch_far(): source[:, remainder:]]
    gather x6 -> x0, local copies, waits for them, and re-layouts: 12.1 us -> none  [per_device(): picked = jnp.take(source, np.array(needed), axis=0)]
    dot_general x26 -> x0, matrix products: 10.8 us -> none  [product(): jnp.einsum('ixk,iky->ixy', lefts, rights, preferred_element_type=jnp.floa...]
    pallas_call x0 -> x5, Pallas kernels: none -> 7.97 us  [the longest x1 5.76 us: per_device(): call(purify_body, [quarter] * LAYERS, 2, 9, scratch=[pltpu.VMEM((WIDTH, W...]
  transfers between devices with their start and end apart: 13 -> 14, of which waited for: 5 -> 8; matrix products, arithmetic and copies ran while one was open for 10% -> 0% of each run, Pallas kernels for 0% -> 0%
where the time goes in v1:
time: 132 us; the launch traced here: 131 us
  waiting for transfers between devices  84.6 us (64%)
  starting transfers between devices  36.8 us (28%)
  Pallas kernels  7.97 us (6%)
  local copies, waits for them, and re-layouts  1.92 us (1%)
    ppermute x14, waiting for transfers between devices, moved(): return lax.ppermute(x, AXES, route)  84.6 us
    ppermute x14, starting transfers between devices, moved(): return lax.ppermute(x, AXES, route)  36.8 us
    pallas_call x1, Pallas kernels, per_device(): call(purify_body, [quarter] * LAYERS, 2, 9, scratch=[pltpu.VMEM((WIDTH, W...  5.76 us
  transfers between devices with their start and end apart: 14, of which 8 were waited for; matrix products, arithmetic and copies ran while one was open for 0% of the time, Pallas kernels for 0%

profile of v1, /device:TPU:1, one launch (start us, length us, event | category | flops | bytes accessed | tf_op | source)
XLA Modules:
  0.0 131.4 jit_solution(4980065937947890821)
XLA Ops:
  0.0 0.0 copy-start.1
  0.0 0.7 copy-done.1
  0.7 0.1 copy.4.presence_ref
  0.8 0.0 copy-start
  0.8 1.2 copy-done
  1.9 0.9 shard_map.28
  2.9 3.4 %collective-permute-start = (bf16[13,2,32,128]{3,2,1,0:T(8,128)(2,1)S(1)}, bf16[13,2,32,128]{3,2,1,0:T(8,128)(2,1)S(1)}, u32[]{:S(2)}, u32[]{:S(2)}) collective-permute-start(bf16[13,2,32,128]{3,2,1,0:T(8,128)(2,1)S(1)} %get-tuple-element.23), channel_id=1, source_target_pairs={{64,0},{128,64},{192,128},{0,192},{65,1},{129,65},{193,129},{1,193... | collective-permute-start | bytes 638984 | tf_op jit(solution)/shard_map/ppermute | solution.py:69
  6.2 0.5 collective-permute-start.1
  6.8 0.6 collective-permute-start.2
  7.4 7.4 %collective-permute-done.refs_1_ = bf16[13,2,32,128]{3,2,1,0:T(8,128)(2,1)S(1)} collective-permute-done((bf16[13,2,32,128]{3,2,1,0:T(8,128)(2,1)S(1)}, bf16[13,2,32,128]{3,2,1,0:T(8,128)(2,1)S(1)}, u32[]{:S(2)}, u32[]{:S(2)}) %collective-permute-start) | collective-permute-done | bytes 213024 | tf_op jit(solution)/shard_map/ppermute | solution.py:69
  14.8 0.0 collective-permute-done.1.refs_2_
  14.8 4.7 %collective-permute-done.2.refs_3_ = bf16[13,2,32,128]{3,2,1,0:T(8,128)(2,1)S(1)} collective-permute-done((bf16[13,2,32,128]{3,2,1,0:T(8,128)(2,1)S(1)}, bf16[13,2,32,128]{3,2,1,0:T(8,128)(2,1)S(1)}, u32[]{:S(2)}, u32[]{:S(2)}) %collective-permute-start.2) | collective-permute-done | bytes 213024 | tf_op jit(solution)/shard_map/ppermute | solution.py:69
  19.5 0.3 shard_map.29
  19.8 9.8 %collective-permute-start.3 = (bf16[16,128,128]{2,1,0:T(8,128)(2,1)S(1)}, bf16[16,128,128]{2,1,0:T(8,128)(2,1)S(1)}, u32[]{:S(2)}, u32[]{:S(2)}) collective-permute-start(bf16[16,128,128]{2,1,0:T(8,128)(2,1)S(1)} %get-tuple-element.27), channel_id=1, source_target_pairs={{20,0},{84,64},{148,128},{212,192},{21,1},{85,65},{149,129},{213,1... | collective-permute-start | bytes 1572872 | tf_op jit(solution)/shard_map/ppermute | solution.py:69
  29.6 0.0 collective-permute-start.4
  29.6 0.0 collective-permute-start.5
  29.6 5.1 %collective-permute-start.6 = (bf16[17,128,128]{2,1,0:T(8,128)(2,1)S(1)}, bf16[17,128,128]{2,1,0:T(8,128)(2,1)S(1)}, u32[]{:S(2)}, u32[]{:S(2)}) collective-permute-start(bf16[17,128,128]{2,1,0:T(8,128)(2,1)S(1)} %get-tuple-element.30), channel_id=1, source_target_pairs={{64,0},{128,64},{192,128},{1,192},{65,1},{129,65},{193,129},{2,193... | collective-permute-start | bytes 1671176 | tf_op jit(solution)/shard_map/ppermute | solution.py:69
  34.7 8.6 %collective-permute-done.3.plus_ref.refs_1_ = bf16[16,128,128]{2,1,0:T(8,128)(2,1)S(1)} collective-permute-done((bf16[16,128,128]{2,1,0:T(8,128)(2,1)S(1)}, bf16[16,128,128]{2,1,0:T(8,128)(2,1)S(1)}, u32[]{:S(2)}, u32[]{:S(2)}) %collective-permute-start.3) | collective-permute-done | bytes 524320 | tf_op jit(solution)/shard_map/ppermute | solution.py:69
  43.3 31.7 %collective-permute-done.4.minus_ref.refs_2_ = bf16[16,128,128]{2,1,0:T(8,128)(2,1)S(1)} collective-permute-done((bf16[16,128,128]{2,1,0:T(8,128)(2,1)S(1)}, bf16[16,128,128]{2,1,0:T(8,128)(2,1)S(1)}, u32[]{:S(2)}, u32[]{:S(2)}) %collective-permute-start.4) | collective-permute-done | bytes 524320 | tf_op jit(solution)/shard_map/ppermute | solution.py:69
  75.0 0.1 shard_map.30
  75.0 0.1 collective-permute-start.9
  75.1 5.1 %collective-permute-start.10 = (bf16[12,128,128]{2,1,0:T(8,128)(2,1)S(1)}, bf16[12,128,128]{2,1,0:T(8,128)(2,1)S(1)}, u32[]{:S(2)}, u32[]{:S(2)}) collective-permute-start(bf16[12,128,128]{2,1,0:T(8,128)(2,1)S(1)} %get-tuple-element.34), channel_id=1, source_target_pairs={{64,0},{128,64},{192,128},{1,192},{65,1},{129,65},{193,129},{2,193... | collective-permute-start | bytes 1179656 | tf_op jit(solution)/shard_map/ppermute | solution.py:69
  80.2 0.0 collective-permute-start.7
  80.2 11.1 %collective-permute-done.7.refs_5_ = bf16[4,128,128]{2,1,0:T(8,128)(2,1)S(1)} collective-permute-done((bf16[4,128,128]{2,1,0:T(8,128)(2,1)S(1)}, bf16[4,128,128]{2,1,0:T(8,128)(2,1)S(1)}, u32[]{:S(2)}, u32[]{:S(2)}) %collective-permute-start.7) | collective-permute-done | bytes 131104 | tf_op jit(solution)/shard_map/ppermute | solution.py:69
  91.2 0.9 collective-permute-start.8
  92.1 9.2 %collective-permute-done.8.refs_6_ = bf16[4,128,128]{2,1,0:T(8,128)(2,1)S(1)} collective-permute-done((bf16[4,128,128]{2,1,0:T(8,128)(2,1)S(1)}, bf16[4,128,128]{2,1,0:T(8,128)(2,1)S(1)}, u32[]{:S(2)}, u32[]{:S(2)}) %collective-permute-start.8) | collective-permute-done | bytes 131104 | tf_op jit(solution)/shard_map/ppermute | solution.py:69
  101.3 0.0 collective-permute-done.5.refs_3_
  101.3 0.0 collective-permute-done.6.refs_4_
  101.3 0.0 collective-permute-done.9.refs_7_
  101.3 0.0 collective-permute-done.10.refs_8_
  101.3 5.8 %shard_map.31 = (bf16[13,2,32,128]{3,2,1,0:T(8,128)(2,1)S(1)}, bf16[13,2,32,128]{3,2,1,0:T(8,128)(2,1)S(1)}, bf16[13,2,32,128]{3,2,1,0:T(8,128)(2,1)S(1)}, bf16[13,2,32,128]{3,2,1,0:T(8,128)(2,1)S(1)}) custom-call(s32[1]{0:T(128)} %bitcast.me_ref, s32[13,8]{1,0:T(8,128)S(1)} %copy.4.presence_ref, bf16[13,2,128,128]{3,2,1,0:T(8,128)(2,1)S(1)} %get-tuple-element.26.refs_0_, ...), custom_call_target="tpu_custom_call" | custom-call | flops 3758096384 | bytes 4194304 | tf_op jit(solution)/shard_map/pallas_call | solution.py:258
  107.1 10.7 %collective-permute-start.11 = (bf16[13,2,32,128]{3,2,1,0:T(8,128)(2,1)S(1)}, bf16[13,2,32,128]{3,2,1,0:T(8,128)(2,1)S(1)}, u32[]{:S(2)}, u32[]{:S(2)}) collective-permute-start(bf16[13,2,32,128]{3,2,1,0:T(8,128)(2,1)S(1)} %get-tuple-element.36), channel_id=1, source_target_pairs={{64,0},{128,64},{192,128},{0,192},{65,1},{129,65},{193,129},{1,193... | collective-permute-start | bytes 638984 | tf_op jit(solution)/shard_map/ppermute | solution.py:69
  117.8 0.0 collective-permute-start.12
  117.8 0.7 collective-permute-start.13
  118.5 8.5 %collective-permute-done.11.refs_1_ = bf16[13,2,32,128]{3,2,1,0:T(8,128)(2,1)S(1)} collective-permute-done((bf16[13,2,32,128]{3,2,1,0:T(8,128)(2,1)S(1)}, bf16[13,2,32,128]{3,2,1,0:T(8,128)(2,1)S(1)}, u32[]{:S(2)}, u32[]{:S(2)}) %collective-permute-start.11) | collective-permute-done | bytes 213024 | tf_op jit(solution)/shard_map/ppermute | solution.py:69
  127.0 0.0 collective-permute-done.12.refs_2_
  127.0 3.5 %collective-permute-done.13.refs_3_ = bf16[13,2,32,128]{3,2,1,0:T(8,128)(2,1)S(1)} collective-permute-done((bf16[13,2,32,128]{3,2,1,0:T(8,128)(2,1)S(1)}, bf16[13,2,32,128]{3,2,1,0:T(8,128)(2,1)S(1)}, u32[]{:S(2)}, u32[]{:S(2)}) %collective-permute-start.13) | collective-permute-done | bytes 213024 | tf_op jit(solution)/shard_map/ppermute | solution.py:69
  130.5 1.0 shard_map.32
Async XLA Ops:
  0.0 0.7 copy-start.1
  0.8 1.2 copy-start
  2.9 11.9 %collective-permute-start = (bf16[13,2,32,128]{3,2,1,0:T(8,128)(2,1)S(1)}, bf16[13,2,32,128]{3,2,1,0:T(8,128)(2,1)S(1)}, u32[]{:S(2)}, u32[]{:S(2)}) collective-permute-start(bf16[13,2,32,128]{3,2,1,0:T(8,128)(2,1)S(1)} %get-tuple-element.23), channel_id=1, source_target_pairs={{64,0},{128,64},{192,128},{0,192},{65,1},{129,65},{193,129},{1,193... | collective-permute-start | bytes 638984 | tf_op jit(solution)/shard_map/ppermute | solution.py:69
  6.2 8.5 %collective-permute-start.1 = (bf16[13,2,32,128]{3,2,1,0:T(8,128)(2,1)S(1)}, bf16[13,2,32,128]{3,2,1,0:T(8,128)(2,1)S(1)}, u32[]{:S(2)}, u32[]{:S(2)}) collective-permute-start(bf16[13,2,32,128]{3,2,1,0:T(8,128)(2,1)S(1)} %get-tuple-element.24), channel_id=1, source_target_pairs={{128,0},{192,64},{0,128},{64,192},{129,1},{193,65},{1,129},{65,193... | collective-permute-start | bytes 638984 | tf_op jit(solution)/shard_map/ppermute | solution.py:69
  6.8 12.7 %collective-permute-start.2 = (bf16[13,2,32,128]{3,2,1,0:T(8,128)(2,1)S(1)}, bf16[13,2,32,128]{3,2,1,0:T(8,128)(2,1)S(1)}, u32[]{:S(2)}, u32[]{:S(2)}) collective-permute-start(bf16[13,2,32,128]{3,2,1,0:T(8,128)(2,1)S(1)} %get-tuple-element.25), channel_id=1, source_target_pairs={{192,0},{0,64},{64,128},{128,192},{193,1},{1,65},{65,129},{129,193... | collective-permute-start | bytes 638984 | tf_op jit(solution)/shard_map/ppermute | solution.py:69
  19.8 23.5 %collective-permute-start.3 = (bf16[16,128,128]{2,1,0:T(8,128)(2,1)S(1)}, bf16[16,128,128]{2,1,0:T(8,128)(2,1)S(1)}, u32[]{:S(2)}, u32[]{:S(2)}) collective-permute-start(bf16[16,128,128]{2,1,0:T(8,128)(2,1)S(1)} %get-tuple-element.27), channel_id=1, source_target_pairs={{20,0},{84,64},{148,128},{212,192},{21,1},{85,65},{149,129},{213,1... | collective-permute-start | bytes 1572872 | tf_op jit(solution)/shard_map/ppermute | solution.py:69
  29.6 45.4 %collective-permute-start.4 = (bf16[16,128,128]{2,1,0:T(8,128)(2,1)S(1)}, bf16[16,128,128]{2,1,0:T(8,128)(2,1)S(1)}, u32[]{:S(2)}, u32[]{:S(2)}) collective-permute-start(bf16[16,128,128]{2,1,0:T(8,128)(2,1)S(1)} %get-tuple-element.28), channel_id=1, source_target_pairs={{44,0},{108,64},{172,128},{236,192},{45,1},{109,65},{173,129},{237... | collective-permute-start | bytes 1572872 | tf_op jit(solution)/shard_map/ppermute | solution.py:69
  29.6 71.7 %collective-permute-start.5 = (bf16[17,128,128]{2,1,0:T(8,128)(2,1)S(1)}, bf16[17,128,128]{2,1,0:T(8,128)(2,1)S(1)}, u32[]{:S(2)}, u32[]{:S(2)}) collective-permute-start(bf16[17,128,128]{2,1,0:T(8,128)(2,1)S(1)} %get-tuple-element.29), channel_id=1, source_target_pairs={{255,0},{0,64},{64,128},{128,192},{192,1},{1,65},{65,129},{129,193... | collective-permute-start | bytes 1671176 | tf_op jit(solution)/shard_map/ppermute | solution.py:69
  29.6 71.7 %collective-permute-start.6 = (bf16[17,128,128]{2,1,0:T(8,128)(2,1)S(1)}, bf16[17,128,128]{2,1,0:T(8,128)(2,1)S(1)}, u32[]{:S(2)}, u32[]{:S(2)}) collective-permute-start(bf16[17,128,128]{2,1,0:T(8,128)(2,1)S(1)} %get-tuple-element.30), channel_id=1, source_target_pairs={{64,0},{128,64},{192,128},{1,192},{65,1},{129,65},{193,129},{2,193... | collective-permute-start | bytes 1671176 | tf_op jit(solution)/shard_map/ppermute | solution.py:69
  75.0 26.3 %collective-permute-start.9 = (bf16[12,128,128]{2,1,0:T(8,128)(2,1)S(1)}, bf16[12,128,128]{2,1,0:T(8,128)(2,1)S(1)}, u32[]{:S(2)}, u32[]{:S(2)}) collective-permute-start(bf16[12,128,128]{2,1,0:T(8,128)(2,1)S(1)} %get-tuple-element.33), channel_id=1, source_target_pairs={{255,0},{0,64},{64,128},{128,192},{192,1},{1,65},{65,129},{129,193... | collective-permute-start | bytes 1179656 | tf_op jit(solution)/shard_map/ppermute | solution.py:69
  75.1 26.2 %collective-permute-start.10 = (bf16[12,128,128]{2,1,0:T(8,128)(2,1)S(1)}, bf16[12,128,128]{2,1,0:T(8,128)(2,1)S(1)}, u32[]{:S(2)}, u32[]{:S(2)}) collective-permute-start(bf16[12,128,128]{2,1,0:T(8,128)(2,1)S(1)} %get-tuple-element.34), channel_id=1, source_target_pairs={{64,0},{128,64},{192,128},{1,192},{65,1},{129,65},{193,129},{2,193... | collective-permute-start | bytes 1179656 | tf_op jit(solution)/shard_map/ppermute | solution.py:69
  80.2 11.1 %collective-permute-start.7 = (bf16[4,128,128]{2,1,0:T(8,128)(2,1)S(1)}, bf16[4,128,128]{2,1,0:T(8,128)(2,1)S(1)}, u32[]{:S(2)}, u32[]{:S(2)}) collective-permute-start(bf16[4,128,128]{2,1,0:T(8,128)(2,1)S(1)} %get-tuple-element.31), channel_id=1, source_target_pairs={{191,0},{255,64},{0,128},{64,192},{128,1},{192,65},{1,129},{65,193... | collective-permute-start | bytes 393224 | tf_op jit(solution)/shard_map/ppermute | solution.py:69
  91.2 10.1 %collective-permute-start.8 = (bf16[4,128,128]{2,1,0:T(8,128)(2,1)S(1)}, bf16[4,128,128]{2,1,0:T(8,128)(2,1)S(1)}, u32[]{:S(2)}, u32[]{:S(2)}) collective-permute-start(bf16[4,128,128]{2,1,0:T(8,128)(2,1)S(1)} %get-tuple-element.32), channel_id=1, source_target_pairs={{128,0},{192,64},{1,128},{65,192},{129,1},{193,65},{2,129},{66,193... | collective-permute-start | bytes 393224 | tf_op jit(solution)/shard_map/ppermute | solution.py:69
  107.1 19.9 %collective-permute-start.11 = (bf16[13,2,32,128]{3,2,1,0:T(8,128)(2,1)S(1)}, bf16[13,2,32,128]{3,2,1,0:T(8,128)(2,1)S(1)}, u32[]{:S(2)}, u32[]{:S(2)}) collective-permute-start(bf16[13,2,32,128]{3,2,1,0:T(8,128)(2,1)S(1)} %get-tuple-element.36), channel_id=1, source_target_pairs={{64,0},{128,64},{192,128},{0,192},{65,1},{129,65},{193,129},{1,193... | collective-permute-start | bytes 638984 | tf_op jit(solution)/shard_map/ppermute | solution.py:69
  117.8 9.1 %collective-permute-start.12 = (bf16[13,2,32,128]{3,2,1,0:T(8,128)(2,1)S(1)}, bf16[13,2,32,128]{3,2,1,0:T(8,128)(2,1)S(1)}, u32[]{:S(2)}, u32[]{:S(2)}) collective-permute-start(bf16[13,2,32,128]{3,2,1,0:T(8,128)(2,1)S(1)} %get-tuple-element.37), channel_id=1, source_target_pairs={{128,0},{192,64},{0,128},{64,192},{129,1},{193,65},{1,129},{65,193... | collective-permute-start | bytes 638984 | tf_op jit(solution)/shard_map/ppermute | solution.py:69
  117.8 12.6 %collective-permute-start.13 = (bf16[13,2,32,128]{3,2,1,0:T(8,128)(2,1)S(1)}, bf16[13,2,32,128]{3,2,1,0:T(8,128)(2,1)S(1)}, u32[]{:S(2)}, u32[]{:S(2)}) collective-permute-start(bf16[13,2,32,128]{3,2,1,0:T(8,128)(2,1)S(1)} %get-tuple-element.38), channel_id=1, source_target_pairs={{192,0},{0,64},{64,128},{128,192},{193,1},{1,65},{65,129},{129,193... | collective-permute-start | bytes 638984 | tf_op jit(solution)/shard_map/ppermute | solution.py:69

commit v2 on v1

--- a/solution.py
+++ b/solution.py
@@ -41,23 +41,40 @@
     return sorted(found)
 
 
-def tiles_of(rows):
-    return [
-        (t, b)
-        for t in range(2)
-        for b in sorted(set().union(*(needed(j) for j in rows[t])))
-    ]
-
-
-LOW = (-1, tiles_of(([-2], [-1])))
-HIGH = (1, tiles_of(([2], [3])))
-LOWER = (-2, tiles_of(([], [-3])))
-HIGHER = (2, tiles_of(([4], [])))
-PLUS = (FAR_PAIRS, tiles_of(([FAR, FAR + 2], [FAR + 1, FAR - 1])))
-MINUS = (-FAR_PAIRS, tiles_of(([-FAR, -FAR + 2], [-FAR + 1, -FAR - 1])))
-DIRECT = [PLUS, MINUS, LOW, HIGH, LOWER, HIGHER]
-FAR_LOW = [(0, 1, b) for b in needed(FAR - 1)] + [(1, 1, b) for b in needed(-FAR - 1)]
-FAR_HIGH = [(0, 0, b) for b in needed(FAR + 2)] + [(1, 0, b) for b in needed(-FAR + 2)]
+BANDS = range(2 * BAND + 1)
+SHARED = sorted(b for b in set().union(*(needed(FAR + t) for t in range(-1, 3))) if b in BANDS)
+
+
+def band_of(j):
+    return [b for b in needed(j) if b in BANDS]
+
+
+def far_of(j):
+    return [b for b in needed(j) if b not in BANDS]
+
+
+def tiles(rows, which=needed):
+    return [(j, b) for j in rows for b in which(j)]
+
+
+OWN = [(t, b) for b in range(DIAGS) for t in range(2)]
+LOW, HIGH = tiles([-2, -1]), tiles([2, 3])
+LOWER, HIGHER = tiles([-3]), tiles([4])
+PLUS_BAND = tiles(range(FAR - 1, FAR + 3), band_of)
+MINUS_BAND = tiles(range(-FAR - 1, -FAR + 3), band_of)
+PLUS_FAR = tiles([FAR, FAR + 1], far_of)
+MINUS_FAR = tiles([-FAR, -FAR + 1], far_of)
+LOW_FAR = tiles([FAR - 1, -FAR - 1], far_of)
+HIGH_FAR = tiles([FAR + 2, -FAR + 2], far_of)
+ARRIVE = [
+    OWN, LOW, HIGH, LOWER, HIGHER, PLUS_BAND, MINUS_BAND,
+    PLUS_FAR, MINUS_FAR, LOW_FAR, HIGH_FAR,
+]
+assert [(j - FAR, b) for j, b in PLUS_BAND] == [(j + FAR, b) for j, b in MINUS_BAND]
+NEAR = [[(j % 2, b) for j, b in message] for message in (LOW, HIGH, LOWER, HIGHER)]
+DIRECT = [[(j % 2, b) for j, b in message] for message in (PLUS_FAR, MINUS_FAR)]
+EDGE_LOW = [(1, b) for b in band_of(FAR - 1)]
+EDGE_HIGH = [(0, b) for b in band_of(FAR + 2)]
 
 
 def place_of(p):
@@ -69,12 +86,33 @@
     return lax.ppermute(x, AXES, route)
 
 
+def across(p):
+    cols = LAYERS * 8
+    return p - p % cols + (p + cols // 2) % cols
+
+
 def from_pair(x, distance):
     return moved(x, lambda p: (p + distance) % PAIRS)
 
 
+def same_group(p, distance):
+    return p - p % LAYERS + (p + distance) % LAYERS
+
+
 def from_layer(x, distance):
-    return moved(x, lambda p: p - p % LAYERS + (p + distance) % LAYERS)
+    return moved(x, lambda p: same_group(p, distance))
+
+
+def from_layer_across(x, distance):
+    return moved(x, lambda p: across(same_group(p, distance)))
+
+
+def edge_across(x, distance):
+    return moved(x, lambda p: across((across(p) + distance) % PAIRS))
+
+
+def far_across(x, distance):
+    return moved(x, lambda p: across((p + distance) % PAIRS))
 
 
 def bf16(*shape):
@@ -101,63 +139,75 @@
 
 def split_body(me_ref, presence_ref, blocks_ref, *out_refs):
     me = me_ref[0]
-    for s, out_ref in enumerate(out_refs):
+    for s in range(LAYERS):
+        own_ref, shared_ref = out_refs[s], out_refs[LAYERS + s]
         other = lax.rem(me - s + LAYERS, LAYERS)
         for t in range(2):
             row = 2 * other + t
             for d in range(DIAGS):
                 tile = blocks_ref[d, row]
                 present = presence_ref[d, row] != 0
-                out_ref[d, t] = jnp.where(present, tile, jnp.zeros_like(tile))
-
-
-def pack_body(me_ref, *refs):
-    me = me_ref[0]
-    pieces, own_ref, out_refs = refs[:LAYERS], refs[LAYERS], refs[LAYERS + 1 :]
+                tile = jnp.where(present, tile, jnp.zeros_like(tile))
+                own_ref[d, t] = tile
+                if d in SHARED:
+                    shared_ref[SHARED.index(d), t] = tile
+
+
+def gather_pieces(me, pieces, out_ref):
     for s, piece in enumerate(pieces):
         other = lax.rem(me + s, LAYERS)
         start = pl.multiple_of(other * (BS // LAYERS), BS // LAYERS)
-        own_ref[:, :, pl.ds(start, BS // LAYERS), :] = piece[...]
-    for (_, tiles), out_ref in zip(DIRECT, out_refs):
-        for k, (t, b) in enumerate(tiles):
+        out_ref[:, :, pl.ds(start, BS // LAYERS), :] = piece[...]
+
+
+def pack_body(me_ref, *refs):
+    pieces, own_ref, out_refs = refs[:LAYERS], refs[LAYERS], refs[LAYERS + 1 :]
+    gather_pieces(me_ref[0], pieces, own_ref)
+    for message, out_ref in zip(DIRECT + NEAR, out_refs):
+        for k, (t, b) in enumerate(message):
             out_ref[k] = own_ref[b, t]
 
 
+def edge_body(me_ref, *refs):
+    pieces, shared_ref, out_refs = refs[:LAYERS], refs[LAYERS], refs[LAYERS + 1 :]
+    gather_pieces(me_ref[0], pieces, shared_ref)
+    for message, out_ref in zip((EDGE_LOW, EDGE_HIGH), out_refs):
+        for k, (t, b) in enumerate(message):
+            out_ref[k] = shared_ref[SHARED.index(b), t]
+
+
+def fan_body(shared_ref, low_ref, high_ref, out_ref):
+    for k, (j, b) in enumerate(PLUS_BAND):
+        t = j - FAR
+        if t < 0:
+            out_ref[k] = low_ref[EDGE_LOW.index((1, b))]
+        elif t > 1:
+            out_ref[k] = high_ref[EDGE_HIGH.index((0, b))]
+        else:
+            out_ref[k] = shared_ref[SHARED.index(b), t]
+
+
 def far_body(plus_ref, minus_ref, low_ref, high_ref):
-    sources = ((plus_ref, PLUS[1]), (minus_ref, MINUS[1]))
-    for message, out_ref in ((FAR_LOW, low_ref), (FAR_HIGH, high_ref)):
-        for k, (which, t, b) in enumerate(message):
-            ref, tiles = sources[which]
-            out_ref[k] = ref[tiles.index((t, b))]
+    for shift, message, out_ref in ((2, LOW_FAR, low_ref), (-2, HIGH_FAR, high_ref)):
+        for k, (j, b) in enumerate(message):
+            if j > 0:
+                out_ref[k] = plus_ref[PLUS_FAR.index((j + shift, b))]
+            else:
+                out_ref[k] = minus_ref[MINUS_FAR.index((j + shift, b))]
 
 
 def placements():
     found = {}
-
-    def place(operand, index, j, b):
-        row, column = SLOT[j % NBG], SLOT[(j + OFFSETS[b]) % NBG]
-        found[row, column] = (operand, index)
-
-    for t in range(2):
-        for b in range(DIAGS):
-            place(0, (b, t), t, b)
-    for operand, (distance, tiles) in enumerate(DIRECT):
-        for k, (t, b) in enumerate(tiles):
-            j = 2 * distance + t
-            if b in needed(j):
-                place(1 + operand, k, j, b)
-    for operand, message, rows in (
-        (7, FAR_LOW, (FAR - 1, -FAR - 1)),
-        (8, FAR_HIGH, (FAR + 2, -FAR + 2)),
-    ):
-        for k, (which, t, b) in enumerate(message):
-            place(operand, k, rows[which], b)
+    for operand, message in enumerate(ARRIVE):
+        for k, (j, b) in enumerate(message):
+            column = SLOT[(j + OFFSETS[b]) % NBG]
+            found[SLOT[j % NBG], column] = (operand, k if operand else (b, j))
     return found
 
 
 def purify_body(me_ref, presence_ref, *refs):
-    sources, outs = refs[:9], refs[9:13]
-    right_ref, left_ref, result_ref = refs[13:]
+    sources, outs = refs[: len(ARRIVE)], refs[len(ARRIVE) : len(ARRIVE) + LAYERS]
+    right_ref, left_ref, result_ref = refs[len(ARRIVE) + LAYERS :]
     me = me_ref[0]
     own_ref = sources[0]
     placed = placements()
@@ -240,33 +290,51 @@
 def per_device(blocks, presence):
     me = lax.axis_index("layer").astype(jnp.int32).reshape(1)
     quarter = bf16(DIAGS, 2, BS // LAYERS, BS)
-    tiles = [bf16(len(message), BS, BS) for _, message in DIRECT]
-
-    pieces = call(split_body, [quarter] * LAYERS, 2, 1)(me, presence, blocks)
+    shared_quarter = bf16(len(SHARED), 2, BS // LAYERS, BS)
+
+    def packed(messages):
+        return [bf16(len(message), BS, BS) for message in messages]
+
+    pieces = call(split_body, [quarter] * LAYERS + [shared_quarter] * LAYERS, 2, 1)(
+        me, presence, blocks
+    )
+    shared = [from_layer_across(pieces[LAYERS + s], s) for s in range(LAYERS)]
     pieces = [pieces[0]] + [from_layer(pieces[s], s) for s in range(1, LAYERS)]
-    own, *messages = call(
-        pack_body, [bf16(DIAGS, 2, BS, BS)] + tiles, 1, LAYERS
+    shared, edge_low, edge_high = call(
+        edge_body,
+        [bf16(len(SHARED), 2, BS, BS)] + packed([EDGE_LOW, EDGE_HIGH]),
+        1,
+        LAYERS,
+    )(me, *shared)
+    edge_low, edge_high = edge_across(edge_low, -1), edge_across(edge_high, 1)
+    own, plus_far, minus_far, low, high, lower, higher = call(
+        pack_body, [bf16(DIAGS, 2, BS, BS)] + packed(DIRECT + NEAR), 1, LAYERS
     )(me, *pieces)
-    arrived = [
-        from_pair(message, distance)
-        for message, (distance, _) in zip(messages, DIRECT)
-    ]
-    far_low, far_high = call(
-        far_body, [bf16(len(FAR_LOW), BS, BS), bf16(len(FAR_HIGH), BS, BS)], 0, 2
-    )(arrived[0], arrived[1])
-    far_low, far_high = from_pair(far_low, -1), from_pair(far_high, 1)
+    plus_far = from_pair(plus_far, FAR_PAIRS)
+    minus_far = from_pair(minus_far, -FAR_PAIRS)
+    low, high = from_pair(low, -1), from_pair(high, 1)
+    lower, higher = from_pair(lower, -2), from_pair(higher, 2)
+    band = call(fan_body, packed([PLUS_BAND])[0], 0, 3)(shared, edge_low, edge_high)
+    plus_band, minus_band = far_across(band, FAR_PAIRS), far_across(band, -FAR_PAIRS)
+    low_far, high_far = call(far_body, packed([LOW_FAR, HIGH_FAR]), 0, 2)(
+        plus_far, minus_far
+    )
+    low_far, high_far = from_pair(low_far, -1), from_pair(high_far, 1)
     results = call(
         purify_body,
         [quarter] * LAYERS,
         2,
-        9,
+        len(ARRIVE),
         scratch=[
             pltpu.VMEM((WIDTH, WIDTH), jnp.bfloat16),
             pltpu.VMEM((2 * BS, WIDTH), jnp.bfloat16),
             pltpu.VMEM((DIAGS, 2, BS, BS), jnp.bfloat16),
         ],
         flops=4 * 224 * 2 * BS**3,
-    )(me, presence, own, *arrived, far_low, far_high)
+    )(
+        me, presence, own, low, high, lower, higher, plus_band, minus_band,
+        plus_far, minus_far, low_far, high_far,
+    )
     results = [results[0]] + [from_layer(results[s], s) for s in range(1, LAYERS)]
     return call(join_body, bf16(DIAGS, 2 * LAYERS, BS // LAYERS, BS), 1, LAYERS)(
         me, *results

time: 132 us -> 122 us (0.924)
  the two profiles are of different devices: /device:TPU:1 before, /device:TPU:9 now
where the time goes in v2:
time: 122 us
  waiting for transfers between devices  62.2 us (51%)
  starting transfers between devices  49.7 us (41%)
  Pallas kernels  7.97 us (7%)
  local copies, waits for them, and re-layouts  1.92 us (2%)
    ppermute x22, waiting for transfers between devices, moved(): return lax.ppermute(x, AXES, route)  62.2 us
    ppermute x22, starting transfers between devices, moved(): return lax.ppermute(x, AXES, route)  49.7 us
    pallas_call x1, Pallas kernels, per_device(): call(purify_body, [quarter] * LAYERS, 2, len(ARRIVE), scratch=[pltpu.VMEM...  5.76 us
  transfers between devices with their start and end apart: 22, of which 10 were waited for; matrix products, arithmetic and copies ran while one was open for 0% of the time, Pallas kernels for 0%

profile of v2, /device:TPU:9, one launch (start us, length us, event | category | flops | bytes accessed | tf_op | source)
XLA Modules:
  0.0 121.9 jit_solution(986409419483539792)
XLA Ops:
  0.0 0.0 copy-start.1
  0.0 0.7 copy-done.1
  0.7 0.1 copy.4.presence_ref
  0.8 0.0 copy-start
  0.8 1.2 copy-done
  1.9 0.9 shard_map.28
  2.9 2.6 %collective-permute-start = (bf16[13,2,32,128]{3,2,1,0:T(8,128)(2,1)S(1)}, bf16[13,2,32,128]{3,2,1,0:T(8,128)(2,1)S(1)}, u32[]{:S(2)}, u32[]{:S(2)}) collective-permute-start(bf16[13,2,32,128]{3,2,1,0:T(8,128)(2,1)S(1)} %get-tuple-element.30), channel_id=1, source_target_pairs={{64,0},{128,64},{192,128},{0,192},{65,1},{129,65},{193,129},{1,193... | collective-permute-start | bytes 638984 | tf_op jit(solution)/shard_map/ppermute | solution.py:86
  5.4 0.5 collective-permute-start.1
  6.0 0.6 collective-permute-start.2
  6.6 6.9 %collective-permute-start.7 = (bf16[5,2,32,128]{3,2,1,0:T(8,128)(2,1)S(1)}, bf16[5,2,32,128]{3,2,1,0:T(8,128)(2,1)S(1)}, u32[]{:S(2)}, u32[]{:S(2)}) collective-permute-start(bf16[5,2,32,128]{3,2,1,0:T(8,128)(2,1)S(1)} %get-tuple-element.38), channel_id=1, source_target_pairs={{4,0},{68,64},{132,128},{196,192},{5,1},{69,65},{133,129},{197,193... | collective-permute-start | bytes 245768 | tf_op jit(solution)/shard_map/ppermute | solution.py:86
  13.5 1.8 %collective-permute-start.8 = (bf16[5,2,32,128]{3,2,1,0:T(8,128)(2,1)S(1)}, bf16[5,2,32,128]{3,2,1,0:T(8,128)(2,1)S(1)}, u32[]{:S(2)}, u32[]{:S(2)}) collective-permute-start(bf16[5,2,32,128]{3,2,1,0:T(8,128)(2,1)S(1)} %get-tuple-element.39), channel_id=1, source_target_pairs={{68,0},{132,64},{196,128},{4,192},{69,1},{133,65},{197,129},{5,193... | collective-permute-start | bytes 245768 | tf_op jit(solution)/shard_map/ppermute | solution.py:86
  15.3 0.1 collective-permute-done.7.refs_0_
  15.4 7.3 %collective-permute-start.9 = (bf16[5,2,32,128]{3,2,1,0:T(8,128)(2,1)S(1)}, bf16[5,2,32,128]{3,2,1,0:T(8,128)(2,1)S(1)}, u32[]{:S(2)}, u32[]{:S(2)}) collective-permute-start(bf16[5,2,32,128]{3,2,1,0:T(8,128)(2,1)S(1)} %get-tuple-element.40), channel_id=1, source_target_pairs={{132,0},{196,64},{4,128},{68,192},{133,1},{197,65},{5,129},{69,193... | collective-permute-start | bytes 245768 | tf_op jit(solution)/shard_map/ppermute | solution.py:86
  22.7 0.0 collective-permute-done.8.refs_1_
  22.7 1.5 %collective-permute-start.10 = (bf16[5,2,32,128]{3,2,1,0:T(8,128)(2,1)S(1)}, bf16[5,2,32,128]{3,2,1,0:T(8,128)(2,1)S(1)}, u32[]{:S(2)}, u32[]{:S(2)}) collective-permute-start(bf16[5,2,32,128]{3,2,1,0:T(8,128)(2,1)S(1)} %get-tuple-element.41), channel_id=1, source_target_pairs={{196,0},{4,64},{68,128},{132,192},{197,1},{5,65},{69,129},{133,193... | collective-permute-start | bytes 245768 | tf_op jit(solution)/shard_map/ppermute | solution.py:86
  24.1 1.2 collective-permute-done.9.refs_2_
  25.3 6.7 %collective-permute-done.10.refs_3_ = bf16[5,2,32,128]{3,2,1,0:T(8,128)(2,1)S(1)} collective-permute-done((bf16[5,2,32,128]{3,2,1,0:T(8,128)(2,1)S(1)}, bf16[5,2,32,128]{3,2,1,0:T(8,128)(2,1)S(1)}, u32[]{:S(2)}, u32[]{:S(2)}) %collective-permute-start.10) | collective-permute-done | bytes 81952 | tf_op jit(solution)/shard_map/ppermute | solution.py:86
  32.0 0.0 collective-permute-done.refs_1_
  32.0 0.0 collective-permute-done.1.refs_2_
  32.1 0.0 collective-permute-done.2.refs_3_
  32.1 0.2 shard_map.29
  32.3 0.1 collective-permute-start.5
  32.4 1.9 %collective-permute-start.11 = (bf16[3,128,128]{2,1,0:T(8,128)(2,1)S(1)}, bf16[3,128,128]{2,1,0:T(8,128)(2,1)S(1)}, u32[]{:S(2)}, u32[]{:S(2)}) collective-permute-start(bf16[3,128,128]{2,1,0:T(8,128)(2,1)S(1)} %get-tuple-element.43), channel_id=1, source_target_pairs={{199,0},{0,64},{64,128},{128,192},{192,1},{1,65},{65,129},{129,193... | collective-permute-start | bytes 294920 | tf_op jit(solution)/shard_map/ppermute | solution.py:86
  34.2 6.1 %collective-permute-start.15 = (bf16[6,128,128]{2,1,0:T(8,128)(2,1)S(1)}, bf16[6,128,128]{2,1,0:T(8,128)(2,1)S(1)}, u32[]{:S(2)}, u32[]{:S(2)}) collective-permute-start(bf16[6,128,128]{2,1,0:T(8,128)(2,1)S(1)} %get-tuple-element.45), channel_id=1, source_target_pairs={{20,0},{84,64},{148,128},{212,192},{21,1},{85,65},{149,129},{213,1... | collective-permute-start | bytes 589832 | tf_op jit(solution)/shard_map/ppermute | solution.py:86
  40.3 0.2 collective-permute-start.16
  40.5 10.9 %collective-permute-start.12 = (bf16[3,128,128]{2,1,0:T(8,128)(2,1)S(1)}, bf16[3,128,128]{2,1,0:T(8,128)(2,1)S(1)}, u32[]{:S(2)}, u32[]{:S(2)}) collective-permute-start(bf16[3,128,128]{2,1,0:T(8,128)(2,1)S(1)} %get-tuple-element.44), channel_id=1, source_target_pairs={{64,0},{128,64},{192,128},{1,192},{65,1},{129,65},{193,129},{2,193... | collective-permute-start | bytes 294920 | tf_op jit(solution)/shard_map/ppermute | solution.py:86
  51.5 12.2 %collective-permute-done.11.low_ref = bf16[3,128,128]{2,1,0:T(8,128)(2,1)S(1)} collective-permute-done((bf16[3,128,128]{2,1,0:T(8,128)(2,1)S(1)}, bf16[3,128,128]{2,1,0:T(8,128)(2,1)S(1)}, u32[]{:S(2)}, u32[]{:S(2)}) %collective-permute-start.11) | collective-permute-done | bytes 98336 | tf_op jit(solution)/shard_map/ppermute | solution.py:86
  63.7 0.0 collective-permute-start.3
  63.7 0.0 collective-permute-done.12.high_ref
  63.7 5.1 %collective-permute-start.4 = (bf16[17,128,128]{2,1,0:T(8,128)(2,1)S(1)}, bf16[17,128,128]{2,1,0:T(8,128)(2,1)S(1)}, u32[]{:S(2)}, u32[]{:S(2)}) collective-permute-start(bf16[17,128,128]{2,1,0:T(8,128)(2,1)S(1)} %get-tuple-element.35), channel_id=1, source_target_pairs={{64,0},{128,64},{192,128},{1,192},{65,1},{129,65},{193,129},{2,193... | collective-permute-start | bytes 1671176 | tf_op jit(solution)/shard_map/ppermute | solution.py:86
  68.7 0.0 collective-permute-done.5.refs_3_
  68.7 0.0 collective-permute-start.6
  68.8 0.0 collective-permute-done.15.plus_ref.refs_7_
  68.8 0.7 collective-permute-start.14
  69.5 0.0 collective-permute-done.16.minus_ref.refs_8_
  69.5 0.8 collective-permute-start.13
  70.3 15.7 %collective-permute-done.6.refs_4_ = bf16[4,128,128]{2,1,0:T(8,128)(2,1)S(1)} collective-permute-done((bf16[4,128,128]{2,1,0:T(8,128)(2,1)S(1)}, bf16[4,128,128]{2,1,0:T(8,128)(2,1)S(1)}, u32[]{:S(2)}, u32[]{:S(2)}) %collective-permute-start.6) | collective-permute-done | bytes 131104 | tf_op jit(solution)/shard_map/ppermute | solution.py:86
  86.0 0.0 collective-permute-start.17
  86.0 9.1 %collective-permute-done.17.refs_9_ = bf16[6,128,128]{2,1,0:T(8,128)(2,1)S(1)} collective-permute-done((bf16[6,128,128]{2,1,0:T(8,128)(2,1)S(1)}, bf16[6,128,128]{2,1,0:T(8,128)(2,1)S(1)}, u32[]{:S(2)}, u32[]{:S(2)}) %collective-permute-start.17) | collective-permute-done | bytes 196640 | tf_op jit(solution)/shard_map/ppermute | solution.py:86
  95.1 1.3 %collective-permute-start.18 = (bf16[6,128,128]{2,1,0:T(8,128)(2,1)S(1)}, bf16[6,128,128]{2,1,0:T(8,128)(2,1)S(1)}, u32[]{:S(2)}, u32[]{:S(2)}) collective-permute-start(bf16[6,128,128]{2,1,0:T(8,128)(2,1)S(1)} %get-tuple-element.48), channel_id=1, source_target_pairs={{64,0},{128,64},{192,128},{1,192},{65,1},{129,65},{193,129},{2,193... | collective-permute-start | bytes 589832 | tf_op jit(solution)/shard_map/ppermute | solution.py:86
  96.4 5.3 %collective-permute-done.18.refs_10_ = bf16[6,128,128]{2,1,0:T(8,128)(2,1)S(1)} collective-permute-done((bf16[6,128,128]{2,1,0:T(8,128)(2,1)S(1)}, bf16[6,128,128]{2,1,0:T(8,128)(2,1)S(1)}, u32[]{:S(2)}, u32[]{:S(2)}) %collective-permute-start.18) | collective-permute-done | bytes 196640 | tf_op jit(solution)/shard_map/ppermute | solution.py:86
  101.8 0.0 collective-permute-done.14.refs_6_
  101.8 0.0 collective-permute-done.13.refs_5_
  101.8 0.0 collective-permute-done.3.refs_1_
  101.8 0.0 collective-permute-done.4.refs_2_
  101.8 5.8 %shard_map.33 = (bf16[13,2,32,128]{3,2,1,0:T(8,128)(2,1)S(1)}, bf16[13,2,32,128]{3,2,1,0:T(8,128)(2,1)S(1)}, bf16[13,2,32,128]{3,2,1,0:T(8,128)(2,1)S(1)}, bf16[13,2,32,128]{3,2,1,0:T(8,128)(2,1)S(1)}) custom-call(s32[1]{0:T(128)} %bitcast.me_ref, s32[13,8]{1,0:T(8,128)S(1)} %copy.4.presence_ref, bf16[13,2,128,128]{3,2,1,0:T(8,128)(2,1)S(1)} %get-tuple-element.33.refs_0_, ...), custom_call_target="tpu_custom_call" | custom-call | flops 3758096384 | bytes 4194304 | tf_op jit(solution)/shard_map/pallas_call | solution.py:323
  107.6 0.1 collective-permute-start.19
  107.7 1.0 collective-permute-start.20
  108.7 0.4 collective-permute-start.21
  109.1 4.7 %collective-permute-done.19.refs_1_ = bf16[13,2,32,128]{3,2,1,0:T(8,128)(2,1)S(1)} collective-permute-done((bf16[13,2,32,128]{3,2,1,0:T(8,128)(2,1)S(1)}, bf16[13,2,32,128]{3,2,1,0:T(8,128)(2,1)S(1)}, u32[]{:S(2)}, u32[]{:S(2)}) %collective-permute-start.19) | collective-permute-done | bytes 213024 | tf_op jit(solution)/shard_map/ppermute | solution.py:86
  113.8 1.6 %collective-permute-done.20.refs_2_ = bf16[13,2,32,128]{3,2,1,0:T(8,128)(2,1)S(1)} collective-permute-done((bf16[13,2,32,128]{3,2,1,0:T(8,128)(2,1)S(1)}, bf16[13,2,32,128]{3,2,1,0:T(8,128)(2,1)S(1)}, u32[]{:S(2)}, u32[]{:S(2)}) %collective-permute-start.20) | collective-permute-done | bytes 213024 | tf_op jit(solution)/shard_map/ppermute | solution.py:86
  115.4 5.6 %collective-permute-done.21.refs_3_ = bf16[13,2,32,128]{3,2,1,0:T(8,128)(2,1)S(1)} collective-permute-done((bf16[13,2,32,128]{3,2,1,0:T(8,128)(2,1)S(1)}, bf16[13,2,32,128]{3,2,1,0:T(8,128)(2,1)S(1)}, u32[]{:S(2)}, u32[]{:S(2)}) %collective-permute-start.21) | collective-permute-done | bytes 213024 | tf_op jit(solution)/shard_map/ppermute | solution.py:86
  121.0 1.0 shard_map.34
  (3 shorter events, 0.1 us)
Async XLA Ops:
  0.0 0.7 copy-start.1
  0.8 1.2 copy-start
  2.9 29.2 %collective-permute-start = (bf16[13,2,32,128]{3,2,1,0:T(8,128)(2,1)S(1)}, bf16[13,2,32,128]{3,2,1,0:T(8,128)(2,1)S(1)}, u32[]{:S(2)}, u32[]{:S(2)}) collective-permute-start(bf16[13,2,32,128]{3,2,1,0:T(8,128)(2,1)S(1)} %get-tuple-element.30), channel_id=1, source_target_pairs={{64,0},{128,64},{192,128},{0,192},{65,1},{129,65},{193,129},{1,193... | collective-permute-start | bytes 638984 | tf_op jit(solution)/shard_map/ppermute | solution.py:86
  5.4 26.6 %collective-permute-start.1 = (bf16[13,2,32,128]{3,2,1,0:T(8,128)(2,1)S(1)}, bf16[13,2,32,128]{3,2,1,0:T(8,128)(2,1)S(1)}, u32[]{:S(2)}, u32[]{:S(2)}) collective-permute-start(bf16[13,2,32,128]{3,2,1,0:T(8,128)(2,1)S(1)} %get-tuple-element.31), channel_id=1, source_target_pairs={{128,0},{192,64},{0,128},{64,192},{129,1},{193,65},{1,129},{65,193... | collective-permute-start | bytes 638984 | tf_op jit(solution)/shard_map/ppermute | solution.py:86
  6.0 26.1 %collective-permute-start.2 = (bf16[13,2,32,128]{3,2,1,0:T(8,128)(2,1)S(1)}, bf16[13,2,32,128]{3,2,1,0:T(8,128)(2,1)S(1)}, u32[]{:S(2)}, u32[]{:S(2)}) collective-permute-start(bf16[13,2,32,128]{3,2,1,0:T(8,128)(2,1)S(1)} %get-tuple-element.32), channel_id=1, source_target_pairs={{192,0},{0,64},{64,128},{128,192},{193,1},{1,65},{65,129},{129,193... | collective-permute-start | bytes 638984 | tf_op jit(solution)/shard_map/ppermute | solution.py:86
  6.6 8.8 %collective-permute-start.7 = (bf16[5,2,32,128]{3,2,1,0:T(8,128)(2,1)S(1)}, bf16[5,2,32,128]{3,2,1,0:T(8,128)(2,1)S(1)}, u32[]{:S(2)}, u32[]{:S(2)}) collective-permute-start(bf16[5,2,32,128]{3,2,1,0:T(8,128)(2,1)S(1)} %get-tuple-element.38), channel_id=1, source_target_pairs={{4,0},{68,64},{132,128},{196,192},{5,1},{69,65},{133,129},{197,193... | collective-permute-start | bytes 245768 | tf_op jit(solution)/shard_map/ppermute | solution.py:86
  13.5 9.2 %collective-permute-start.8 = (bf16[5,2,32,128]{3,2,1,0:T(8,128)(2,1)S(1)}, bf16[5,2,32,128]{3,2,1,0:T(8,128)(2,1)S(1)}, u32[]{:S(2)}, u32[]{:S(2)}) collective-permute-start(bf16[5,2,32,128]{3,2,1,0:T(8,128)(2,1)S(1)} %get-tuple-element.39), channel_id=1, source_target_pairs={{68,0},{132,64},{196,128},{4,192},{69,1},{133,65},{197,129},{5,193... | collective-permute-start | bytes 245768 | tf_op jit(solution)/shard_map/ppermute | solution.py:86
  15.4 9.9 %collective-permute-start.9 = (bf16[5,2,32,128]{3,2,1,0:T(8,128)(2,1)S(1)}, bf16[5,2,32,128]{3,2,1,0:T(8,128)(2,1)S(1)}, u32[]{:S(2)}, u32[]{:S(2)}) collective-permute-start(bf16[5,2,32,128]{3,2,1,0:T(8,128)(2,1)S(1)} %get-tuple-element.40), channel_id=1, source_target_pairs={{132,0},{196,64},{4,128},{68,192},{133,1},{197,65},{5,129},{69,193... | collective-permute-start | bytes 245768 | tf_op jit(solution)/shard_map/ppermute | solution.py:86
  22.7 9.3 %collective-permute-start.10 = (bf16[5,2,32,128]{3,2,1,0:T(8,128)(2,1)S(1)}, bf16[5,2,32,128]{3,2,1,0:T(8,128)(2,1)S(1)}, u32[]{:S(2)}, u32[]{:S(2)}) collective-permute-start(bf16[5,2,32,128]{3,2,1,0:T(8,128)(2,1)S(1)} %get-tuple-element.41), channel_id=1, source_target_pairs={{196,0},{4,64},{68,128},{132,192},{197,1},{5,65},{69,129},{133,193... | collective-permute-start | bytes 245768 | tf_op jit(solution)/shard_map/ppermute | solution.py:86
  32.3 36.5 %collective-permute-start.5 = (bf16[4,128,128]{2,1,0:T(8,128)(2,1)S(1)}, bf16[4,128,128]{2,1,0:T(8,128)(2,1)S(1)}, u32[]{:S(2)}, u32[]{:S(2)}) collective-permute-start(bf16[4,128,128]{2,1,0:T(8,128)(2,1)S(1)} %get-tuple-element.36), channel_id=1, source_target_pairs={{191,0},{255,64},{0,128},{64,192},{128,1},{192,65},{1,129},{65,193... | collective-permute-start | bytes 393224 | tf_op jit(solution)/shard_map/ppermute | solution.py:86
  32.4 31.3 %collective-permute-start.11 = (bf16[3,128,128]{2,1,0:T(8,128)(2,1)S(1)}, bf16[3,128,128]{2,1,0:T(8,128)(2,1)S(1)}, u32[]{:S(2)}, u32[]{:S(2)}) collective-permute-start(bf16[3,128,128]{2,1,0:T(8,128)(2,1)S(1)} %get-tuple-element.43), channel_id=1, source_target_pairs={{199,0},{0,64},{64,128},{128,192},{192,1},{1,65},{65,129},{129,193... | collective-permute-start | bytes 294920 | tf_op jit(solution)/shard_map/ppermute | solution.py:86
  34.2 34.6 %collective-permute-start.15 = (bf16[6,128,128]{2,1,0:T(8,128)(2,1)S(1)}, bf16[6,128,128]{2,1,0:T(8,128)(2,1)S(1)}, u32[]{:S(2)}, u32[]{:S(2)}) collective-permute-start(bf16[6,128,128]{2,1,0:T(8,128)(2,1)S(1)} %get-tuple-element.45), channel_id=1, source_target_pairs={{20,0},{84,64},{148,128},{212,192},{21,1},{85,65},{149,129},{213,1... | collective-permute-start | bytes 589832 | tf_op jit(solution)/shard_map/ppermute | solution.py:86
  40.3 29.2 %collective-permute-start.16 = (bf16[6,128,128]{2,1,0:T(8,128)(2,1)S(1)}, bf16[6,128,128]{2,1,0:T(8,128)(2,1)S(1)}, u32[]{:S(2)}, u32[]{:S(2)}) collective-permute-start(bf16[6,128,128]{2,1,0:T(8,128)(2,1)S(1)} %get-tuple-element.46), channel_id=1, source_target_pairs={{44,0},{108,64},{172,128},{236,192},{45,1},{109,65},{173,129},{237... | collective-permute-start | bytes 589832 | tf_op jit(solution)/shard_map/ppermute | solution.py:86
  40.5 23.2 %collective-permute-start.12 = (bf16[3,128,128]{2,1,0:T(8,128)(2,1)S(1)}, bf16[3,128,128]{2,1,0:T(8,128)(2,1)S(1)}, u32[]{:S(2)}, u32[]{:S(2)}) collective-permute-start(bf16[3,128,128]{2,1,0:T(8,128)(2,1)S(1)} %get-tuple-element.44), channel_id=1, source_target_pairs={{64,0},{128,64},{192,128},{1,192},{65,1},{129,65},{193,129},{2,193... | collective-permute-start | bytes 294920 | tf_op jit(solution)/shard_map/ppermute | solution.py:86
  63.7 38.1 %collective-permute-start.3 = (bf16[17,128,128]{2,1,0:T(8,128)(2,1)S(1)}, bf16[17,128,128]{2,1,0:T(8,128)(2,1)S(1)}, u32[]{:S(2)}, u32[]{:S(2)}) collective-permute-start(bf16[17,128,128]{2,1,0:T(8,128)(2,1)S(1)} %get-tuple-element.34), channel_id=1, source_target_pairs={{255,0},{0,64},{64,128},{128,192},{192,1},{1,65},{65,129},{129,193... | collective-permute-start | bytes 1671176 | tf_op jit(solution)/shard_map/ppermute | solution.py:86
  63.7 38.1 %collective-permute-start.4 = (bf16[17,128,128]{2,1,0:T(8,128)(2,1)S(1)}, bf16[17,128,128]{2,1,0:T(8,128)(2,1)S(1)}, u32[]{:S(2)}, u32[]{:S(2)}) collective-permute-start(bf16[17,128,128]{2,1,0:T(8,128)(2,1)S(1)} %get-tuple-element.35), channel_id=1, source_target_pairs={{64,0},{128,64},{192,128},{1,192},{65,1},{129,65},{193,129},{2,193... | collective-permute-start | bytes 1671176 | tf_op jit(solution)/shard_map/ppermute | solution.py:86
  68.7 17.3 %collective-permute-start.6 = (bf16[4,128,128]{2,1,0:T(8,128)(2,1)S(1)}, bf16[4,128,128]{2,1,0:T(8,128)(2,1)S(1)}, u32[]{:S(2)}, u32[]{:S(2)}) collective-permute-start(bf16[4,128,128]{2,1,0:T(8,128)(2,1)S(1)} %get-tuple-element.37), channel_id=1, source_target_pairs={{128,0},{192,64},{1,128},{65,192},{129,1},{193,65},{2,129},{66,193... | collective-permute-start | bytes 393224 | tf_op jit(solution)/shard_map/ppermute | solution.py:86
  68.8 33.0 %collective-permute-start.14 = (bf16[14,128,128]{2,1,0:T(8,128)(2,1)S(1)}, bf16[14,128,128]{2,1,0:T(8,128)(2,1)S(1)}, u32[]{:S(2)}, u32[]{:S(2)}) collective-permute-start(bf16[14,128,128]{2,1,0:T(8,128)(2,1)S(1)} %shard_map.31), channel_id=1, source_target_pairs={{40,0},{104,64},{168,128},{232,192},{41,1},{105,65},{169,129},{233... | collective-permute-start | bytes 1376264 | tf_op jit(solution)/shard_map/ppermute | solution.py:86
  69.5 32.3 %collective-permute-start.13 = (bf16[14,128,128]{2,1,0:T(8,128)(2,1)S(1)}, bf16[14,128,128]{2,1,0:T(8,128)(2,1)S(1)}, u32[]{:S(2)}, u32[]{:S(2)}) collective-permute-start(bf16[14,128,128]{2,1,0:T(8,128)(2,1)S(1)} %shard_map.31), channel_id=1, source_target_pairs={{16,0},{80,64},{144,128},{208,192},{17,1},{81,65},{145,129},{209,1... | collective-permute-start | bytes 1376264 | tf_op jit(solution)/shard_map/ppermute | solution.py:86
  86.0 9.1 %collective-permute-start.17 = (bf16[6,128,128]{2,1,0:T(8,128)(2,1)S(1)}, bf16[6,128,128]{2,1,0:T(8,128)(2,1)S(1)}, u32[]{:S(2)}, u32[]{:S(2)}) collective-permute-start(bf16[6,128,128]{2,1,0:T(8,128)(2,1)S(1)} %get-tuple-element.47), channel_id=1, source_target_pairs={{255,0},{0,64},{64,128},{128,192},{192,1},{1,65},{65,129},{129,193... | collective-permute-start | bytes 589832 | tf_op jit(solution)/shard_map/ppermute | solution.py:86
  95.1 6.6 %collective-permute-start.18 = (bf16[6,128,128]{2,1,0:T(8,128)(2,1)S(1)}, bf16[6,128,128]{2,1,0:T(8,128)(2,1)S(1)}, u32[]{:S(2)}, u32[]{:S(2)}) collective-permute-start(bf16[6,128,128]{2,1,0:T(8,128)(2,1)S(1)} %get-tuple-element.48), channel_id=1, source_target_pairs={{64,0},{128,64},{192,128},{1,192},{65,1},{129,65},{193,129},{2,193... | collective-permute-start | bytes 589832 | tf_op jit(solution)/shard_map/ppermute | solution.py:86
  107.6 6.2 %collective-permute-start.19 = (bf16[13,2,32,128]{3,2,1,0:T(8,128)(2,1)S(1)}, bf16[13,2,32,128]{3,2,1,0:T(8,128)(2,1)S(1)}, u32[]{:S(2)}, u32[]{:S(2)}) collective-permute-start(bf16[13,2,32,128]{3,2,1,0:T(8,128)(2,1)S(1)} %get-tuple-element.50), channel_id=1, source_target_pairs={{64,0},{128,64},{192,128},{0,192},{65,1},{129,65},{193,129},{1,193... | collective-permute-start | bytes 638984 | tf_op jit(solution)/shard_map/ppermute | solution.py:86
  107.7 7.8 %collective-permute-start.20 = (bf16[13,2,32,128]{3,2,1,0:T(8,128)(2,1)S(1)}, bf16[13,2,32,128]{3,2,1,0:T(8,128)(2,1)S(1)}, u32[]{:S(2)}, u32[]{:S(2)}) collective-permute-start(bf16[13,2,32,128]{3,2,1,0:T(8,128)(2,1)S(1)} %get-tuple-element.51), channel_id=1, source_target_pairs={{128,0},{192,64},{0,128},{64,192},{129,1},{193,65},{1,129},{65,193... | collective-permute-start | bytes 638984 | tf_op jit(solution)/shard_map/ppermute | solution.py:86
  108.7 12.3 %collective-permute-start.21 = (bf16[13,2,32,128]{3,2,1,0:T(8,128)(2,1)S(1)}, bf16[13,2,32,128]{3,2,1,0:T(8,128)(2,1)S(1)}, u32[]{:S(2)}, u32[]{:S(2)}) collective-permute-start(bf16[13,2,32,128]{3,2,1,0:T(8,128)(2,1)S(1)} %get-tuple-element.52), channel_id=1, source_target_pairs={{192,0},{0,64},{64,128},{128,192},{193,1},{1,65},{65,129},{129,193... | collective-permute-start | bytes 638984 | tf_op jit(solution)/shard_map/ppermute | solution.py:86

commit v3 on v2

--- a/solution.py
+++ b/solution.py
@@ -59,22 +59,17 @@
 
 OWN = [(t, b) for b in range(DIAGS) for t in range(2)]
 LOW, HIGH = tiles([-2, -1]), tiles([2, 3])
-LOWER, HIGHER = tiles([-3]), tiles([4])
-PLUS_BAND = tiles(range(FAR - 1, FAR + 3), band_of)
-MINUS_BAND = tiles(range(-FAR - 1, -FAR + 3), band_of)
+FAN = [(t, b) for t in range(2) for b in SHARED]
+PLUS_BAND = [(t + FAR, b) for t, b in FAN]
+MINUS_BAND = [(t - FAR, b) for t, b in FAN]
 PLUS_FAR = tiles([FAR, FAR + 1], far_of)
 MINUS_FAR = tiles([-FAR, -FAR + 1], far_of)
-LOW_FAR = tiles([FAR - 1, -FAR - 1], far_of)
-HIGH_FAR = tiles([FAR + 2, -FAR + 2], far_of)
-ARRIVE = [
-    OWN, LOW, HIGH, LOWER, HIGHER, PLUS_BAND, MINUS_BAND,
-    PLUS_FAR, MINUS_FAR, LOW_FAR, HIGH_FAR,
-]
-assert [(j - FAR, b) for j, b in PLUS_BAND] == [(j + FAR, b) for j, b in MINUS_BAND]
-NEAR = [[(j % 2, b) for j, b in message] for message in (LOW, HIGH, LOWER, HIGHER)]
+EDGE_LOW = tiles([-3, FAR - 1, -FAR - 1])
+EDGE_HIGH = tiles([4, FAR + 2, -FAR + 2])
+MAIN = [OWN, LOW, HIGH, PLUS_BAND, MINUS_BAND, PLUS_FAR, MINUS_FAR]
+ARRIVE = MAIN + [EDGE_LOW, EDGE_HIGH]
+NEAR = [[(j % 2, b) for j, b in message] for message in (LOW, HIGH)]
 DIRECT = [[(j % 2, b) for j, b in message] for message in (PLUS_FAR, MINUS_FAR)]
-EDGE_LOW = [(1, b) for b in band_of(FAR - 1)]
-EDGE_HIGH = [(0, b) for b in band_of(FAR + 2)]
 
 
 def place_of(p):
@@ -105,10 +100,6 @@
 
 def from_layer_across(x, distance):
     return moved(x, lambda p: across(same_group(p, distance)))
-
-
-def edge_across(x, distance):
-    return moved(x, lambda p: across((across(p) + distance) % PAIRS))
 
 
 def far_across(x, distance):
@@ -163,45 +154,44 @@
 def pack_body(me_ref, *refs):
     pieces, own_ref, out_refs = refs[:LAYERS], refs[LAYERS], refs[LAYERS + 1 :]
     gather_pieces(me_ref[0], pieces, own_ref)
-    for message, out_ref in zip(DIRECT + NEAR, out_refs):
+    for message, out_ref in zip(DIRECT, out_refs):
         for k, (t, b) in enumerate(message):
             out_ref[k] = own_ref[b, t]
 
 
-def edge_body(me_ref, *refs):
-    pieces, shared_ref, out_refs = refs[:LAYERS], refs[LAYERS], refs[LAYERS + 1 :]
+def near_body(own_ref, after_ref, *out_refs):
+    del after_ref
+    for message, out_ref in zip(NEAR, out_refs):
+        for k, (t, b) in enumerate(message):
+            out_ref[k] = own_ref[b, t]
+
+
+def fan_body(me_ref, *refs):
+    pieces, out_ref, shared_ref = refs[:LAYERS], refs[LAYERS], refs[LAYERS + 1]
     gather_pieces(me_ref[0], pieces, shared_ref)
-    for message, out_ref in zip((EDGE_LOW, EDGE_HIGH), out_refs):
-        for k, (t, b) in enumerate(message):
-            out_ref[k] = shared_ref[SHARED.index(b), t]
-
-
-def fan_body(shared_ref, low_ref, high_ref, out_ref):
-    for k, (j, b) in enumerate(PLUS_BAND):
-        t = j - FAR
-        if t < 0:
-            out_ref[k] = low_ref[EDGE_LOW.index((1, b))]
-        elif t > 1:
-            out_ref[k] = high_ref[EDGE_HIGH.index((0, b))]
-        else:
-            out_ref[k] = shared_ref[SHARED.index(b), t]
-
-
-def far_body(plus_ref, minus_ref, low_ref, high_ref):
-    for shift, message, out_ref in ((2, LOW_FAR, low_ref), (-2, HIGH_FAR, high_ref)):
+    for k, (t, b) in enumerate(FAN):
+        out_ref[k] = shared_ref[SHARED.index(b), t]
+
+
+def edge_body(*refs):
+    sources, out_refs = refs[: len(MAIN) - 1], refs[len(MAIN) - 1 :]
+    for shift, message, out_ref in zip((2, -2), (EDGE_LOW, EDGE_HIGH), out_refs):
         for k, (j, b) in enumerate(message):
-            if j > 0:
-                out_ref[k] = plus_ref[PLUS_FAR.index((j + shift, b))]
-            else:
-                out_ref[k] = minus_ref[MINUS_FAR.index((j + shift, b))]
+            [(ref, held)] = [
+                (ref, held)
+                for ref, held in zip(sources, MAIN[1:])
+                if (j + shift, b) in held
+            ]
+            out_ref[k] = ref[held.index((j + shift, b))]
 
 
 def placements():
     found = {}
     for operand, message in enumerate(ARRIVE):
         for k, (j, b) in enumerate(message):
-            column = SLOT[(j + OFFSETS[b]) % NBG]
-            found[SLOT[j % NBG], column] = (operand, k if operand else (b, j))
+            column = SLOT.get((j + OFFSETS[b]) % NBG)
+            if column is not None:
+                found[SLOT[j % NBG], column] = (operand, k if operand else (b, j))
     return found
 
 
@@ -300,26 +290,26 @@
     )
     shared = [from_layer_across(pieces[LAYERS + s], s) for s in range(LAYERS)]
     pieces = [pieces[0]] + [from_layer(pieces[s], s) for s in range(1, LAYERS)]
-    shared, edge_low, edge_high = call(
-        edge_body,
-        [bf16(len(SHARED), 2, BS, BS)] + packed([EDGE_LOW, EDGE_HIGH]),
+    band = call(
+        fan_body,
+        packed([FAN])[0],
         1,
         LAYERS,
+        scratch=[pltpu.VMEM((len(SHARED), 2, BS, BS), jnp.bfloat16)],
     )(me, *shared)
-    edge_low, edge_high = edge_across(edge_low, -1), edge_across(edge_high, 1)
-    own, plus_far, minus_far, low, high, lower, higher = call(
-        pack_body, [bf16(DIAGS, 2, BS, BS)] + packed(DIRECT + NEAR), 1, LAYERS
+    own, plus_far, minus_far = call(
+        pack_body, [bf16(DIAGS, 2, BS, BS)] + packed(DIRECT), 1, LAYERS
     )(me, *pieces)
     plus_far = from_pair(plus_far, FAR_PAIRS)
     minus_far = from_pair(minus_far, -FAR_PAIRS)
+    plus_band, minus_band = far_across(band, FAR_PAIRS), far_across(band, -FAR_PAIRS)
+    low, high = call(near_body, packed([LOW, HIGH]), 0, 2)(own, band)
     low, high = from_pair(low, -1), from_pair(high, 1)
-    lower, higher = from_pair(lower, -2), from_pair(higher, 2)
-    band = call(fan_body, packed([PLUS_BAND])[0], 0, 3)(shared, edge_low, edge_high)
-    plus_band, minus_band = far_across(band, FAR_PAIRS), far_across(band, -FAR_PAIRS)
-    low_far, high_far = call(far_body, packed([LOW_FAR, HIGH_FAR]), 0, 2)(
-        plus_far, minus_far
-    )
-    low_far, high_far = from_pair(low_far, -1), from_pair(high_far, 1)
+    arrived = [low, high, plus_band, minus_band, plus_far, minus_far]
+    edge_low, edge_high = call(
+        edge_body, packed([EDGE_LOW, EDGE_HIGH]), 0, len(arrived)
+    )(*arrived)
+    edge_low, edge_high = from_pair(edge_low, -1), from_pair(edge_high, 1)
     results = call(
         purify_body,
         [quarter] * LAYERS,
@@ -331,10 +321,7 @@
             pltpu.VMEM((DIAGS, 2, BS, BS), jnp.bfloat16),
         ],
         flops=4 * 224 * 2 * BS**3,
-    )(
-        me, presence, own, low, high, lower, higher, plus_band, minus_band,
-        plus_far, minus_far, low_far, high_far,
-    )
+    )(me, presence, own, *arrived, edge_low, edge_high)
     results = [results[0]] + [from_layer(results[s], s) for s in range(1, LAYERS)]
     return call(join_body, bf16(DIAGS, 2 * LAYERS, BS // LAYERS, BS), 1, LAYERS)(
         me, *results

time: 122 us -> 111 us (0.910)
  the two profiles are of different devices: /device:TPU:9 before, /device:TPU:1 now
where the time goes in v3:
time: 111 us
  waiting for transfers between devices  56.8 us (51%)
  starting transfers between devices  44.1 us (40%)
  Pallas kernels  7.95 us (7%)
  local copies, waits for them, and re-layouts  1.92 us (2%)
    ppermute x18, waiting for transfers between devices, moved(): return lax.ppermute(x, AXES, route)  56.8 us
    ppermute x18, starting transfers between devices, moved(): return lax.ppermute(x, AXES, route)  44.1 us
    pallas_call x1, Pallas kernels, per_device(): call(purify_body, [quarter] * LAYERS, 2, len(ARRIVE), scratch=[pltpu.VMEM...  5.76 us
  transfers between devices with their start and end apart: 18, of which 11 were waited for; matrix products, arithmetic and copies ran while one was open for 0% of the time, Pallas kernels for 0%

profile of v3, /device:TPU:1, one launch (start us, length us, event | category | flops | bytes accessed | tf_op | source)
XLA Modules:
  0.0 110.8 jit_solution(11556492790461287503)
XLA Ops:
  0.0 0.0 copy-start.1
  0.0 0.7 copy-done.1
  0.7 0.1 copy.4.presence_ref
  0.8 0.0 copy-start
  0.8 1.2 %copy-done = bf16[13,8,32,128]{3,2,1,0:T(8,128)(2,1)S(1)} copy-done((bf16[13,8,32,128]{3,2,1,0:T(8,128)(2,1)S(1)}, bf16[13,8,32,128]{3,2,1,0:T(8,128)(2,1)}, u32[]{:S(2)}) %copy-start) | copy-done | bytes 851992
  1.9 0.9 shard_map.28
  2.9 3.4 %collective-permute-start = (bf16[13,2,32,128]{3,2,1,0:T(8,128)(2,1)S(1)}, bf16[13,2,32,128]{3,2,1,0:T(8,128)(2,1)S(1)}, u32[]{:S(2)}, u32[]{:S(2)}) collective-permute-start(bf16[13,2,32,128]{3,2,1,0:T(8,128)(2,1)S(1)} %get-tuple-element.25), channel_id=1, source_target_pairs={{64,0},{128,64},{192,128},{0,192},{65,1},{129,65},{193,129},{1,193... | collective-permute-start | bytes 638984 | tf_op jit(solution)/shard_map/ppermute | solution.py:81
  6.3 0.5 collective-permute-start.1
  6.8 0.6 collective-permute-start.2
  7.4 6.9 %collective-permute-start.3 = (bf16[5,2,32,128]{3,2,1,0:T(8,128)(2,1)S(1)}, bf16[5,2,32,128]{3,2,1,0:T(8,128)(2,1)S(1)}, u32[]{:S(2)}, u32[]{:S(2)}) collective-permute-start(bf16[5,2,32,128]{3,2,1,0:T(8,128)(2,1)S(1)} %get-tuple-element.29), channel_id=1, source_target_pairs={{4,0},{68,64},{132,128},{196,192},{5,1},{69,65},{133,129},{197,193... | collective-permute-start | bytes 245768 | tf_op jit(solution)/shard_map/ppermute | solution.py:81
  14.3 1.8 %collective-permute-start.4 = (bf16[5,2,32,128]{3,2,1,0:T(8,128)(2,1)S(1)}, bf16[5,2,32,128]{3,2,1,0:T(8,128)(2,1)S(1)}, u32[]{:S(2)}, u32[]{:S(2)}) collective-permute-start(bf16[5,2,32,128]{3,2,1,0:T(8,128)(2,1)S(1)} %get-tuple-element.30), channel_id=1, source_target_pairs={{68,0},{132,64},{196,128},{4,192},{69,1},{133,65},{197,129},{5,193... | collective-permute-start | bytes 245768 | tf_op jit(solution)/shard_map/ppermute | solution.py:81
  16.1 0.1 collective-permute-done.3.refs_0_
  16.2 7.8 %collective-permute-start.5 = (bf16[5,2,32,128]{3,2,1,0:T(8,128)(2,1)S(1)}, bf16[5,2,32,128]{3,2,1,0:T(8,128)(2,1)S(1)}, u32[]{:S(2)}, u32[]{:S(2)}) collective-permute-start(bf16[5,2,32,128]{3,2,1,0:T(8,128)(2,1)S(1)} %get-tuple-element.31), channel_id=1, source_target_pairs={{132,0},{196,64},{4,128},{68,192},{133,1},{197,65},{5,129},{69,193... | collective-permute-start | bytes 245768 | tf_op jit(solution)/shard_map/ppermute | solution.py:81
  24.0 0.0 collective-permute-done.4.refs_1_
  24.1 1.2 %collective-permute-start.6 = (bf16[5,2,32,128]{3,2,1,0:T(8,128)(2,1)S(1)}, bf16[5,2,32,128]{3,2,1,0:T(8,128)(2,1)S(1)}, u32[]{:S(2)}, u32[]{:S(2)}) collective-permute-start(bf16[5,2,32,128]{3,2,1,0:T(8,128)(2,1)S(1)} %get-tuple-element.32), channel_id=1, source_target_pairs={{196,0},{4,64},{68,128},{132,192},{197,1},{5,65},{69,129},{133,193... | collective-permute-start | bytes 245768 | tf_op jit(solution)/shard_map/ppermute | solution.py:81
  25.2 1.5 %collective-permute-done.5.refs_2_ = bf16[5,2,32,128]{3,2,1,0:T(8,128)(2,1)S(1)} collective-permute-done((bf16[5,2,32,128]{3,2,1,0:T(8,128)(2,1)S(1)}, bf16[5,2,32,128]{3,2,1,0:T(8,128)(2,1)S(1)}, u32[]{:S(2)}, u32[]{:S(2)}) %collective-permute-start.5) | collective-permute-done | bytes 81952 | tf_op jit(solution)/shard_map/ppermute | solution.py:81
  26.8 6.6 %collective-permute-done.6.refs_3_ = bf16[5,2,32,128]{3,2,1,0:T(8,128)(2,1)S(1)} collective-permute-done((bf16[5,2,32,128]{3,2,1,0:T(8,128)(2,1)S(1)}, bf16[5,2,32,128]{3,2,1,0:T(8,128)(2,1)S(1)}, u32[]{:S(2)}, u32[]{:S(2)}) %collective-permute-start.6) | collective-permute-done | bytes 81952 | tf_op jit(solution)/shard_map/ppermute | solution.py:81
  33.4 0.0 collective-permute-done.refs_1_
  33.4 0.0 collective-permute-done.1.refs_2_
  33.4 0.0 collective-permute-done.2.refs_3_
  33.4 0.1 shard_map.29
  33.5 0.1 shard_map.31
  33.6 0.1 collective-permute-start.7
  33.7 5.1 %collective-permute-start.8 = (bf16[17,128,128]{2,1,0:T(8,128)(2,1)S(1)}, bf16[17,128,128]{2,1,0:T(8,128)(2,1)S(1)}, u32[]{:S(2)}, u32[]{:S(2)}) collective-permute-start(bf16[17,128,128]{2,1,0:T(8,128)(2,1)S(1)} %get-tuple-element.34), channel_id=1, source_target_pairs={{64,0},{128,64},{192,128},{1,192},{65,1},{129,65},{193,129},{2,193... | collective-permute-start | bytes 1671176 | tf_op jit(solution)/shard_map/ppermute | solution.py:81
  38.8 8.7 %collective-permute-start.10 = (bf16[10,128,128]{2,1,0:T(8,128)(2,1)S(1)}, bf16[10,128,128]{2,1,0:T(8,128)(2,1)S(1)}, u32[]{:S(2)}, u32[]{:S(2)}) collective-permute-start(bf16[10,128,128]{2,1,0:T(8,128)(2,1)S(1)} %shard_map.30.after_ref), channel_id=1, source_target_pairs={{40,0},{104,64},{168,128},{232,192},{41,1},{105,65},{169,129},{233... | collective-permute-start | bytes 983048 | tf_op jit(solution)/shard_map/ppermute | solution.py:81
  47.4 0.8 collective-permute-start.9
  48.2 0.0 collective-permute-start.11
  48.2 11.5 %collective-permute-done.10.refs_3_.refs_4_ = bf16[10,128,128]{2,1,0:T(8,128)(2,1)S(1)} collective-permute-done((bf16[10,128,128]{2,1,0:T(8,128)(2,1)S(1)}, bf16[10,128,128]{2,1,0:T(8,128)(2,1)S(1)}, u32[]{:S(2)}, u32[]{:S(2)}) %collective-permute-start.10) | collective-permute-done | bytes 327712 | tf_op jit(solution)/shard_map/ppermute | solution.py:81
  59.7 0.0 collective-permute-start.12
  59.7 3.6 %collective-permute-done.9.refs_2_.refs_3_ = bf16[10,128,128]{2,1,0:T(8,128)(2,1)S(1)} collective-permute-done((bf16[10,128,128]{2,1,0:T(8,128)(2,1)S(1)}, bf16[10,128,128]{2,1,0:T(8,128)(2,1)S(1)}, u32[]{:S(2)}, u32[]{:S(2)}) %collective-permute-start.9) | collective-permute-done | bytes 327712 | tf_op jit(solution)/shard_map/ppermute | solution.py:81
  63.3 3.9 %collective-permute-done.11.refs_4_.refs_5_ = bf16[6,128,128]{2,1,0:T(8,128)(2,1)S(1)} collective-permute-done((bf16[6,128,128]{2,1,0:T(8,128)(2,1)S(1)}, bf16[6,128,128]{2,1,0:T(8,128)(2,1)S(1)}, u32[]{:S(2)}, u32[]{:S(2)}) %collective-permute-start.11) | collective-permute-done | bytes 196640 | tf_op jit(solution)/shard_map/ppermute | solution.py:81
  67.2 5.6 %collective-permute-done.12.refs_5_.refs_6_ = bf16[6,128,128]{2,1,0:T(8,128)(2,1)S(1)} collective-permute-done((bf16[6,128,128]{2,1,0:T(8,128)(2,1)S(1)}, bf16[6,128,128]{2,1,0:T(8,128)(2,1)S(1)}, u32[]{:S(2)}, u32[]{:S(2)}) %collective-permute-start.12) | collective-permute-done | bytes 196640 | tf_op jit(solution)/shard_map/ppermute | solution.py:81
  72.8 0.0 collective-permute-done.7.refs_0_.refs_1_
  72.8 0.0 collective-permute-done.8.refs_1_.refs_2_
  72.8 0.1 shard_map.32
  72.9 0.1 collective-permute-start.13
  73.0 5.1 %collective-permute-start.14 = (bf16[16,128,128]{2,1,0:T(8,128)(2,1)S(1)}, bf16[16,128,128]{2,1,0:T(8,128)(2,1)S(1)}, u32[]{:S(2)}, u32[]{:S(2)}) collective-permute-start(bf16[16,128,128]{2,1,0:T(8,128)(2,1)S(1)} %get-tuple-element.38), channel_id=1, source_target_pairs={{64,0},{128,64},{192,128},{1,192},{65,1},{129,65},{193,129},{2,193... | collective-permute-start | bytes 1572872 | tf_op jit(solution)/shard_map/ppermute | solution.py:81
  78.1 12.0 %collective-permute-done.13.refs_7_ = bf16[16,128,128]{2,1,0:T(8,128)(2,1)S(1)} collective-permute-done((bf16[16,128,128]{2,1,0:T(8,128)(2,1)S(1)}, bf16[16,128,128]{2,1,0:T(8,128)(2,1)S(1)}, u32[]{:S(2)}, u32[]{:S(2)}) %collective-permute-start.13) | collective-permute-done | bytes 524320 | tf_op jit(solution)/shard_map/ppermute | solution.py:81
  90.0 0.0 collective-permute-done.14.refs_8_
  90.0 5.8 %shard_map.33 = (bf16[13,2,32,128]{3,2,1,0:T(8,128)(2,1)S(1)}, bf16[13,2,32,128]{3,2,1,0:T(8,128)(2,1)S(1)}, bf16[13,2,32,128]{3,2,1,0:T(8,128)(2,1)S(1)}, bf16[13,2,32,128]{3,2,1,0:T(8,128)(2,1)S(1)}) custom-call(s32[1]{0:T(128)} %bitcast.me_ref, s32[13,8]{1,0:T(8,128)S(1)} %copy.4.presence_ref, ...), custom_call_target="tpu_custom_call" | custom-call | flops 3758096384 | bytes 4194304 | tf_op jit(solution)/shard_map/pallas_call | solution.py:313
  95.8 1.4 %collective-permute-start.15 = (bf16[13,2,32,128]{3,2,1,0:T(8,128)(2,1)S(1)}, bf16[13,2,32,128]{3,2,1,0:T(8,128)(2,1)S(1)}, u32[]{:S(2)}, u32[]{:S(2)}) collective-permute-start(bf16[13,2,32,128]{3,2,1,0:T(8,128)(2,1)S(1)} %get-tuple-element.40), channel_id=1, source_target_pairs={{64,0},{128,64},{192,128},{0,192},{65,1},{129,65},{193,129},{1,193... | collective-permute-start | bytes 638984 | tf_op jit(solution)/shard_map/ppermute | solution.py:81
  97.2 0.0 collective-permute-start.16
  97.3 0.7 collective-permute-start.17
  97.9 4.7 %collective-permute-done.15.refs_1_ = bf16[13,2,32,128]{3,2,1,0:T(8,128)(2,1)S(1)} collective-permute-done((bf16[13,2,32,128]{3,2,1,0:T(8,128)(2,1)S(1)}, bf16[13,2,32,128]{3,2,1,0:T(8,128)(2,1)S(1)}, u32[]{:S(2)}, u32[]{:S(2)}) %collective-permute-start.15) | collective-permute-done | bytes 213024 | tf_op jit(solution)/shard_map/ppermute | solution.py:81
  102.6 1.3 %collective-permute-done.16.refs_2_ = bf16[13,2,32,128]{3,2,1,0:T(8,128)(2,1)S(1)} collective-permute-done((bf16[13,2,32,128]{3,2,1,0:T(8,128)(2,1)S(1)}, bf16[13,2,32,128]{3,2,1,0:T(8,128)(2,1)S(1)}, u32[]{:S(2)}, u32[]{:S(2)}) %collective-permute-start.16) | collective-permute-done | bytes 213024 | tf_op jit(solution)/shard_map/ppermute | solution.py:81
  103.9 6.0 %collective-permute-done.17.refs_3_ = bf16[13,2,32,128]{3,2,1,0:T(8,128)(2,1)S(1)} collective-permute-done((bf16[13,2,32,128]{3,2,1,0:T(8,128)(2,1)S(1)}, bf16[13,2,32,128]{3,2,1,0:T(8,128)(2,1)S(1)}, u32[]{:S(2)}, u32[]{:S(2)}) %collective-permute-start.17) | collective-permute-done | bytes 213024 | tf_op jit(solution)/shard_map/ppermute | solution.py:81
  109.8 1.0 shard_map.34
  (1 shorter events, 0.0 us)
Async XLA Ops:
  0.0 0.7 copy-start.1
  0.8 1.2 %copy-start = (bf16[13,8,32,128]{3,2,1,0:T(8,128)(2,1)S(1)}, bf16[13,8,32,128]{3,2,1,0:T(8,128)(2,1)}, u32[]{:S(2)}) copy-start(bf16[13,8,32,128]{3,2,1,0:T(8,128)(2,1)} %blocks_ref.1) | copy-start | bytes 2555908
  2.9 30.5 %collective-permute-start = (bf16[13,2,32,128]{3,2,1,0:T(8,128)(2,1)S(1)}, bf16[13,2,32,128]{3,2,1,0:T(8,128)(2,1)S(1)}, u32[]{:S(2)}, u32[]{:S(2)}) collective-permute-start(bf16[13,2,32,128]{3,2,1,0:T(8,128)(2,1)S(1)} %get-tuple-element.25), channel_id=1, source_target_pairs={{64,0},{128,64},{192,128},{0,192},{65,1},{129,65},{193,129},{1,193... | collective-permute-start | bytes 638984 | tf_op jit(solution)/shard_map/ppermute | solution.py:81
  6.3 27.2 %collective-permute-start.1 = (bf16[13,2,32,128]{3,2,1,0:T(8,128)(2,1)S(1)}, bf16[13,2,32,128]{3,2,1,0:T(8,128)(2,1)S(1)}, u32[]{:S(2)}, u32[]{:S(2)}) collective-permute-start(bf16[13,2,32,128]{3,2,1,0:T(8,128)(2,1)S(1)} %get-tuple-element.26), channel_id=1, source_target_pairs={{128,0},{192,64},{0,128},{64,192},{129,1},{193,65},{1,129},{65,193... | collective-permute-start | bytes 638984 | tf_op jit(solution)/shard_map/ppermute | solution.py:81
  6.8 26.7 %collective-permute-start.2 = (bf16[13,2,32,128]{3,2,1,0:T(8,128)(2,1)S(1)}, bf16[13,2,32,128]{3,2,1,0:T(8,128)(2,1)S(1)}, u32[]{:S(2)}, u32[]{:S(2)}) collective-permute-start(bf16[13,2,32,128]{3,2,1,0:T(8,128)(2,1)S(1)} %get-tuple-element.27), channel_id=1, source_target_pairs={{192,0},{0,64},{64,128},{128,192},{193,1},{1,65},{65,129},{129,193... | collective-permute-start | bytes 638984 | tf_op jit(solution)/shard_map/ppermute | solution.py:81
  7.4 8.8 %collective-permute-start.3 = (bf16[5,2,32,128]{3,2,1,0:T(8,128)(2,1)S(1)}, bf16[5,2,32,128]{3,2,1,0:T(8,128)(2,1)S(1)}, u32[]{:S(2)}, u32[]{:S(2)}) collective-permute-start(bf16[5,2,32,128]{3,2,1,0:T(8,128)(2,1)S(1)} %get-tuple-element.29), channel_id=1, source_target_pairs={{4,0},{68,64},{132,128},{196,192},{5,1},{69,65},{133,129},{197,193... | collective-permute-start | bytes 245768 | tf_op jit(solution)/shard_map/ppermute | solution.py:81
  14.3 9.7 %collective-permute-start.4 = (bf16[5,2,32,128]{3,2,1,0:T(8,128)(2,1)S(1)}, bf16[5,2,32,128]{3,2,1,0:T(8,128)(2,1)S(1)}, u32[]{:S(2)}, u32[]{:S(2)}) collective-permute-start(bf16[5,2,32,128]{3,2,1,0:T(8,128)(2,1)S(1)} %get-tuple-element.30), channel_id=1, source_target_pairs={{68,0},{132,64},{196,128},{4,192},{69,1},{133,65},{197,129},{5,193... | collective-permute-start | bytes 245768 | tf_op jit(solution)/shard_map/ppermute | solution.py:81
  16.2 10.5 %collective-permute-start.5 = (bf16[5,2,32,128]{3,2,1,0:T(8,128)(2,1)S(1)}, bf16[5,2,32,128]{3,2,1,0:T(8,128)(2,1)S(1)}, u32[]{:S(2)}, u32[]{:S(2)}) collective-permute-start(bf16[5,2,32,128]{3,2,1,0:T(8,128)(2,1)S(1)} %get-tuple-element.31), channel_id=1, source_target_pairs={{132,0},{196,64},{4,128},{68,192},{133,1},{197,65},{5,129},{69,193... | collective-permute-start | bytes 245768 | tf_op jit(solution)/shard_map/ppermute | solution.py:81
  24.1 9.3 %collective-permute-start.6 = (bf16[5,2,32,128]{3,2,1,0:T(8,128)(2,1)S(1)}, bf16[5,2,32,128]{3,2,1,0:T(8,128)(2,1)S(1)}, u32[]{:S(2)}, u32[]{:S(2)}) collective-permute-start(bf16[5,2,32,128]{3,2,1,0:T(8,128)(2,1)S(1)} %get-tuple-element.32), channel_id=1, source_target_pairs={{196,0},{4,64},{68,128},{132,192},{197,1},{5,65},{69,129},{133,193... | collective-permute-start | bytes 245768 | tf_op jit(solution)/shard_map/ppermute | solution.py:81
  33.6 39.2 %collective-permute-start.7 = (bf16[17,128,128]{2,1,0:T(8,128)(2,1)S(1)}, bf16[17,128,128]{2,1,0:T(8,128)(2,1)S(1)}, u32[]{:S(2)}, u32[]{:S(2)}) collective-permute-start(bf16[17,128,128]{2,1,0:T(8,128)(2,1)S(1)} %get-tuple-element.33), channel_id=1, source_target_pairs={{255,0},{0,64},{64,128},{128,192},{192,1},{1,65},{65,129},{129,193... | collective-permute-start | bytes 1671176 | tf_op jit(solution)/shard_map/ppermute | solution.py:81
  33.7 39.1 %collective-permute-start.8 = (bf16[17,128,128]{2,1,0:T(8,128)(2,1)S(1)}, bf16[17,128,128]{2,1,0:T(8,128)(2,1)S(1)}, u32[]{:S(2)}, u32[]{:S(2)}) collective-permute-start(bf16[17,128,128]{2,1,0:T(8,128)(2,1)S(1)} %get-tuple-element.34), channel_id=1, source_target_pairs={{64,0},{128,64},{192,128},{1,192},{65,1},{129,65},{193,129},{2,193... | collective-permute-start | bytes 1671176 | tf_op jit(solution)/shard_map/ppermute | solution.py:81
  38.8 20.9 %collective-permute-start.10 = (bf16[10,128,128]{2,1,0:T(8,128)(2,1)S(1)}, bf16[10,128,128]{2,1,0:T(8,128)(2,1)S(1)}, u32[]{:S(2)}, u32[]{:S(2)}) collective-permute-start(bf16[10,128,128]{2,1,0:T(8,128)(2,1)S(1)} %shard_map.30.after_ref), channel_id=1, source_target_pairs={{40,0},{104,64},{168,128},{232,192},{41,1},{105,65},{169,129},{233... | collective-permute-start | bytes 983048 | tf_op jit(solution)/shard_map/ppermute | solution.py:81
  47.4 15.9 %collective-permute-start.9 = (bf16[10,128,128]{2,1,0:T(8,128)(2,1)S(1)}, bf16[10,128,128]{2,1,0:T(8,128)(2,1)S(1)}, u32[]{:S(2)}, u32[]{:S(2)}) collective-permute-start(bf16[10,128,128]{2,1,0:T(8,128)(2,1)S(1)} %shard_map.30.after_ref), channel_id=1, source_target_pairs={{16,0},{80,64},{144,128},{208,192},{17,1},{81,65},{145,129},{209,1... | collective-permute-start | bytes 983048 | tf_op jit(solution)/shard_map/ppermute | solution.py:81
  48.2 19.0 %collective-permute-start.11 = (bf16[6,128,128]{2,1,0:T(8,128)(2,1)S(1)}, bf16[6,128,128]{2,1,0:T(8,128)(2,1)S(1)}, u32[]{:S(2)}, u32[]{:S(2)}) collective-permute-start(bf16[6,128,128]{2,1,0:T(8,128)(2,1)S(1)} %get-tuple-element.35), channel_id=1, source_target_pairs={{20,0},{84,64},{148,128},{212,192},{21,1},{85,65},{149,129},{213,1... | collective-permute-start | bytes 589832 | tf_op jit(solution)/shard_map/ppermute | solution.py:81
  59.7 13.1 %collective-permute-start.12 = (bf16[6,128,128]{2,1,0:T(8,128)(2,1)S(1)}, bf16[6,128,128]{2,1,0:T(8,128)(2,1)S(1)}, u32[]{:S(2)}, u32[]{:S(2)}) collective-permute-start(bf16[6,128,128]{2,1,0:T(8,128)(2,1)S(1)} %get-tuple-element.36), channel_id=1, source_target_pairs={{44,0},{108,64},{172,128},{236,192},{45,1},{109,65},{173,129},{237... | collective-permute-start | bytes 589832 | tf_op jit(solution)/shard_map/ppermute | solution.py:81
  72.9 17.1 %collective-permute-start.13 = (bf16[16,128,128]{2,1,0:T(8,128)(2,1)S(1)}, bf16[16,128,128]{2,1,0:T(8,128)(2,1)S(1)}, u32[]{:S(2)}, u32[]{:S(2)}) collective-permute-start(bf16[16,128,128]{2,1,0:T(8,128)(2,1)S(1)} %get-tuple-element.37), channel_id=1, source_target_pairs={{255,0},{0,64},{64,128},{128,192},{192,1},{1,65},{65,129},{129,193... | collective-permute-start | bytes 1572872 | tf_op jit(solution)/shard_map/ppermute | solution.py:81
  73.0 17.0 %collective-permute-start.14 = (bf16[16,128,128]{2,1,0:T(8,128)(2,1)S(1)}, bf16[16,128,128]{2,1,0:T(8,128)(2,1)S(1)}, u32[]{:S(2)}, u32[]{:S(2)}) collective-permute-start(bf16[16,128,128]{2,1,0:T(8,128)(2,1)S(1)} %get-tuple-element.38), channel_id=1, source_target_pairs={{64,0},{128,64},{192,128},{1,192},{65,1},{129,65},{193,129},{2,193... | collective-permute-start | bytes 1572872 | tf_op jit(solution)/shard_map/ppermute | solution.py:81
  95.8 6.8 %collective-permute-start.15 = (bf16[13,2,32,128]{3,2,1,0:T(8,128)(2,1)S(1)}, bf16[13,2,32,128]{3,2,1,0:T(8,128)(2,1)S(1)}, u32[]{:S(2)}, u32[]{:S(2)}) collective-permute-start(bf16[13,2,32,128]{3,2,1,0:T(8,128)(2,1)S(1)} %get-tuple-element.40), channel_id=1, source_target_pairs={{64,0},{128,64},{192,128},{0,192},{65,1},{129,65},{193,129},{1,193... | collective-permute-start | bytes 638984 | tf_op jit(solution)/shard_map/ppermute | solution.py:81
  97.2 6.6 %collective-permute-start.16 = (bf16[13,2,32,128]{3,2,1,0:T(8,128)(2,1)S(1)}, bf16[13,2,32,128]{3,2,1,0:T(8,128)(2,1)S(1)}, u32[]{:S(2)}, u32[]{:S(2)}) collective-permute-start(bf16[13,2,32,128]{3,2,1,0:T(8,128)(2,1)S(1)} %get-tuple-element.41), channel_id=1, source_target_pairs={{128,0},{192,64},{0,128},{64,192},{129,1},{193,65},{1,129},{65,193... | collective-permute-start | bytes 638984 | tf_op jit(solution)/shard_map/ppermute | solution.py:81
  97.3 12.6 %collective-permute-start.17 = (bf16[13,2,32,128]{3,2,1,0:T(8,128)(2,1)S(1)}, bf16[13,2,32,128]{3,2,1,0:T(8,128)(2,1)S(1)}, u32[]{:S(2)}, u32[]{:S(2)}) collective-permute-start(bf16[13,2,32,128]{3,2,1,0:T(8,128)(2,1)S(1)} %get-tuple-element.42), channel_id=1, source_target_pairs={{192,0},{0,64},{64,128},{128,192},{193,1},{1,65},{65,129},{129,193... | collective-permute-start | bytes 638984 | tf_op jit(solution)/shard_map/ppermute | solution.py:81

commit v4 on v3

--- a/solution.py
+++ b/solution.py
@@ -1,3 +1,5 @@
+import functools
+
 import jax
 import jax.numpy as jnp
 from jax import lax
@@ -57,7 +59,9 @@
     return [(j, b) for j in rows for b in which(j)]
 
 
-OWN = [(t, b) for b in range(DIAGS) for t in range(2)]
+PARTS = [list(range(DIAGS))]
+
+OWN = [[(t, b) for b in part for t in range(2)] for part in PARTS]
 LOW, HIGH = tiles([-2, -1]), tiles([2, 3])
 FAN = [(t, b) for t in range(2) for b in SHARED]
 PLUS_BAND = [(t + FAR, b) for t, b in FAN]
@@ -66,10 +70,15 @@
 MINUS_FAR = tiles([-FAR, -FAR + 1], far_of)
 EDGE_LOW = tiles([-3, FAR - 1, -FAR - 1])
 EDGE_HIGH = tiles([4, FAR + 2, -FAR + 2])
-MAIN = [OWN, LOW, HIGH, PLUS_BAND, MINUS_BAND, PLUS_FAR, MINUS_FAR]
-ARRIVE = MAIN + [EDGE_LOW, EDGE_HIGH]
+MAIN = [LOW, HIGH, PLUS_BAND, MINUS_BAND, PLUS_FAR, MINUS_FAR]
+ARRIVE = OWN + MAIN + [EDGE_LOW, EDGE_HIGH]
 NEAR = [[(j % 2, b) for j, b in message] for message in (LOW, HIGH)]
 DIRECT = [[(j % 2, b) for j, b in message] for message in (PLUS_FAR, MINUS_FAR)]
+
+
+def made_in(message):
+    [index] = [k for k, part in enumerate(PARTS) if {b for _, b in message} <= set(part)]
+    return index
 
 
 def place_of(p):
@@ -98,8 +107,8 @@
     return moved(x, lambda p: same_group(p, distance))
 
 
-def from_layer_across(x, distance):
-    return moved(x, lambda p: across(same_group(p, distance)))
+def swapped(x):
+    return moved(x, across)
 
 
 def far_across(x, distance):
@@ -130,56 +139,48 @@
 
 def split_body(me_ref, presence_ref, blocks_ref, *out_refs):
     me = me_ref[0]
-    for s in range(LAYERS):
-        own_ref, shared_ref = out_refs[s], out_refs[LAYERS + s]
+    for index, out_ref in enumerate(out_refs):
+        part, s = divmod(index, LAYERS)
         other = lax.rem(me - s + LAYERS, LAYERS)
         for t in range(2):
             row = 2 * other + t
-            for d in range(DIAGS):
+            for k, d in enumerate(PARTS[part]):
                 tile = blocks_ref[d, row]
                 present = presence_ref[d, row] != 0
-                tile = jnp.where(present, tile, jnp.zeros_like(tile))
-                own_ref[d, t] = tile
-                if d in SHARED:
-                    shared_ref[SHARED.index(d), t] = tile
-
-
-def gather_pieces(me, pieces, out_ref):
+                out_ref[k, t] = jnp.where(present, tile, jnp.zeros_like(tile))
+
+
+def gather_body(part, messages, me_ref, *refs):
+    pieces, own_ref, out_refs = refs[:LAYERS], refs[LAYERS], refs[LAYERS + 1 :]
     for s, piece in enumerate(pieces):
-        other = lax.rem(me + s, LAYERS)
+        other = lax.rem(me_ref[0] + s, LAYERS)
         start = pl.multiple_of(other * (BS // LAYERS), BS // LAYERS)
-        out_ref[:, :, pl.ds(start, BS // LAYERS), :] = piece[...]
-
-
-def pack_body(me_ref, *refs):
-    pieces, own_ref, out_refs = refs[:LAYERS], refs[LAYERS], refs[LAYERS + 1 :]
-    gather_pieces(me_ref[0], pieces, own_ref)
-    for message, out_ref in zip(DIRECT, out_refs):
+        own_ref[:, :, pl.ds(start, BS // LAYERS), :] = piece[...]
+    for message, out_ref in zip(messages, out_refs):
         for k, (t, b) in enumerate(message):
-            out_ref[k] = own_ref[b, t]
-
-
-def near_body(own_ref, after_ref, *out_refs):
-    del after_ref
+            out_ref[k] = own_ref[part.index(b), t]
+
+
+def near_body(*refs):
+    own_refs, out_refs = refs[: len(PARTS)], refs[len(PARTS) :]
     for message, out_ref in zip(NEAR, out_refs):
         for k, (t, b) in enumerate(message):
-            out_ref[k] = own_ref[b, t]
-
-
-def fan_body(me_ref, *refs):
-    pieces, out_ref, shared_ref = refs[:LAYERS], refs[LAYERS], refs[LAYERS + 1]
-    gather_pieces(me_ref[0], pieces, shared_ref)
-    for k, (t, b) in enumerate(FAN):
-        out_ref[k] = shared_ref[SHARED.index(b), t]
+            [(part, ref)] = [(p, r) for p, r in zip(PARTS, own_refs) if b in p]
+            out_ref[k] = ref[part.index(b), t]
+
+
+def fan_body(low_ref, high_ref, band_ref, out_ref):
+    del low_ref, high_ref
+    out_ref[...] = band_ref[...]
 
 
 def edge_body(*refs):
-    sources, out_refs = refs[: len(MAIN) - 1], refs[len(MAIN) - 1 :]
+    sources, out_refs = refs[: len(MAIN)], refs[len(MAIN) :]
     for shift, message, out_ref in zip((2, -2), (EDGE_LOW, EDGE_HIGH), out_refs):
         for k, (j, b) in enumerate(message):
             [(ref, held)] = [
                 (ref, held)
-                for ref, held in zip(sources, MAIN[1:])
+                for ref, held in zip(sources, MAIN)
                 if (j + shift, b) in held
             ]
             out_ref[k] = ref[held.index((j + shift, b))]
@@ -191,7 +192,7 @@
         for k, (j, b) in enumerate(message):
             column = SLOT.get((j + OFFSETS[b]) % NBG)
             if column is not None:
-                found[SLOT[j % NBG], column] = (operand, k if operand else (b, j))
+                found[SLOT[j % NBG], column] = (operand, divmod(k, 2) if operand < len(OWN) else k)
     return found
 
 
@@ -199,7 +200,6 @@
     sources, outs = refs[: len(ARRIVE)], refs[len(ARRIVE) : len(ARRIVE) + LAYERS]
     right_ref, left_ref, result_ref = refs[len(ARRIVE) + LAYERS :]
     me = me_ref[0]
-    own_ref = sources[0]
     placed = placements()
     zero = jnp.zeros((BS, BS), jnp.bfloat16)
     for row in range(16):
@@ -219,7 +219,11 @@
         for column in range(16):
             where = (pl.ds(i * BS, BS), pl.ds(column * BS, BS))
             d = targets.get((i, column))
-            left_ref[where] = zero if d is None else own_ref[d, i]
+            if d is None:
+                left_ref[where] = zero
+            else:
+                [part] = [p for p, held in enumerate(PARTS) if d in held]
+                left_ref[where] = sources[part][PARTS[part].index(d), i]
 
     def dot(left, right):
         return jnp.dot(left, right, preferred_element_type=jnp.float32)
@@ -280,31 +284,37 @@
 def per_device(blocks, presence):
     me = lax.axis_index("layer").astype(jnp.int32).reshape(1)
     quarter = bf16(DIAGS, 2, BS // LAYERS, BS)
-    shared_quarter = bf16(len(SHARED), 2, BS // LAYERS, BS)
 
     def packed(messages):
         return [bf16(len(message), BS, BS) for message in messages]
 
-    pieces = call(split_body, [quarter] * LAYERS + [shared_quarter] * LAYERS, 2, 1)(
-        me, presence, blocks
-    )
-    shared = [from_layer_across(pieces[LAYERS + s], s) for s in range(LAYERS)]
-    pieces = [pieces[0]] + [from_layer(pieces[s], s) for s in range(1, LAYERS)]
-    band = call(
-        fan_body,
-        packed([FAN])[0],
+    pieces = call(
+        split_body,
+        [bf16(len(part), 2, BS // LAYERS, BS) for part in PARTS for _ in range(LAYERS)],
+        2,
         1,
-        LAYERS,
-        scratch=[pltpu.VMEM((len(SHARED), 2, BS, BS), jnp.bfloat16)],
-    )(me, *shared)
-    own, plus_far, minus_far = call(
-        pack_body, [bf16(DIAGS, 2, BS, BS)] + packed(DIRECT), 1, LAYERS
-    )(me, *pieces)
+    )(me, presence, blocks)
+    own, made = [], []
+    for index, part in enumerate(PARTS):
+        some = pieces[LAYERS * index : LAYERS * (index + 1)]
+        some = [some[0]] + [from_layer(some[s], s) for s in range(1, LAYERS)]
+        messages = [m for m in [FAN] + DIRECT if made_in(m) == index]
+        whole, *outs = call(
+            functools.partial(gather_body, part, messages),
+            [bf16(len(part), 2, BS, BS)] + packed(messages),
+            1,
+            LAYERS,
+        )(me, *some)
+        own.append(whole)
+        made += outs
+    band, plus_far, minus_far = made
+    band = swapped(band)
     plus_far = from_pair(plus_far, FAR_PAIRS)
     minus_far = from_pair(minus_far, -FAR_PAIRS)
+    low, high = call(near_body, packed([LOW, HIGH]), 0, len(own))(*own)
+    low, high = from_pair(low, -1), from_pair(high, 1)
+    band = call(fan_body, packed([FAN])[0], 0, 3)(low, high, band)
     plus_band, minus_band = far_across(band, FAR_PAIRS), far_across(band, -FAR_PAIRS)
-    low, high = call(near_body, packed([LOW, HIGH]), 0, 2)(own, band)
-    low, high = from_pair(low, -1), from_pair(high, 1)
     arrived = [low, high, plus_band, minus_band, plus_far, minus_far]
     edge_low, edge_high = call(
         edge_body, packed([EDGE_LOW, EDGE_HIGH]), 0, len(arrived)
@@ -321,7 +331,7 @@
             pltpu.VMEM((DIAGS, 2, BS, BS), jnp.bfloat16),
         ],
         flops=4 * 224 * 2 * BS**3,
-    )(me, presence, own, *arrived, edge_low, edge_high)
+    )(me, presence, *own, *arrived, edge_low, edge_high)
     results = [results[0]] + [from_layer(results[s], s) for s in range(1, LAYERS)]
     return call(join_body, bf16(DIAGS, 2 * LAYERS, BS // LAYERS, BS), 1, LAYERS)(
         me, *results

time: 111 us -> 116 us (1.045)
  waiting for transfers between devices: 56.8 us -> 60.2 us
  starting transfers between devices: 44.1 us -> 45.7 us
    ppermute x18 -> x15, waiting for transfers between devices: 56.8 us -> 60.2 us  [moved(): return lax.ppermute(x, AXES, route)]
    ppermute x18 -> x15, starting transfers between devices: 44.1 us -> 45.7 us  [moved(): return lax.ppermute(x, AXES, route)]
  transfers between devices with their start and end apart: 18 -> 15, of which waited for: 11 -> 9; matrix products, arithmetic and copies ran while one was open for 0% -> 0% of each run, Pallas kernels for 0% -> 0%
where the time goes in v4:
time: 116 us
  waiting for transfers between devices  60.2 us (52%)
  starting transfers between devices  45.7 us (39%)
  Pallas kernels  7.87 us (7%)
  local copies, waits for them, and re-layouts  1.92 us (2%)
    ppermute x15, waiting for transfers between devices, moved(): return lax.ppermute(x, AXES, route)  60.2 us
    ppermute x15, starting transfers between devices, moved(): return lax.ppermute(x, AXES, route)  45.7 us
    pallas_call x1, Pallas kernels, per_device(): call(purify_body, [quarter] * LAYERS, 2, len(ARRIVE), scratch=[pltpu.VMEM...  5.72 us
  transfers between devices with their start and end apart: 15, of which 9 were waited for; matrix products, arithmetic and copies ran while one was open for 0% of the time, Pallas kernels for 0%

profile of v4, /device:TPU:1, one launch (start us, length us, event | category | flops | bytes accessed | tf_op | source)
XLA Modules:
  0.0 115.8 jit_solution(17284462423258572147)
XLA Ops:
  0.0 0.0 copy-start.1
  0.0 0.7 copy-done.1
  0.7 0.1 copy.4.presence_ref
  0.8 0.0 copy-start
  0.8 1.2 copy-done
  1.9 0.9 shard_map.28
  2.9 3.4 %collective-permute-start = (bf16[13,2,32,128]{3,2,1,0:T(8,128)(2,1)S(1)}, bf16[13,2,32,128]{3,2,1,0:T(8,128)(2,1)S(1)}, u32[]{:S(2)}, u32[]{:S(2)}) collective-permute-start(bf16[13,2,32,128]{3,2,1,0:T(8,128)(2,1)S(1)} %get-tuple-element.22), channel_id=1, source_target_pairs={{64,0},{128,64},{192,128},{0,192},{65,1},{129,65},{193,129},{1,193... | collective-permute-start | bytes 638984 | tf_op jit(solution)/shard_map/ppermute | solution.py:90
  6.2 0.5 collective-permute-start.1
  6.8 0.6 collective-permute-start.2
  7.4 7.4 %collective-permute-done.refs_1_ = bf16[13,2,32,128]{3,2,1,0:T(8,128)(2,1)S(1)} collective-permute-done((bf16[13,2,32,128]{3,2,1,0:T(8,128)(2,1)S(1)}, bf16[13,2,32,128]{3,2,1,0:T(8,128)(2,1)S(1)}, u32[]{:S(2)}, u32[]{:S(2)}) %collective-permute-start) | collective-permute-done | bytes 213024 | tf_op jit(solution)/shard_map/ppermute | solution.py:90
  14.8 0.0 collective-permute-done.1.refs_2_
  14.8 4.7 %collective-permute-done.2.refs_3_ = bf16[13,2,32,128]{3,2,1,0:T(8,128)(2,1)S(1)} collective-permute-done((bf16[13,2,32,128]{3,2,1,0:T(8,128)(2,1)S(1)}, bf16[13,2,32,128]{3,2,1,0:T(8,128)(2,1)S(1)}, u32[]{:S(2)}, u32[]{:S(2)}) %collective-permute-start.2) | collective-permute-done | bytes 213024 | tf_op jit(solution)/shard_map/ppermute | solution.py:90
  19.5 0.1 shard_map.29
  19.6 0.1 shard_map.30
  19.7 0.1 collective-permute-start.3
  19.8 6.1 %collective-permute-start.4 = (bf16[17,128,128]{2,1,0:T(8,128)(2,1)S(1)}, bf16[17,128,128]{2,1,0:T(8,128)(2,1)S(1)}, u32[]{:S(2)}, u32[]{:S(2)}) collective-permute-start(bf16[17,128,128]{2,1,0:T(8,128)(2,1)S(1)} %get-tuple-element.27), channel_id=1, source_target_pairs={{64,0},{128,64},{192,128},{1,192},{65,1},{129,65},{193,129},{2,193... | collective-permute-start | bytes 1671176 | tf_op jit(solution)/shard_map/ppermute | solution.py:90
  25.8 5.6 %collective-permute-start.5 = (bf16[10,128,128]{2,1,0:T(8,128)(2,1)S(1)}, bf16[10,128,128]{2,1,0:T(8,128)(2,1)S(1)}, u32[]{:S(2)}, u32[]{:S(2)}) collective-permute-start(bf16[10,128,128]{2,1,0:T(8,128)(2,1)S(1)} %get-tuple-element.28), channel_id=1, source_target_pairs={{4,0},{68,64},{132,128},{196,192},{5,1},{69,65},{133,129},{197,193... | collective-permute-start | bytes 983048 | tf_op jit(solution)/shard_map/ppermute | solution.py:90
  31.5 8.6 %collective-permute-done.5.band_ref = bf16[10,128,128]{2,1,0:T(8,128)(2,1)S(1)} collective-permute-done((bf16[10,128,128]{2,1,0:T(8,128)(2,1)S(1)}, bf16[10,128,128]{2,1,0:T(8,128)(2,1)S(1)}, u32[]{:S(2)}, u32[]{:S(2)}) %collective-permute-start.5) | collective-permute-done | bytes 327712 | tf_op jit(solution)/shard_map/ppermute | solution.py:90
  40.1 0.0 collective-permute-done.3.low_ref.refs_0_.refs_1_
  40.1 0.0 collective-permute-done.4.high_ref.refs_1_.refs_2_
  40.1 13.1 %collective-permute-start.7 = (bf16[10,128,128]{2,1,0:T(8,128)(2,1)S(1)}, bf16[10,128,128]{2,1,0:T(8,128)(2,1)S(1)}, u32[]{:S(2)}, u32[]{:S(2)}) collective-permute-start(bf16[10,128,128]{2,1,0:T(8,128)(2,1)S(1)} %shard_map.31), channel_id=1, source_target_pairs={{40,0},{104,64},{168,128},{232,192},{41,1},{105,65},{169,129},{233... | collective-permute-start | bytes 983048 | tf_op jit(solution)/shard_map/ppermute | solution.py:90
  53.2 0.8 collective-permute-start.6
  54.0 8.8 %collective-permute-start.8 = (bf16[6,128,128]{2,1,0:T(8,128)(2,1)S(1)}, bf16[6,128,128]{2,1,0:T(8,128)(2,1)S(1)}, u32[]{:S(2)}, u32[]{:S(2)}) collective-permute-start(bf16[6,128,128]{2,1,0:T(8,128)(2,1)S(1)} %get-tuple-element.29), channel_id=1, source_target_pairs={{20,0},{84,64},{148,128},{212,192},{21,1},{85,65},{149,129},{213,1... | collective-permute-start | bytes 589832 | tf_op jit(solution)/shard_map/ppermute | solution.py:90
  62.8 0.0 collective-permute-start.9
  62.8 9.8 %collective-permute-done.8.refs_4_.refs_5_ = bf16[6,128,128]{2,1,0:T(8,128)(2,1)S(1)} collective-permute-done((bf16[6,128,128]{2,1,0:T(8,128)(2,1)S(1)}, bf16[6,128,128]{2,1,0:T(8,128)(2,1)S(1)}, u32[]{:S(2)}, u32[]{:S(2)}) %collective-permute-start.8) | collective-permute-done | bytes 196640 | tf_op jit(solution)/shard_map/ppermute | solution.py:90
  72.7 5.1 %collective-permute-done.9.refs_5_.refs_6_ = bf16[6,128,128]{2,1,0:T(8,128)(2,1)S(1)} collective-permute-done((bf16[6,128,128]{2,1,0:T(8,128)(2,1)S(1)}, bf16[6,128,128]{2,1,0:T(8,128)(2,1)S(1)}, u32[]{:S(2)}, u32[]{:S(2)}) %collective-permute-start.9) | collective-permute-done | bytes 196640 | tf_op jit(solution)/shard_map/ppermute | solution.py:90
  77.7 0.0 collective-permute-done.7.refs_3_.refs_4_
  77.7 0.0 collective-permute-done.6.refs_2_.refs_3_
  77.7 0.1 shard_map.32
  77.8 0.1 collective-permute-start.10
  77.9 5.1 %collective-permute-start.11 = (bf16[16,128,128]{2,1,0:T(8,128)(2,1)S(1)}, bf16[16,128,128]{2,1,0:T(8,128)(2,1)S(1)}, u32[]{:S(2)}, u32[]{:S(2)}) collective-permute-start(bf16[16,128,128]{2,1,0:T(8,128)(2,1)S(1)} %get-tuple-element.32), channel_id=1, source_target_pairs={{64,0},{128,64},{192,128},{1,192},{65,1},{129,65},{193,129},{2,193... | collective-permute-start | bytes 1572872 | tf_op jit(solution)/shard_map/ppermute | solution.py:90
  83.0 12.7 %collective-permute-done.10.refs_7_ = bf16[16,128,128]{2,1,0:T(8,128)(2,1)S(1)} collective-permute-done((bf16[16,128,128]{2,1,0:T(8,128)(2,1)S(1)}, bf16[16,128,128]{2,1,0:T(8,128)(2,1)S(1)}, u32[]{:S(2)}, u32[]{:S(2)}) %collective-permute-start.10) | collective-permute-done | bytes 524320 | tf_op jit(solution)/shard_map/ppermute | solution.py:90
  95.7 0.0 collective-permute-done.11.refs_8_
  95.7 5.7 %shard_map.33 = (bf16[13,2,32,128]{3,2,1,0:T(8,128)(2,1)S(1)}, bf16[13,2,32,128]{3,2,1,0:T(8,128)(2,1)S(1)}, bf16[13,2,32,128]{3,2,1,0:T(8,128)(2,1)S(1)}, bf16[13,2,32,128]{3,2,1,0:T(8,128)(2,1)S(1)}) custom-call(s32[1]{0:T(128)} %bitcast.me_ref, s32[13,8]{1,0:T(8,128)S(1)} %copy.4.presence_ref, bf16[13,2,128,128]{3,2,1,0:T(8,128)(2,1)S(1)} %get-tuple-element.25.refs_0_, ...), custom_call_target="tpu_custom_call" | custom-call | flops 3758096384 | bytes 4194304 | tf_op jit(solution)/shard_map/pallas_call | solution.py:323
  101.4 0.1 collective-permute-start.12
  101.5 0.1 collective-permute-start.13
  101.6 1.4 %collective-permute-start.14 = (bf16[13,2,32,128]{3,2,1,0:T(8,128)(2,1)S(1)}, bf16[13,2,32,128]{3,2,1,0:T(8,128)(2,1)S(1)}, u32[]{:S(2)}, u32[]{:S(2)}) collective-permute-start(bf16[13,2,32,128]{3,2,1,0:T(8,128)(2,1)S(1)} %get-tuple-element.36), channel_id=1, source_target_pairs={{192,0},{0,64},{64,128},{128,192},{193,1},{1,65},{65,129},{129,193... | collective-permute-start | bytes 638984 | tf_op jit(solution)/shard_map/ppermute | solution.py:90
  103.0 4.8 %collective-permute-done.12.refs_1_ = bf16[13,2,32,128]{3,2,1,0:T(8,128)(2,1)S(1)} collective-permute-done((bf16[13,2,32,128]{3,2,1,0:T(8,128)(2,1)S(1)}, bf16[13,2,32,128]{3,2,1,0:T(8,128)(2,1)S(1)}, u32[]{:S(2)}, u32[]{:S(2)}) %collective-permute-start.12) | collective-permute-done | bytes 213024 | tf_op jit(solution)/shard_map/ppermute | solution.py:90
  107.8 1.6 %collective-permute-done.13.refs_2_ = bf16[13,2,32,128]{3,2,1,0:T(8,128)(2,1)S(1)} collective-permute-done((bf16[13,2,32,128]{3,2,1,0:T(8,128)(2,1)S(1)}, bf16[13,2,32,128]{3,2,1,0:T(8,128)(2,1)S(1)}, u32[]{:S(2)}, u32[]{:S(2)}) %collective-permute-start.13) | collective-permute-done | bytes 213024 | tf_op jit(solution)/shard_map/ppermute | solution.py:90
  109.4 5.4 %collective-permute-done.14.refs_3_ = bf16[13,2,32,128]{3,2,1,0:T(8,128)(2,1)S(1)} collective-permute-done((bf16[13,2,32,128]{3,2,1,0:T(8,128)(2,1)S(1)}, bf16[13,2,32,128]{3,2,1,0:T(8,128)(2,1)S(1)}, u32[]{:S(2)}, u32[]{:S(2)}) %collective-permute-start.14) | collective-permute-done | bytes 213024 | tf_op jit(solution)/shard_map/ppermute | solution.py:90
  114.8 1.0 shard_map.34
  (1 shorter events, 0.0 us)
Async XLA Ops:
  0.0 0.7 copy-start.1
  0.8 1.2 copy-start
  2.9 11.9 %collective-permute-start = (bf16[13,2,32,128]{3,2,1,0:T(8,128)(2,1)S(1)}, bf16[13,2,32,128]{3,2,1,0:T(8,128)(2,1)S(1)}, u32[]{:S(2)}, u32[]{:S(2)}) collective-permute-start(bf16[13,2,32,128]{3,2,1,0:T(8,128)(2,1)S(1)} %get-tuple-element.22), channel_id=1, source_target_pairs={{64,0},{128,64},{192,128},{0,192},{65,1},{129,65},{193,129},{1,193... | collective-permute-start | bytes 638984 | tf_op jit(solution)/shard_map/ppermute | solution.py:90
  6.2 8.5 %collective-permute-start.1 = (bf16[13,2,32,128]{3,2,1,0:T(8,128)(2,1)S(1)}, bf16[13,2,32,128]{3,2,1,0:T(8,128)(2,1)S(1)}, u32[]{:S(2)}, u32[]{:S(2)}) collective-permute-start(bf16[13,2,32,128]{3,2,1,0:T(8,128)(2,1)S(1)} %get-tuple-element.23), channel_id=1, source_target_pairs={{128,0},{192,64},{0,128},{64,192},{129,1},{193,65},{1,129},{65,193... | collective-permute-start | bytes 638984 | tf_op jit(solution)/shard_map/ppermute | solution.py:90
  6.8 12.7 %collective-permute-start.2 = (bf16[13,2,32,128]{3,2,1,0:T(8,128)(2,1)S(1)}, bf16[13,2,32,128]{3,2,1,0:T(8,128)(2,1)S(1)}, u32[]{:S(2)}, u32[]{:S(2)}) collective-permute-start(bf16[13,2,32,128]{3,2,1,0:T(8,128)(2,1)S(1)} %get-tuple-element.24), channel_id=1, source_target_pairs={{192,0},{0,64},{64,128},{128,192},{193,1},{1,65},{65,129},{129,193... | collective-permute-start | bytes 638984 | tf_op jit(solution)/shard_map/ppermute | solution.py:90
  19.7 20.4 %collective-permute-start.3 = (bf16[17,128,128]{2,1,0:T(8,128)(2,1)S(1)}, bf16[17,128,128]{2,1,0:T(8,128)(2,1)S(1)}, u32[]{:S(2)}, u32[]{:S(2)}) collective-permute-start(bf16[17,128,128]{2,1,0:T(8,128)(2,1)S(1)} %get-tuple-element.26), channel_id=1, source_target_pairs={{255,0},{0,64},{64,128},{128,192},{192,1},{1,65},{65,129},{129,193... | collective-permute-start | bytes 1671176 | tf_op jit(solution)/shard_map/ppermute | solution.py:90
  19.8 20.3 %collective-permute-start.4 = (bf16[17,128,128]{2,1,0:T(8,128)(2,1)S(1)}, bf16[17,128,128]{2,1,0:T(8,128)(2,1)S(1)}, u32[]{:S(2)}, u32[]{:S(2)}) collective-permute-start(bf16[17,128,128]{2,1,0:T(8,128)(2,1)S(1)} %get-tuple-element.27), channel_id=1, source_target_pairs={{64,0},{128,64},{192,128},{1,192},{65,1},{129,65},{193,129},{2,193... | collective-permute-start | bytes 1671176 | tf_op jit(solution)/shard_map/ppermute | solution.py:90
  25.8 14.2 %collective-permute-start.5 = (bf16[10,128,128]{2,1,0:T(8,128)(2,1)S(1)}, bf16[10,128,128]{2,1,0:T(8,128)(2,1)S(1)}, u32[]{:S(2)}, u32[]{:S(2)}) collective-permute-start(bf16[10,128,128]{2,1,0:T(8,128)(2,1)S(1)} %get-tuple-element.28), channel_id=1, source_target_pairs={{4,0},{68,64},{132,128},{196,192},{5,1},{69,65},{133,129},{197,193... | collective-permute-start | bytes 983048 | tf_op jit(solution)/shard_map/ppermute | solution.py:90
  40.1 37.6 %collective-permute-start.7 = (bf16[10,128,128]{2,1,0:T(8,128)(2,1)S(1)}, bf16[10,128,128]{2,1,0:T(8,128)(2,1)S(1)}, u32[]{:S(2)}, u32[]{:S(2)}) collective-permute-start(bf16[10,128,128]{2,1,0:T(8,128)(2,1)S(1)} %shard_map.31), channel_id=1, source_target_pairs={{40,0},{104,64},{168,128},{232,192},{41,1},{105,65},{169,129},{233... | collective-permute-start | bytes 983048 | tf_op jit(solution)/shard_map/ppermute | solution.py:90
  53.2 24.5 %collective-permute-start.6 = (bf16[10,128,128]{2,1,0:T(8,128)(2,1)S(1)}, bf16[10,128,128]{2,1,0:T(8,128)(2,1)S(1)}, u32[]{:S(2)}, u32[]{:S(2)}) collective-permute-start(bf16[10,128,128]{2,1,0:T(8,128)(2,1)S(1)} %shard_map.31), channel_id=1, source_target_pairs={{16,0},{80,64},{144,128},{208,192},{17,1},{81,65},{145,129},{209,1... | collective-permute-start | bytes 983048 | tf_op jit(solution)/shard_map/ppermute | solution.py:90
  54.0 18.6 %collective-permute-start.8 = (bf16[6,128,128]{2,1,0:T(8,128)(2,1)S(1)}, bf16[6,128,128]{2,1,0:T(8,128)(2,1)S(1)}, u32[]{:S(2)}, u32[]{:S(2)}) collective-permute-start(bf16[6,128,128]{2,1,0:T(8,128)(2,1)S(1)} %get-tuple-element.29), channel_id=1, source_target_pairs={{20,0},{84,64},{148,128},{212,192},{21,1},{85,65},{149,129},{213,1... | collective-permute-start | bytes 589832 | tf_op jit(solution)/shard_map/ppermute | solution.py:90
  62.8 14.9 %collective-permute-start.9 = (bf16[6,128,128]{2,1,0:T(8,128)(2,1)S(1)}, bf16[6,128,128]{2,1,0:T(8,128)(2,1)S(1)}, u32[]{:S(2)}, u32[]{:S(2)}) collective-permute-start(bf16[6,128,128]{2,1,0:T(8,128)(2,1)S(1)} %get-tuple-element.30), channel_id=1, source_target_pairs={{44,0},{108,64},{172,128},{236,192},{45,1},{109,65},{173,129},{237... | collective-permute-start | bytes 589832 | tf_op jit(solution)/shard_map/ppermute | solution.py:90
  77.8 17.9 %collective-permute-start.10 = (bf16[16,128,128]{2,1,0:T(8,128)(2,1)S(1)}, bf16[16,128,128]{2,1,0:T(8,128)(2,1)S(1)}, u32[]{:S(2)}, u32[]{:S(2)}) collective-permute-start(bf16[16,128,128]{2,1,0:T(8,128)(2,1)S(1)} %get-tuple-element.31), channel_id=1, source_target_pairs={{255,0},{0,64},{64,128},{128,192},{192,1},{1,65},{65,129},{129,193... | collective-permute-start | bytes 1572872 | tf_op jit(solution)/shard_map/ppermute | solution.py:90
  77.9 17.8 %collective-permute-start.11 = (bf16[16,128,128]{2,1,0:T(8,128)(2,1)S(1)}, bf16[16,128,128]{2,1,0:T(8,128)(2,1)S(1)}, u32[]{:S(2)}, u32[]{:S(2)}) collective-permute-start(bf16[16,128,128]{2,1,0:T(8,128)(2,1)S(1)} %get-tuple-element.32), channel_id=1, source_target_pairs={{64,0},{128,64},{192,128},{1,192},{65,1},{129,65},{193,129},{2,193... | collective-permute-start | bytes 1572872 | tf_op jit(solution)/shard_map/ppermute | solution.py:90
  101.4 6.4 %collective-permute-start.12 = (bf16[13,2,32,128]{3,2,1,0:T(8,128)(2,1)S(1)}, bf16[13,2,32,128]{3,2,1,0:T(8,128)(2,1)S(1)}, u32[]{:S(2)}, u32[]{:S(2)}) collective-permute-start(bf16[13,2,32,128]{3,2,1,0:T(8,128)(2,1)S(1)} %get-tuple-element.34), channel_id=1, source_target_pairs={{64,0},{128,64},{192,128},{0,192},{65,1},{129,65},{193,129},{1,193... | collective-permute-start | bytes 638984 | tf_op jit(solution)/shard_map/ppermute | solution.py:90
  101.5 7.9 %collective-permute-start.13 = (bf16[13,2,32,128]{3,2,1,0:T(8,128)(2,1)S(1)}, bf16[13,2,32,128]{3,2,1,0:T(8,128)(2,1)S(1)}, u32[]{:S(2)}, u32[]{:S(2)}) collective-permute-start(bf16[13,2,32,128]{3,2,1,0:T(8,128)(2,1)S(1)} %get-tuple-element.35), channel_id=1, source_target_pairs={{128,0},{192,64},{0,128},{64,192},{129,1},{193,65},{1,129},{65,193... | collective-permute-start | bytes 638984 | tf_op jit(solution)/shard_map/ppermute | solution.py:90
  101.6 13.2 %collective-permute-start.14 = (bf16[13,2,32,128]{3,2,1,0:T(8,128)(2,1)S(1)}, bf16[13,2,32,128]{3,2,1,0:T(8,128)(2,1)S(1)}, u32[]{:S(2)}, u32[]{:S(2)}) collective-permute-start(bf16[13,2,32,128]{3,2,1,0:T(8,128)(2,1)S(1)} %get-tuple-element.36), channel_id=1, source_target_pairs={{192,0},{0,64},{64,128},{128,192},{193,1},{1,65},{65,129},{129,193... | collective-permute-start | bytes 638984 | tf_op jit(solution)/shard_map/ppermute | solution.py:90

commit v5 on v3

--- a/solution.py
+++ b/solution.py
@@ -1,3 +1,5 @@
+import functools
+
 import jax
 import jax.numpy as jnp
 from jax import lax
@@ -59,16 +61,18 @@
 
 OWN = [(t, b) for b in range(DIAGS) for t in range(2)]
 LOW, HIGH = tiles([-2, -1]), tiles([2, 3])
-FAN = [(t, b) for t in range(2) for b in SHARED]
-PLUS_BAND = [(t + FAR, b) for t, b in FAN]
-MINUS_BAND = [(t - FAR, b) for t, b in FAN]
+FAN = tiles(range(FAR - 1, FAR + 3), band_of)
+PLUS_BAND = FAN
+MINUS_BAND = [(j - 2 * FAR, b) for j, b in FAN]
 PLUS_FAR = tiles([FAR, FAR + 1], far_of)
 MINUS_FAR = tiles([-FAR, -FAR + 1], far_of)
-EDGE_LOW = tiles([-3, FAR - 1, -FAR - 1])
-EDGE_HIGH = tiles([4, FAR + 2, -FAR + 2])
-MAIN = [OWN, LOW, HIGH, PLUS_BAND, MINUS_BAND, PLUS_FAR, MINUS_FAR]
-ARRIVE = MAIN + [EDGE_LOW, EDGE_HIGH]
+EDGE_LOW = tiles([-3]) + tiles([FAR - 1, -FAR - 1], far_of)
+EDGE_HIGH = tiles([4]) + tiles([FAR + 2, -FAR + 2], far_of)
+MAIN = [LOW, HIGH, PLUS_FAR, MINUS_FAR]
+ARRIVE = [OWN] + MAIN + [PLUS_BAND, MINUS_BAND, EDGE_LOW, EDGE_HIGH]
 NEAR = [[(j % 2, b) for j, b in message] for message in (LOW, HIGH)]
+SWAP_LOW = [(1, b) for b in band_of(FAR - 1)]
+SWAP_HIGH = [(0, b) for b in band_of(FAR + 2)]
 DIRECT = [[(j % 2, b) for j, b in message] for message in (PLUS_FAR, MINUS_FAR)]
 
 
@@ -98,8 +102,12 @@
     return moved(x, lambda p: same_group(p, distance))
 
 
-def from_layer_across(x, distance):
-    return moved(x, lambda p: across(same_group(p, distance)))
+def swapped(x):
+    return moved(x, across)
+
+
+def edge_across(x, distance):
+    return moved(x, lambda p: across((across(p) + distance) % PAIRS))
 
 
 def far_across(x, distance):
@@ -130,8 +138,8 @@
 
 def split_body(me_ref, presence_ref, blocks_ref, *out_refs):
     me = me_ref[0]
+    shared_ref = out_refs[LAYERS]
     for s in range(LAYERS):
-        own_ref, shared_ref = out_refs[s], out_refs[LAYERS + s]
         other = lax.rem(me - s + LAYERS, LAYERS)
         for t in range(2):
             row = 2 * other + t
@@ -139,9 +147,17 @@
                 tile = blocks_ref[d, row]
                 present = presence_ref[d, row] != 0
                 tile = jnp.where(present, tile, jnp.zeros_like(tile))
-                own_ref[d, t] = tile
+                out_refs[s][d, t] = tile
                 if d in SHARED:
-                    shared_ref[SHARED.index(d), t] = tile
+                    shared_ref[SHARED.index(d), row] = tile
+
+
+def resplit_body(me_ref, shared_ref, *out_refs):
+    for s, out_ref in enumerate(out_refs[-LAYERS:]):
+        row = 2 * lax.rem(me_ref[0] - s + LAYERS, LAYERS)
+        for t in range(2):
+            for k in range(len(SHARED)):
+                out_ref[k, t] = shared_ref[k, row + t]
 
 
 def gather_pieces(me, pieces, out_ref):
@@ -151,35 +167,47 @@
         out_ref[:, :, pl.ds(start, BS // LAYERS), :] = piece[...]
 
 
-def pack_body(me_ref, *refs):
+def pack_body(messages, me_ref, *refs):
     pieces, own_ref, out_refs = refs[:LAYERS], refs[LAYERS], refs[LAYERS + 1 :]
     gather_pieces(me_ref[0], pieces, own_ref)
-    for message, out_ref in zip(DIRECT, out_refs):
+    for message, out_ref in zip(messages, out_refs):
         for k, (t, b) in enumerate(message):
             out_ref[k] = own_ref[b, t]
 
 
-def near_body(own_ref, after_ref, *out_refs):
-    del after_ref
-    for message, out_ref in zip(NEAR, out_refs):
+def near_body(own_ref, *refs):
+    for message, out_ref in zip(NEAR, refs[-2:]):
         for k, (t, b) in enumerate(message):
             out_ref[k] = own_ref[b, t]
 
 
-def fan_body(me_ref, *refs):
-    pieces, out_ref, shared_ref = refs[:LAYERS], refs[LAYERS], refs[LAYERS + 1]
+def shared_body(me_ref, *refs):
+    pieces, shared_ref, out_refs = refs[:LAYERS], refs[LAYERS], refs[LAYERS + 1 :]
     gather_pieces(me_ref[0], pieces, shared_ref)
-    for k, (t, b) in enumerate(FAN):
-        out_ref[k] = shared_ref[SHARED.index(b), t]
+    for message, out_ref in zip((SWAP_LOW, SWAP_HIGH), out_refs):
+        for k, (t, b) in enumerate(message):
+            out_ref[k] = shared_ref[SHARED.index(b), t]
+
+
+def fan_body(shared_ref, low_ref, high_ref, *refs):
+    out_ref = refs[-1]
+    for k, (j, b) in enumerate(FAN):
+        t = j - FAR
+        if t < 0:
+            out_ref[k] = low_ref[SWAP_LOW.index((1, b))]
+        elif t > 1:
+            out_ref[k] = high_ref[SWAP_HIGH.index((0, b))]
+        else:
+            out_ref[k] = shared_ref[SHARED.index(b), t]
 
 
 def edge_body(*refs):
-    sources, out_refs = refs[: len(MAIN) - 1], refs[len(MAIN) - 1 :]
+    sources, out_refs = refs[: len(MAIN)], refs[len(MAIN) :]
     for shift, message, out_ref in zip((2, -2), (EDGE_LOW, EDGE_HIGH), out_refs):
         for k, (j, b) in enumerate(message):
             [(ref, held)] = [
                 (ref, held)
-                for ref, held in zip(sources, MAIN[1:])
+                for ref, held in zip(sources, MAIN)
                 if (j + shift, b) in held
             ]
             out_ref[k] = ref[held.index((j + shift, b))]
@@ -199,7 +227,6 @@
     sources, outs = refs[: len(ARRIVE)], refs[len(ARRIVE) : len(ARRIVE) + LAYERS]
     right_ref, left_ref, result_ref = refs[len(ARRIVE) + LAYERS :]
     me = me_ref[0]
-    own_ref = sources[0]
     placed = placements()
     zero = jnp.zeros((BS, BS), jnp.bfloat16)
     for row in range(16):
@@ -219,7 +246,7 @@
         for column in range(16):
             where = (pl.ds(i * BS, BS), pl.ds(column * BS, BS))
             d = targets.get((i, column))
-            left_ref[where] = zero if d is None else own_ref[d, i]
+            left_ref[where] = zero if d is None else sources[0][d, i]
 
     def dot(left, right):
         return jnp.dot(left, right, preferred_element_type=jnp.float32)
@@ -277,35 +304,52 @@
                 out_ref[d, row + t] = refs[s][d, t]
 
 
+def exchanged(pieces):
+    far = from_layer(pieces[2], 2)
+    return [pieces[0], from_layer(pieces[1], 1), far, from_layer(pieces[3], 3)]
+
+
 def per_device(blocks, presence):
     me = lax.axis_index("layer").astype(jnp.int32).reshape(1)
+
+    def packed(messages):
+        return [bf16(len(message), BS, BS) for message in messages]
+
     quarter = bf16(DIAGS, 2, BS // LAYERS, BS)
     shared_quarter = bf16(len(SHARED), 2, BS // LAYERS, BS)
-
-    def packed(messages):
-        return [bf16(len(message), BS, BS) for message in messages]
-
-    pieces = call(split_body, [quarter] * LAYERS + [shared_quarter] * LAYERS, 2, 1)(
-        me, presence, blocks
-    )
-    shared = [from_layer_across(pieces[LAYERS + s], s) for s in range(LAYERS)]
-    pieces = [pieces[0]] + [from_layer(pieces[s], s) for s in range(1, LAYERS)]
-    band = call(
-        fan_body,
-        packed([FAN])[0],
+    *pieces, shared = call(
+        split_body,
+        [quarter] * LAYERS + [bf16(len(SHARED), 2 * LAYERS, BS // LAYERS, BS)],
+        2,
+        1,
+    )(me, presence, blocks)
+    shared = swapped(shared)
+    pieces = exchanged(pieces)
+    own, plus_far, minus_far = call(
+        functools.partial(pack_body, DIRECT),
+        [bf16(DIAGS, 2, BS, BS)] + packed(DIRECT),
         1,
         LAYERS,
-        scratch=[pltpu.VMEM((len(SHARED), 2, BS, BS), jnp.bfloat16)],
-    )(me, *shared)
-    own, plus_far, minus_far = call(
-        pack_body, [bf16(DIAGS, 2, BS, BS)] + packed(DIRECT), 1, LAYERS
     )(me, *pieces)
     plus_far = from_pair(plus_far, FAR_PAIRS)
     minus_far = from_pair(minus_far, -FAR_PAIRS)
+    some = [shared]
+    some = call(resplit_body, [shared_quarter] * LAYERS, 1, len(some))(me, *some)
+    some = exchanged(some)
+    shared, swap_low, swap_high = call(
+        shared_body,
+        [bf16(len(SHARED), 2, BS, BS)] + packed([SWAP_LOW, SWAP_HIGH]),
+        1,
+        LAYERS,
+    )(me, *some)
+    swap_low, swap_high = edge_across(swap_low, -1), edge_across(swap_high, 1)
+    before = [own]
+    low, high = call(near_body, packed([LOW, HIGH]), 0, len(before))(*before)
+    low, high = from_pair(low, -1), from_pair(high, 1)
+    before = [shared, swap_low, swap_high, plus_far, minus_far]
+    band = call(fan_body, packed([FAN])[0], 0, len(before))(*before)
     plus_band, minus_band = far_across(band, FAR_PAIRS), far_across(band, -FAR_PAIRS)
-    low, high = call(near_body, packed([LOW, HIGH]), 0, 2)(own, band)
-    low, high = from_pair(low, -1), from_pair(high, 1)
-    arrived = [low, high, plus_band, minus_band, plus_far, minus_far]
+    arrived = [low, high, plus_far, minus_far]
     edge_low, edge_high = call(
         edge_body, packed([EDGE_LOW, EDGE_HIGH]), 0, len(arrived)
     )(*arrived)
@@ -321,8 +365,8 @@
             pltpu.VMEM((DIAGS, 2, BS, BS), jnp.bfloat16),
         ],
         flops=4 * 224 * 2 * BS**3,
-    )(me, presence, own, *arrived, edge_low, edge_high)
-    results = [results[0]] + [from_layer(results[s], s) for s in range(1, LAYERS)]
+    )(me, presence, own, *arrived, plus_band, minus_band, edge_low, edge_high)
+    results = exchanged(results)
     return call(join_body, bf16(DIAGS, 2 * LAYERS, BS // LAYERS, BS), 1, LAYERS)(
         me, *results
     )

time: 111 us -> 107 us (0.964)
  waiting for transfers between devices: 56.8 us -> 50.4 us
  starting transfers between devices: 44.1 us -> 46 us
    ppermute x18 -> x20, waiting for transfers between devices: 56.8 us -> 50.4 us  [moved(): return lax.ppermute(x, AXES, route)]
    ppermute x18 -> x20, starting transfers between devices: 44.1 us -> 46 us  [moved(): return lax.ppermute(x, AXES, route)]
  transfers between devices with their start and end apart: 18 -> 20, of which waited for: 11 -> 11; matrix products, arithmetic and copies ran while one was open for 0% -> 0% of each run, Pallas kernels for 0% -> 0%
where the time goes in v5:
time: 107 us; the launch traced here: 106 us
  waiting for transfers between devices  50.4 us (47%)
  starting transfers between devices  46 us (43%)
  Pallas kernels  7.97 us (7%)
  local copies, waits for them, and re-layouts  1.92 us (2%)
    ppermute x20, waiting for transfers between devices, moved(): return lax.ppermute(x, AXES, route)  50.4 us
    ppermute x20, starting transfers between devices, moved(): return lax.ppermute(x, AXES, route)  46 us
    pallas_call x1, Pallas kernels, per_device(): call(purify_body, [quarter] * LAYERS, 2, len(ARRIVE), scratch=[pltpu.VMEM...  5.76 us
  transfers between devices with their start and end apart: 20, of which 11 were waited for; matrix products, arithmetic and copies ran while one was open for 0% of the time, Pallas kernels for 0%

profile of v5, /device:TPU:1, one launch (start us, length us, event | category | flops | bytes accessed | tf_op | source)
XLA Modules:
  0.0 106.4 jit_solution(4686055630043344790)
XLA Ops:
  0.0 0.0 copy-start.1
  0.0 0.7 copy-done.1
  0.7 0.1 copy.4.presence_ref
  0.8 0.0 copy-start
  0.8 1.2 %copy-done = bf16[13,8,32,128]{3,2,1,0:T(8,128)(2,1)S(1)} copy-done((bf16[13,8,32,128]{3,2,1,0:T(8,128)(2,1)S(1)}, bf16[13,8,32,128]{3,2,1,0:T(8,128)(2,1)}, u32[]{:S(2)}) %copy-start) | copy-done | bytes 851992
  1.9 0.9 shard_map.28
  2.9 3.4 %collective-permute-start = (bf16[13,2,32,128]{3,2,1,0:T(8,128)(2,1)S(1)}, bf16[13,2,32,128]{3,2,1,0:T(8,128)(2,1)S(1)}, u32[]{:S(2)}, u32[]{:S(2)}) collective-permute-start(bf16[13,2,32,128]{3,2,1,0:T(8,128)(2,1)S(1)} %get-tuple-element.29), channel_id=1, source_target_pairs={{64,0},{128,64},{192,128},{0,192},{65,1},{129,65},{193,129},{1,193... | collective-permute-start | bytes 638984 | tf_op jit(solution)/shard_map/ppermute | solution.py:85
  6.3 0.5 collective-permute-start.1
  6.8 0.6 collective-permute-start.2
  7.4 6.9 %collective-permute-start.7 = (bf16[5,8,32,128]{3,2,1,0:T(8,128)(2,1)S(1)}, bf16[5,8,32,128]{3,2,1,0:T(8,128)(2,1)S(1)}, u32[]{:S(2)}, u32[]{:S(2)}) collective-permute-start(bf16[5,8,32,128]{3,2,1,0:T(8,128)(2,1)S(1)} %get-tuple-element.37), channel_id=1, source_target_pairs={{4,0},{68,64},{132,128},{196,192},{5,1},{69,65},{133,129},{197,193... | collective-permute-start | bytes 983048 | tf_op jit(solution)/shard_map/ppermute | solution.py:85
  14.3 0.5 collective-permute-done.refs_1_
  14.8 0.0 collective-permute-done.1.refs_2_
  14.8 4.7 %collective-permute-done.2.refs_3_ = bf16[13,2,32,128]{3,2,1,0:T(8,128)(2,1)S(1)} collective-permute-done((bf16[13,2,32,128]{3,2,1,0:T(8,128)(2,1)S(1)}, bf16[13,2,32,128]{3,2,1,0:T(8,128)(2,1)S(1)}, u32[]{:S(2)}, u32[]{:S(2)}) %collective-permute-start.2) | collective-permute-done | bytes 213024 | tf_op jit(solution)/shard_map/ppermute | solution.py:85
  19.5 0.1 shard_map.29
  19.6 0.1 shard_map.30
  19.7 0.1 collective-permute-start.3
  19.8 6.1 %collective-permute-start.4 = (bf16[17,128,128]{2,1,0:T(8,128)(2,1)S(1)}, bf16[17,128,128]{2,1,0:T(8,128)(2,1)S(1)}, u32[]{:S(2)}, u32[]{:S(2)}) collective-permute-start(bf16[17,128,128]{2,1,0:T(8,128)(2,1)S(1)} %get-tuple-element.34), channel_id=1, source_target_pairs={{64,0},{128,64},{192,128},{1,192},{65,1},{129,65},{193,129},{2,193... | collective-permute-start | bytes 1671176 | tf_op jit(solution)/shard_map/ppermute | solution.py:85
  25.9 9.0 %collective-permute-start.5 = (bf16[6,128,128]{2,1,0:T(8,128)(2,1)S(1)}, bf16[6,128,128]{2,1,0:T(8,128)(2,1)S(1)}, u32[]{:S(2)}, u32[]{:S(2)}) collective-permute-start(bf16[6,128,128]{2,1,0:T(8,128)(2,1)S(1)} %get-tuple-element.35), channel_id=1, source_target_pairs={{20,0},{84,64},{148,128},{212,192},{21,1},{85,65},{149,129},{213,1... | collective-permute-start | bytes 589832 | tf_op jit(solution)/shard_map/ppermute | solution.py:85
  34.9 0.0 collective-permute-done.7.shared_ref
  34.9 0.1 collective-permute-start.8
  35.0 0.1 collective-permute-start.9
  35.1 9.7 %collective-permute-done.8.refs_1_ = bf16[5,2,32,128]{3,2,1,0:T(8,128)(2,1)S(1)} collective-permute-done((bf16[5,2,32,128]{3,2,1,0:T(8,128)(2,1)S(1)}, bf16[5,2,32,128]{3,2,1,0:T(8,128)(2,1)S(1)}, u32[]{:S(2)}, u32[]{:S(2)}) %collective-permute-start.8) | collective-permute-done | bytes 81952 | tf_op jit(solution)/shard_map/ppermute | solution.py:85
  44.8 2.8 %collective-permute-start.6 = (bf16[6,128,128]{2,1,0:T(8,128)(2,1)S(1)}, bf16[6,128,128]{2,1,0:T(8,128)(2,1)S(1)}, u32[]{:S(2)}, u32[]{:S(2)}) collective-permute-start(bf16[6,128,128]{2,1,0:T(8,128)(2,1)S(1)} %get-tuple-element.36), channel_id=1, source_target_pairs={{44,0},{108,64},{172,128},{236,192},{45,1},{109,65},{173,129},{237... | collective-permute-start | bytes 589832 | tf_op jit(solution)/shard_map/ppermute | solution.py:85
  47.6 0.0 collective-permute-done.9.refs_2_
  47.6 0.0 collective-permute-start.10
  47.6 5.2 %collective-permute-done.10.refs_3_ = bf16[5,2,32,128]{3,2,1,0:T(8,128)(2,1)S(1)} collective-permute-done((bf16[5,2,32,128]{3,2,1,0:T(8,128)(2,1)S(1)}, bf16[5,2,32,128]{3,2,1,0:T(8,128)(2,1)S(1)}, u32[]{:S(2)}, u32[]{:S(2)}) %collective-permute-start.10) | collective-permute-done | bytes 81952 | tf_op jit(solution)/shard_map/ppermute | solution.py:85
  52.9 0.1 collective-permute-start.11
  53.0 0.0 collective-permute-done.5.refs_0_.refs_2_.refs_3_
  53.0 5.3 %collective-permute-start.12 = (bf16[3,128,128]{2,1,0:T(8,128)(2,1)S(1)}, bf16[3,128,128]{2,1,0:T(8,128)(2,1)S(1)}, u32[]{:S(2)}, u32[]{:S(2)}) collective-permute-start(bf16[3,128,128]{2,1,0:T(8,128)(2,1)S(1)} %get-tuple-element.44), channel_id=1, source_target_pairs={{64,0},{128,64},{192,128},{1,192},{65,1},{129,65},{193,129},{2,193... | collective-permute-start | bytes 294920 | tf_op jit(solution)/shard_map/ppermute | solution.py:85
  58.3 1.9 %collective-permute-done.6.refs_1_.refs_3_.refs_4_ = bf16[6,128,128]{2,1,0:T(8,128)(2,1)S(1)} collective-permute-done((bf16[6,128,128]{2,1,0:T(8,128)(2,1)S(1)}, bf16[6,128,128]{2,1,0:T(8,128)(2,1)S(1)}, u32[]{:S(2)}, u32[]{:S(2)}) %collective-permute-start.6) | collective-permute-done | bytes 196640 | tf_op jit(solution)/shard_map/ppermute | solution.py:85
  60.2 7.5 %collective-permute-done.11.low_ref = bf16[3,128,128]{2,1,0:T(8,128)(2,1)S(1)} collective-permute-done((bf16[3,128,128]{2,1,0:T(8,128)(2,1)S(1)}, bf16[3,128,128]{2,1,0:T(8,128)(2,1)S(1)}, u32[]{:S(2)}, u32[]{:S(2)}) %collective-permute-start.11) | collective-permute-done | bytes 98336 | tf_op jit(solution)/shard_map/ppermute | solution.py:85
  67.7 0.0 collective-permute-done.12.high_ref
  67.8 2.2 %collective-permute-start.14 = (bf16[14,128,128]{2,1,0:T(8,128)(2,1)S(1)}, bf16[14,128,128]{2,1,0:T(8,128)(2,1)S(1)}, u32[]{:S(2)}, u32[]{:S(2)}) collective-permute-start(bf16[14,128,128]{2,1,0:T(8,128)(2,1)S(1)} %shard_map.33), channel_id=1, source_target_pairs={{40,0},{104,64},{168,128},{232,192},{41,1},{105,65},{169,129},{233... | collective-permute-start | bytes 1376264 | tf_op jit(solution)/shard_map/ppermute | solution.py:85
  69.9 2.0 %collective-permute-start.13 = (bf16[14,128,128]{2,1,0:T(8,128)(2,1)S(1)}, bf16[14,128,128]{2,1,0:T(8,128)(2,1)S(1)}, u32[]{:S(2)}, u32[]{:S(2)}) collective-permute-start(bf16[14,128,128]{2,1,0:T(8,128)(2,1)S(1)} %shard_map.33), channel_id=1, source_target_pairs={{16,0},{80,64},{144,128},{208,192},{17,1},{81,65},{145,129},{209,1... | collective-permute-start | bytes 1376264 | tf_op jit(solution)/shard_map/ppermute | solution.py:85
  71.9 0.0 collective-permute-done.3.refs_0_.refs_1_
  71.9 0.0 collective-permute-done.4.refs_1_.refs_2_
  72.0 0.3 collective-permute-start.15
  72.2 5.1 %collective-permute-start.16 = (bf16[10,128,128]{2,1,0:T(8,128)(2,1)S(1)}, bf16[10,128,128]{2,1,0:T(8,128)(2,1)S(1)}, u32[]{:S(2)}, u32[]{:S(2)}) collective-permute-start(bf16[10,128,128]{2,1,0:T(8,128)(2,1)S(1)} %get-tuple-element.46), channel_id=1, source_target_pairs={{64,0},{128,64},{192,128},{1,192},{65,1},{129,65},{193,129},{2,193... | collective-permute-start | bytes 983048 | tf_op jit(solution)/shard_map/ppermute | solution.py:85
  77.3 6.3 %collective-permute-done.14.refs_6_ = bf16[14,128,128]{2,1,0:T(8,128)(2,1)S(1)} collective-permute-done((bf16[14,128,128]{2,1,0:T(8,128)(2,1)S(1)}, bf16[14,128,128]{2,1,0:T(8,128)(2,1)S(1)}, u32[]{:S(2)}, u32[]{:S(2)}) %collective-permute-start.14) | collective-permute-done | bytes 458784 | tf_op jit(solution)/shard_map/ppermute | solution.py:85
  83.6 2.6 %collective-permute-done.13.refs_5_ = bf16[14,128,128]{2,1,0:T(8,128)(2,1)S(1)} collective-permute-done((bf16[14,128,128]{2,1,0:T(8,128)(2,1)S(1)}, bf16[14,128,128]{2,1,0:T(8,128)(2,1)S(1)}, u32[]{:S(2)}, u32[]{:S(2)}) %collective-permute-start.13) | collective-permute-done | bytes 458784 | tf_op jit(solution)/shard_map/ppermute | solution.py:85
  86.2 0.0 collective-permute-done.15.refs_7_
  86.2 0.0 collective-permute-done.16.refs_8_
  86.2 5.8 %shard_map.35 = (bf16[13,2,32,128]{3,2,1,0:T(8,128)(2,1)S(1)}, bf16[13,2,32,128]{3,2,1,0:T(8,128)(2,1)S(1)}, bf16[13,2,32,128]{3,2,1,0:T(8,128)(2,1)S(1)}, bf16[13,2,32,128]{3,2,1,0:T(8,128)(2,1)S(1)}) custom-call(s32[1]{0:T(128)} %bitcast.me_ref, s32[13,8]{1,0:T(8,128)S(1)} %copy.4.presence_ref, ...), custom_call_target="tpu_custom_call" | custom-call | flops 3758096384 | bytes 4194304 | tf_op jit(solution)/shard_map/pallas_call | solution.py:357
  92.0 0.1 collective-permute-start.17
  92.1 0.1 collective-permute-start.18
  92.2 1.4 %collective-permute-start.19 = (bf16[13,2,32,128]{3,2,1,0:T(8,128)(2,1)S(1)}, bf16[13,2,32,128]{3,2,1,0:T(8,128)(2,1)S(1)}, u32[]{:S(2)}, u32[]{:S(2)}) collective-permute-start(bf16[13,2,32,128]{3,2,1,0:T(8,128)(2,1)S(1)} %get-tuple-element.50), channel_id=1, source_target_pairs={{192,0},{0,64},{64,128},{128,192},{193,1},{1,65},{65,129},{129,193... | collective-permute-start | bytes 638984 | tf_op jit(solution)/shard_map/ppermute | solution.py:85
  93.5 5.2 %collective-permute-done.17.refs_1_ = bf16[13,2,32,128]{3,2,1,0:T(8,128)(2,1)S(1)} collective-permute-done((bf16[13,2,32,128]{3,2,1,0:T(8,128)(2,1)S(1)}, bf16[13,2,32,128]{3,2,1,0:T(8,128)(2,1)S(1)}, u32[]{:S(2)}, u32[]{:S(2)}) %collective-permute-start.17) | collective-permute-done | bytes 213024 | tf_op jit(solution)/shard_map/ppermute | solution.py:85
  98.8 1.6 %collective-permute-done.18.refs_2_ = bf16[13,2,32,128]{3,2,1,0:T(8,128)(2,1)S(1)} collective-permute-done((bf16[13,2,32,128]{3,2,1,0:T(8,128)(2,1)S(1)}, bf16[13,2,32,128]{3,2,1,0:T(8,128)(2,1)S(1)}, u32[]{:S(2)}, u32[]{:S(2)}) %collective-permute-start.18) | collective-permute-done | bytes 213024 | tf_op jit(solution)/shard_map/ppermute | solution.py:85
  100.4 5.0 %collective-permute-done.19.refs_3_ = bf16[13,2,32,128]{3,2,1,0:T(8,128)(2,1)S(1)} collective-permute-done((bf16[13,2,32,128]{3,2,1,0:T(8,128)(2,1)S(1)}, bf16[13,2,32,128]{3,2,1,0:T(8,128)(2,1)S(1)}, u32[]{:S(2)}, u32[]{:S(2)}) %collective-permute-start.19) | collective-permute-done | bytes 213024 | tf_op jit(solution)/shard_map/ppermute | solution.py:85
  105.4 1.0 shard_map.36
  (4 shorter events, 0.1 us)
Async XLA Ops:
  0.0 0.7 copy-start.1
  0.8 1.2 %copy-start = (bf16[13,8,32,128]{3,2,1,0:T(8,128)(2,1)S(1)}, bf16[13,8,32,128]{3,2,1,0:T(8,128)(2,1)}, u32[]{:S(2)}) copy-start(bf16[13,8,32,128]{3,2,1,0:T(8,128)(2,1)} %blocks_ref.1) | copy-start | bytes 2555908
  2.9 11.9 %collective-permute-start = (bf16[13,2,32,128]{3,2,1,0:T(8,128)(2,1)S(1)}, bf16[13,2,32,128]{3,2,1,0:T(8,128)(2,1)S(1)}, u32[]{:S(2)}, u32[]{:S(2)}) collective-permute-start(bf16[13,2,32,128]{3,2,1,0:T(8,128)(2,1)S(1)} %get-tuple-element.29), channel_id=1, source_target_pairs={{64,0},{128,64},{192,128},{0,192},{65,1},{129,65},{193,129},{1,193... | collective-permute-start | bytes 638984 | tf_op jit(solution)/shard_map/ppermute | solution.py:85
  6.3 8.5 %collective-permute-start.1 = (bf16[13,2,32,128]{3,2,1,0:T(8,128)(2,1)S(1)}, bf16[13,2,32,128]{3,2,1,0:T(8,128)(2,1)S(1)}, u32[]{:S(2)}, u32[]{:S(2)}) collective-permute-start(bf16[13,2,32,128]{3,2,1,0:T(8,128)(2,1)S(1)} %get-tuple-element.30), channel_id=1, source_target_pairs={{128,0},{192,64},{0,128},{64,192},{129,1},{193,65},{1,129},{65,193... | collective-permute-start | bytes 638984 | tf_op jit(solution)/shard_map/ppermute | solution.py:85
  6.8 12.7 %collective-permute-start.2 = (bf16[13,2,32,128]{3,2,1,0:T(8,128)(2,1)S(1)}, bf16[13,2,32,128]{3,2,1,0:T(8,128)(2,1)S(1)}, u32[]{:S(2)}, u32[]{:S(2)}) collective-permute-start(bf16[13,2,32,128]{3,2,1,0:T(8,128)(2,1)S(1)} %get-tuple-element.31), channel_id=1, source_target_pairs={{192,0},{0,64},{64,128},{128,192},{193,1},{1,65},{65,129},{129,193... | collective-permute-start | bytes 638984 | tf_op jit(solution)/shard_map/ppermute | solution.py:85
  7.4 27.5 %collective-permute-start.7 = (bf16[5,8,32,128]{3,2,1,0:T(8,128)(2,1)S(1)}, bf16[5,8,32,128]{3,2,1,0:T(8,128)(2,1)S(1)}, u32[]{:S(2)}, u32[]{:S(2)}) collective-permute-start(bf16[5,8,32,128]{3,2,1,0:T(8,128)(2,1)S(1)} %get-tuple-element.37), channel_id=1, source_target_pairs={{4,0},{68,64},{132,128},{196,192},{5,1},{69,65},{133,129},{197,193... | collective-permute-start | bytes 983048 | tf_op jit(solution)/shard_map/ppermute | solution.py:85
  19.7 52.2 %collective-permute-start.3 = (bf16[17,128,128]{2,1,0:T(8,128)(2,1)S(1)}, bf16[17,128,128]{2,1,0:T(8,128)(2,1)S(1)}, u32[]{:S(2)}, u32[]{:S(2)}) collective-permute-start(bf16[17,128,128]{2,1,0:T(8,128)(2,1)S(1)} %get-tuple-element.33), channel_id=1, source_target_pairs={{255,0},{0,64},{64,128},{128,192},{192,1},{1,65},{65,129},{129,193... | collective-permute-start | bytes 1671176 | tf_op jit(solution)/shard_map/ppermute | solution.py:85
  19.8 52.1 %collective-permute-start.4 = (bf16[17,128,128]{2,1,0:T(8,128)(2,1)S(1)}, bf16[17,128,128]{2,1,0:T(8,128)(2,1)S(1)}, u32[]{:S(2)}, u32[]{:S(2)}) collective-permute-start(bf16[17,128,128]{2,1,0:T(8,128)(2,1)S(1)} %get-tuple-element.34), channel_id=1, source_target_pairs={{64,0},{128,64},{192,128},{1,192},{65,1},{129,65},{193,129},{2,193... | collective-permute-start | bytes 1671176 | tf_op jit(solution)/shard_map/ppermute | solution.py:85
  25.9 27.1 %collective-permute-start.5 = (bf16[6,128,128]{2,1,0:T(8,128)(2,1)S(1)}, bf16[6,128,128]{2,1,0:T(8,128)(2,1)S(1)}, u32[]{:S(2)}, u32[]{:S(2)}) collective-permute-start(bf16[6,128,128]{2,1,0:T(8,128)(2,1)S(1)} %get-tuple-element.35), channel_id=1, source_target_pairs={{20,0},{84,64},{148,128},{212,192},{21,1},{85,65},{149,129},{213,1... | collective-permute-start | bytes 589832 | tf_op jit(solution)/shard_map/ppermute | solution.py:85
  34.9 9.9 %collective-permute-start.8 = (bf16[5,2,32,128]{3,2,1,0:T(8,128)(2,1)S(1)}, bf16[5,2,32,128]{3,2,1,0:T(8,128)(2,1)S(1)}, u32[]{:S(2)}, u32[]{:S(2)}) collective-permute-start(bf16[5,2,32,128]{3,2,1,0:T(8,128)(2,1)S(1)} %get-tuple-element.39), channel_id=1, source_target_pairs={{64,0},{128,64},{192,128},{0,192},{65,1},{129,65},{193,129},{1,193... | collective-permute-start | bytes 245768 | tf_op jit(solution)/shard_map/ppermute | solution.py:85
  35.0 12.6 %collective-permute-start.9 = (bf16[5,2,32,128]{3,2,1,0:T(8,128)(2,1)S(1)}, bf16[5,2,32,128]{3,2,1,0:T(8,128)(2,1)S(1)}, u32[]{:S(2)}, u32[]{:S(2)}) collective-permute-start(bf16[5,2,32,128]{3,2,1,0:T(8,128)(2,1)S(1)} %get-tuple-element.40), channel_id=1, source_target_pairs={{128,0},{192,64},{0,128},{64,192},{129,1},{193,65},{1,129},{65,193... | collective-permute-start | bytes 245768 | tf_op jit(solution)/shard_map/ppermute | solution.py:85
  44.8 15.4 %collective-permute-start.6 = (bf16[6,128,128]{2,1,0:T(8,128)(2,1)S(1)}, bf16[6,128,128]{2,1,0:T(8,128)(2,1)S(1)}, u32[]{:S(2)}, u32[]{:S(2)}) collective-permute-start(bf16[6,128,128]{2,1,0:T(8,128)(2,1)S(1)} %get-tuple-element.36), channel_id=1, source_target_pairs={{44,0},{108,64},{172,128},{236,192},{45,1},{109,65},{173,129},{237... | collective-permute-start | bytes 589832 | tf_op jit(solution)/shard_map/ppermute | solution.py:85
  47.6 5.2 %collective-permute-start.10 = (bf16[5,2,32,128]{3,2,1,0:T(8,128)(2,1)S(1)}, bf16[5,2,32,128]{3,2,1,0:T(8,128)(2,1)S(1)}, u32[]{:S(2)}, u32[]{:S(2)}) collective-permute-start(bf16[5,2,32,128]{3,2,1,0:T(8,128)(2,1)S(1)} %get-tuple-element.41), channel_id=1, source_target_pairs={{192,0},{0,64},{64,128},{128,192},{193,1},{1,65},{65,129},{129,193... | collective-permute-start | bytes 245768 | tf_op jit(solution)/shard_map/ppermute | solution.py:85
  52.9 14.9 %collective-permute-start.11 = (bf16[3,128,128]{2,1,0:T(8,128)(2,1)S(1)}, bf16[3,128,128]{2,1,0:T(8,128)(2,1)S(1)}, u32[]{:S(2)}, u32[]{:S(2)}) collective-permute-start(bf16[3,128,128]{2,1,0:T(8,128)(2,1)S(1)} %get-tuple-element.43), channel_id=1, source_target_pairs={{199,0},{0,64},{64,128},{128,192},{192,1},{1,65},{65,129},{129,193... | collective-permute-start | bytes 294920 | tf_op jit(solution)/shard_map/ppermute | solution.py:85
  53.0 14.8 %collective-permute-start.12 = (bf16[3,128,128]{2,1,0:T(8,128)(2,1)S(1)}, bf16[3,128,128]{2,1,0:T(8,128)(2,1)S(1)}, u32[]{:S(2)}, u32[]{:S(2)}) collective-permute-start(bf16[3,128,128]{2,1,0:T(8,128)(2,1)S(1)} %get-tuple-element.44), channel_id=1, source_target_pairs={{64,0},{128,64},{192,128},{1,192},{65,1},{129,65},{193,129},{2,193... | collective-permute-start | bytes 294920 | tf_op jit(solution)/shard_map/ppermute | solution.py:85
  67.8 15.8 %collective-permute-start.14 = (bf16[14,128,128]{2,1,0:T(8,128)(2,1)S(1)}, bf16[14,128,128]{2,1,0:T(8,128)(2,1)S(1)}, u32[]{:S(2)}, u32[]{:S(2)}) collective-permute-start(bf16[14,128,128]{2,1,0:T(8,128)(2,1)S(1)} %shard_map.33), channel_id=1, source_target_pairs={{40,0},{104,64},{168,128},{232,192},{41,1},{105,65},{169,129},{233... | collective-permute-start | bytes 1376264 | tf_op jit(solution)/shard_map/ppermute | solution.py:85
  69.9 16.3 %collective-permute-start.13 = (bf16[14,128,128]{2,1,0:T(8,128)(2,1)S(1)}, bf16[14,128,128]{2,1,0:T(8,128)(2,1)S(1)}, u32[]{:S(2)}, u32[]{:S(2)}) collective-permute-start(bf16[14,128,128]{2,1,0:T(8,128)(2,1)S(1)} %shard_map.33), channel_id=1, source_target_pairs={{16,0},{80,64},{144,128},{208,192},{17,1},{81,65},{145,129},{209,1... | collective-permute-start | bytes 1376264 | tf_op jit(solution)/shard_map/ppermute | solution.py:85
  72.0 14.2 %collective-permute-start.15 = (bf16[10,128,128]{2,1,0:T(8,128)(2,1)S(1)}, bf16[10,128,128]{2,1,0:T(8,128)(2,1)S(1)}, u32[]{:S(2)}, u32[]{:S(2)}) collective-permute-start(bf16[10,128,128]{2,1,0:T(8,128)(2,1)S(1)} %get-tuple-element.45), channel_id=1, source_target_pairs={{255,0},{0,64},{64,128},{128,192},{192,1},{1,65},{65,129},{129,193... | collective-permute-start | bytes 983048 | tf_op jit(solution)/shard_map/ppermute | solution.py:85
  72.2 14.0 %collective-permute-start.16 = (bf16[10,128,128]{2,1,0:T(8,128)(2,1)S(1)}, bf16[10,128,128]{2,1,0:T(8,128)(2,1)S(1)}, u32[]{:S(2)}, u32[]{:S(2)}) collective-permute-start(bf16[10,128,128]{2,1,0:T(8,128)(2,1)S(1)} %get-tuple-element.46), channel_id=1, source_target_pairs={{64,0},{128,64},{192,128},{1,192},{65,1},{129,65},{193,129},{2,193... | collective-permute-start | bytes 983048 | tf_op jit(solution)/shard_map/ppermute | solution.py:85
  92.0 6.8 %collective-permute-start.17 = (bf16[13,2,32,128]{3,2,1,0:T(8,128)(2,1)S(1)}, bf16[13,2,32,128]{3,2,1,0:T(8,128)(2,1)S(1)}, u32[]{:S(2)}, u32[]{:S(2)}) collective-permute-start(bf16[13,2,32,128]{3,2,1,0:T(8,128)(2,1)S(1)} %get-tuple-element.48), channel_id=1, source_target_pairs={{64,0},{128,64},{192,128},{0,192},{65,1},{129,65},{193,129},{1,193... | collective-permute-start | bytes 638984 | tf_op jit(solution)/shard_map/ppermute | solution.py:85
  92.1 8.4 %collective-permute-start.18 = (bf16[13,2,32,128]{3,2,1,0:T(8,128)(2,1)S(1)}, bf16[13,2,32,128]{3,2,1,0:T(8,128)(2,1)S(1)}, u32[]{:S(2)}, u32[]{:S(2)}) collective-permute-start(bf16[13,2,32,128]{3,2,1,0:T(8,128)(2,1)S(1)} %get-tuple-element.49), channel_id=1, source_target_pairs={{128,0},{192,64},{0,128},{64,192},{129,1},{193,65},{1,129},{65,193... | collective-permute-start | bytes 638984 | tf_op jit(solution)/shard_map/ppermute | solution.py:85
  92.2 13.2 %collective-permute-start.19 = (bf16[13,2,32,128]{3,2,1,0:T(8,128)(2,1)S(1)}, bf16[13,2,32,128]{3,2,1,0:T(8,128)(2,1)S(1)}, u32[]{:S(2)}, u32[]{:S(2)}) collective-permute-start(bf16[13,2,32,128]{3,2,1,0:T(8,128)(2,1)S(1)} %get-tuple-element.50), channel_id=1, source_target_pairs={{192,0},{0,64},{64,128},{128,192},{193,1},{1,65},{65,129},{129,193... | collective-permute-start | bytes 638984 | tf_op jit(solution)/shard_map/ppermute | solution.py:85

commit v6 on v1

v6 whole, which is shorter than its diff:
```python
import functools

import jax
import jax.numpy as jnp
from jax import lax
from jax.experimental import pallas as pl
from jax.experimental.pallas import tpu as pltpu
from jax.sharding import PartitionSpec as P

NBG = 512
BAND = 3
FAR = 160
BS = 128
LAYERS = 4
PAIRS = NBG // 2
FAR_PAIRS = FAR // 2
AXES = ("layer", "row", "col")
OFFSETS = list(range(-BAND, BAND + 1)) + [
    FAR - 1, FAR, FAR + 1, -FAR - 1, -FAR, -FAR + 1,
]
DIAGS = len(OFFSETS)
OFFSET_SET = {value % NBG for value in OFFSETS}

REACH = (
    list(range(-BAND, BAND + 2))
    + list(range(FAR - 1, FAR + 3))
    + list(range(-FAR - 1, -FAR + 3))
)
SLOT = {value % NBG: index for index, value in enumerate(REACH)}
NEAR_END = 8 * BS
PLUS_END = 12 * BS
WIDTH = 16 * BS


def needed(j):
    found = set()
    for i in range(2):
        for left in OFFSETS:
            if (i + left - j) % NBG == 0:
                for b, right in enumerate(OFFSETS):
                    if (left + right) % NBG in OFFSET_SET:
                        found.add(b)
    return sorted(found)


def tiles(rows):
    return [(j, b) for j in rows for b in needed(j)]


BANDS = range(2 * BAND + 1)
ROWS = 2 * LAYERS
SHARED = [1, 2, 3, 4]
PLUS_ROWS = list(range(FAR - 1, FAR + 3))
MINUS_ROWS = list(range(-FAR - 1, -FAR + 3))


def direct_of(rows):
    return sorted({b for j in rows for b in needed(j)} - set(SHARED))


DIRECT = [direct_of(PLUS_ROWS), direct_of(MINUS_ROWS)]
NEAR = [(t, b) for b in range(DIAGS) for t in range(2)] + tiles([-3, -2, -1, 2, 3, 4])
FARS = tiles(PLUS_ROWS) + tiles(MINUS_ROWS)
ARRIVE = [NEAR, FARS]
HALO_LOW = tiles([-3, -2, -1])
HALO_HIGH = [(j + ROWS - 2, b) for j, b in tiles([2, 3, 4])]
EDGE_LOW = [(w, b) for w, j in enumerate((FAR - 1, -FAR - 1)) for b in needed(j)]
EDGE_HIGH = [(w, b) for w, j in enumerate((FAR + 2, -FAR + 2)) for b in needed(j)]


def place_of(p):
    return p % LAYERS * (PAIRS // LAYERS) + p // LAYERS


def moved(x, source_of):
    route = [(place_of(source_of(p)), place_of(p)) for p in range(PAIRS)]
    return lax.ppermute(x, AXES, route)


def across(p):
    cols = LAYERS * 8
    return p - p % cols + (p + cols // 2) % cols


def from_pair(x, distance):
    return moved(x, lambda p: (p + distance) % PAIRS)


def from_group(x, distance):
    return from_pair(x, LAYERS * distance)


def same_group(p, distance):
    return p - p % LAYERS + (p + distance) % LAYERS


def from_layer(x, distance):
    return moved(x, lambda p: same_group(p, distance))


def swapped(x):
    return moved(x, across)


def far_across(x, distance):
    return moved(x, lambda p: across((p + distance) % PAIRS))


def bf16(*shape):
    return jax.ShapeDtypeStruct(shape, jnp.bfloat16)


def call(body, out_shape, n_smem, n_vmem, scratch=(), flops=0, traffic=1 << 22):
    in_specs = [pl.BlockSpec(memory_space=pltpu.SMEM)] * n_smem
    in_specs += [pl.BlockSpec(memory_space=pltpu.VMEM)] * n_vmem
    return pl.pallas_call(
        body,
        out_shape=out_shape,
        in_specs=in_specs,
        out_specs=jax.tree.map(
            lambda _: pl.BlockSpec(memory_space=pltpu.VMEM), out_shape
        ),
        scratch_shapes=list(scratch),
        compiler_params=pltpu.CompilerParams(vmem_limit_bytes=48 << 20),
        cost_estimate=pl.CostEstimate(
            flops=flops, bytes_accessed=traffic, transcendentals=0
        ),
    )


def mask_body(presence_ref, blocks_ref, *out_refs):
    masked_ref, low_ref, high_ref, shared_ref, plus_ref, minus_ref = out_refs
    for row in range(ROWS):
        for d in range(DIAGS):
            tile = blocks_ref[d, row]
            tile = jnp.where(presence_ref[d, row] != 0, tile, jnp.zeros_like(tile))
            masked_ref[d, row] = tile
            if (row - ROWS, d) in HALO_LOW:
                low_ref[HALO_LOW.index((row - ROWS, d))] = tile
            if (row + ROWS, d) in HALO_HIGH:
                high_ref[HALO_HIGH.index((row + ROWS, d))] = tile
            if d in SHARED:
                shared_ref[SHARED.index(d), row] = tile
            for held, ref in zip(DIRECT, (plus_ref, minus_ref)):
                if d in held:
                    ref[held.index(d), row] = tile


def window_pieces(me, message, padded_ref, out_refs, lookup):
    for s, out_ref in enumerate(out_refs):
        start = 2 * lax.rem(me - s + LAYERS, LAYERS)
        for k, tile in enumerate(message):
            slot, row = lookup(tile)
            out_ref[k] = padded_ref[slot, start + row]


def near_body(masked_ref, low_ref, high_ref, *refs):
    out_ref, padded_ref = refs
    padded_ref[:, BAND : BAND + ROWS] = masked_ref[...]
    for message, ref in ((HALO_LOW, low_ref), (HALO_HIGH, high_ref)):
        for k, (row, b) in enumerate(message):
            padded_ref[b, row + BAND] = ref[k]
    for layer in range(LAYERS):
        for k, (j, b) in enumerate(NEAR):
            out_ref[layer, k] = padded_ref[b, 2 * layer + j + BAND]


def held_in(which, b, shared_refs, direct_refs):
    if b in SHARED:
        return shared_refs[which], SHARED.index(b)
    return direct_refs[which], DIRECT[which].index(b)


def edge_body(*refs):
    shared_refs, direct_refs = refs[0:2], refs[2:4]
    for message, row, out_ref in zip((EDGE_LOW, EDGE_HIGH), (ROWS - 1, 0), refs[4:]):
        for k, (which, b) in enumerate(message):
            ref, slot = held_in(which, b, shared_refs, direct_refs)
            out_ref[k] = ref[slot, row]


def fars_body(me_ref, *refs):
    shared_refs, direct_refs, edge_refs = refs[0:2], refs[2:4], refs[4:6]
    out_refs, padded_ref = refs[6 : 6 + LAYERS], refs[6 + LAYERS]
    for which in range(2):
        first = which * DIAGS
        for b in SHARED + DIRECT[which]:
            ref, slot = held_in(which, b, shared_refs, direct_refs)
            padded_ref[first + b, 1 : 1 + ROWS] = ref[slot]
    for message, row, ref in zip((EDGE_LOW, EDGE_HIGH), (0, ROWS + 1), edge_refs):
        for k, (which, b) in enumerate(message):
            padded_ref[which * DIAGS + b, row] = ref[k]

    def lookup(tile):
        j, b = tile
        which = 0 if j > 0 else 1
        return which * DIAGS + b, j - (FAR - 1 if which == 0 else -FAR - 1)

    window_pieces(me_ref[0], FARS, padded_ref, out_refs, lookup)


def placements():
    found = {}
    for operand, message in enumerate(ARRIVE):
        for k, (j, b) in enumerate(message):
            column = SLOT.get((j + OFFSETS[b]) % NBG)
            if column is not None:
                found[SLOT[j % NBG], column] = (operand, k)
    return found


def purify_body(me_ref, presence_ref, *refs):
    fars, outs = refs[1 : 1 + LAYERS], refs[1 + LAYERS : 1 + 2 * LAYERS]
    right_ref, left_ref, result_ref = refs[1 + 2 * LAYERS :]
    sources = ([refs[0].at[layer] for layer in range(LAYERS)], fars)
    me = me_ref[0]
    placed = placements()
    zero = jnp.zeros((BS, BS), jnp.bfloat16)
    starts = [
        [s * (BS // LAYERS) for s in range(LAYERS)],
        [lax.rem(me + s, LAYERS) * (BS // LAYERS) for s in range(LAYERS)],
    ]

    def gather(out_ref, row, column, operand, k):
        for s, piece in enumerate(sources[operand]):
            start = pl.multiple_of(row * BS + starts[operand][s], BS // LAYERS)
            out_ref[pl.ds(start, BS // LAYERS), pl.ds(column * BS, BS)] = piece[k]

    for row in range(16):
        for column in range(16):
            if (row, column) in placed:
                operand, k = placed[row, column]
                gather(right_ref, row, column, operand, k)
            else:
                right_ref[pl.ds(row * BS, BS), pl.ds(column * BS, BS)] = zero
    targets = {
        (i, SLOT[(i + offset) % NBG]): d
        for i in range(2)
        for d, offset in enumerate(OFFSETS)
    }
    for i in range(2):
        for column in range(16):
            d = targets.get((i, column))
            if d is None:
                left_ref[pl.ds(i * BS, BS), pl.ds(column * BS, BS)] = zero
            else:
                gather(left_ref, i, column, 0, NEAR.index((i, d)))

    def dot(left, right):
        return jnp.dot(left, right, preferred_element_type=jnp.float32)

    def product(columns):
        start = columns[0] * BS
        wide = pl.ds(start, len(columns) * BS)
        if start < NEAR_END:
            return dot(left_ref[...], right_ref[:, wide])
        if start < PLUS_END:
            return dot(left_ref[:, :PLUS_END], right_ref[:PLUS_END, wide])
        return dot(left_ref[:, :NEAR_END], right_ref[:NEAR_END, wide]) + dot(
            left_ref[:, PLUS_END:], right_ref[PLUS_END:, wide]
        )

    def each(columns, total, use):
        for at, column in enumerate(columns):
            for i in range(2):
                d = targets.get((i, column))
                if d is not None:
                    tile = total[i * BS : (i + 1) * BS, at * BS : (at + 1) * BS]
                    use(i, column, d, presence_ref[d, 2 * me + i] != 0, tile)

    groups = [[c, c + 1] for c in range(0, 16, 2)]

    def keep_second(i, column, d, present, tile):
        second = jnp.where(present, tile, jnp.zeros_like(tile)).astype(jnp.bfloat16)
        result_ref[d, i] = second

    for columns in groups:
        each(columns, product(columns), keep_second)
    for (i, column), d in targets.items():
        left_ref[pl.ds(i * BS, BS), pl.ds(column * BS, BS)] = result_ref[d, i]

    def keep_result(i, column, d, present, tile):
        third = jnp.where(present, tile, jnp.zeros_like(tile))
        second = result_ref[d, i].astype(jnp.float32)
        result_ref[d, i] = (3.0 * second - 2.0 * third).astype(jnp.bfloat16)

    for columns in groups:
        each(columns, product(columns), keep_result)
    for s, out_ref in enumerate(outs):
        other = lax.rem(me - s + LAYERS, LAYERS)
        start = pl.multiple_of(other * (BS // LAYERS), BS // LAYERS)
        out_ref[...] = result_ref[:, :, pl.ds(start, BS // LAYERS), :]


def join_body(me_ref, *refs):
    me = me_ref[0]
    out_ref = refs[LAYERS]
    for s in range(LAYERS):
        row = 2 * lax.rem(me + s, LAYERS)
        for t in range(2):
            for d in range(DIAGS):
                out_ref[d, row + t] = refs[s][d, t]


def exchanged(pieces):
    far = from_layer(pieces[2], 2)
    return [pieces[0], from_layer(pieces[1], 1), far, from_layer(pieces[3], 3)]


def per_device(blocks, presence):
    me = lax.axis_index("layer").astype(jnp.int32).reshape(1)

    quarters = [
        bf16(DIAGS, ROWS, BS // LAYERS, BS),
        bf16(len(HALO_LOW), BS // LAYERS, BS),
        bf16(len(HALO_HIGH), BS // LAYERS, BS),
    ] + [bf16(len(held), ROWS, BS // LAYERS, BS) for held in [SHARED] + DIRECT]
    masked, low, high, shared, plus, minus = call(mask_body, quarters, 1, 1)(
        presence, blocks
    )
    low, high = from_group(low, -1), from_group(high, 1)
    shared = swapped(shared)
    plus, minus = from_pair(plus, FAR_PAIRS), from_pair(minus, -FAR_PAIRS)
    near = call(
        near_body,
        bf16(LAYERS, len(NEAR), BS // LAYERS, BS),
        0,
        3,
        scratch=[pltpu.VMEM((DIAGS, ROWS + 2 * BAND, BS // LAYERS, BS), jnp.bfloat16)],
    )(masked, low, high)
    near = lax.all_to_all(near, "layer", 0, 0)
    fars = [far_across(shared, FAR_PAIRS), far_across(shared, -FAR_PAIRS), plus, minus]
    edges = call(
        edge_body,
        [bf16(len(m), BS // LAYERS, BS) for m in (EDGE_LOW, EDGE_HIGH)],
        0,
        4,
    )(*fars)
    edges = [from_group(edges[0], -1), from_group(edges[1], 1)]
    fars = call(
        fars_body,
        [bf16(len(FARS), BS // LAYERS, BS)] * LAYERS,
        1,
        6,
        scratch=[pltpu.VMEM((2 * DIAGS, ROWS + 2, BS // LAYERS, BS), jnp.bfloat16)],
    )(me, *fars, *edges)
    fars = exchanged(fars)
    results = call(
        purify_body,
        [bf16(DIAGS, 2, BS // LAYERS, BS)] * LAYERS,
        2,
        1 + LAYERS,
        scratch=[
            pltpu.VMEM((WIDTH, WIDTH), jnp.bfloat16),
            pltpu.VMEM((2 * BS, WIDTH), jnp.bfloat16),
            pltpu.VMEM((DIAGS, 2, BS, BS), jnp.bfloat16),
        ],
        flops=4 * 224 * 2 * BS**3,
    )(me, presence, near, *fars)
    results = exchanged(results)
    return call(join_body, bf16(DIAGS, 2 * LAYERS, BS // LAYERS, BS), 1, LAYERS)(
        me, *results
    )


def solution(mesh):
    placed = (P(None, ("row", "col"), "layer", None), P(None, ("row", "col")))
    return jax.shard_map(
        per_device,
        mesh=mesh,
        in_specs=placed,
        out_specs=P(None, ("row", "col"), "layer", None),
        check_vma=False,
    )
```

time: 132 us -> 125 us (0.947)
  waiting for transfers between devices: 84.6 us -> 64.1 us
  local copies, waits for them, and re-layouts: 1.92 us -> 7.22 us
  starting transfers between devices: 36.8 us -> 41.9 us
  Pallas kernels: 7.97 us -> 11.2 us
    ppermute x14 -> x15, waiting for transfers between devices: 84.6 us -> 64.1 us  [moved(): return lax.ppermute(x, AXES, route)]
    unnamed x5 -> x15, local copies, waits for them, and re-layouts: 1.92 us -> 7.22 us
    all_to_all x0 -> x1, starting transfers between devices: none -> 4.01 us  [per_device(): near = lax.all_to_all(near, 'layer', 0, 0)]
    pallas_call x4 -> x5, Pallas kernels: 7.01 us -> 10.3 us  [the longest x1 5.93 us: per_device(): call(purify_body, [bf16(DIAGS, 2, BS // LAYERS, BS)] * LAYERS, 2, 1 + LAY...]
    ppermute x14 -> x15, starting transfers between devices: 36.8 us -> 37.9 us  [moved(): return lax.ppermute(x, AXES, route)]
  transfers between devices with their start and end apart: 14 -> 16, of which waited for: 8 -> 10; matrix products, arithmetic and copies ran while one was open for 0% -> 0% of each run, Pallas kernels for 0% -> 1%
where the time goes in v6:
time: 125 us
  waiting for transfers between devices  64.1 us (51%)
  starting transfers between devices  41.9 us (34%)
  Pallas kernels  11.2 us (9%)
  local copies, waits for them, and re-layouts  7.22 us (6%)
    ppermute x15, waiting for transfers between devices, moved(): return lax.ppermute(x, AXES, route)  64.1 us
    ppermute x15, starting transfers between devices, moved(): return lax.ppermute(x, AXES, route)  37.9 us
    unnamed x15, local copies, waits for them, and re-layouts  7.22 us
    pallas_call x1, Pallas kernels, per_device(): call(purify_body, [bf16(DIAGS, 2, BS // LAYERS, BS)] * LAYERS, 2, 1 + LAY...  5.93 us
    all_to_all x1, starting transfers between devices, per_device(): near = lax.all_to_all(near, 'layer', 0, 0)  4.01 us
  transfers between devices with their start and end apart: 16, of which 10 were waited for; matrix products, arithmetic and copies ran while one was open for 0% of the time, Pallas kernels for 1%

profile of v6, /device:TPU:1, one launch (start us, length us, event | category | flops | bytes accessed | tf_op | source)
XLA Modules:
  0.0 124.5 jit_solution(9572404240983399879)
XLA Ops:
  0.0 0.8 copy.4.presence_ref
  0.8 0.0 copy-start
  0.8 1.2 copy-done
  1.9 1.8 %shard_map.28 = (bf16[13,8,32,128]{3,2,1,0:T(8,128)(2,1)S(1)}, bf16[21,32,128]{2,1,0:T(8,128)(2,1)S(1)}, bf16[21,32,128]{2,1,0:T(8,128)(2,1)S(1)}, bf16[4,8,32,1...) custom-call(s32[13,8]{1,0:T(8,128)S(1)} %copy.4.presence_ref, ...), custom_call_target="tpu_custom_call" | custom-call | bytes 4194304 | tf_op jit(solution)/shard_map/pallas_call | solution.py:318
  3.7 2.5 %collective-permute-start = (bf16[21,32,128]{2,1,0:T(8,128)(2,1)S(1)}, bf16[21,32,128]{2,1,0:T(8,128)(2,1)S(1)}, u32[]{:S(2)}, u32[]{:S(2)}) collective-permute-start(bf16[21,32,128]{2,1,0:T(8,128)(2,1)S(1)} %get-tuple-element.22), channel_id=1, source_target_pairs={{63,0},{127,64},{191,128},{255,192},{0,1},{64,65},{128,129},{192,1... | collective-permute-start | bytes 516104 | tf_op jit(solution)/shard_map/ppermute | solution.py:77
  6.2 4.5 %collective-permute-start.1 = (bf16[21,32,128]{2,1,0:T(8,128)(2,1)S(1)}, bf16[21,32,128]{2,1,0:T(8,128)(2,1)S(1)}, u32[]{:S(2)}, u32[]{:S(2)}) collective-permute-start(bf16[21,32,128]{2,1,0:T(8,128)(2,1)S(1)} %get-tuple-element.23), channel_id=1, source_target_pairs={{1,0},{65,64},{129,128},{193,192},{2,1},{66,65},{130,129},{194,193... | collective-permute-start | bytes 516104 | tf_op jit(solution)/shard_map/ppermute | solution.py:77
  10.7 4.4 %collective-permute-done.low_ref = bf16[21,32,128]{2,1,0:T(8,128)(2,1)S(1)} collective-permute-done((bf16[21,32,128]{2,1,0:T(8,128)(2,1)S(1)}, bf16[21,32,128]{2,1,0:T(8,128)(2,1)S(1)}, u32[]{:S(2)}, u32[]{:S(2)}) %collective-permute-start) | collective-permute-done | bytes 172064 | tf_op jit(solution)/shard_map/ppermute | solution.py:77
  15.0 0.0 collective-permute-done.1.high_ref
  15.0 1.7 %shard_map.29 = bf16[4,68,32,128]{3,2,1,0:T(8,128)(2,1)} custom-call(bf16[13,8,32,128]{3,2,1,0:T(8,128)(2,1)S(1)} %get-tuple-element.21.masked_ref, bf16[21,32,128]{2,1,0:T(8,128)(2,1)S(1)} %collective-permute-done.low_ref, bf16[21,32,128]{2,1,0:T(8,128)(2,1)S(1)} %collective-permute-done.1.high_ref), custom_call_target="tpu_custom_call" | custom-call | bytes 4194304 | tf_op jit(solution)/shard_map/pallas_call | solution.py:324
  16.7 4.0 %all-to-all-start = ((bf16[4,68,32,128]{3,2,1,0:T(8,128)(2,1)}), bf16[4,68,32,128]{3,2,1,0:T(8,128)(2,1)S(1)}, u32[]{:S(2)}, u32[]{:S(2)}) async-start(bf16[4,68,32,128]{3,2,1,0:T(8,128)(2,1)} %shard_map.29), calls=%async_computation | async-start | bytes 4456448 | tf_op jit(solution)/shard_map/all_to_all | solution.py:331
  20.7 2.9 %collective-permute-start.2 = (bf16[4,8,32,128]{3,2,1,0:T(8,128)(2,1)S(1)}, bf16[4,8,32,128]{3,2,1,0:T(8,128)(2,1)S(1)}, u32[]{:S(2)}, u32[]{:S(2)}) collective-permute-start(bf16[4,8,32,128]{3,2,1,0:T(8,128)(2,1)S(1)} %get-tuple-element.24), channel_id=1, source_target_pairs={{4,0},{68,64},{132,128},{196,192},{5,1},{69,65},{133,129},{197,193... | collective-permute-start | bytes 786440 | tf_op jit(solution)/shard_map/ppermute | solution.py:77
  23.6 5.6 %collective-permute-start.5 = (bf16[4,8,32,128]{3,2,1,0:T(8,128)(2,1)}, bf16[4,8,32,128]{3,2,1,0:T(8,128)(2,1)S(1)}, u32[]{:S(2)}, u32[]{:S(2)}) collective-permute-start(bf16[4,8,32,128]{3,2,1,0:T(8,128)(2,1)} %get-tuple-element.25), channel_id=1, source_target_pairs={{20,0},{84,64},{148,128},{212,192},{21,1},{85,65},{149,129},{213,1... | collective-permute-start | bytes 786440 | tf_op jit(solution)/shard_map/ppermute | solution.py:77
  29.2 0.6 collective-permute-start.6
  29.9 8.7 %collective-permute-done.2 = bf16[4,8,32,128]{3,2,1,0:T(8,128)(2,1)S(1)} collective-permute-done((bf16[4,8,32,128]{3,2,1,0:T(8,128)(2,1)S(1)}, bf16[4,8,32,128]{3,2,1,0:T(8,128)(2,1)S(1)}, u32[]{:S(2)}, u32[]{:S(2)}) %collective-permute-start.2) | collective-permute-done | bytes 262176 | tf_op jit(solution)/shard_map/ppermute | solution.py:77
  38.5 0.5 collective-permute-start.3
  39.0 8.2 %collective-permute-start.4 = (bf16[4,8,32,128]{3,2,1,0:T(8,128)(2,1)S(1)}, bf16[4,8,32,128]{3,2,1,0:T(8,128)(2,1)S(1)}, u32[]{:S(2)}, u32[]{:S(2)}) collective-permute-start(bf16[4,8,32,128]{3,2,1,0:T(8,128)(2,1)S(1)} %collective-permute-done.2), channel_id=1, source_target_pairs={{40,0},{104,64},{168,128},{232,192},{41,1},{105,65},{169,129},{233... | collective-permute-start | bytes 786440 | tf_op jit(solution)/shard_map/ppermute | solution.py:77
  47.1 7.8 %collective-permute-done.5.refs_2_ = bf16[4,8,32,128]{3,2,1,0:T(8,128)(2,1)S(1)} collective-permute-done((bf16[4,8,32,128]{3,2,1,0:T(8,128)(2,1)}, bf16[4,8,32,128]{3,2,1,0:T(8,128)(2,1)S(1)}, u32[]{:S(2)}, u32[]{:S(2)}) %collective-permute-start.5) | collective-permute-done | bytes 262176 | tf_op jit(solution)/shard_map/ppermute | solution.py:77
  54.9 8.5 %collective-permute-done.6.refs_3_ = bf16[4,8,32,128]{3,2,1,0:T(8,128)(2,1)S(1)} collective-permute-done((bf16[4,8,32,128]{3,2,1,0:T(8,128)(2,1)}, bf16[4,8,32,128]{3,2,1,0:T(8,128)(2,1)S(1)}, u32[]{:S(2)}, u32[]{:S(2)}) %collective-permute-start.6) | collective-permute-done | bytes 262176 | tf_op jit(solution)/shard_map/ppermute | solution.py:77
  63.4 0.0 collective-permute-done.3.refs_0_
  63.4 0.0 collective-permute-done.4.refs_1_
  63.4 0.7 shard_map.30
  64.1 0.0 collective-permute-start.7
  64.1 7.8 %collective-permute-start.8 = (bf16[12,32,128]{2,1,0:T(8,128)(2,1)}, bf16[12,32,128]{2,1,0:T(8,128)(2,1)S(1)}, u32[]{:S(2)}, u32[]{:S(2)}) collective-permute-start(bf16[12,32,128]{2,1,0:T(8,128)(2,1)} %get-tuple-element.28), channel_id=1, source_target_pairs={{1,0},{65,64},{129,128},{193,192},{2,1},{66,65},{130,129},{194,193... | collective-permute-start | bytes 294920 | tf_op jit(solution)/shard_map/ppermute | solution.py:77
  71.9 2.9 %collective-permute-done.7.refs_4_ = bf16[12,32,128]{2,1,0:T(8,128)(2,1)S(1)} collective-permute-done((bf16[12,32,128]{2,1,0:T(8,128)(2,1)}, bf16[12,32,128]{2,1,0:T(8,128)(2,1)S(1)}, u32[]{:S(2)}, u32[]{:S(2)}) %collective-permute-start.7) | collective-permute-done | bytes 98336 | tf_op jit(solution)/shard_map/ppermute | solution.py:77
  74.8 0.0 collective-permute-done.8.refs_5_
  74.8 0.2 shard_map.31
  75.0 0.0 copy-start.1
  75.0 0.7 copy-done.1
  75.7 2.7 %collective-permute-start.9 = (bf16[52,32,128]{2,1,0:T(8,128)(2,1)S(1)}, bf16[52,32,128]{2,1,0:T(8,128)(2,1)S(1)}, u32[]{:S(2)}, u32[]{:S(2)}) collective-permute-start(bf16[52,32,128]{2,1,0:T(8,128)(2,1)S(1)} %get-tuple-element.30), channel_id=1, source_target_pairs={{64,0},{128,64},{192,128},{0,192},{65,1},{129,65},{193,129},{1,193... | collective-permute-start | bytes 1277960 | tf_op jit(solution)/shard_map/ppermute | solution.py:77
  78.4 0.6 collective-permute-start.10
  79.0 0.6 collective-permute-start.11
  79.6 16.9 %collective-permute-done.9.refs_2_ = bf16[52,32,128]{2,1,0:T(8,128)(2,1)S(1)} collective-permute-done((bf16[52,32,128]{2,1,0:T(8,128)(2,1)S(1)}, bf16[52,32,128]{2,1,0:T(8,128)(2,1)S(1)}, u32[]{:S(2)}, u32[]{:S(2)}) %collective-permute-start.9) | collective-permute-done | bytes 426016 | tf_op jit(solution)/shard_map/ppermute | solution.py:77
  96.4 0.0 collective-permute-done.10.refs_3_
  96.4 0.0 copy-start.3
  96.4 0.8 copy-done.3
  97.2 3.2 %collective-permute-done.11.refs_4_ = bf16[52,32,128]{2,1,0:T(8,128)(2,1)S(1)} collective-permute-done((bf16[52,32,128]{2,1,0:T(8,128)(2,1)S(1)}, bf16[52,32,128]{2,1,0:T(8,128)(2,1)S(1)}, u32[]{:S(2)}, u32[]{:S(2)}) %collective-permute-start.11) | collective-permute-done | bytes 426016 | tf_op jit(solution)/shard_map/ppermute | solution.py:77
  100.4 0.0 copy-start.5
  100.4 0.8 copy-done.5
  101.2 0.0 all-to-all-done.refs_0_
  101.2 0.0 copy-start.2
  101.2 1.0 copy-done.2
  102.2 0.0 copy-start.4
  102.2 1.0 copy-done.4
  103.2 0.0 copy-start.6
  103.2 1.0 copy-done.6
  104.2 5.9 %shard_map.32 = (bf16[13,2,32,128]{3,2,1,0:T(8,128)(2,1)S(1)}, bf16[13,2,32,128]{3,2,1,0:T(8,128)(2,1)S(1)}, bf16[13,2,32,128]{3,2,1,0:T(8,128)(2,1)S(1)}, bf16[13,2,32,128]{3,2,1,0:T(8,128)(2,1)S(1)}) custom-call(s32[1]{0:T(128)} %bitcast.me_ref, s32[13,8]{1,0:T(8,128)S(1)} %copy.4.presence_ref, bf16[4,68,32,128]{3,2,1,0:T(8,128)(2,1)S(1)} %all-to-all-done.refs_0_, ...), custom_call_target="tpu_custom_call" | custom-call | flops 3758096384 | bytes 4194304 | tf_op jit(solution)/shard_map/pallas_call | solution.py:348
  110.1 0.1 collective-permute-start.12
  110.3 0.6 collective-permute-start.13
  110.9 0.8 collective-permute-start.14
  111.7 5.0 %collective-permute-done.12.refs_1_ = bf16[13,2,32,128]{3,2,1,0:T(8,128)(2,1)S(1)} collective-permute-done((bf16[13,2,32,128]{3,2,1,0:T(8,128)(2,1)S(1)}, bf16[13,2,32,128]{3,2,1,0:T(8,128)(2,1)S(1)}, u32[]{:S(2)}, u32[]{:S(2)}) %collective-permute-start.12) | collective-permute-done | bytes 213024 | tf_op jit(solution)/shard_map/ppermute | solution.py:77
  116.7 1.5 %collective-permute-done.13.refs_2_ = bf16[13,2,32,128]{3,2,1,0:T(8,128)(2,1)S(1)} collective-permute-done((bf16[13,2,32,128]{3,2,1,0:T(8,128)(2,1)S(1)}, bf16[13,2,32,128]{3,2,1,0:T(8,128)(2,1)S(1)}, u32[]{:S(2)}, u32[]{:S(2)}) %collective-permute-start.13) | collective-permute-done | bytes 213024 | tf_op jit(solution)/shard_map/ppermute | solution.py:77
  118.1 5.4 %collective-permute-done.14.refs_3_ = bf16[13,2,32,128]{3,2,1,0:T(8,128)(2,1)S(1)} collective-permute-done((bf16[13,2,32,128]{3,2,1,0:T(8,128)(2,1)S(1)}, bf16[13,2,32,128]{3,2,1,0:T(8,128)(2,1)S(1)}, u32[]{:S(2)}, u32[]{:S(2)}) %collective-permute-start.14) | collective-permute-done | bytes 213024 | tf_op jit(solution)/shard_map/ppermute | solution.py:77
  123.6 1.0 shard_map.33
Async XLA Ops:
  0.8 1.2 copy-start
  3.7 11.3 %collective-permute-start = (bf16[21,32,128]{2,1,0:T(8,128)(2,1)S(1)}, bf16[21,32,128]{2,1,0:T(8,128)(2,1)S(1)}, u32[]{:S(2)}, u32[]{:S(2)}) collective-permute-start(bf16[21,32,128]{2,1,0:T(8,128)(2,1)S(1)} %get-tuple-element.22), channel_id=1, source_target_pairs={{63,0},{127,64},{191,128},{255,192},{0,1},{64,65},{128,129},{192,1... | collective-permute-start | bytes 516104 | tf_op jit(solution)/shard_map/ppermute | solution.py:77
  6.2 8.9 %collective-permute-start.1 = (bf16[21,32,128]{2,1,0:T(8,128)(2,1)S(1)}, bf16[21,32,128]{2,1,0:T(8,128)(2,1)S(1)}, u32[]{:S(2)}, u32[]{:S(2)}) collective-permute-start(bf16[21,32,128]{2,1,0:T(8,128)(2,1)S(1)} %get-tuple-element.23), channel_id=1, source_target_pairs={{1,0},{65,64},{129,128},{193,192},{2,1},{66,65},{130,129},{194,193... | collective-permute-start | bytes 516104 | tf_op jit(solution)/shard_map/ppermute | solution.py:77
  16.7 84.5 %all-to-all-start = ((bf16[4,68,32,128]{3,2,1,0:T(8,128)(2,1)}), bf16[4,68,32,128]{3,2,1,0:T(8,128)(2,1)S(1)}, u32[]{:S(2)}, u32[]{:S(2)}) async-start(bf16[4,68,32,128]{3,2,1,0:T(8,128)(2,1)} %shard_map.29), calls=%async_computation | async-start | bytes 4456448 | tf_op jit(solution)/shard_map/all_to_all | solution.py:331
  20.7 17.8 %collective-permute-start.2 = (bf16[4,8,32,128]{3,2,1,0:T(8,128)(2,1)S(1)}, bf16[4,8,32,128]{3,2,1,0:T(8,128)(2,1)S(1)}, u32[]{:S(2)}, u32[]{:S(2)}) collective-permute-start(bf16[4,8,32,128]{3,2,1,0:T(8,128)(2,1)S(1)} %get-tuple-element.24), channel_id=1, source_target_pairs={{4,0},{68,64},{132,128},{196,192},{5,1},{69,65},{133,129},{197,193... | collective-permute-start | bytes 786440 | tf_op jit(solution)/shard_map/ppermute | solution.py:77
  23.6 31.3 %collective-permute-start.5 = (bf16[4,8,32,128]{3,2,1,0:T(8,128)(2,1)}, bf16[4,8,32,128]{3,2,1,0:T(8,128)(2,1)S(1)}, u32[]{:S(2)}, u32[]{:S(2)}) collective-permute-start(bf16[4,8,32,128]{3,2,1,0:T(8,128)(2,1)} %get-tuple-element.25), channel_id=1, source_target_pairs={{20,0},{84,64},{148,128},{212,192},{21,1},{85,65},{149,129},{213,1... | collective-permute-start | bytes 786440 | tf_op jit(solution)/shard_map/ppermute | solution.py:77
  29.2 34.2 %collective-permute-start.6 = (bf16[4,8,32,128]{3,2,1,0:T(8,128)(2,1)}, bf16[4,8,32,128]{3,2,1,0:T(8,128)(2,1)S(1)}, u32[]{:S(2)}, u32[]{:S(2)}) collective-permute-start(bf16[4,8,32,128]{3,2,1,0:T(8,128)(2,1)} %get-tuple-element.26), channel_id=1, source_target_pairs={{44,0},{108,64},{172,128},{236,192},{45,1},{109,65},{173,129},{237... | collective-permute-start | bytes 786440 | tf_op jit(solution)/shard_map/ppermute | solution.py:77
  38.5 24.9 %collective-permute-start.3 = (bf16[4,8,32,128]{3,2,1,0:T(8,128)(2,1)S(1)}, bf16[4,8,32,128]{3,2,1,0:T(8,128)(2,1)S(1)}, u32[]{:S(2)}, u32[]{:S(2)}) collective-permute-start(bf16[4,8,32,128]{3,2,1,0:T(8,128)(2,1)S(1)} %collective-permute-done.2), channel_id=1, source_target_pairs={{16,0},{80,64},{144,128},{208,192},{17,1},{81,65},{145,129},{209,1... | collective-permute-start | bytes 786440 | tf_op jit(solution)/shard_map/ppermute | solution.py:77
  39.0 24.5 %collective-permute-start.4 = (bf16[4,8,32,128]{3,2,1,0:T(8,128)(2,1)S(1)}, bf16[4,8,32,128]{3,2,1,0:T(8,128)(2,1)S(1)}, u32[]{:S(2)}, u32[]{:S(2)}) collective-permute-start(bf16[4,8,32,128]{3,2,1,0:T(8,128)(2,1)S(1)} %collective-permute-done.2), channel_id=1, source_target_pairs={{40,0},{104,64},{168,128},{232,192},{41,1},{105,65},{169,129},{233... | collective-permute-start | bytes 786440 | tf_op jit(solution)/shard_map/ppermute | solution.py:77
  64.1 10.6 %collective-permute-start.7 = (bf16[12,32,128]{2,1,0:T(8,128)(2,1)}, bf16[12,32,128]{2,1,0:T(8,128)(2,1)S(1)}, u32[]{:S(2)}, u32[]{:S(2)}) collective-permute-start(bf16[12,32,128]{2,1,0:T(8,128)(2,1)} %get-tuple-element.27), channel_id=1, source_target_pairs={{63,0},{127,64},{191,128},{255,192},{0,1},{64,65},{128,129},{192,1... | collective-permute-start | bytes 294920 | tf_op jit(solution)/shard_map/ppermute | solution.py:77
  64.1 10.6 %collective-permute-start.8 = (bf16[12,32,128]{2,1,0:T(8,128)(2,1)}, bf16[12,32,128]{2,1,0:T(8,128)(2,1)S(1)}, u32[]{:S(2)}, u32[]{:S(2)}) collective-permute-start(bf16[12,32,128]{2,1,0:T(8,128)(2,1)} %get-tuple-element.28), channel_id=1, source_target_pairs={{1,0},{65,64},{129,128},{193,192},{2,1},{66,65},{130,129},{194,193... | collective-permute-start | bytes 294920 | tf_op jit(solution)/shard_map/ppermute | solution.py:77
  75.0 0.8 copy-start.1
  75.7 20.7 %collective-permute-start.9 = (bf16[52,32,128]{2,1,0:T(8,128)(2,1)S(1)}, bf16[52,32,128]{2,1,0:T(8,128)(2,1)S(1)}, u32[]{:S(2)}, u32[]{:S(2)}) collective-permute-start(bf16[52,32,128]{2,1,0:T(8,128)(2,1)S(1)} %get-tuple-element.30), channel_id=1, source_target_pairs={{64,0},{128,64},{192,128},{0,192},{65,1},{129,65},{193,129},{1,193... | collective-permute-start | bytes 1277960 | tf_op jit(solution)/shard_map/ppermute | solution.py:77
  78.4 18.0 %collective-permute-start.10 = (bf16[52,32,128]{2,1,0:T(8,128)(2,1)S(1)}, bf16[52,32,128]{2,1,0:T(8,128)(2,1)S(1)}, u32[]{:S(2)}, u32[]{:S(2)}) collective-permute-start(bf16[52,32,128]{2,1,0:T(8,128)(2,1)S(1)} %get-tuple-element.31), channel_id=1, source_target_pairs={{128,0},{192,64},{0,128},{64,192},{129,1},{193,65},{1,129},{65,193... | collective-permute-start | bytes 1277960 | tf_op jit(solution)/shard_map/ppermute | solution.py:77
  79.0 21.4 %collective-permute-start.11 = (bf16[52,32,128]{2,1,0:T(8,128)(2,1)S(1)}, bf16[52,32,128]{2,1,0:T(8,128)(2,1)S(1)}, u32[]{:S(2)}, u32[]{:S(2)}) collective-permute-start(bf16[52,32,128]{2,1,0:T(8,128)(2,1)S(1)} %get-tuple-element.32), channel_id=1, source_target_pairs={{192,0},{0,64},{64,128},{128,192},{193,1},{1,65},{65,129},{129,193... | collective-permute-start | bytes 1277960 | tf_op jit(solution)/shard_map/ppermute | solution.py:77
  96.4 0.8 copy-start.3
  100.4 0.8 copy-start.5
  101.2 1.0 copy-start.2
  102.2 1.0 copy-start.4
  103.2 1.0 copy-start.6
  110.1 6.5 %collective-permute-start.12 = (bf16[13,2,32,128]{3,2,1,0:T(8,128)(2,1)S(1)}, bf16[13,2,32,128]{3,2,1,0:T(8,128)(2,1)S(1)}, u32[]{:S(2)}, u32[]{:S(2)}) collective-permute-start(bf16[13,2,32,128]{3,2,1,0:T(8,128)(2,1)S(1)} %get-tuple-element.34), channel_id=1, source_target_pairs={{64,0},{128,64},{192,128},{0,192},{65,1},{129,65},{193,129},{1,193... | collective-permute-start | bytes 638984 | tf_op jit(solution)/shard_map/ppermute | solution.py:77
  110.3 7.9 %collective-permute-start.13 = (bf16[13,2,32,128]{3,2,1,0:T(8,128)(2,1)S(1)}, bf16[13,2,32,128]{3,2,1,0:T(8,128)(2,1)S(1)}, u32[]{:S(2)}, u32[]{:S(2)}) collective-permute-start(bf16[13,2,32,128]{3,2,1,0:T(8,128)(2,1)S(1)} %get-tuple-element.35), channel_id=1, source_target_pairs={{128,0},{192,64},{0,128},{64,192},{129,1},{193,65},{1,129},{65,193... | collective-permute-start | bytes 638984 | tf_op jit(solution)/shard_map/ppermute | solution.py:77
  110.9 12.7 %collective-permute-start.14 = (bf16[13,2,32,128]{3,2,1,0:T(8,128)(2,1)S(1)}, bf16[13,2,32,128]{3,2,1,0:T(8,128)(2,1)S(1)}, u32[]{:S(2)}, u32[]{:S(2)}) collective-permute-start(bf16[13,2,32,128]{3,2,1,0:T(8,128)(2,1)S(1)} %get-tuple-element.36), channel_id=1, source_target_pairs={{192,0},{0,64},{64,128},{128,192},{193,1},{1,65},{65,129},{129,193... | collective-permute-start | bytes 638984 | tf_op jit(solution)/shard_map/ppermute | solution.py:77

commit v7 on v5

--- a/solution.py
+++ b/solution.py
@@ -152,12 +152,12 @@
                     shared_ref[SHARED.index(d), row] = tile
 
 
-def resplit_body(me_ref, shared_ref, *out_refs):
-    for s, out_ref in enumerate(out_refs[-LAYERS:]):
-        row = 2 * lax.rem(me_ref[0] - s + LAYERS, LAYERS)
+def resplit_body(shared_ref, *refs):
+    out_ref = refs[-1]
+    for layer in range(LAYERS):
         for t in range(2):
             for k in range(len(SHARED)):
-                out_ref[k, t] = shared_ref[k, row + t]
+                out_ref[layer, k, t] = shared_ref[k, 2 * layer + t]
 
 
 def gather_pieces(me, pieces, out_ref):
@@ -181,9 +181,10 @@
             out_ref[k] = own_ref[b, t]
 
 
-def shared_body(me_ref, *refs):
-    pieces, shared_ref, out_refs = refs[:LAYERS], refs[LAYERS], refs[LAYERS + 1 :]
-    gather_pieces(me_ref[0], pieces, shared_ref)
+def shared_body(pieces_ref, shared_ref, *out_refs):
+    for layer in range(LAYERS):
+        rows = pl.ds(layer * (BS // LAYERS), BS // LAYERS)
+        shared_ref[:, :, rows, :] = pieces_ref[layer]
     for message, out_ref in zip((SWAP_LOW, SWAP_HIGH), out_refs):
         for k, (t, b) in enumerate(message):
             out_ref[k] = shared_ref[SHARED.index(b), t]
@@ -316,7 +317,6 @@
         return [bf16(len(message), BS, BS) for message in messages]
 
     quarter = bf16(DIAGS, 2, BS // LAYERS, BS)
-    shared_quarter = bf16(len(SHARED), 2, BS // LAYERS, BS)
     *pieces, shared = call(
         split_body,
         [quarter] * LAYERS + [bf16(len(SHARED), 2 * LAYERS, BS // LAYERS, BS)],
@@ -334,16 +334,19 @@
     plus_far = from_pair(plus_far, FAR_PAIRS)
     minus_far = from_pair(minus_far, -FAR_PAIRS)
     some = [shared]
-    some = call(resplit_body, [shared_quarter] * LAYERS, 1, len(some))(me, *some)
-    some = exchanged(some)
+    some = call(
+        resplit_body, bf16(LAYERS, len(SHARED), 2, BS // LAYERS, BS), 0, len(some)
+    )(*some)
+    piece = some
+    some = lax.all_to_all(some, "layer", 0, 0)
     shared, swap_low, swap_high = call(
         shared_body,
         [bf16(len(SHARED), 2, BS, BS)] + packed([SWAP_LOW, SWAP_HIGH]),
+        0,
         1,
-        LAYERS,
-    )(me, *some)
+    )(some)
     swap_low, swap_high = edge_across(swap_low, -1), edge_across(swap_high, 1)
-    before = [own]
+    before = [own, piece]
     low, high = call(near_body, packed([LOW, HIGH]), 0, len(before))(*before)
     low, high = from_pair(low, -1), from_pair(high, 1)
     before = [shared, swap_low, swap_high, plus_far, minus_far]

time: 107 us -> 110 us (1.028)
  Pallas kernels: 7.97 us -> 11.1 us
  starting transfers between devices: 46 us -> 43.9 us
  waiting for transfers between devices: 50.4 us -> 52.3 us
    all_to_all x0 -> x1, waiting for transfers between devices: none -> 5.72 us  [per_device(): some = lax.all_to_all(some, 'layer', 0, 0)]
    ppermute x20 -> x17, starting transfers between devices: 46 us -> 40.4 us  [moved(): return lax.ppermute(x, AXES, route)]
    ppermute x20 -> x17, waiting for transfers between devices: 50.4 us -> 46.6 us  [moved(): return lax.ppermute(x, AXES, route)]
    all_to_all x0 -> x1, starting transfers between devices: none -> 3.45 us  [per_device(): some = lax.all_to_all(some, 'layer', 0, 0)]
    pallas_call x1, Pallas kernels: 0.07 us -> 1.85 us  [per_device(): low, high = call(near_body, packed([LOW, HIGH]), 0, len(before))(*before)]
  transfers between devices with their start and end apart: 20 -> 18, of which waited for: 11 -> 10; matrix products, arithmetic and copies ran while one was open for 0% -> 0% of each run, Pallas kernels for 0% -> 1%
where the time goes in v7:
time: 110 us; the launch traced here: 109 us
  waiting for transfers between devices  52.3 us (48%)
  starting transfers between devices  43.9 us (40%)
  Pallas kernels  11.1 us (10%)
  local copies, waits for them, and re-layouts  1.92 us (2%)
    ppermute x17, waiting for transfers between devices, moved(): return lax.ppermute(x, AXES, route)  46.6 us
    ppermute x17, starting transfers between devices, moved(): return lax.ppermute(x, AXES, route)  40.4 us
    all_to_all x1, waiting for transfers between devices, per_device(): some = lax.all_to_all(some, 'layer', 0, 0)  5.72 us
    pallas_call x1, Pallas kernels, per_device(): call(purify_body, [quarter] * LAYERS, 2, len(ARRIVE), scratch=[pltpu.VMEM...  5.68 us
    all_to_all x1, starting transfers between devices, per_device(): some = lax.all_to_all(some, 'layer', 0, 0)  3.45 us
  transfers between devices with their start and end apart: 18, of which 10 were waited for; matrix products, arithmetic and copies ran while one was open for 0% of the time, Pallas kernels for 1%

profile of v7, /device:TPU:1, one launch (start us, length us, event | category | flops | bytes accessed | tf_op | source)
XLA Modules:
  0.0 109.3 jit_solution(13314149527847327479)
XLA Ops:
  0.0 0.0 copy-start.1
  0.0 0.7 copy-done.1
  0.7 0.1 copy.4.presence_ref
  0.8 0.0 copy-start
  0.8 1.2 %copy-done = bf16[13,8,32,128]{3,2,1,0:T(8,128)(2,1)S(1)} copy-done((bf16[13,8,32,128]{3,2,1,0:T(8,128)(2,1)S(1)}, bf16[13,8,32,128]{3,2,1,0:T(8,128)(2,1)}, u32[]{:S(2)}) %copy-start) | copy-done | bytes 851992
  1.9 0.9 shard_map.28
  2.9 7.8 %collective-permute-start.3 = (bf16[5,8,32,128]{3,2,1,0:T(8,128)(2,1)S(1)}, bf16[5,8,32,128]{3,2,1,0:T(8,128)(2,1)S(1)}, u32[]{:S(2)}, u32[]{:S(2)}) collective-permute-start(bf16[5,8,32,128]{3,2,1,0:T(8,128)(2,1)S(1)} %get-tuple-element.29), channel_id=1, source_target_pairs={{4,0},{68,64},{132,128},{196,192},{5,1},{69,65},{133,129},{197,193... | collective-permute-start | bytes 983048 | tf_op jit(solution)/shard_map/ppermute | solution.py:85
  10.7 2.5 %collective-permute-start = (bf16[13,2,32,128]{3,2,1,0:T(8,128)(2,1)S(1)}, bf16[13,2,32,128]{3,2,1,0:T(8,128)(2,1)S(1)}, u32[]{:S(2)}, u32[]{:S(2)}) collective-permute-start(bf16[13,2,32,128]{3,2,1,0:T(8,128)(2,1)S(1)} %get-tuple-element.25), channel_id=1, source_target_pairs={{64,0},{128,64},{192,128},{0,192},{65,1},{129,65},{193,129},{1,193... | collective-permute-start | bytes 638984 | tf_op jit(solution)/shard_map/ppermute | solution.py:85
  13.2 0.5 collective-permute-start.1
  13.7 0.6 collective-permute-start.2
  14.3 3.3 %collective-permute-done.refs_1_ = bf16[13,2,32,128]{3,2,1,0:T(8,128)(2,1)S(1)} collective-permute-done((bf16[13,2,32,128]{3,2,1,0:T(8,128)(2,1)S(1)}, bf16[13,2,32,128]{3,2,1,0:T(8,128)(2,1)S(1)}, u32[]{:S(2)}, u32[]{:S(2)}) %collective-permute-start) | collective-permute-done | bytes 213024 | tf_op jit(solution)/shard_map/ppermute | solution.py:85
  17.6 2.7 %collective-permute-done.1.refs_2_ = bf16[13,2,32,128]{3,2,1,0:T(8,128)(2,1)S(1)} collective-permute-done((bf16[13,2,32,128]{3,2,1,0:T(8,128)(2,1)S(1)}, bf16[13,2,32,128]{3,2,1,0:T(8,128)(2,1)S(1)}, u32[]{:S(2)}, u32[]{:S(2)}) %collective-permute-start.1) | collective-permute-done | bytes 213024 | tf_op jit(solution)/shard_map/ppermute | solution.py:85
  20.2 6.2 %collective-permute-done.2.refs_3_ = bf16[13,2,32,128]{3,2,1,0:T(8,128)(2,1)S(1)} collective-permute-done((bf16[13,2,32,128]{3,2,1,0:T(8,128)(2,1)S(1)}, bf16[13,2,32,128]{3,2,1,0:T(8,128)(2,1)S(1)}, u32[]{:S(2)}, u32[]{:S(2)}) %collective-permute-start.2) | collective-permute-done | bytes 213024 | tf_op jit(solution)/shard_map/ppermute | solution.py:85
  26.4 0.8 shard_map.29
  27.2 0.0 collective-permute-done.3.shared_ref
  27.2 0.8 shard_map.30.refs_0_
  28.0 1.8 %shard_map.31 = (bf16[17,128,128]{2,1,0:T(8,128)(2,1)}, bf16[17,128,128]{2,1,0:T(8,128)(2,1)S(1)}) custom-call(bf16[13,2,128,128]{3,2,1,0:T(8,128)(2,1)S(1)} %get-tuple-element.28.own_ref.refs_0_, bf16[4,5,2,32,128]{4,3,2,1,0:T(8,128)(2,1)} %shard_map.30.refs_0_), custom_call_target="tpu_custom_call" | custom-call | bytes 4194304 | tf_op jit(solution)/shard_map/pallas_call | solution.py:350
  29.8 0.0 collective-permute-start.4
  29.8 5.1 %collective-permute-start.5 = (bf16[17,128,128]{2,1,0:T(8,128)(2,1)S(1)}, bf16[17,128,128]{2,1,0:T(8,128)(2,1)S(1)}, u32[]{:S(2)}, u32[]{:S(2)}) collective-permute-start(bf16[17,128,128]{2,1,0:T(8,128)(2,1)S(1)} %get-tuple-element.31), channel_id=1, source_target_pairs={{64,0},{128,64},{192,128},{1,192},{65,1},{129,65},{193,129},{2,193... | collective-permute-start | bytes 1671176 | tf_op jit(solution)/shard_map/ppermute | solution.py:85
  34.9 3.5 %all-to-all-start = ((bf16[4,5,2,32,128]{4,3,2,1,0:T(8,128)(2,1)}), bf16[4,5,2,32,128]{4,3,2,1,0:T(8,128)(2,1)S(1)}, u32[]{:S(2)}, u32[]{:S(2)}) async-start(bf16[4,5,2,32,128]{4,3,2,1,0:T(8,128)(2,1)} %shard_map.30.refs_0_), calls=%async_computation | async-start | bytes 655360 | tf_op jit(solution)/shard_map/all_to_all | solution.py:341
  38.3 6.6 %collective-permute-start.6 = (bf16[6,128,128]{2,1,0:T(8,128)(2,1)}, bf16[6,128,128]{2,1,0:T(8,128)(2,1)S(1)}, u32[]{:S(2)}, u32[]{:S(2)}) collective-permute-start(bf16[6,128,128]{2,1,0:T(8,128)(2,1)} %get-tuple-element.32), channel_id=1, source_target_pairs={{20,0},{84,64},{148,128},{212,192},{21,1},{85,65},{149,129},{213,1... | collective-permute-start | bytes 589832 | tf_op jit(solution)/shard_map/ppermute | solution.py:85
  45.0 0.0 collective-permute-start.7
  45.0 5.7 %all-to-all-done.pieces_ref = bf16[4,5,2,32,128]{4,3,2,1,0:T(8,128)(2,1)S(1)} async-done(((bf16[4,5,2,32,128]{4,3,2,1,0:T(8,128)(2,1)}), bf16[4,5,2,32,128]{4,3,2,1,0:T(8,128)(2,1)S(1)}, u32[]{:S(2)}, u32[]{:S(2)}) %all-to-all-start) | async-done | bytes 327712 | tf_op jit(solution)/shard_map/all_to_all | solution.py:341
  50.7 0.1 collective-permute-start.8
  50.8 0.0 collective-permute-done.6.refs_0_.refs_2_.refs_3_
  50.8 4.8 %collective-permute-start.9 = (bf16[3,128,128]{2,1,0:T(8,128)(2,1)S(1)}, bf16[3,128,128]{2,1,0:T(8,128)(2,1)S(1)}, u32[]{:S(2)}, u32[]{:S(2)}) collective-permute-start(bf16[3,128,128]{2,1,0:T(8,128)(2,1)S(1)} %get-tuple-element.36), channel_id=1, source_target_pairs={{64,0},{128,64},{192,128},{1,192},{65,1},{129,65},{193,129},{2,193... | collective-permute-start | bytes 294920 | tf_op jit(solution)/shard_map/ppermute | solution.py:85
  55.6 8.4 %collective-permute-done.7.refs_1_.refs_3_.refs_4_ = bf16[6,128,128]{2,1,0:T(8,128)(2,1)S(1)} collective-permute-done((bf16[6,128,128]{2,1,0:T(8,128)(2,1)S(1)}, bf16[6,128,128]{2,1,0:T(8,128)(2,1)S(1)}, u32[]{:S(2)}, u32[]{:S(2)}) %collective-permute-start.7) | collective-permute-done | bytes 196640 | tf_op jit(solution)/shard_map/ppermute | solution.py:85
  64.0 3.7 %collective-permute-done.8.low_ref = bf16[3,128,128]{2,1,0:T(8,128)(2,1)S(1)} collective-permute-done((bf16[3,128,128]{2,1,0:T(8,128)(2,1)S(1)}, bf16[3,128,128]{2,1,0:T(8,128)(2,1)S(1)}, u32[]{:S(2)}, u32[]{:S(2)}) %collective-permute-start.8) | collective-permute-done | bytes 98336 | tf_op jit(solution)/shard_map/ppermute | solution.py:85
  67.7 0.0 collective-permute-done.9.high_ref
  67.7 2.7 %collective-permute-start.11 = (bf16[14,128,128]{2,1,0:T(8,128)(2,1)S(1)}, bf16[14,128,128]{2,1,0:T(8,128)(2,1)S(1)}, u32[]{:S(2)}, u32[]{:S(2)}) collective-permute-start(bf16[14,128,128]{2,1,0:T(8,128)(2,1)S(1)} %shard_map.33), channel_id=1, source_target_pairs={{40,0},{104,64},{168,128},{232,192},{41,1},{105,65},{169,129},{233... | collective-permute-start | bytes 1376264 | tf_op jit(solution)/shard_map/ppermute | solution.py:85
  70.4 0.4 collective-permute-start.10
  70.8 0.0 collective-permute-done.4.refs_0_.refs_1_
  70.9 0.0 collective-permute-done.5.refs_1_.refs_2_
  70.9 0.1 collective-permute-start.12
  71.0 5.1 %collective-permute-start.13 = (bf16[10,128,128]{2,1,0:T(8,128)(2,1)S(1)}, bf16[10,128,128]{2,1,0:T(8,128)(2,1)S(1)}, u32[]{:S(2)}, u32[]{:S(2)}) collective-permute-start(bf16[10,128,128]{2,1,0:T(8,128)(2,1)S(1)} %get-tuple-element.38), channel_id=1, source_target_pairs={{64,0},{128,64},{192,128},{1,192},{65,1},{129,65},{193,129},{2,193... | collective-permute-start | bytes 983048 | tf_op jit(solution)/shard_map/ppermute | solution.py:85
  76.1 8.6 %collective-permute-done.11.refs_6_ = bf16[14,128,128]{2,1,0:T(8,128)(2,1)S(1)} collective-permute-done((bf16[14,128,128]{2,1,0:T(8,128)(2,1)S(1)}, bf16[14,128,128]{2,1,0:T(8,128)(2,1)S(1)}, u32[]{:S(2)}, u32[]{:S(2)}) %collective-permute-start.11) | collective-permute-done | bytes 458784 | tf_op jit(solution)/shard_map/ppermute | solution.py:85
  84.7 1.7 %collective-permute-done.10.refs_5_ = bf16[14,128,128]{2,1,0:T(8,128)(2,1)S(1)} collective-permute-done((bf16[14,128,128]{2,1,0:T(8,128)(2,1)S(1)}, bf16[14,128,128]{2,1,0:T(8,128)(2,1)S(1)}, u32[]{:S(2)}, u32[]{:S(2)}) %collective-permute-start.10) | collective-permute-done | bytes 458784 | tf_op jit(solution)/shard_map/ppermute | solution.py:85
  86.4 0.0 collective-permute-done.12.refs_7_
  86.4 0.0 collective-permute-done.13.refs_8_
  86.4 5.7 %shard_map.35 = (bf16[13,2,32,128]{3,2,1,0:T(8,128)(2,1)S(1)}, bf16[13,2,32,128]{3,2,1,0:T(8,128)(2,1)S(1)}, bf16[13,2,32,128]{3,2,1,0:T(8,128)(2,1)S(1)}, bf16[13,2,32,128]{3,2,1,0:T(8,128)(2,1)S(1)}) custom-call(s32[1]{0:T(128)} %bitcast.me_ref, s32[13,8]{1,0:T(8,128)S(1)} %copy.4.presence_ref, ...), custom_call_target="tpu_custom_call" | custom-call | flops 3758096384 | bytes 4194304 | tf_op jit(solution)/shard_map/pallas_call | solution.py:360
  92.1 3.5 %collective-permute-start.14 = (bf16[13,2,32,128]{3,2,1,0:T(8,128)(2,1)S(1)}, bf16[13,2,32,128]{3,2,1,0:T(8,128)(2,1)S(1)}, u32[]{:S(2)}, u32[]{:S(2)}) collective-permute-start(bf16[13,2,32,128]{3,2,1,0:T(8,128)(2,1)S(1)} %get-tuple-element.40), channel_id=1, source_target_pairs={{64,0},{128,64},{192,128},{0,192},{65,1},{129,65},{193,129},{1,193... | collective-permute-start | bytes 638984 | tf_op jit(solution)/shard_map/ppermute | solution.py:85
  95.6 0.0 collective-permute-start.15
  95.6 0.7 collective-permute-start.16
  96.3 8.5 %collective-permute-done.14.refs_1_ = bf16[13,2,32,128]{3,2,1,0:T(8,128)(2,1)S(1)} collective-permute-done((bf16[13,2,32,128]{3,2,1,0:T(8,128)(2,1)S(1)}, bf16[13,2,32,128]{3,2,1,0:T(8,128)(2,1)S(1)}, u32[]{:S(2)}, u32[]{:S(2)}) %collective-permute-start.14) | collective-permute-done | bytes 213024 | tf_op jit(solution)/shard_map/ppermute | solution.py:85
  104.8 0.0 collective-permute-done.15.refs_2_
  104.8 3.5 %collective-permute-done.16.refs_3_ = bf16[13,2,32,128]{3,2,1,0:T(8,128)(2,1)S(1)} collective-permute-done((bf16[13,2,32,128]{3,2,1,0:T(8,128)(2,1)S(1)}, bf16[13,2,32,128]{3,2,1,0:T(8,128)(2,1)S(1)}, u32[]{:S(2)}, u32[]{:S(2)}) %collective-permute-start.16) | collective-permute-done | bytes 213024 | tf_op jit(solution)/shard_map/ppermute | solution.py:85
  108.3 1.0 shard_map.36
  (3 shorter events, 0.1 us)
Async XLA Ops:
  0.0 0.7 copy-start.1
  0.8 1.2 %copy-start = (bf16[13,8,32,128]{3,2,1,0:T(8,128)(2,1)S(1)}, bf16[13,8,32,128]{3,2,1,0:T(8,128)(2,1)}, u32[]{:S(2)}) copy-start(bf16[13,8,32,128]{3,2,1,0:T(8,128)(2,1)} %blocks_ref.1) | copy-start | bytes 2555908
  2.9 24.3 %collective-permute-start.3 = (bf16[5,8,32,128]{3,2,1,0:T(8,128)(2,1)S(1)}, bf16[5,8,32,128]{3,2,1,0:T(8,128)(2,1)S(1)}, u32[]{:S(2)}, u32[]{:S(2)}) collective-permute-start(bf16[5,8,32,128]{3,2,1,0:T(8,128)(2,1)S(1)} %get-tuple-element.29), channel_id=1, source_target_pairs={{4,0},{68,64},{132,128},{196,192},{5,1},{69,65},{133,129},{197,193... | collective-permute-start | bytes 983048 | tf_op jit(solution)/shard_map/ppermute | solution.py:85
  10.7 6.9 %collective-permute-start = (bf16[13,2,32,128]{3,2,1,0:T(8,128)(2,1)S(1)}, bf16[13,2,32,128]{3,2,1,0:T(8,128)(2,1)S(1)}, u32[]{:S(2)}, u32[]{:S(2)}) collective-permute-start(bf16[13,2,32,128]{3,2,1,0:T(8,128)(2,1)S(1)} %get-tuple-element.25), channel_id=1, source_target_pairs={{64,0},{128,64},{192,128},{0,192},{65,1},{129,65},{193,129},{1,193... | collective-permute-start | bytes 638984 | tf_op jit(solution)/shard_map/ppermute | solution.py:85
  13.2 7.1 %collective-permute-start.1 = (bf16[13,2,32,128]{3,2,1,0:T(8,128)(2,1)S(1)}, bf16[13,2,32,128]{3,2,1,0:T(8,128)(2,1)S(1)}, u32[]{:S(2)}, u32[]{:S(2)}) collective-permute-start(bf16[13,2,32,128]{3,2,1,0:T(8,128)(2,1)S(1)} %get-tuple-element.26), channel_id=1, source_target_pairs={{128,0},{192,64},{0,128},{64,192},{129,1},{193,65},{1,129},{65,193... | collective-permute-start | bytes 638984 | tf_op jit(solution)/shard_map/ppermute | solution.py:85
  13.7 12.7 %collective-permute-start.2 = (bf16[13,2,32,128]{3,2,1,0:T(8,128)(2,1)S(1)}, bf16[13,2,32,128]{3,2,1,0:T(8,128)(2,1)S(1)}, u32[]{:S(2)}, u32[]{:S(2)}) collective-permute-start(bf16[13,2,32,128]{3,2,1,0:T(8,128)(2,1)S(1)} %get-tuple-element.27), channel_id=1, source_target_pairs={{192,0},{0,64},{64,128},{128,192},{193,1},{1,65},{65,129},{129,193... | collective-permute-start | bytes 638984 | tf_op jit(solution)/shard_map/ppermute | solution.py:85
  29.8 41.1 %collective-permute-start.4 = (bf16[17,128,128]{2,1,0:T(8,128)(2,1)}, bf16[17,128,128]{2,1,0:T(8,128)(2,1)S(1)}, u32[]{:S(2)}, u32[]{:S(2)}) collective-permute-start(bf16[17,128,128]{2,1,0:T(8,128)(2,1)} %get-tuple-element.30), channel_id=1, source_target_pairs={{255,0},{0,64},{64,128},{128,192},{192,1},{1,65},{65,129},{129,193... | collective-permute-start | bytes 1671176 | tf_op jit(solution)/shard_map/ppermute | solution.py:85
  29.8 41.1 %collective-permute-start.5 = (bf16[17,128,128]{2,1,0:T(8,128)(2,1)S(1)}, bf16[17,128,128]{2,1,0:T(8,128)(2,1)S(1)}, u32[]{:S(2)}, u32[]{:S(2)}) collective-permute-start(bf16[17,128,128]{2,1,0:T(8,128)(2,1)S(1)} %get-tuple-element.31), channel_id=1, source_target_pairs={{64,0},{128,64},{192,128},{1,192},{65,1},{129,65},{193,129},{2,193... | collective-permute-start | bytes 1671176 | tf_op jit(solution)/shard_map/ppermute | solution.py:85
  34.9 15.8 %all-to-all-start = ((bf16[4,5,2,32,128]{4,3,2,1,0:T(8,128)(2,1)}), bf16[4,5,2,32,128]{4,3,2,1,0:T(8,128)(2,1)S(1)}, u32[]{:S(2)}, u32[]{:S(2)}) async-start(bf16[4,5,2,32,128]{4,3,2,1,0:T(8,128)(2,1)} %shard_map.30.refs_0_), calls=%async_computation | async-start | bytes 655360 | tf_op jit(solution)/shard_map/all_to_all | solution.py:341
  38.3 12.5 %collective-permute-start.6 = (bf16[6,128,128]{2,1,0:T(8,128)(2,1)}, bf16[6,128,128]{2,1,0:T(8,128)(2,1)S(1)}, u32[]{:S(2)}, u32[]{:S(2)}) collective-permute-start(bf16[6,128,128]{2,1,0:T(8,128)(2,1)} %get-tuple-element.32), channel_id=1, source_target_pairs={{20,0},{84,64},{148,128},{212,192},{21,1},{85,65},{149,129},{213,1... | collective-permute-start | bytes 589832 | tf_op jit(solution)/shard_map/ppermute | solution.py:85
  45.0 19.0 %collective-permute-start.7 = (bf16[6,128,128]{2,1,0:T(8,128)(2,1)S(1)}, bf16[6,128,128]{2,1,0:T(8,128)(2,1)S(1)}, u32[]{:S(2)}, u32[]{:S(2)}) collective-permute-start(bf16[6,128,128]{2,1,0:T(8,128)(2,1)S(1)} %get-tuple-element.33), channel_id=1, source_target_pairs={{44,0},{108,64},{172,128},{236,192},{45,1},{109,65},{173,129},{237... | collective-permute-start | bytes 589832 | tf_op jit(solution)/shard_map/ppermute | solution.py:85
  50.7 17.0 %collective-permute-start.8 = (bf16[3,128,128]{2,1,0:T(8,128)(2,1)S(1)}, bf16[3,128,128]{2,1,0:T(8,128)(2,1)S(1)}, u32[]{:S(2)}, u32[]{:S(2)}) collective-permute-start(bf16[3,128,128]{2,1,0:T(8,128)(2,1)S(1)} %get-tuple-element.35), channel_id=1, source_target_pairs={{199,0},{0,64},{64,128},{128,192},{192,1},{1,65},{65,129},{129,193... | collective-permute-start | bytes 294920 | tf_op jit(solution)/shard_map/ppermute | solution.py:85
  50.8 16.9 %collective-permute-start.9 = (bf16[3,128,128]{2,1,0:T(8,128)(2,1)S(1)}, bf16[3,128,128]{2,1,0:T(8,128)(2,1)S(1)}, u32[]{:S(2)}, u32[]{:S(2)}) collective-permute-start(bf16[3,128,128]{2,1,0:T(8,128)(2,1)S(1)} %get-tuple-element.36), channel_id=1, source_target_pairs={{64,0},{128,64},{192,128},{1,192},{65,1},{129,65},{193,129},{2,193... | collective-permute-start | bytes 294920 | tf_op jit(solution)/shard_map/ppermute | solution.py:85
  67.7 17.0 %collective-permute-start.11 = (bf16[14,128,128]{2,1,0:T(8,128)(2,1)S(1)}, bf16[14,128,128]{2,1,0:T(8,128)(2,1)S(1)}, u32[]{:S(2)}, u32[]{:S(2)}) collective-permute-start(bf16[14,128,128]{2,1,0:T(8,128)(2,1)S(1)} %shard_map.33), channel_id=1, source_target_pairs={{40,0},{104,64},{168,128},{232,192},{41,1},{105,65},{169,129},{233... | collective-permute-start | bytes 1376264 | tf_op jit(solution)/shard_map/ppermute | solution.py:85
  70.4 16.0 %collective-permute-start.10 = (bf16[14,128,128]{2,1,0:T(8,128)(2,1)S(1)}, bf16[14,128,128]{2,1,0:T(8,128)(2,1)S(1)}, u32[]{:S(2)}, u32[]{:S(2)}) collective-permute-start(bf16[14,128,128]{2,1,0:T(8,128)(2,1)S(1)} %shard_map.33), channel_id=1, source_target_pairs={{16,0},{80,64},{144,128},{208,192},{17,1},{81,65},{145,129},{209,1... | collective-permute-start | bytes 1376264 | tf_op jit(solution)/shard_map/ppermute | solution.py:85
  70.9 15.5 %collective-permute-start.12 = (bf16[10,128,128]{2,1,0:T(8,128)(2,1)S(1)}, bf16[10,128,128]{2,1,0:T(8,128)(2,1)S(1)}, u32[]{:S(2)}, u32[]{:S(2)}) collective-permute-start(bf16[10,128,128]{2,1,0:T(8,128)(2,1)S(1)} %get-tuple-element.37), channel_id=1, source_target_pairs={{255,0},{0,64},{64,128},{128,192},{192,1},{1,65},{65,129},{129,193... | collective-permute-start | bytes 983048 | tf_op jit(solution)/shard_map/ppermute | solution.py:85
  71.0 15.4 %collective-permute-start.13 = (bf16[10,128,128]{2,1,0:T(8,128)(2,1)S(1)}, bf16[10,128,128]{2,1,0:T(8,128)(2,1)S(1)}, u32[]{:S(2)}, u32[]{:S(2)}) collective-permute-start(bf16[10,128,128]{2,1,0:T(8,128)(2,1)S(1)} %get-tuple-element.38), channel_id=1, source_target_pairs={{64,0},{128,64},{192,128},{1,192},{65,1},{129,65},{193,129},{2,193... | collective-permute-start | bytes 983048 | tf_op jit(solution)/shard_map/ppermute | solution.py:85
  92.1 12.7 %collective-permute-start.14 = (bf16[13,2,32,128]{3,2,1,0:T(8,128)(2,1)S(1)}, bf16[13,2,32,128]{3,2,1,0:T(8,128)(2,1)S(1)}, u32[]{:S(2)}, u32[]{:S(2)}) collective-permute-start(bf16[13,2,32,128]{3,2,1,0:T(8,128)(2,1)S(1)} %get-tuple-element.40), channel_id=1, source_target_pairs={{64,0},{128,64},{192,128},{0,192},{65,1},{129,65},{193,129},{1,193... | collective-permute-start | bytes 638984 | tf_op jit(solution)/shard_map/ppermute | solution.py:85
  95.6 9.2 %collective-permute-start.15 = (bf16[13,2,32,128]{3,2,1,0:T(8,128)(2,1)S(1)}, bf16[13,2,32,128]{3,2,1,0:T(8,128)(2,1)S(1)}, u32[]{:S(2)}, u32[]{:S(2)}) collective-permute-start(bf16[13,2,32,128]{3,2,1,0:T(8,128)(2,1)S(1)} %get-tuple-element.41), channel_id=1, source_target_pairs={{128,0},{192,64},{0,128},{64,192},{129,1},{193,65},{1,129},{65,193... | collective-permute-start | bytes 638984 | tf_op jit(solution)/shard_map/ppermute | solution.py:85
  95.6 12.7 %collective-permute-start.16 = (bf16[13,2,32,128]{3,2,1,0:T(8,128)(2,1)S(1)}, bf16[13,2,32,128]{3,2,1,0:T(8,128)(2,1)S(1)}, u32[]{:S(2)}, u32[]{:S(2)}) collective-permute-start(bf16[13,2,32,128]{3,2,1,0:T(8,128)(2,1)S(1)} %get-tuple-element.42), channel_id=1, source_target_pairs={{192,0},{0,64},{64,128},{128,192},{193,1},{1,65},{65,129},{129,193... | collective-permute-start | bytes 638984 | tf_op jit(solution)/shard_map/ppermute | solution.py:85

commit v8 on v5

--- a/solution.py
+++ b/solution.py
@@ -61,18 +61,17 @@
 
 OWN = [(t, b) for b in range(DIAGS) for t in range(2)]
 LOW, HIGH = tiles([-2, -1]), tiles([2, 3])
-FAN = tiles(range(FAR - 1, FAR + 3), band_of)
+LOWER, HIGHER = tiles([-3]), tiles([4])
+FAN = [(FAR + t, b) for t in range(2) for b in SHARED]
 PLUS_BAND = FAN
 MINUS_BAND = [(j - 2 * FAR, b) for j, b in FAN]
 PLUS_FAR = tiles([FAR, FAR + 1], far_of)
 MINUS_FAR = tiles([-FAR, -FAR + 1], far_of)
-EDGE_LOW = tiles([-3]) + tiles([FAR - 1, -FAR - 1], far_of)
-EDGE_HIGH = tiles([4]) + tiles([FAR + 2, -FAR + 2], far_of)
-MAIN = [LOW, HIGH, PLUS_FAR, MINUS_FAR]
-ARRIVE = [OWN] + MAIN + [PLUS_BAND, MINUS_BAND, EDGE_LOW, EDGE_HIGH]
-NEAR = [[(j % 2, b) for j, b in message] for message in (LOW, HIGH)]
-SWAP_LOW = [(1, b) for b in band_of(FAR - 1)]
-SWAP_HIGH = [(0, b) for b in band_of(FAR + 2)]
+EDGE_LOW = tiles([FAR - 1, -FAR - 1])
+EDGE_HIGH = tiles([FAR + 2, -FAR + 2])
+MAIN = [PLUS_FAR, MINUS_FAR, PLUS_BAND, MINUS_BAND]
+ARRIVE = [OWN, LOW, HIGH, LOWER, HIGHER] + MAIN + [EDGE_LOW, EDGE_HIGH]
+NEAR = [[(j % 2, b) for j, b in message] for message in (LOW, HIGH, LOWER, HIGHER)]
 DIRECT = [[(j % 2, b) for j, b in message] for message in (PLUS_FAR, MINUS_FAR)]
 
 
@@ -104,10 +103,6 @@
 
 def swapped(x):
     return moved(x, across)
-
-
-def edge_across(x, distance):
-    return moved(x, lambda p: across((across(p) + distance) % PAIRS))
 
 
 def far_across(x, distance):
@@ -176,29 +171,18 @@
 
 
 def near_body(own_ref, *refs):
-    for message, out_ref in zip(NEAR, refs[-2:]):
+    for message, out_ref in zip(NEAR, refs[-len(NEAR) :]):
         for k, (t, b) in enumerate(message):
             out_ref[k] = own_ref[b, t]
 
 
-def shared_body(me_ref, *refs):
-    pieces, shared_ref, out_refs = refs[:LAYERS], refs[LAYERS], refs[LAYERS + 1 :]
-    gather_pieces(me_ref[0], pieces, shared_ref)
-    for message, out_ref in zip((SWAP_LOW, SWAP_HIGH), out_refs):
-        for k, (t, b) in enumerate(message):
-            out_ref[k] = shared_ref[SHARED.index(b), t]
-
-
-def fan_body(shared_ref, low_ref, high_ref, *refs):
-    out_ref = refs[-1]
-    for k, (j, b) in enumerate(FAN):
-        t = j - FAR
-        if t < 0:
-            out_ref[k] = low_ref[SWAP_LOW.index((1, b))]
-        elif t > 1:
-            out_ref[k] = high_ref[SWAP_HIGH.index((0, b))]
-        else:
-            out_ref[k] = shared_ref[SHARED.index(b), t]
+def fan_body(me_ref, *refs):
+    pieces, out_ref = refs[:LAYERS], refs[LAYERS]
+    for s, piece in enumerate(pieces):
+        other = lax.rem(me_ref[0] + s, LAYERS)
+        rows = pl.ds(pl.multiple_of(other * (BS // LAYERS), BS // LAYERS), BS // LAYERS)
+        for k, (j, b) in enumerate(FAN):
+            out_ref[k, rows, :] = piece[SHARED.index(b), j - FAR]
 
 
 def edge_body(*refs):
@@ -333,23 +317,16 @@
     )(me, *pieces)
     plus_far = from_pair(plus_far, FAR_PAIRS)
     minus_far = from_pair(minus_far, -FAR_PAIRS)
-    some = [shared]
+    some = [shared, own]
     some = call(resplit_body, [shared_quarter] * LAYERS, 1, len(some))(me, *some)
     some = exchanged(some)
-    shared, swap_low, swap_high = call(
-        shared_body,
-        [bf16(len(SHARED), 2, BS, BS)] + packed([SWAP_LOW, SWAP_HIGH]),
-        1,
-        LAYERS,
-    )(me, *some)
-    swap_low, swap_high = edge_across(swap_low, -1), edge_across(swap_high, 1)
-    before = [own]
-    low, high = call(near_body, packed([LOW, HIGH]), 0, len(before))(*before)
+    band = call(fan_body, packed([FAN])[0], 1, LAYERS)(me, *some)
+    plus_band, minus_band = far_across(band, FAR_PAIRS), far_across(band, -FAR_PAIRS)
+    before = [own, band]
+    low, high, lower, higher = call(near_body, packed(NEAR), 0, len(before))(*before)
     low, high = from_pair(low, -1), from_pair(high, 1)
-    before = [shared, swap_low, swap_high, plus_far, minus_far]
-    band = call(fan_body, packed([FAN])[0], 0, len(before))(*before)
-    plus_band, minus_band = far_across(band, FAR_PAIRS), far_across(band, -FAR_PAIRS)
-    arrived = [low, high, plus_far, minus_far]
+    lower, higher = from_pair(lower, -2), from_pair(higher, 2)
+    arrived = [plus_far, minus_far, plus_band, minus_band]
     edge_low, edge_high = call(
         edge_body, packed([EDGE_LOW, EDGE_HIGH]), 0, len(arrived)
     )(*arrived)
@@ -365,7 +342,7 @@
             pltpu.VMEM((DIAGS, 2, BS, BS), jnp.bfloat16),
         ],
         flops=4 * 224 * 2 * BS**3,
-    )(me, presence, own, *arrived, plus_band, minus_band, edge_low, edge_high)
+    )(me, presence, own, low, high, lower, higher, *arrived, edge_low, edge_high)
     results = exchanged(results)
     return call(join_body, bf16(DIAGS, 2 * LAYERS, BS // LAYERS, BS), 1, LAYERS)(
         me, *results

time: 107 us -> 112 us (1.047)
  starting transfers between devices: 46 us -> 53.5 us
  waiting for transfers between devices: 50.4 us -> 48.5 us
    ppermute x20, starting transfers between devices: 46 us -> 53.5 us  [moved(): return lax.ppermute(x, AXES, route)]
    ppermute x20, waiting for transfers between devices: 50.4 us -> 48.5 us  [moved(): return lax.ppermute(x, AXES, route)]
  transfers between devices with their start and end apart: 20 -> 20, of which waited for: 11 -> 9; matrix products, arithmetic and copies ran while one was open for 0% -> 0% of each run, Pallas kernels for 0% -> 0%
where the time goes in v8:
time: 112 us
  starting transfers between devices  53.5 us (48%)
  waiting for transfers between devices  48.5 us (43%)
  Pallas kernels  7.97 us (7%)
  local copies, waits for them, and re-layouts  1.92 us (2%)
    ppermute x20, starting transfers between devices, moved(): return lax.ppermute(x, AXES, route)  53.5 us
    ppermute x20, waiting for transfers between devices, moved(): return lax.ppermute(x, AXES, route)  48.5 us
    pallas_call x1, Pallas kernels, per_device(): call(purify_body, [quarter] * LAYERS, 2, len(ARRIVE), scratch=[pltpu.VMEM...  5.76 us
  transfers between devices with their start and end apart: 20, of which 9 were waited for; matrix products, arithmetic and copies ran while one was open for 0% of the time, Pallas kernels for 0%

profile of v8, /device:TPU:1, one launch (start us, length us, event | category | flops | bytes accessed | tf_op | source)
XLA Modules:
  0.0 111.9 jit_solution(11156072877317928341)
XLA Ops:
  0.0 0.0 copy-start.1
  0.0 0.7 copy-done.1
  0.7 0.1 copy.4.presence_ref
  0.8 0.0 copy-start
  0.8 1.2 %copy-done = bf16[13,8,32,128]{3,2,1,0:T(8,128)(2,1)S(1)} copy-done((bf16[13,8,32,128]{3,2,1,0:T(8,128)(2,1)S(1)}, bf16[13,8,32,128]{3,2,1,0:T(8,128)(2,1)}, u32[]{:S(2)}) %copy-start) | copy-done | bytes 851992
  1.9 0.9 shard_map.28
  2.9 7.8 %collective-permute-start.3 = (bf16[5,8,32,128]{3,2,1,0:T(8,128)(2,1)S(1)}, bf16[5,8,32,128]{3,2,1,0:T(8,128)(2,1)S(1)}, u32[]{:S(2)}, u32[]{:S(2)}) collective-permute-start(bf16[5,8,32,128]{3,2,1,0:T(8,128)(2,1)S(1)} %get-tuple-element.32), channel_id=1, source_target_pairs={{4,0},{68,64},{132,128},{196,192},{5,1},{69,65},{133,129},{197,193... | collective-permute-start | bytes 983048 | tf_op jit(solution)/shard_map/ppermute | solution.py:84
  10.7 2.5 %collective-permute-start = (bf16[13,2,32,128]{3,2,1,0:T(8,128)(2,1)S(1)}, bf16[13,2,32,128]{3,2,1,0:T(8,128)(2,1)S(1)}, u32[]{:S(2)}, u32[]{:S(2)}) collective-permute-start(bf16[13,2,32,128]{3,2,1,0:T(8,128)(2,1)S(1)} %get-tuple-element.28), channel_id=1, source_target_pairs={{64,0},{128,64},{192,128},{0,192},{65,1},{129,65},{193,129},{1,193... | collective-permute-start | bytes 638984 | tf_op jit(solution)/shard_map/ppermute | solution.py:84
  13.2 0.5 collective-permute-start.1
  13.7 0.6 collective-permute-start.2
  14.3 3.3 %collective-permute-done.refs_1_ = bf16[13,2,32,128]{3,2,1,0:T(8,128)(2,1)S(1)} collective-permute-done((bf16[13,2,32,128]{3,2,1,0:T(8,128)(2,1)S(1)}, bf16[13,2,32,128]{3,2,1,0:T(8,128)(2,1)S(1)}, u32[]{:S(2)}, u32[]{:S(2)}) %collective-permute-start) | collective-permute-done | bytes 213024 | tf_op jit(solution)/shard_map/ppermute | solution.py:84
  17.6 2.7 %collective-permute-done.1.refs_2_ = bf16[13,2,32,128]{3,2,1,0:T(8,128)(2,1)S(1)} collective-permute-done((bf16[13,2,32,128]{3,2,1,0:T(8,128)(2,1)S(1)}, bf16[13,2,32,128]{3,2,1,0:T(8,128)(2,1)S(1)}, u32[]{:S(2)}, u32[]{:S(2)}) %collective-permute-start.1) | collective-permute-done | bytes 213024 | tf_op jit(solution)/shard_map/ppermute | solution.py:84
  20.2 6.2 %collective-permute-done.2.refs_3_ = bf16[13,2,32,128]{3,2,1,0:T(8,128)(2,1)S(1)} collective-permute-done((bf16[13,2,32,128]{3,2,1,0:T(8,128)(2,1)S(1)}, bf16[13,2,32,128]{3,2,1,0:T(8,128)(2,1)S(1)}, u32[]{:S(2)}, u32[]{:S(2)}) %collective-permute-start.2) | collective-permute-done | bytes 213024 | tf_op jit(solution)/shard_map/ppermute | solution.py:84
  26.4 0.1 shard_map.29
  26.5 0.0 collective-permute-done.3.shared_ref
  26.6 0.1 collective-permute-start.4
  26.7 0.6 collective-permute-start.5
  27.3 0.9 collective-permute-start.6
  28.1 9.9 %collective-permute-start.11 = (bf16[6,128,128]{2,1,0:T(8,128)(2,1)S(1)}, bf16[6,128,128]{2,1,0:T(8,128)(2,1)S(1)}, u32[]{:S(2)}, u32[]{:S(2)}) collective-permute-start(bf16[6,128,128]{2,1,0:T(8,128)(2,1)S(1)} %get-tuple-element.41), channel_id=1, source_target_pairs={{20,0},{84,64},{148,128},{212,192},{21,1},{85,65},{149,129},{213,1... | collective-permute-start | bytes 589832 | tf_op jit(solution)/shard_map/ppermute | solution.py:84
  38.0 0.0 collective-permute-done.4.refs_1_
  38.0 0.0 collective-permute-done.5.refs_2_
  38.0 0.0 collective-permute-done.6.refs_3_
  38.1 0.1 collective-permute-start.14
  38.1 0.5 collective-permute-start.13
  38.7 4.9 %collective-permute-start.12 = (bf16[6,128,128]{2,1,0:T(8,128)(2,1)S(1)}, bf16[6,128,128]{2,1,0:T(8,128)(2,1)S(1)}, u32[]{:S(2)}, u32[]{:S(2)}) collective-permute-start(bf16[6,128,128]{2,1,0:T(8,128)(2,1)S(1)} %get-tuple-element.42), channel_id=1, source_target_pairs={{44,0},{108,64},{172,128},{236,192},{45,1},{109,65},{173,129},{237... | collective-permute-start | bytes 589832 | tf_op jit(solution)/shard_map/ppermute | solution.py:84
  43.6 0.1 shard_map.32
  43.7 0.1 collective-permute-start.7
  43.8 0.0 collective-permute-done.11.refs_0_.refs_5_
  43.8 5.0 %collective-permute-start.8 = (bf16[17,128,128]{2,1,0:T(8,128)(2,1)S(1)}, bf16[17,128,128]{2,1,0:T(8,128)(2,1)S(1)}, u32[]{:S(2)}, u32[]{:S(2)}) collective-permute-start(bf16[17,128,128]{2,1,0:T(8,128)(2,1)S(1)} %get-tuple-element.38), channel_id=1, source_target_pairs={{64,0},{128,64},{192,128},{1,192},{65,1},{129,65},{193,129},{2,193... | collective-permute-start | bytes 1671176 | tf_op jit(solution)/shard_map/ppermute | solution.py:84
  48.8 9.0 %collective-permute-done.12.refs_1_.refs_6_ = bf16[6,128,128]{2,1,0:T(8,128)(2,1)S(1)} collective-permute-done((bf16[6,128,128]{2,1,0:T(8,128)(2,1)S(1)}, bf16[6,128,128]{2,1,0:T(8,128)(2,1)S(1)}, u32[]{:S(2)}, u32[]{:S(2)}) %collective-permute-start.12) | collective-permute-done | bytes 196640 | tf_op jit(solution)/shard_map/ppermute | solution.py:84
  57.8 0.0 collective-permute-done.14.refs_3_.refs_8_
  57.8 0.0 collective-permute-done.13.refs_2_.refs_7_
  57.8 0.1 shard_map.33
  57.9 1.6 %collective-permute-start.15 = (bf16[12,128,128]{2,1,0:T(8,128)(2,1)S(1)}, bf16[12,128,128]{2,1,0:T(8,128)(2,1)S(1)}, u32[]{:S(2)}, u32[]{:S(2)}) collective-permute-start(bf16[12,128,128]{2,1,0:T(8,128)(2,1)S(1)} %get-tuple-element.43), channel_id=1, source_target_pairs={{255,0},{0,64},{64,128},{128,192},{192,1},{1,65},{65,129},{129,193... | collective-permute-start | bytes 1179656 | tf_op jit(solution)/shard_map/ppermute | solution.py:84
  59.5 3.5 %collective-permute-start.16 = (bf16[12,128,128]{2,1,0:T(8,128)(2,1)S(1)}, bf16[12,128,128]{2,1,0:T(8,128)(2,1)S(1)}, u32[]{:S(2)}, u32[]{:S(2)}) collective-permute-start(bf16[12,128,128]{2,1,0:T(8,128)(2,1)S(1)} %get-tuple-element.44), channel_id=1, source_target_pairs={{64,0},{128,64},{192,128},{1,192},{65,1},{129,65},{193,129},{2,193... | collective-permute-start | bytes 1179656 | tf_op jit(solution)/shard_map/ppermute | solution.py:84
  63.0 0.0 collective-permute-start.9
  63.0 10.3 %collective-permute-done.9.refs_3_ = bf16[4,128,128]{2,1,0:T(8,128)(2,1)S(1)} collective-permute-done((bf16[4,128,128]{2,1,0:T(8,128)(2,1)S(1)}, bf16[4,128,128]{2,1,0:T(8,128)(2,1)S(1)}, u32[]{:S(2)}, u32[]{:S(2)}) %collective-permute-start.9) | collective-permute-done | bytes 131104 | tf_op jit(solution)/shard_map/ppermute | solution.py:84
  73.3 2.3 %collective-permute-start.10 = (bf16[4,128,128]{2,1,0:T(8,128)(2,1)S(1)}, bf16[4,128,128]{2,1,0:T(8,128)(2,1)S(1)}, u32[]{:S(2)}, u32[]{:S(2)}) collective-permute-start(bf16[4,128,128]{2,1,0:T(8,128)(2,1)S(1)} %get-tuple-element.40), channel_id=1, source_target_pairs={{128,0},{192,64},{1,128},{65,192},{129,1},{193,65},{2,129},{66,193... | collective-permute-start | bytes 393224 | tf_op jit(solution)/shard_map/ppermute | solution.py:84
  75.6 5.0 %collective-permute-done.10.refs_4_ = bf16[4,128,128]{2,1,0:T(8,128)(2,1)S(1)} collective-permute-done((bf16[4,128,128]{2,1,0:T(8,128)(2,1)S(1)}, bf16[4,128,128]{2,1,0:T(8,128)(2,1)S(1)}, u32[]{:S(2)}, u32[]{:S(2)}) %collective-permute-start.10) | collective-permute-done | bytes 131104 | tf_op jit(solution)/shard_map/ppermute | solution.py:84
  80.5 0.0 collective-permute-done.7.refs_1_
  80.5 0.0 collective-permute-done.8.refs_2_
  80.5 0.2 collective-permute-done.15.refs_9_
  80.7 0.0 collective-permute-done.16.refs_10_
  80.7 5.8 %shard_map.34 = (bf16[13,2,32,128]{3,2,1,0:T(8,128)(2,1)S(1)}, bf16[13,2,32,128]{3,2,1,0:T(8,128)(2,1)S(1)}, bf16[13,2,32,128]{3,2,1,0:T(8,128)(2,1)S(1)}, bf16[13,2,32,128]{3,2,1,0:T(8,128)(2,1)S(1)}) custom-call(s32[1]{0:T(128)} %bitcast.me_ref, s32[13,8]{1,0:T(8,128)S(1)} %copy.4.presence_ref, ...), custom_call_target="tpu_custom_call" | custom-call | flops 3758096384 | bytes 4194304 | tf_op jit(solution)/shard_map/pallas_call | solution.py:334
  86.5 11.9 %collective-permute-start.17 = (bf16[13,2,32,128]{3,2,1,0:T(8,128)(2,1)S(1)}, bf16[13,2,32,128]{3,2,1,0:T(8,128)(2,1)S(1)}, u32[]{:S(2)}, u32[]{:S(2)}) collective-permute-start(bf16[13,2,32,128]{3,2,1,0:T(8,128)(2,1)S(1)} %get-tuple-element.46), channel_id=1, source_target_pairs={{64,0},{128,64},{192,128},{0,192},{65,1},{129,65},{193,129},{1,193... | collective-permute-start | bytes 638984 | tf_op jit(solution)/shard_map/ppermute | solution.py:84
  98.4 0.0 collective-permute-start.18
  98.4 0.7 collective-permute-start.19
  99.1 8.0 %collective-permute-done.17.refs_1_ = bf16[13,2,32,128]{3,2,1,0:T(8,128)(2,1)S(1)} collective-permute-done((bf16[13,2,32,128]{3,2,1,0:T(8,128)(2,1)S(1)}, bf16[13,2,32,128]{3,2,1,0:T(8,128)(2,1)S(1)}, u32[]{:S(2)}, u32[]{:S(2)}) %collective-permute-start.17) | collective-permute-done | bytes 213024 | tf_op jit(solution)/shard_map/ppermute | solution.py:84
  107.0 0.0 collective-permute-done.18.refs_2_
  107.0 3.9 %collective-permute-done.19.refs_3_ = bf16[13,2,32,128]{3,2,1,0:T(8,128)(2,1)S(1)} collective-permute-done((bf16[13,2,32,128]{3,2,1,0:T(8,128)(2,1)S(1)}, bf16[13,2,32,128]{3,2,1,0:T(8,128)(2,1)S(1)}, u32[]{:S(2)}, u32[]{:S(2)}) %collective-permute-start.19) | collective-permute-done | bytes 213024 | tf_op jit(solution)/shard_map/ppermute | solution.py:84
  111.0 1.0 shard_map.35
  (2 shorter events, 0.1 us)
Async XLA Ops:
  0.0 0.7 copy-start.1
  0.8 1.2 %copy-start = (bf16[13,8,32,128]{3,2,1,0:T(8,128)(2,1)S(1)}, bf16[13,8,32,128]{3,2,1,0:T(8,128)(2,1)}, u32[]{:S(2)}) copy-start(bf16[13,8,32,128]{3,2,1,0:T(8,128)(2,1)} %blocks_ref.1) | copy-start | bytes 2555908
  2.9 23.6 %collective-permute-start.3 = (bf16[5,8,32,128]{3,2,1,0:T(8,128)(2,1)S(1)}, bf16[5,8,32,128]{3,2,1,0:T(8,128)(2,1)S(1)}, u32[]{:S(2)}, u32[]{:S(2)}) collective-permute-start(bf16[5,8,32,128]{3,2,1,0:T(8,128)(2,1)S(1)} %get-tuple-element.32), channel_id=1, source_target_pairs={{4,0},{68,64},{132,128},{196,192},{5,1},{69,65},{133,129},{197,193... | collective-permute-start | bytes 983048 | tf_op jit(solution)/shard_map/ppermute | solution.py:84
  10.7 6.9 %collective-permute-start = (bf16[13,2,32,128]{3,2,1,0:T(8,128)(2,1)S(1)}, bf16[13,2,32,128]{3,2,1,0:T(8,128)(2,1)S(1)}, u32[]{:S(2)}, u32[]{:S(2)}) collective-permute-start(bf16[13,2,32,128]{3,2,1,0:T(8,128)(2,1)S(1)} %get-tuple-element.28), channel_id=1, source_target_pairs={{64,0},{128,64},{192,128},{0,192},{65,1},{129,65},{193,129},{1,193... | collective-permute-start | bytes 638984 | tf_op jit(solution)/shard_map/ppermute | solution.py:84
  13.2 7.1 %collective-permute-start.1 = (bf16[13,2,32,128]{3,2,1,0:T(8,128)(2,1)S(1)}, bf16[13,2,32,128]{3,2,1,0:T(8,128)(2,1)S(1)}, u32[]{:S(2)}, u32[]{:S(2)}) collective-permute-start(bf16[13,2,32,128]{3,2,1,0:T(8,128)(2,1)S(1)} %get-tuple-element.29), channel_id=1, source_target_pairs={{128,0},{192,64},{0,128},{64,192},{129,1},{193,65},{1,129},{65,193... | collective-permute-start | bytes 638984 | tf_op jit(solution)/shard_map/ppermute | solution.py:84
  13.7 12.7 %collective-permute-start.2 = (bf16[13,2,32,128]{3,2,1,0:T(8,128)(2,1)S(1)}, bf16[13,2,32,128]{3,2,1,0:T(8,128)(2,1)S(1)}, u32[]{:S(2)}, u32[]{:S(2)}) collective-permute-start(bf16[13,2,32,128]{3,2,1,0:T(8,128)(2,1)S(1)} %get-tuple-element.30), channel_id=1, source_target_pairs={{192,0},{0,64},{64,128},{128,192},{193,1},{1,65},{65,129},{129,193... | collective-permute-start | bytes 638984 | tf_op jit(solution)/shard_map/ppermute | solution.py:84
  26.6 11.4 %collective-permute-start.4 = (bf16[5,2,32,128]{3,2,1,0:T(8,128)(2,1)S(1)}, bf16[5,2,32,128]{3,2,1,0:T(8,128)(2,1)S(1)}, u32[]{:S(2)}, u32[]{:S(2)}) collective-permute-start(bf16[5,2,32,128]{3,2,1,0:T(8,128)(2,1)S(1)} %get-tuple-element.34), channel_id=1, source_target_pairs={{64,0},{128,64},{192,128},{0,192},{65,1},{129,65},{193,129},{1,193... | collective-permute-start | bytes 245768 | tf_op jit(solution)/shard_map/ppermute | solution.py:84
  26.7 11.3 %collective-permute-start.5 = (bf16[5,2,32,128]{3,2,1,0:T(8,128)(2,1)S(1)}, bf16[5,2,32,128]{3,2,1,0:T(8,128)(2,1)S(1)}, u32[]{:S(2)}, u32[]{:S(2)}) collective-permute-start(bf16[5,2,32,128]{3,2,1,0:T(8,128)(2,1)S(1)} %get-tuple-element.35), channel_id=1, source_target_pairs={{128,0},{192,64},{0,128},{64,192},{129,1},{193,65},{1,129},{65,193... | collective-permute-start | bytes 245768 | tf_op jit(solution)/shard_map/ppermute | solution.py:84
  27.3 10.7 %collective-permute-start.6 = (bf16[5,2,32,128]{3,2,1,0:T(8,128)(2,1)S(1)}, bf16[5,2,32,128]{3,2,1,0:T(8,128)(2,1)S(1)}, u32[]{:S(2)}, u32[]{:S(2)}) collective-permute-start(bf16[5,2,32,128]{3,2,1,0:T(8,128)(2,1)S(1)} %get-tuple-element.36), channel_id=1, source_target_pairs={{192,0},{0,64},{64,128},{128,192},{193,1},{1,65},{65,129},{129,193... | collective-permute-start | bytes 245768 | tf_op jit(solution)/shard_map/ppermute | solution.py:84
  28.1 15.6 %collective-permute-start.11 = (bf16[6,128,128]{2,1,0:T(8,128)(2,1)S(1)}, bf16[6,128,128]{2,1,0:T(8,128)(2,1)S(1)}, u32[]{:S(2)}, u32[]{:S(2)}) collective-permute-start(bf16[6,128,128]{2,1,0:T(8,128)(2,1)S(1)} %get-tuple-element.41), channel_id=1, source_target_pairs={{20,0},{84,64},{148,128},{212,192},{21,1},{85,65},{149,129},{213,1... | collective-permute-start | bytes 589832 | tf_op jit(solution)/shard_map/ppermute | solution.py:84
  38.1 19.8 %collective-permute-start.14 = (bf16[10,128,128]{2,1,0:T(8,128)(2,1)S(1)}, bf16[10,128,128]{2,1,0:T(8,128)(2,1)S(1)}, u32[]{:S(2)}, u32[]{:S(2)}) collective-permute-start(bf16[10,128,128]{2,1,0:T(8,128)(2,1)S(1)} %shard_map.31.refs_0_), channel_id=1, source_target_pairs={{40,0},{104,64},{168,128},{232,192},{41,1},{105,65},{169,129},{233... | collective-permute-start | bytes 983048 | tf_op jit(solution)/shard_map/ppermute | solution.py:84
  38.1 19.7 %collective-permute-start.13 = (bf16[10,128,128]{2,1,0:T(8,128)(2,1)S(1)}, bf16[10,128,128]{2,1,0:T(8,128)(2,1)S(1)}, u32[]{:S(2)}, u32[]{:S(2)}) collective-permute-start(bf16[10,128,128]{2,1,0:T(8,128)(2,1)S(1)} %shard_map.31.refs_0_), channel_id=1, source_target_pairs={{16,0},{80,64},{144,128},{208,192},{17,1},{81,65},{145,129},{209,1... | collective-permute-start | bytes 983048 | tf_op jit(solution)/shard_map/ppermute | solution.py:84
  38.7 19.1 %collective-permute-start.12 = (bf16[6,128,128]{2,1,0:T(8,128)(2,1)S(1)}, bf16[6,128,128]{2,1,0:T(8,128)(2,1)S(1)}, u32[]{:S(2)}, u32[]{:S(2)}) collective-permute-start(bf16[6,128,128]{2,1,0:T(8,128)(2,1)S(1)} %get-tuple-element.42), channel_id=1, source_target_pairs={{44,0},{108,64},{172,128},{236,192},{45,1},{109,65},{173,129},{237... | collective-permute-start | bytes 589832 | tf_op jit(solution)/shard_map/ppermute | solution.py:84
  43.7 36.9 %collective-permute-start.7 = (bf16[17,128,128]{2,1,0:T(8,128)(2,1)S(1)}, bf16[17,128,128]{2,1,0:T(8,128)(2,1)S(1)}, u32[]{:S(2)}, u32[]{:S(2)}) collective-permute-start(bf16[17,128,128]{2,1,0:T(8,128)(2,1)S(1)} %get-tuple-element.37), channel_id=1, source_target_pairs={{255,0},{0,64},{64,128},{128,192},{192,1},{1,65},{65,129},{129,193... | collective-permute-start | bytes 1671176 | tf_op jit(solution)/shard_map/ppermute | solution.py:84
  43.8 36.8 %collective-permute-start.8 = (bf16[17,128,128]{2,1,0:T(8,128)(2,1)S(1)}, bf16[17,128,128]{2,1,0:T(8,128)(2,1)S(1)}, u32[]{:S(2)}, u32[]{:S(2)}) collective-permute-start(bf16[17,128,128]{2,1,0:T(8,128)(2,1)S(1)} %get-tuple-element.38), channel_id=1, source_target_pairs={{64,0},{128,64},{192,128},{1,192},{65,1},{129,65},{193,129},{2,193... | collective-permute-start | bytes 1671176 | tf_op jit(solution)/shard_map/ppermute | solution.py:84
  57.9 22.8 %collective-permute-start.15 = (bf16[12,128,128]{2,1,0:T(8,128)(2,1)S(1)}, bf16[12,128,128]{2,1,0:T(8,128)(2,1)S(1)}, u32[]{:S(2)}, u32[]{:S(2)}) collective-permute-start(bf16[12,128,128]{2,1,0:T(8,128)(2,1)S(1)} %get-tuple-element.43), channel_id=1, source_target_pairs={{255,0},{0,64},{64,128},{128,192},{192,1},{1,65},{65,129},{129,193... | collective-permute-start | bytes 1179656 | tf_op jit(solution)/shard_map/ppermute | solution.py:84
  59.5 21.2 %collective-permute-start.16 = (bf16[12,128,128]{2,1,0:T(8,128)(2,1)S(1)}, bf16[12,128,128]{2,1,0:T(8,128)(2,1)S(1)}, u32[]{:S(2)}, u32[]{:S(2)}) collective-permute-start(bf16[12,128,128]{2,1,0:T(8,128)(2,1)S(1)} %get-tuple-element.44), channel_id=1, source_target_pairs={{64,0},{128,64},{192,128},{1,192},{65,1},{129,65},{193,129},{2,193... | collective-permute-start | bytes 1179656 | tf_op jit(solution)/shard_map/ppermute | solution.py:84
  63.0 10.3 %collective-permute-start.9 = (bf16[4,128,128]{2,1,0:T(8,128)(2,1)S(1)}, bf16[4,128,128]{2,1,0:T(8,128)(2,1)S(1)}, u32[]{:S(2)}, u32[]{:S(2)}) collective-permute-start(bf16[4,128,128]{2,1,0:T(8,128)(2,1)S(1)} %get-tuple-element.39), channel_id=1, source_target_pairs={{191,0},{255,64},{0,128},{64,192},{128,1},{192,65},{1,129},{65,193... | collective-permute-start | bytes 393224 | tf_op jit(solution)/shard_map/ppermute | solution.py:84
  73.3 7.2 %collective-permute-start.10 = (bf16[4,128,128]{2,1,0:T(8,128)(2,1)S(1)}, bf16[4,128,128]{2,1,0:T(8,128)(2,1)S(1)}, u32[]{:S(2)}, u32[]{:S(2)}) collective-permute-start(bf16[4,128,128]{2,1,0:T(8,128)(2,1)S(1)} %get-tuple-element.40), channel_id=1, source_target_pairs={{128,0},{192,64},{1,128},{65,192},{129,1},{193,65},{2,129},{66,193... | collective-permute-start | bytes 393224 | tf_op jit(solution)/shard_map/ppermute | solution.py:84
  86.5 20.6 %collective-permute-start.17 = (bf16[13,2,32,128]{3,2,1,0:T(8,128)(2,1)S(1)}, bf16[13,2,32,128]{3,2,1,0:T(8,128)(2,1)S(1)}, u32[]{:S(2)}, u32[]{:S(2)}) collective-permute-start(bf16[13,2,32,128]{3,2,1,0:T(8,128)(2,1)S(1)} %get-tuple-element.46), channel_id=1, source_target_pairs={{64,0},{128,64},{192,128},{0,192},{65,1},{129,65},{193,129},{1,193... | collective-permute-start | bytes 638984 | tf_op jit(solution)/shard_map/ppermute | solution.py:84
  98.4 8.7 %collective-permute-start.18 = (bf16[13,2,32,128]{3,2,1,0:T(8,128)(2,1)S(1)}, bf16[13,2,32,128]{3,2,1,0:T(8,128)(2,1)S(1)}, u32[]{:S(2)}, u32[]{:S(2)}) collective-permute-start(bf16[13,2,32,128]{3,2,1,0:T(8,128)(2,1)S(1)} %get-tuple-element.47), channel_id=1, source_target_pairs={{128,0},{192,64},{0,128},{64,192},{129,1},{193,65},{1,129},{65,193... | collective-permute-start | bytes 638984 | tf_op jit(solution)/shard_map/ppermute | solution.py:84
  98.4 12.6 %collective-permute-start.19 = (bf16[13,2,32,128]{3,2,1,0:T(8,128)(2,1)S(1)}, bf16[13,2,32,128]{3,2,1,0:T(8,128)(2,1)S(1)}, u32[]{:S(2)}, u32[]{:S(2)}) collective-permute-start(bf16[13,2,32,128]{3,2,1,0:T(8,128)(2,1)S(1)} %get-tuple-element.48), channel_id=1, source_target_pairs={{192,0},{0,64},{64,128},{128,192},{193,1},{1,65},{65,129},{129,193... | collective-permute-start | bytes 638984 | tf_op jit(solution)/shard_map/ppermute | solution.py:84

commit v9 on v8

--- a/solution.py
+++ b/solution.py
@@ -171,7 +171,7 @@
 
 
 def near_body(own_ref, *refs):
-    for message, out_ref in zip(NEAR, refs[-len(NEAR) :]):
+    for message, out_ref in zip(NEAR[:2], refs[-2:]):
         for k, (t, b) in enumerate(message):
             out_ref[k] = own_ref[b, t]
 
@@ -309,23 +309,24 @@
     )(me, presence, blocks)
     shared = swapped(shared)
     pieces = exchanged(pieces)
-    own, plus_far, minus_far = call(
-        functools.partial(pack_body, DIRECT),
-        [bf16(DIAGS, 2, BS, BS)] + packed(DIRECT),
+    own, plus_far, minus_far, lower, higher = call(
+        functools.partial(pack_body, DIRECT + NEAR[2:]),
+        [bf16(DIAGS, 2, BS, BS)] + packed(DIRECT + NEAR[2:]),
         1,
         LAYERS,
     )(me, *pieces)
     plus_far = from_pair(plus_far, FAR_PAIRS)
     minus_far = from_pair(minus_far, -FAR_PAIRS)
+    lower, higher = from_pair(lower, -2), from_pair(higher, 2)
     some = [shared, own]
     some = call(resplit_body, [shared_quarter] * LAYERS, 1, len(some))(me, *some)
     some = exchanged(some)
     band = call(fan_body, packed([FAN])[0], 1, LAYERS)(me, *some)
     plus_band, minus_band = far_across(band, FAR_PAIRS), far_across(band, -FAR_PAIRS)
     before = [own, band]
-    low, high, lower, higher = call(near_body, packed(NEAR), 0, len(before))(*before)
+    before += [lower, higher]
+    low, high = call(near_body, packed(NEAR[:2]), 0, len(before))(*before)
     low, high = from_pair(low, -1), from_pair(high, 1)
-    lower, higher = from_pair(lower, -2), from_pair(higher, 2)
     arrived = [plus_far, minus_far, plus_band, minus_band]
     edge_low, edge_high = call(
         edge_body, packed([EDGE_LOW, EDGE_HIGH]), 0, len(arrived)

time: 112 us -> 103 us (0.920)
  the two profiles are of different devices: /device:TPU:1 before, /device:TPU:56 now
where the time goes in v9:
time: 103 us; the launch traced here: 102 us
  starting transfers between devices  51 us (50%)
  waiting for transfers between devices  41.4 us (40%)
  Pallas kernels  7.96 us (8%)
  local copies, waits for them, and re-layouts  1.92 us (2%)
    ppermute x20, starting transfers between devices, moved(): return lax.ppermute(x, AXES, route)  51 us
    ppermute x20, waiting for transfers between devices, moved(): return lax.ppermute(x, AXES, route)  41.4 us
    pallas_call x1, Pallas kernels, per_device(): call(purify_body, [quarter] * LAYERS, 2, len(ARRIVE), scratch=[pltpu.VMEM...  5.76 us
  transfers between devices with their start and end apart: 20, of which 12 were waited for; matrix products, arithmetic and copies ran while one was open for 0% of the time, Pallas kernels for 0%

profile of v9, /device:TPU:56, one launch (start us, length us, event | category | flops | bytes accessed | tf_op | source)
XLA Modules:
  0.0 102.4 jit_solution(1648407905687930274)
XLA Ops:
  0.0 0.0 copy-start.1
  0.0 0.7 copy-done.1
  0.7 0.1 copy.4.presence_ref
  0.8 0.0 copy-start
  0.8 1.2 %copy-done = bf16[13,8,32,128]{3,2,1,0:T(8,128)(2,1)S(1)} copy-done((bf16[13,8,32,128]{3,2,1,0:T(8,128)(2,1)S(1)}, bf16[13,8,32,128]{3,2,1,0:T(8,128)(2,1)}, u32[]{:S(2)}) %copy-start) | copy-done | bytes 851992
  1.9 0.9 shard_map.28
  2.9 6.4 %collective-permute-start.3 = (bf16[5,8,32,128]{3,2,1,0:T(8,128)(2,1)S(1)}, bf16[5,8,32,128]{3,2,1,0:T(8,128)(2,1)S(1)}, u32[]{:S(2)}, u32[]{:S(2)}) collective-permute-start(bf16[5,8,32,128]{3,2,1,0:T(8,128)(2,1)S(1)} %get-tuple-element.32), channel_id=1, source_target_pairs={{4,0},{68,64},{132,128},{196,192},{5,1},{69,65},{133,129},{197,193... | collective-permute-start | bytes 983048 | tf_op jit(solution)/shard_map/ppermute | solution.py:84
  9.3 2.8 %collective-permute-start = (bf16[13,2,32,128]{3,2,1,0:T(8,128)(2,1)S(1)}, bf16[13,2,32,128]{3,2,1,0:T(8,128)(2,1)S(1)}, u32[]{:S(2)}, u32[]{:S(2)}) collective-permute-start(bf16[13,2,32,128]{3,2,1,0:T(8,128)(2,1)S(1)} %get-tuple-element.28), channel_id=1, source_target_pairs={{64,0},{128,64},{192,128},{0,192},{65,1},{129,65},{193,129},{1,193... | collective-permute-start | bytes 638984 | tf_op jit(solution)/shard_map/ppermute | solution.py:84
  12.0 0.8 collective-permute-start.1
  12.8 0.9 collective-permute-start.2
  13.7 7.1 %collective-permute-done.refs_1_ = bf16[13,2,32,128]{3,2,1,0:T(8,128)(2,1)S(1)} collective-permute-done((bf16[13,2,32,128]{3,2,1,0:T(8,128)(2,1)S(1)}, bf16[13,2,32,128]{3,2,1,0:T(8,128)(2,1)S(1)}, u32[]{:S(2)}, u32[]{:S(2)}) %collective-permute-start) | collective-permute-done | bytes 213024 | tf_op jit(solution)/shard_map/ppermute | solution.py:84
  20.8 0.9 collective-permute-done.1.refs_2_
  21.8 2.8 %collective-permute-done.2.refs_3_ = bf16[13,2,32,128]{3,2,1,0:T(8,128)(2,1)S(1)} collective-permute-done((bf16[13,2,32,128]{3,2,1,0:T(8,128)(2,1)S(1)}, bf16[13,2,32,128]{3,2,1,0:T(8,128)(2,1)S(1)}, u32[]{:S(2)}, u32[]{:S(2)}) %collective-permute-start.2) | collective-permute-done | bytes 213024 | tf_op jit(solution)/shard_map/ppermute | solution.py:84
  24.5 0.1 shard_map.29
  24.6 0.0 collective-permute-done.3.shared_ref
  24.7 2.3 %collective-permute-start.4 = (bf16[5,2,32,128]{3,2,1,0:T(8,128)(2,1)S(1)}, bf16[5,2,32,128]{3,2,1,0:T(8,128)(2,1)S(1)}, u32[]{:S(2)}, u32[]{:S(2)}) collective-permute-start(bf16[5,2,32,128]{3,2,1,0:T(8,128)(2,1)S(1)} %get-tuple-element.34), channel_id=1, source_target_pairs={{64,0},{128,64},{192,128},{0,192},{65,1},{129,65},{193,129},{1,193... | collective-permute-start | bytes 245768 | tf_op jit(solution)/shard_map/ppermute | solution.py:84
  26.9 0.8 collective-permute-start.5
  27.7 0.9 collective-permute-start.6
  28.6 3.3 %collective-permute-start.11 = (bf16[6,128,128]{2,1,0:T(8,128)(2,1)S(1)}, bf16[6,128,128]{2,1,0:T(8,128)(2,1)S(1)}, u32[]{:S(2)}, u32[]{:S(2)}) collective-permute-start(bf16[6,128,128]{2,1,0:T(8,128)(2,1)S(1)} %get-tuple-element.41), channel_id=1, source_target_pairs={{20,0},{84,64},{148,128},{212,192},{21,1},{85,65},{149,129},{213,1... | collective-permute-start | bytes 589832 | tf_op jit(solution)/shard_map/ppermute | solution.py:84
  31.9 2.1 %collective-permute-start.7 = (bf16[4,128,128]{2,1,0:T(8,128)(2,1)S(1)}, bf16[4,128,128]{2,1,0:T(8,128)(2,1)S(1)}, u32[]{:S(2)}, u32[]{:S(2)}) collective-permute-start(bf16[4,128,128]{2,1,0:T(8,128)(2,1)S(1)} %get-tuple-element.37), channel_id=1, source_target_pairs={{191,0},{255,64},{0,128},{64,192},{128,1},{192,65},{1,129},{65,193... | collective-permute-start | bytes 393224 | tf_op jit(solution)/shard_map/ppermute | solution.py:84
  34.0 0.0 collective-permute-done.4.refs_1_
  34.0 0.0 collective-permute-done.5.refs_2_
  34.0 0.0 collective-permute-done.6.refs_3_
  34.1 4.2 %collective-permute-start.14 = (bf16[10,128,128]{2,1,0:T(8,128)(2,1)S(1)}, bf16[10,128,128]{2,1,0:T(8,128)(2,1)S(1)}, u32[]{:S(2)}, u32[]{:S(2)}) collective-permute-start(bf16[10,128,128]{2,1,0:T(8,128)(2,1)S(1)} %shard_map.31.refs_0_), channel_id=1, source_target_pairs={{40,0},{104,64},{168,128},{232,192},{41,1},{105,65},{169,129},{233... | collective-permute-start | bytes 983048 | tf_op jit(solution)/shard_map/ppermute | solution.py:84
  38.3 0.0 collective-permute-start.13
  38.3 2.6 %collective-permute-start.8 = (bf16[4,128,128]{2,1,0:T(8,128)(2,1)S(1)}, bf16[4,128,128]{2,1,0:T(8,128)(2,1)S(1)}, u32[]{:S(2)}, u32[]{:S(2)}) collective-permute-start(bf16[4,128,128]{2,1,0:T(8,128)(2,1)S(1)} %get-tuple-element.38), channel_id=1, source_target_pairs={{128,0},{192,64},{1,128},{65,192},{129,1},{193,65},{2,129},{66,193... | collective-permute-start | bytes 393224 | tf_op jit(solution)/shard_map/ppermute | solution.py:84
  40.9 2.1 %collective-permute-done.7.refs_1_.refs_3_ = bf16[4,128,128]{2,1,0:T(8,128)(2,1)S(1)} collective-permute-done((bf16[4,128,128]{2,1,0:T(8,128)(2,1)S(1)}, bf16[4,128,128]{2,1,0:T(8,128)(2,1)S(1)}, u32[]{:S(2)}, u32[]{:S(2)}) %collective-permute-start.7) | collective-permute-done | bytes 131104 | tf_op jit(solution)/shard_map/ppermute | solution.py:84
  43.0 7.7 %collective-permute-start.12 = (bf16[6,128,128]{2,1,0:T(8,128)(2,1)S(1)}, bf16[6,128,128]{2,1,0:T(8,128)(2,1)S(1)}, u32[]{:S(2)}, u32[]{:S(2)}) collective-permute-start(bf16[6,128,128]{2,1,0:T(8,128)(2,1)S(1)} %get-tuple-element.42), channel_id=1, source_target_pairs={{44,0},{108,64},{172,128},{236,192},{45,1},{109,65},{173,129},{237... | collective-permute-start | bytes 589832 | tf_op jit(solution)/shard_map/ppermute | solution.py:84
  50.7 0.0 collective-permute-done.8.refs_2_.refs_4_
  50.7 0.1 shard_map.32
  50.8 0.1 collective-permute-start.9
  50.9 0.0 collective-permute-done.11.refs_0_.refs_5_
  50.9 4.1 %collective-permute-start.10 = (bf16[17,128,128]{2,1,0:T(8,128)(2,1)S(1)}, bf16[17,128,128]{2,1,0:T(8,128)(2,1)S(1)}, u32[]{:S(2)}, u32[]{:S(2)}) collective-permute-start(bf16[17,128,128]{2,1,0:T(8,128)(2,1)S(1)} %get-tuple-element.40), channel_id=1, source_target_pairs={{64,0},{128,64},{192,128},{1,192},{65,1},{129,65},{193,129},{2,193... | collective-permute-start | bytes 1671176 | tf_op jit(solution)/shard_map/ppermute | solution.py:84
  55.0 3.9 %collective-permute-done.12.refs_1_.refs_6_ = bf16[6,128,128]{2,1,0:T(8,128)(2,1)S(1)} collective-permute-done((bf16[6,128,128]{2,1,0:T(8,128)(2,1)S(1)}, bf16[6,128,128]{2,1,0:T(8,128)(2,1)S(1)}, u32[]{:S(2)}, u32[]{:S(2)}) %collective-permute-start.12) | collective-permute-done | bytes 196640 | tf_op jit(solution)/shard_map/ppermute | solution.py:84
  58.9 0.0 collective-permute-done.14.refs_3_.refs_8_
  58.9 0.0 collective-permute-done.13.refs_2_.refs_7_
  58.9 0.1 shard_map.33
  59.0 5.3 %collective-permute-start.15 = (bf16[12,128,128]{2,1,0:T(8,128)(2,1)S(1)}, bf16[12,128,128]{2,1,0:T(8,128)(2,1)S(1)}, u32[]{:S(2)}, u32[]{:S(2)}) collective-permute-start(bf16[12,128,128]{2,1,0:T(8,128)(2,1)S(1)} %get-tuple-element.43), channel_id=1, source_target_pairs={{255,0},{0,64},{64,128},{128,192},{192,1},{1,65},{65,129},{129,193... | collective-permute-start | bytes 1179656 | tf_op jit(solution)/shard_map/ppermute | solution.py:84
  64.3 0.0 collective-permute-start.16
  64.3 4.8 %collective-permute-done.9.refs_1_ = bf16[17,128,128]{2,1,0:T(8,128)(2,1)S(1)} collective-permute-done((bf16[17,128,128]{2,1,0:T(8,128)(2,1)S(1)}, bf16[17,128,128]{2,1,0:T(8,128)(2,1)S(1)}, u32[]{:S(2)}, u32[]{:S(2)}) %collective-permute-start.9) | collective-permute-done | bytes 557088 | tf_op jit(solution)/shard_map/ppermute | solution.py:84
  69.1 2.2 %collective-permute-done.10.refs_2_ = bf16[17,128,128]{2,1,0:T(8,128)(2,1)S(1)} collective-permute-done((bf16[17,128,128]{2,1,0:T(8,128)(2,1)S(1)}, bf16[17,128,128]{2,1,0:T(8,128)(2,1)S(1)}, u32[]{:S(2)}, u32[]{:S(2)}) %collective-permute-start.10) | collective-permute-done | bytes 557088 | tf_op jit(solution)/shard_map/ppermute | solution.py:84
  71.2 4.8 %collective-permute-done.15.refs_9_ = bf16[12,128,128]{2,1,0:T(8,128)(2,1)S(1)} collective-permute-done((bf16[12,128,128]{2,1,0:T(8,128)(2,1)S(1)}, bf16[12,128,128]{2,1,0:T(8,128)(2,1)S(1)}, u32[]{:S(2)}, u32[]{:S(2)}) %collective-permute-start.15) | collective-permute-done | bytes 393248 | tf_op jit(solution)/shard_map/ppermute | solution.py:84
  76.0 1.2 %collective-permute-done.16.refs_10_ = bf16[12,128,128]{2,1,0:T(8,128)(2,1)S(1)} collective-permute-done((bf16[12,128,128]{2,1,0:T(8,128)(2,1)S(1)}, bf16[12,128,128]{2,1,0:T(8,128)(2,1)S(1)}, u32[]{:S(2)}, u32[]{:S(2)}) %collective-permute-start.16) | collective-permute-done | bytes 393248 | tf_op jit(solution)/shard_map/ppermute | solution.py:84
  77.2 5.8 %shard_map.34 = (bf16[13,2,32,128]{3,2,1,0:T(8,128)(2,1)S(1)}, bf16[13,2,32,128]{3,2,1,0:T(8,128)(2,1)S(1)}, bf16[13,2,32,128]{3,2,1,0:T(8,128)(2,1)S(1)}, bf16[13,2,32,128]{3,2,1,0:T(8,128)(2,1)S(1)}) custom-call(s32[1]{0:T(128)} %bitcast.me_ref, s32[13,8]{1,0:T(8,128)S(1)} %copy.4.presence_ref, ...), custom_call_target="tpu_custom_call" | custom-call | flops 3758096384 | bytes 4194304 | tf_op jit(solution)/shard_map/pallas_call | solution.py:335
  83.0 5.9 %collective-permute-start.17 = (bf16[13,2,32,128]{3,2,1,0:T(8,128)(2,1)S(1)}, bf16[13,2,32,128]{3,2,1,0:T(8,128)(2,1)S(1)}, u32[]{:S(2)}, u32[]{:S(2)}) collective-permute-start(bf16[13,2,32,128]{3,2,1,0:T(8,128)(2,1)S(1)} %get-tuple-element.46), channel_id=1, source_target_pairs={{64,0},{128,64},{192,128},{0,192},{65,1},{129,65},{193,129},{1,193... | collective-permute-start | bytes 638984 | tf_op jit(solution)/shard_map/ppermute | solution.py:84
  88.8 0.0 collective-permute-start.18
  88.8 1.0 collective-permute-start.19
  89.8 8.2 %collective-permute-done.17.refs_1_ = bf16[13,2,32,128]{3,2,1,0:T(8,128)(2,1)S(1)} collective-permute-done((bf16[13,2,32,128]{3,2,1,0:T(8,128)(2,1)S(1)}, bf16[13,2,32,128]{3,2,1,0:T(8,128)(2,1)S(1)}, u32[]{:S(2)}, u32[]{:S(2)}) %collective-permute-start.17) | collective-permute-done | bytes 213024 | tf_op jit(solution)/shard_map/ppermute | solution.py:84
  98.0 0.5 collective-permute-done.18.refs_2_
  98.5 2.9 %collective-permute-done.19.refs_3_ = bf16[13,2,32,128]{3,2,1,0:T(8,128)(2,1)S(1)} collective-permute-done((bf16[13,2,32,128]{3,2,1,0:T(8,128)(2,1)S(1)}, bf16[13,2,32,128]{3,2,1,0:T(8,128)(2,1)S(1)}, u32[]{:S(2)}, u32[]{:S(2)}) %collective-permute-start.19) | collective-permute-done | bytes 213024 | tf_op jit(solution)/shard_map/ppermute | solution.py:84
  101.5 1.0 shard_map.35
  (2 shorter events, 0.1 us)
Async XLA Ops:
  0.0 0.7 copy-start.1
  0.8 1.2 %copy-start = (bf16[13,8,32,128]{3,2,1,0:T(8,128)(2,1)S(1)}, bf16[13,8,32,128]{3,2,1,0:T(8,128)(2,1)}, u32[]{:S(2)}) copy-start(bf16[13,8,32,128]{3,2,1,0:T(8,128)(2,1)} %blocks_ref.1) | copy-start | bytes 2555908
  2.9 21.8 %collective-permute-start.3 = (bf16[5,8,32,128]{3,2,1,0:T(8,128)(2,1)S(1)}, bf16[5,8,32,128]{3,2,1,0:T(8,128)(2,1)S(1)}, u32[]{:S(2)}, u32[]{:S(2)}) collective-permute-start(bf16[5,8,32,128]{3,2,1,0:T(8,128)(2,1)S(1)} %get-tuple-element.32), channel_id=1, source_target_pairs={{4,0},{68,64},{132,128},{196,192},{5,1},{69,65},{133,129},{197,193... | collective-permute-start | bytes 983048 | tf_op jit(solution)/shard_map/ppermute | solution.py:84
  9.3 11.6 %collective-permute-start = (bf16[13,2,32,128]{3,2,1,0:T(8,128)(2,1)S(1)}, bf16[13,2,32,128]{3,2,1,0:T(8,128)(2,1)S(1)}, u32[]{:S(2)}, u32[]{:S(2)}) collective-permute-start(bf16[13,2,32,128]{3,2,1,0:T(8,128)(2,1)S(1)} %get-tuple-element.28), channel_id=1, source_target_pairs={{64,0},{128,64},{192,128},{0,192},{65,1},{129,65},{193,129},{1,193... | collective-permute-start | bytes 638984 | tf_op jit(solution)/shard_map/ppermute | solution.py:84
  12.0 9.7 %collective-permute-start.1 = (bf16[13,2,32,128]{3,2,1,0:T(8,128)(2,1)S(1)}, bf16[13,2,32,128]{3,2,1,0:T(8,128)(2,1)S(1)}, u32[]{:S(2)}, u32[]{:S(2)}) collective-permute-start(bf16[13,2,32,128]{3,2,1,0:T(8,128)(2,1)S(1)} %get-tuple-element.29), channel_id=1, source_target_pairs={{128,0},{192,64},{0,128},{64,192},{129,1},{193,65},{1,129},{65,193... | collective-permute-start | bytes 638984 | tf_op jit(solution)/shard_map/ppermute | solution.py:84
  12.8 11.7 %collective-permute-start.2 = (bf16[13,2,32,128]{3,2,1,0:T(8,128)(2,1)S(1)}, bf16[13,2,32,128]{3,2,1,0:T(8,128)(2,1)S(1)}, u32[]{:S(2)}, u32[]{:S(2)}) collective-permute-start(bf16[13,2,32,128]{3,2,1,0:T(8,128)(2,1)S(1)} %get-tuple-element.30), channel_id=1, source_target_pairs={{192,0},{0,64},{64,128},{128,192},{193,1},{1,65},{65,129},{129,193... | collective-permute-start | bytes 638984 | tf_op jit(solution)/shard_map/ppermute | solution.py:84
  24.7 9.3 %collective-permute-start.4 = (bf16[5,2,32,128]{3,2,1,0:T(8,128)(2,1)S(1)}, bf16[5,2,32,128]{3,2,1,0:T(8,128)(2,1)S(1)}, u32[]{:S(2)}, u32[]{:S(2)}) collective-permute-start(bf16[5,2,32,128]{3,2,1,0:T(8,128)(2,1)S(1)} %get-tuple-element.34), channel_id=1, source_target_pairs={{64,0},{128,64},{192,128},{0,192},{65,1},{129,65},{193,129},{1,193... | collective-permute-start | bytes 245768 | tf_op jit(solution)/shard_map/ppermute | solution.py:84
  26.9 7.1 %collective-permute-start.5 = (bf16[5,2,32,128]{3,2,1,0:T(8,128)(2,1)S(1)}, bf16[5,2,32,128]{3,2,1,0:T(8,128)(2,1)S(1)}, u32[]{:S(2)}, u32[]{:S(2)}) collective-permute-start(bf16[5,2,32,128]{3,2,1,0:T(8,128)(2,1)S(1)} %get-tuple-element.35), channel_id=1, source_target_pairs={{128,0},{192,64},{0,128},{64,192},{129,1},{193,65},{1,129},{65,193... | collective-permute-start | bytes 245768 | tf_op jit(solution)/shard_map/ppermute | solution.py:84
  27.7 6.3 %collective-permute-start.6 = (bf16[5,2,32,128]{3,2,1,0:T(8,128)(2,1)S(1)}, bf16[5,2,32,128]{3,2,1,0:T(8,128)(2,1)S(1)}, u32[]{:S(2)}, u32[]{:S(2)}) collective-permute-start(bf16[5,2,32,128]{3,2,1,0:T(8,128)(2,1)S(1)} %get-tuple-element.36), channel_id=1, source_target_pairs={{192,0},{0,64},{64,128},{128,192},{193,1},{1,65},{65,129},{129,193... | collective-permute-start | bytes 245768 | tf_op jit(solution)/shard_map/ppermute | solution.py:84
  28.6 22.3 %collective-permute-start.11 = (bf16[6,128,128]{2,1,0:T(8,128)(2,1)S(1)}, bf16[6,128,128]{2,1,0:T(8,128)(2,1)S(1)}, u32[]{:S(2)}, u32[]{:S(2)}) collective-permute-start(bf16[6,128,128]{2,1,0:T(8,128)(2,1)S(1)} %get-tuple-element.41), channel_id=1, source_target_pairs={{20,0},{84,64},{148,128},{212,192},{21,1},{85,65},{149,129},{213,1... | collective-permute-start | bytes 589832 | tf_op jit(solution)/shard_map/ppermute | solution.py:84
  31.9 11.1 %collective-permute-start.7 = (bf16[4,128,128]{2,1,0:T(8,128)(2,1)S(1)}, bf16[4,128,128]{2,1,0:T(8,128)(2,1)S(1)}, u32[]{:S(2)}, u32[]{:S(2)}) collective-permute-start(bf16[4,128,128]{2,1,0:T(8,128)(2,1)S(1)} %get-tuple-element.37), channel_id=1, source_target_pairs={{191,0},{255,64},{0,128},{64,192},{128,1},{192,65},{1,129},{65,193... | collective-permute-start | bytes 393224 | tf_op jit(solution)/shard_map/ppermute | solution.py:84
  34.1 24.8 %collective-permute-start.14 = (bf16[10,128,128]{2,1,0:T(8,128)(2,1)S(1)}, bf16[10,128,128]{2,1,0:T(8,128)(2,1)S(1)}, u32[]{:S(2)}, u32[]{:S(2)}) collective-permute-start(bf16[10,128,128]{2,1,0:T(8,128)(2,1)S(1)} %shard_map.31.refs_0_), channel_id=1, source_target_pairs={{40,0},{104,64},{168,128},{232,192},{41,1},{105,65},{169,129},{233... | collective-permute-start | bytes 983048 | tf_op jit(solution)/shard_map/ppermute | solution.py:84
  38.3 20.6 %collective-permute-start.13 = (bf16[10,128,128]{2,1,0:T(8,128)(2,1)S(1)}, bf16[10,128,128]{2,1,0:T(8,128)(2,1)S(1)}, u32[]{:S(2)}, u32[]{:S(2)}) collective-permute-start(bf16[10,128,128]{2,1,0:T(8,128)(2,1)S(1)} %shard_map.31.refs_0_), channel_id=1, source_target_pairs={{16,0},{80,64},{144,128},{208,192},{17,1},{81,65},{145,129},{209,1... | collective-permute-start | bytes 983048 | tf_op jit(solution)/shard_map/ppermute | solution.py:84
  38.3 12.4 %collective-permute-start.8 = (bf16[4,128,128]{2,1,0:T(8,128)(2,1)S(1)}, bf16[4,128,128]{2,1,0:T(8,128)(2,1)S(1)}, u32[]{:S(2)}, u32[]{:S(2)}) collective-permute-start(bf16[4,128,128]{2,1,0:T(8,128)(2,1)S(1)} %get-tuple-element.38), channel_id=1, source_target_pairs={{128,0},{192,64},{1,128},{65,192},{129,1},{193,65},{2,129},{66,193... | collective-permute-start | bytes 393224 | tf_op jit(solution)/shard_map/ppermute | solution.py:84
  43.0 15.9 %collective-permute-start.12 = (bf16[6,128,128]{2,1,0:T(8,128)(2,1)S(1)}, bf16[6,128,128]{2,1,0:T(8,128)(2,1)S(1)}, u32[]{:S(2)}, u32[]{:S(2)}) collective-permute-start(bf16[6,128,128]{2,1,0:T(8,128)(2,1)S(1)} %get-tuple-element.42), channel_id=1, source_target_pairs={{44,0},{108,64},{172,128},{236,192},{45,1},{109,65},{173,129},{237... | collective-permute-start | bytes 589832 | tf_op jit(solution)/shard_map/ppermute | solution.py:84
  50.8 18.3 %collective-permute-start.9 = (bf16[17,128,128]{2,1,0:T(8,128)(2,1)S(1)}, bf16[17,128,128]{2,1,0:T(8,128)(2,1)S(1)}, u32[]{:S(2)}, u32[]{:S(2)}) collective-permute-start(bf16[17,128,128]{2,1,0:T(8,128)(2,1)S(1)} %get-tuple-element.39), channel_id=1, source_target_pairs={{255,0},{0,64},{64,128},{128,192},{192,1},{1,65},{65,129},{129,193... | collective-permute-start | bytes 1671176 | tf_op jit(solution)/shard_map/ppermute | solution.py:84
  50.9 20.3 %collective-permute-start.10 = (bf16[17,128,128]{2,1,0:T(8,128)(2,1)S(1)}, bf16[17,128,128]{2,1,0:T(8,128)(2,1)S(1)}, u32[]{:S(2)}, u32[]{:S(2)}) collective-permute-start(bf16[17,128,128]{2,1,0:T(8,128)(2,1)S(1)} %get-tuple-element.40), channel_id=1, source_target_pairs={{64,0},{128,64},{192,128},{1,192},{65,1},{129,65},{193,129},{2,193... | collective-permute-start | bytes 1671176 | tf_op jit(solution)/shard_map/ppermute | solution.py:84
  59.0 17.0 %collective-permute-start.15 = (bf16[12,128,128]{2,1,0:T(8,128)(2,1)S(1)}, bf16[12,128,128]{2,1,0:T(8,128)(2,1)S(1)}, u32[]{:S(2)}, u32[]{:S(2)}) collective-permute-start(bf16[12,128,128]{2,1,0:T(8,128)(2,1)S(1)} %get-tuple-element.43), channel_id=1, source_target_pairs={{255,0},{0,64},{64,128},{128,192},{192,1},{1,65},{65,129},{129,193... | collective-permute-start | bytes 1179656 | tf_op jit(solution)/shard_map/ppermute | solution.py:84
  64.3 12.9 %collective-permute-start.16 = (bf16[12,128,128]{2,1,0:T(8,128)(2,1)S(1)}, bf16[12,128,128]{2,1,0:T(8,128)(2,1)S(1)}, u32[]{:S(2)}, u32[]{:S(2)}) collective-permute-start(bf16[12,128,128]{2,1,0:T(8,128)(2,1)S(1)} %get-tuple-element.44), channel_id=1, source_target_pairs={{64,0},{128,64},{192,128},{1,192},{65,1},{129,65},{193,129},{2,193... | collective-permute-start | bytes 1179656 | tf_op jit(solution)/shard_map/ppermute | solution.py:84
  83.0 15.1 %collective-permute-start.17 = (bf16[13,2,32,128]{3,2,1,0:T(8,128)(2,1)S(1)}, bf16[13,2,32,128]{3,2,1,0:T(8,128)(2,1)S(1)}, u32[]{:S(2)}, u32[]{:S(2)}) collective-permute-start(bf16[13,2,32,128]{3,2,1,0:T(8,128)(2,1)S(1)} %get-tuple-element.46), channel_id=1, source_target_pairs={{64,0},{128,64},{192,128},{0,192},{65,1},{129,65},{193,129},{1,193... | collective-permute-start | bytes 638984 | tf_op jit(solution)/shard_map/ppermute | solution.py:84
  88.8 9.7 %collective-permute-start.18 = (bf16[13,2,32,128]{3,2,1,0:T(8,128)(2,1)S(1)}, bf16[13,2,32,128]{3,2,1,0:T(8,128)(2,1)S(1)}, u32[]{:S(2)}, u32[]{:S(2)}) collective-permute-start(bf16[13,2,32,128]{3,2,1,0:T(8,128)(2,1)S(1)} %get-tuple-element.47), channel_id=1, source_target_pairs={{128,0},{192,64},{0,128},{64,192},{129,1},{193,65},{1,129},{65,193... | collective-permute-start | bytes 638984 | tf_op jit(solution)/shard_map/ppermute | solution.py:84
  88.8 12.6 %collective-permute-start.19 = (bf16[13,2,32,128]{3,2,1,0:T(8,128)(2,1)S(1)}, bf16[13,2,32,128]{3,2,1,0:T(8,128)(2,1)S(1)}, u32[]{:S(2)}, u32[]{:S(2)}) collective-permute-start(bf16[13,2,32,128]{3,2,1,0:T(8,128)(2,1)S(1)} %get-tuple-element.48), channel_id=1, source_target_pairs={{192,0},{0,64},{64,128},{128,192},{193,1},{1,65},{65,129},{129,193... | collective-permute-start | bytes 638984 | tf_op jit(solution)/shard_map/ppermute | solution.py:84

commit v10 on v9

--- a/solution.py
+++ b/solution.py
@@ -325,6 +325,7 @@
     plus_band, minus_band = far_across(band, FAR_PAIRS), far_across(band, -FAR_PAIRS)
     before = [own, band]
     before += [lower, higher]
+    before += [plus_far, minus_far]
     low, high = call(near_body, packed(NEAR[:2]), 0, len(before))(*before)
     low, high = from_pair(low, -1), from_pair(high, 1)
     arrived = [plus_far, minus_far, plus_band, minus_band]

time: 103 us -> 107 us (1.039)
  the two profiles are of different devices: /device:TPU:56 before, /device:TPU:1 now
where the time goes in v10:
time: 107 us
  waiting for transfers between devices  51.3 us (48%)
  starting transfers between devices  45.7 us (43%)
  Pallas kernels  7.96 us (7%)
  local copies, waits for them, and re-layouts  1.92 us (2%)
    ppermute x20, waiting for transfers between devices, moved(): return lax.ppermute(x, AXES, route)  51.3 us
    ppermute x20, starting transfers between devices, moved(): return lax.ppermute(x, AXES, route)  45.7 us
    pallas_call x1, Pallas kernels, per_device(): call(purify_body, [quarter] * LAYERS, 2, len(ARRIVE), scratch=[pltpu.VMEM...  5.76 us
  transfers between devices with their start and end apart: 20, of which 9 were waited for; matrix products, arithmetic and copies ran while one was open for 0% of the time, Pallas kernels for 0%

profile of v10, /device:TPU:1, one launch (start us, length us, event | category | flops | bytes accessed | tf_op | source)
XLA Modules:
  0.0 107.0 jit_solution(18059422308104781543)
XLA Ops:
  0.0 0.0 copy-start.1
  0.0 0.7 copy-done.1
  0.7 0.1 copy.4.presence_ref
  0.8 0.0 copy-start
  0.8 1.2 %copy-done = bf16[13,8,32,128]{3,2,1,0:T(8,128)(2,1)S(1)} copy-done((bf16[13,8,32,128]{3,2,1,0:T(8,128)(2,1)S(1)}, bf16[13,8,32,128]{3,2,1,0:T(8,128)(2,1)}, u32[]{:S(2)}) %copy-start) | copy-done | bytes 851992
  1.9 0.9 shard_map.28
  2.9 7.8 %collective-permute-start.3 = (bf16[5,8,32,128]{3,2,1,0:T(8,128)(2,1)S(1)}, bf16[5,8,32,128]{3,2,1,0:T(8,128)(2,1)S(1)}, u32[]{:S(2)}, u32[]{:S(2)}) collective-permute-start(bf16[5,8,32,128]{3,2,1,0:T(8,128)(2,1)S(1)} %get-tuple-element.32), channel_id=1, source_target_pairs={{4,0},{68,64},{132,128},{196,192},{5,1},{69,65},{133,129},{197,193... | collective-permute-start | bytes 983048 | tf_op jit(solution)/shard_map/ppermute | solution.py:84
  10.7 2.5 %collective-permute-start = (bf16[13,2,32,128]{3,2,1,0:T(8,128)(2,1)S(1)}, bf16[13,2,32,128]{3,2,1,0:T(8,128)(2,1)S(1)}, u32[]{:S(2)}, u32[]{:S(2)}) collective-permute-start(bf16[13,2,32,128]{3,2,1,0:T(8,128)(2,1)S(1)} %get-tuple-element.28), channel_id=1, source_target_pairs={{64,0},{128,64},{192,128},{0,192},{65,1},{129,65},{193,129},{1,193... | collective-permute-start | bytes 638984 | tf_op jit(solution)/shard_map/ppermute | solution.py:84
  13.2 0.5 collective-permute-start.1
  13.7 0.6 collective-permute-start.2
  14.3 3.3 %collective-permute-done.refs_1_ = bf16[13,2,32,128]{3,2,1,0:T(8,128)(2,1)S(1)} collective-permute-done((bf16[13,2,32,128]{3,2,1,0:T(8,128)(2,1)S(1)}, bf16[13,2,32,128]{3,2,1,0:T(8,128)(2,1)S(1)}, u32[]{:S(2)}, u32[]{:S(2)}) %collective-permute-start) | collective-permute-done | bytes 213024 | tf_op jit(solution)/shard_map/ppermute | solution.py:84
  17.6 2.7 %collective-permute-done.1.refs_2_ = bf16[13,2,32,128]{3,2,1,0:T(8,128)(2,1)S(1)} collective-permute-done((bf16[13,2,32,128]{3,2,1,0:T(8,128)(2,1)S(1)}, bf16[13,2,32,128]{3,2,1,0:T(8,128)(2,1)S(1)}, u32[]{:S(2)}, u32[]{:S(2)}) %collective-permute-start.1) | collective-permute-done | bytes 213024 | tf_op jit(solution)/shard_map/ppermute | solution.py:84
  20.2 6.2 %collective-permute-done.2.refs_3_ = bf16[13,2,32,128]{3,2,1,0:T(8,128)(2,1)S(1)} collective-permute-done((bf16[13,2,32,128]{3,2,1,0:T(8,128)(2,1)S(1)}, bf16[13,2,32,128]{3,2,1,0:T(8,128)(2,1)S(1)}, u32[]{:S(2)}, u32[]{:S(2)}) %collective-permute-start.2) | collective-permute-done | bytes 213024 | tf_op jit(solution)/shard_map/ppermute | solution.py:84
  26.4 0.1 shard_map.29
  26.5 0.0 collective-permute-done.3.shared_ref
  26.6 0.1 collective-permute-start.4
  26.7 0.6 collective-permute-start.7
  27.3 3.9 %collective-permute-start.5 = (bf16[5,2,32,128]{3,2,1,0:T(8,128)(2,1)S(1)}, bf16[5,2,32,128]{3,2,1,0:T(8,128)(2,1)S(1)}, u32[]{:S(2)}, u32[]{:S(2)}) collective-permute-start(bf16[5,2,32,128]{3,2,1,0:T(8,128)(2,1)S(1)} %get-tuple-element.35), channel_id=1, source_target_pairs={{128,0},{192,64},{0,128},{64,192},{129,1},{193,65},{1,129},{65,193... | collective-permute-start | bytes 245768 | tf_op jit(solution)/shard_map/ppermute | solution.py:84
  31.2 0.4 collective-permute-start.6
  31.6 9.4 %collective-permute-start.9 = (bf16[6,128,128]{2,1,0:T(8,128)(2,1)S(1)}, bf16[6,128,128]{2,1,0:T(8,128)(2,1)S(1)}, u32[]{:S(2)}, u32[]{:S(2)}) collective-permute-start(bf16[6,128,128]{2,1,0:T(8,128)(2,1)S(1)} %get-tuple-element.39), channel_id=1, source_target_pairs={{20,0},{84,64},{148,128},{212,192},{21,1},{85,65},{149,129},{213,1... | collective-permute-start | bytes 589832 | tf_op jit(solution)/shard_map/ppermute | solution.py:84
  41.0 0.0 collective-permute-done.4.refs_1_
  41.0 0.0 collective-permute-start.10
  41.0 0.0 collective-permute-done.5.refs_2_
  41.0 0.0 collective-permute-done.6.refs_3_
  41.0 2.1 %collective-permute-start.14 = (bf16[10,128,128]{2,1,0:T(8,128)(2,1)S(1)}, bf16[10,128,128]{2,1,0:T(8,128)(2,1)S(1)}, u32[]{:S(2)}, u32[]{:S(2)}) collective-permute-start(bf16[10,128,128]{2,1,0:T(8,128)(2,1)S(1)} %shard_map.31.refs_0_), channel_id=1, source_target_pairs={{40,0},{104,64},{168,128},{232,192},{41,1},{105,65},{169,129},{233... | collective-permute-start | bytes 983048 | tf_op jit(solution)/shard_map/ppermute | solution.py:84
  43.1 0.8 collective-permute-start.13
  43.9 0.0 collective-permute-done.7.refs_1_.refs_3_
  43.9 3.4 %collective-permute-start.8 = (bf16[4,128,128]{2,1,0:T(8,128)(2,1)S(1)}, bf16[4,128,128]{2,1,0:T(8,128)(2,1)S(1)}, u32[]{:S(2)}, u32[]{:S(2)}) collective-permute-start(bf16[4,128,128]{2,1,0:T(8,128)(2,1)S(1)} %get-tuple-element.38), channel_id=1, source_target_pairs={{128,0},{192,64},{1,128},{65,192},{129,1},{193,65},{2,129},{66,193... | collective-permute-start | bytes 393224 | tf_op jit(solution)/shard_map/ppermute | solution.py:84
  47.3 12.3 %collective-permute-done.8.refs_2_.refs_4_ = bf16[4,128,128]{2,1,0:T(8,128)(2,1)S(1)} collective-permute-done((bf16[4,128,128]{2,1,0:T(8,128)(2,1)S(1)}, bf16[4,128,128]{2,1,0:T(8,128)(2,1)S(1)}, u32[]{:S(2)}, u32[]{:S(2)}) %collective-permute-start.8) | collective-permute-done | bytes 131104 | tf_op jit(solution)/shard_map/ppermute | solution.py:84
  59.6 0.0 collective-permute-done.9.refs_3_.refs_0_.refs_5_
  59.6 0.0 collective-permute-done.10.refs_4_.refs_1_.refs_6_
  59.6 0.1 shard_map.32
  59.7 0.3 collective-permute-start.11
  59.9 5.6 %collective-permute-start.12 = (bf16[17,128,128]{2,1,0:T(8,128)(2,1)S(1)}, bf16[17,128,128]{2,1,0:T(8,128)(2,1)S(1)}, u32[]{:S(2)}, u32[]{:S(2)}) collective-permute-start(bf16[17,128,128]{2,1,0:T(8,128)(2,1)S(1)} %get-tuple-element.42), channel_id=1, source_target_pairs={{64,0},{128,64},{192,128},{1,192},{65,1},{129,65},{193,129},{2,193... | collective-permute-start | bytes 1671176 | tf_op jit(solution)/shard_map/ppermute | solution.py:84
  65.5 0.0 collective-permute-done.14.refs_3_.refs_8_
  65.5 0.0 collective-permute-done.13.refs_2_.refs_7_
  65.5 0.1 shard_map.33
  65.6 0.3 collective-permute-start.15
  65.9 5.1 %collective-permute-start.16 = (bf16[12,128,128]{2,1,0:T(8,128)(2,1)S(1)}, bf16[12,128,128]{2,1,0:T(8,128)(2,1)S(1)}, u32[]{:S(2)}, u32[]{:S(2)}) collective-permute-start(bf16[12,128,128]{2,1,0:T(8,128)(2,1)S(1)} %get-tuple-element.44), channel_id=1, source_target_pairs={{64,0},{128,64},{192,128},{1,192},{65,1},{129,65},{193,129},{2,193... | collective-permute-start | bytes 1179656 | tf_op jit(solution)/shard_map/ppermute | solution.py:84
  70.9 8.1 %collective-permute-done.11.refs_1_ = bf16[17,128,128]{2,1,0:T(8,128)(2,1)S(1)} collective-permute-done((bf16[17,128,128]{2,1,0:T(8,128)(2,1)S(1)}, bf16[17,128,128]{2,1,0:T(8,128)(2,1)S(1)}, u32[]{:S(2)}, u32[]{:S(2)}) %collective-permute-start.11) | collective-permute-done | bytes 557088 | tf_op jit(solution)/shard_map/ppermute | solution.py:84
  79.0 0.0 collective-permute-done.12.refs_2_
  79.0 6.8 %collective-permute-done.15.refs_9_ = bf16[12,128,128]{2,1,0:T(8,128)(2,1)S(1)} collective-permute-done((bf16[12,128,128]{2,1,0:T(8,128)(2,1)S(1)}, bf16[12,128,128]{2,1,0:T(8,128)(2,1)S(1)}, u32[]{:S(2)}, u32[]{:S(2)}) %collective-permute-start.15) | collective-permute-done | bytes 393248 | tf_op jit(solution)/shard_map/ppermute | solution.py:84
  85.8 0.0 collective-permute-done.16.refs_10_
  85.9 5.8 %shard_map.34 = (bf16[13,2,32,128]{3,2,1,0:T(8,128)(2,1)S(1)}, bf16[13,2,32,128]{3,2,1,0:T(8,128)(2,1)S(1)}, bf16[13,2,32,128]{3,2,1,0:T(8,128)(2,1)S(1)}, bf16[13,2,32,128]{3,2,1,0:T(8,128)(2,1)S(1)}) custom-call(s32[1]{0:T(128)} %bitcast.me_ref, s32[13,8]{1,0:T(8,128)S(1)} %copy.4.presence_ref, ...), custom_call_target="tpu_custom_call" | custom-call | flops 3758096384 | bytes 4194304 | tf_op jit(solution)/shard_map/pallas_call | solution.py:336
  91.6 1.8 %collective-permute-start.17 = (bf16[13,2,32,128]{3,2,1,0:T(8,128)(2,1)S(1)}, bf16[13,2,32,128]{3,2,1,0:T(8,128)(2,1)S(1)}, u32[]{:S(2)}, u32[]{:S(2)}) collective-permute-start(bf16[13,2,32,128]{3,2,1,0:T(8,128)(2,1)S(1)} %get-tuple-element.46), channel_id=1, source_target_pairs={{64,0},{128,64},{192,128},{0,192},{65,1},{129,65},{193,129},{1,193... | collective-permute-start | bytes 638984 | tf_op jit(solution)/shard_map/ppermute | solution.py:84
  93.4 0.0 collective-permute-start.18
  93.4 0.7 collective-permute-start.19
  94.1 3.9 %collective-permute-done.17.refs_1_ = bf16[13,2,32,128]{3,2,1,0:T(8,128)(2,1)S(1)} collective-permute-done((bf16[13,2,32,128]{3,2,1,0:T(8,128)(2,1)S(1)}, bf16[13,2,32,128]{3,2,1,0:T(8,128)(2,1)S(1)}, u32[]{:S(2)}, u32[]{:S(2)}) %collective-permute-start.17) | collective-permute-done | bytes 213024 | tf_op jit(solution)/shard_map/ppermute | solution.py:84
  98.0 2.3 %collective-permute-done.18.refs_2_ = bf16[13,2,32,128]{3,2,1,0:T(8,128)(2,1)S(1)} collective-permute-done((bf16[13,2,32,128]{3,2,1,0:T(8,128)(2,1)S(1)}, bf16[13,2,32,128]{3,2,1,0:T(8,128)(2,1)S(1)}, u32[]{:S(2)}, u32[]{:S(2)}) %collective-permute-start.18) | collective-permute-done | bytes 213024 | tf_op jit(solution)/shard_map/ppermute | solution.py:84
  100.2 5.8 %collective-permute-done.19.refs_3_ = bf16[13,2,32,128]{3,2,1,0:T(8,128)(2,1)S(1)} collective-permute-done((bf16[13,2,32,128]{3,2,1,0:T(8,128)(2,1)S(1)}, bf16[13,2,32,128]{3,2,1,0:T(8,128)(2,1)S(1)}, u32[]{:S(2)}, u32[]{:S(2)}) %collective-permute-start.19) | collective-permute-done | bytes 213024 | tf_op jit(solution)/shard_map/ppermute | solution.py:84
  106.0 1.0 shard_map.35
  (2 shorter events, 0.1 us)
Async XLA Ops:
  0.0 0.7 copy-start.1
  0.8 1.2 %copy-start = (bf16[13,8,32,128]{3,2,1,0:T(8,128)(2,1)S(1)}, bf16[13,8,32,128]{3,2,1,0:T(8,128)(2,1)}, u32[]{:S(2)}) copy-start(bf16[13,8,32,128]{3,2,1,0:T(8,128)(2,1)} %blocks_ref.1) | copy-start | bytes 2555908
  2.9 23.7 %collective-permute-start.3 = (bf16[5,8,32,128]{3,2,1,0:T(8,128)(2,1)S(1)}, bf16[5,8,32,128]{3,2,1,0:T(8,128)(2,1)S(1)}, u32[]{:S(2)}, u32[]{:S(2)}) collective-permute-start(bf16[5,8,32,128]{3,2,1,0:T(8,128)(2,1)S(1)} %get-tuple-element.32), channel_id=1, source_target_pairs={{4,0},{68,64},{132,128},{196,192},{5,1},{69,65},{133,129},{197,193... | collective-permute-start | bytes 983048 | tf_op jit(solution)/shard_map/ppermute | solution.py:84
  10.7 6.9 %collective-permute-start = (bf16[13,2,32,128]{3,2,1,0:T(8,128)(2,1)S(1)}, bf16[13,2,32,128]{3,2,1,0:T(8,128)(2,1)S(1)}, u32[]{:S(2)}, u32[]{:S(2)}) collective-permute-start(bf16[13,2,32,128]{3,2,1,0:T(8,128)(2,1)S(1)} %get-tuple-element.28), channel_id=1, source_target_pairs={{64,0},{128,64},{192,128},{0,192},{65,1},{129,65},{193,129},{1,193... | collective-permute-start | bytes 638984 | tf_op jit(solution)/shard_map/ppermute | solution.py:84
  13.2 7.1 %collective-permute-start.1 = (bf16[13,2,32,128]{3,2,1,0:T(8,128)(2,1)S(1)}, bf16[13,2,32,128]{3,2,1,0:T(8,128)(2,1)S(1)}, u32[]{:S(2)}, u32[]{:S(2)}) collective-permute-start(bf16[13,2,32,128]{3,2,1,0:T(8,128)(2,1)S(1)} %get-tuple-element.29), channel_id=1, source_target_pairs={{128,0},{192,64},{0,128},{64,192},{129,1},{193,65},{1,129},{65,193... | collective-permute-start | bytes 638984 | tf_op jit(solution)/shard_map/ppermute | solution.py:84
  13.7 12.7 %collective-permute-start.2 = (bf16[13,2,32,128]{3,2,1,0:T(8,128)(2,1)S(1)}, bf16[13,2,32,128]{3,2,1,0:T(8,128)(2,1)S(1)}, u32[]{:S(2)}, u32[]{:S(2)}) collective-permute-start(bf16[13,2,32,128]{3,2,1,0:T(8,128)(2,1)S(1)} %get-tuple-element.30), channel_id=1, source_target_pairs={{192,0},{0,64},{64,128},{128,192},{193,1},{1,65},{65,129},{129,193... | collective-permute-start | bytes 638984 | tf_op jit(solution)/shard_map/ppermute | solution.py:84
  26.6 14.4 %collective-permute-start.4 = (bf16[5,2,32,128]{3,2,1,0:T(8,128)(2,1)S(1)}, bf16[5,2,32,128]{3,2,1,0:T(8,128)(2,1)S(1)}, u32[]{:S(2)}, u32[]{:S(2)}) collective-permute-start(bf16[5,2,32,128]{3,2,1,0:T(8,128)(2,1)S(1)} %get-tuple-element.34), channel_id=1, source_target_pairs={{64,0},{128,64},{192,128},{0,192},{65,1},{129,65},{193,129},{1,193... | collective-permute-start | bytes 245768 | tf_op jit(solution)/shard_map/ppermute | solution.py:84
  26.7 17.2 %collective-permute-start.7 = (bf16[4,128,128]{2,1,0:T(8,128)(2,1)S(1)}, bf16[4,128,128]{2,1,0:T(8,128)(2,1)S(1)}, u32[]{:S(2)}, u32[]{:S(2)}) collective-permute-start(bf16[4,128,128]{2,1,0:T(8,128)(2,1)S(1)} %get-tuple-element.37), channel_id=1, source_target_pairs={{191,0},{255,64},{0,128},{64,192},{128,1},{192,65},{1,129},{65,193... | collective-permute-start | bytes 393224 | tf_op jit(solution)/shard_map/ppermute | solution.py:84
  27.3 13.7 %collective-permute-start.5 = (bf16[5,2,32,128]{3,2,1,0:T(8,128)(2,1)S(1)}, bf16[5,2,32,128]{3,2,1,0:T(8,128)(2,1)S(1)}, u32[]{:S(2)}, u32[]{:S(2)}) collective-permute-start(bf16[5,2,32,128]{3,2,1,0:T(8,128)(2,1)S(1)} %get-tuple-element.35), channel_id=1, source_target_pairs={{128,0},{192,64},{0,128},{64,192},{129,1},{193,65},{1,129},{65,193... | collective-permute-start | bytes 245768 | tf_op jit(solution)/shard_map/ppermute | solution.py:84
  31.2 9.8 %collective-permute-start.6 = (bf16[5,2,32,128]{3,2,1,0:T(8,128)(2,1)S(1)}, bf16[5,2,32,128]{3,2,1,0:T(8,128)(2,1)S(1)}, u32[]{:S(2)}, u32[]{:S(2)}) collective-permute-start(bf16[5,2,32,128]{3,2,1,0:T(8,128)(2,1)S(1)} %get-tuple-element.36), channel_id=1, source_target_pairs={{192,0},{0,64},{64,128},{128,192},{193,1},{1,65},{65,129},{129,193... | collective-permute-start | bytes 245768 | tf_op jit(solution)/shard_map/ppermute | solution.py:84
  31.6 28.0 %collective-permute-start.9 = (bf16[6,128,128]{2,1,0:T(8,128)(2,1)S(1)}, bf16[6,128,128]{2,1,0:T(8,128)(2,1)S(1)}, u32[]{:S(2)}, u32[]{:S(2)}) collective-permute-start(bf16[6,128,128]{2,1,0:T(8,128)(2,1)S(1)} %get-tuple-element.39), channel_id=1, source_target_pairs={{20,0},{84,64},{148,128},{212,192},{21,1},{85,65},{149,129},{213,1... | collective-permute-start | bytes 589832 | tf_op jit(solution)/shard_map/ppermute | solution.py:84
  41.0 18.6 %collective-permute-start.10 = (bf16[6,128,128]{2,1,0:T(8,128)(2,1)S(1)}, bf16[6,128,128]{2,1,0:T(8,128)(2,1)S(1)}, u32[]{:S(2)}, u32[]{:S(2)}) collective-permute-start(bf16[6,128,128]{2,1,0:T(8,128)(2,1)S(1)} %get-tuple-element.40), channel_id=1, source_target_pairs={{44,0},{108,64},{172,128},{236,192},{45,1},{109,65},{173,129},{237... | collective-permute-start | bytes 589832 | tf_op jit(solution)/shard_map/ppermute | solution.py:84
  41.0 24.5 %collective-permute-start.14 = (bf16[10,128,128]{2,1,0:T(8,128)(2,1)S(1)}, bf16[10,128,128]{2,1,0:T(8,128)(2,1)S(1)}, u32[]{:S(2)}, u32[]{:S(2)}) collective-permute-start(bf16[10,128,128]{2,1,0:T(8,128)(2,1)S(1)} %shard_map.31.refs_0_), channel_id=1, source_target_pairs={{40,0},{104,64},{168,128},{232,192},{41,1},{105,65},{169,129},{233... | collective-permute-start | bytes 983048 | tf_op jit(solution)/shard_map/ppermute | solution.py:84
  43.1 22.5 %collective-permute-start.13 = (bf16[10,128,128]{2,1,0:T(8,128)(2,1)S(1)}, bf16[10,128,128]{2,1,0:T(8,128)(2,1)S(1)}, u32[]{:S(2)}, u32[]{:S(2)}) collective-permute-start(bf16[10,128,128]{2,1,0:T(8,128)(2,1)S(1)} %shard_map.31.refs_0_), channel_id=1, source_target_pairs={{16,0},{80,64},{144,128},{208,192},{17,1},{81,65},{145,129},{209,1... | collective-permute-start | bytes 983048 | tf_op jit(solution)/shard_map/ppermute | solution.py:84
  43.9 15.7 %collective-permute-start.8 = (bf16[4,128,128]{2,1,0:T(8,128)(2,1)S(1)}, bf16[4,128,128]{2,1,0:T(8,128)(2,1)S(1)}, u32[]{:S(2)}, u32[]{:S(2)}) collective-permute-start(bf16[4,128,128]{2,1,0:T(8,128)(2,1)S(1)} %get-tuple-element.38), channel_id=1, source_target_pairs={{128,0},{192,64},{1,128},{65,192},{129,1},{193,65},{2,129},{66,193... | collective-permute-start | bytes 393224 | tf_op jit(solution)/shard_map/ppermute | solution.py:84
  59.7 19.3 %collective-permute-start.11 = (bf16[17,128,128]{2,1,0:T(8,128)(2,1)S(1)}, bf16[17,128,128]{2,1,0:T(8,128)(2,1)S(1)}, u32[]{:S(2)}, u32[]{:S(2)}) collective-permute-start(bf16[17,128,128]{2,1,0:T(8,128)(2,1)S(1)} %get-tuple-element.41), channel_id=1, source_target_pairs={{255,0},{0,64},{64,128},{128,192},{192,1},{1,65},{65,129},{129,193... | collective-permute-start | bytes 1671176 | tf_op jit(solution)/shard_map/ppermute | solution.py:84
  59.9 19.1 %collective-permute-start.12 = (bf16[17,128,128]{2,1,0:T(8,128)(2,1)S(1)}, bf16[17,128,128]{2,1,0:T(8,128)(2,1)S(1)}, u32[]{:S(2)}, u32[]{:S(2)}) collective-permute-start(bf16[17,128,128]{2,1,0:T(8,128)(2,1)S(1)} %get-tuple-element.42), channel_id=1, source_target_pairs={{64,0},{128,64},{192,128},{1,192},{65,1},{129,65},{193,129},{2,193... | collective-permute-start | bytes 1671176 | tf_op jit(solution)/shard_map/ppermute | solution.py:84
  65.6 20.2 %collective-permute-start.15 = (bf16[12,128,128]{2,1,0:T(8,128)(2,1)S(1)}, bf16[12,128,128]{2,1,0:T(8,128)(2,1)S(1)}, u32[]{:S(2)}, u32[]{:S(2)}) collective-permute-start(bf16[12,128,128]{2,1,0:T(8,128)(2,1)S(1)} %get-tuple-element.43), channel_id=1, source_target_pairs={{255,0},{0,64},{64,128},{128,192},{192,1},{1,65},{65,129},{129,193... | collective-permute-start | bytes 1179656 | tf_op jit(solution)/shard_map/ppermute | solution.py:84
  65.9 20.0 %collective-permute-start.16 = (bf16[12,128,128]{2,1,0:T(8,128)(2,1)S(1)}, bf16[12,128,128]{2,1,0:T(8,128)(2,1)S(1)}, u32[]{:S(2)}, u32[]{:S(2)}) collective-permute-start(bf16[12,128,128]{2,1,0:T(8,128)(2,1)S(1)} %get-tuple-element.44), channel_id=1, source_target_pairs={{64,0},{128,64},{192,128},{1,192},{65,1},{129,65},{193,129},{2,193... | collective-permute-start | bytes 1179656 | tf_op jit(solution)/shard_map/ppermute | solution.py:84
  91.6 6.3 %collective-permute-start.17 = (bf16[13,2,32,128]{3,2,1,0:T(8,128)(2,1)S(1)}, bf16[13,2,32,128]{3,2,1,0:T(8,128)(2,1)S(1)}, u32[]{:S(2)}, u32[]{:S(2)}) collective-permute-start(bf16[13,2,32,128]{3,2,1,0:T(8,128)(2,1)S(1)} %get-tuple-element.46), channel_id=1, source_target_pairs={{64,0},{128,64},{192,128},{0,192},{65,1},{129,65},{193,129},{1,193... | collective-permute-start | bytes 638984 | tf_op jit(solution)/shard_map/ppermute | solution.py:84
  93.4 6.8 %collective-permute-start.18 = (bf16[13,2,32,128]{3,2,1,0:T(8,128)(2,1)S(1)}, bf16[13,2,32,128]{3,2,1,0:T(8,128)(2,1)S(1)}, u32[]{:S(2)}, u32[]{:S(2)}) collective-permute-start(bf16[13,2,32,128]{3,2,1,0:T(8,128)(2,1)S(1)} %get-tuple-element.47), channel_id=1, source_target_pairs={{128,0},{192,64},{0,128},{64,192},{129,1},{193,65},{1,129},{65,193... | collective-permute-start | bytes 638984 | tf_op jit(solution)/shard_map/ppermute | solution.py:84
  93.4 12.6 %collective-permute-start.19 = (bf16[13,2,32,128]{3,2,1,0:T(8,128)(2,1)S(1)}, bf16[13,2,32,128]{3,2,1,0:T(8,128)(2,1)S(1)}, u32[]{:S(2)}, u32[]{:S(2)}) collective-permute-start(bf16[13,2,32,128]{3,2,1,0:T(8,128)(2,1)S(1)} %get-tuple-element.48), channel_id=1, source_target_pairs={{192,0},{0,64},{64,128},{128,192},{193,1},{1,65},{65,129},{129,193... | collective-permute-start | bytes 638984 | tf_op jit(solution)/shard_map/ppermute | solution.py:84

commit v11 on v10

--- a/solution.py
+++ b/solution.py
@@ -140,7 +140,7 @@
             row = 2 * other + t
             for d in range(DIAGS):
                 tile = blocks_ref[d, row]
-                present = presence_ref[d, row] != 0
+                present = presence_ref[row, d] != 0
                 tile = jnp.where(present, tile, jnp.zeros_like(tile))
                 out_refs[s][d, t] = tile
                 if d in SHARED:
@@ -177,7 +177,7 @@
 
 
 def fan_body(me_ref, *refs):
-    pieces, out_ref = refs[:LAYERS], refs[LAYERS]
+    pieces, out_ref = refs[:LAYERS], refs[-1]
     for s, piece in enumerate(pieces):
         other = lax.rem(me_ref[0] + s, LAYERS)
         rows = pl.ds(pl.multiple_of(other * (BS // LAYERS), BS // LAYERS), BS // LAYERS)
@@ -252,7 +252,7 @@
                 d = targets.get((i, column))
                 if d is not None:
                     tile = total[i * BS : (i + 1) * BS, at * BS : (at + 1) * BS]
-                    use(i, column, d, presence_ref[d, 2 * me + i] != 0, tile)
+                    use(i, column, d, presence_ref[2 * me + i, d] != 0, tile)
 
     groups = [[c, c + 1] for c in range(0, 16, 2)]
 
@@ -295,6 +295,7 @@
 
 def per_device(blocks, presence):
     me = lax.axis_index("layer").astype(jnp.int32).reshape(1)
+    presence = presence.T
 
     def packed(messages):
         return [bf16(len(message), BS, BS) for message in messages]
@@ -321,10 +322,9 @@
     some = [shared, own]
     some = call(resplit_body, [shared_quarter] * LAYERS, 1, len(some))(me, *some)
     some = exchanged(some)
-    band = call(fan_body, packed([FAN])[0], 1, LAYERS)(me, *some)
+    band = call(fan_body, packed([FAN])[0], 1, LAYERS + 2)(me, *some, lower, higher)
     plus_band, minus_band = far_across(band, FAR_PAIRS), far_across(band, -FAR_PAIRS)
-    before = [own, band]
-    before += [lower, higher]
+    before = [own]
     before += [plus_far, minus_far]
     low, high = call(near_body, packed(NEAR[:2]), 0, len(before))(*before)
     low, high = from_pair(low, -1), from_pair(high, 1)

time: 107 us -> 108 us (level)
  waiting for transfers between devices: 51.3 us -> 56 us
  starting transfers between devices: 45.7 us -> 42.1 us
    ppermute x20, waiting for transfers between devices: 51.3 us -> 56 us  [moved(): return lax.ppermute(x, AXES, route)]
    ppermute x20, starting transfers between devices: 45.7 us -> 42.1 us  [moved(): return lax.ppermute(x, AXES, route)]
  transfers between devices with their start and end apart: 20 -> 20, of which waited for: 9 -> 11; matrix products, arithmetic and copies ran while one was open for 0% -> 0% of each run, Pallas kernels for 0% -> 0%
where the time goes in v11:
time: 108 us
  waiting for transfers between devices  56 us (52%)
  starting transfers between devices  42.1 us (39%)
  Pallas kernels  7.83 us (7%)
  local copies, waits for them, and re-layouts  1.84 us (2%)
    ppermute x20, waiting for transfers between devices, moved(): return lax.ppermute(x, AXES, route)  56 us
    ppermute x20, starting transfers between devices, moved(): return lax.ppermute(x, AXES, route)  42.1 us
    pallas_call x1, Pallas kernels, per_device(): call(purify_body, [quarter] * LAYERS, 2, len(ARRIVE), scratch=[pltpu.VMEM...  5.71 us
  transfers between devices with their start and end apart: 20, of which 11 were waited for; matrix products, arithmetic and copies ran while one was open for 0% of the time, Pallas kernels for 0%

profile of v11, /device:TPU:1, one launch (start us, length us, event | category | flops | bytes accessed | tf_op | source)
XLA Modules:
  0.0 107.8 jit_solution(10165193327059115186)
XLA Ops:
  0.0 0.0 copy-start.1
  0.0 0.7 copy-done.1
  0.7 0.0 copy-start
  0.7 1.2 %copy-done = bf16[13,8,32,128]{3,2,1,0:T(8,128)(2,1)S(1)} copy-done((bf16[13,8,32,128]{3,2,1,0:T(8,128)(2,1)S(1)}, bf16[13,8,32,128]{3,2,1,0:T(8,128)(2,1)}, u32[]{:S(2)}) %copy-start) | copy-done | bytes 851992
  1.8 0.9 shard_map.28
  2.7 7.8 %collective-permute-start.9 = (bf16[5,8,32,128]{3,2,1,0:T(8,128)(2,1)S(1)}, bf16[5,8,32,128]{3,2,1,0:T(8,128)(2,1)S(1)}, u32[]{:S(2)}, u32[]{:S(2)}) collective-permute-start(bf16[5,8,32,128]{3,2,1,0:T(8,128)(2,1)S(1)} %get-tuple-element.38), channel_id=1, source_target_pairs={{4,0},{68,64},{132,128},{196,192},{5,1},{69,65},{133,129},{197,193... | collective-permute-start | bytes 983048 | tf_op jit(solution)/shard_map/ppermute | solution.py:84
  10.6 2.5 %collective-permute-start = (bf16[13,2,32,128]{3,2,1,0:T(8,128)(2,1)S(1)}, bf16[13,2,32,128]{3,2,1,0:T(8,128)(2,1)S(1)}, u32[]{:S(2)}, u32[]{:S(2)}) collective-permute-start(bf16[13,2,32,128]{3,2,1,0:T(8,128)(2,1)S(1)} %get-tuple-element.28), channel_id=1, source_target_pairs={{64,0},{128,64},{192,128},{0,192},{65,1},{129,65},{193,129},{1,193... | collective-permute-start | bytes 638984 | tf_op jit(solution)/shard_map/ppermute | solution.py:84
  13.0 0.5 collective-permute-start.1
  13.6 0.6 collective-permute-start.2
  14.2 3.3 %collective-permute-done.refs_1_ = bf16[13,2,32,128]{3,2,1,0:T(8,128)(2,1)S(1)} collective-permute-done((bf16[13,2,32,128]{3,2,1,0:T(8,128)(2,1)S(1)}, bf16[13,2,32,128]{3,2,1,0:T(8,128)(2,1)S(1)}, u32[]{:S(2)}, u32[]{:S(2)}) %collective-permute-start) | collective-permute-done | bytes 213024 | tf_op jit(solution)/shard_map/ppermute | solution.py:84
  17.4 2.7 %collective-permute-done.1.refs_2_ = bf16[13,2,32,128]{3,2,1,0:T(8,128)(2,1)S(1)} collective-permute-done((bf16[13,2,32,128]{3,2,1,0:T(8,128)(2,1)S(1)}, bf16[13,2,32,128]{3,2,1,0:T(8,128)(2,1)S(1)}, u32[]{:S(2)}, u32[]{:S(2)}) %collective-permute-start.1) | collective-permute-done | bytes 213024 | tf_op jit(solution)/shard_map/ppermute | solution.py:84
  20.1 6.2 %collective-permute-done.2.refs_3_ = bf16[13,2,32,128]{3,2,1,0:T(8,128)(2,1)S(1)} collective-permute-done((bf16[13,2,32,128]{3,2,1,0:T(8,128)(2,1)S(1)}, bf16[13,2,32,128]{3,2,1,0:T(8,128)(2,1)S(1)}, u32[]{:S(2)}, u32[]{:S(2)}) %collective-permute-start.2) | collective-permute-done | bytes 213024 | tf_op jit(solution)/shard_map/ppermute | solution.py:84
  26.3 0.1 shard_map.29
  26.4 0.6 collective-permute-start.7
  27.0 4.8 %collective-permute-start.8 = (bf16[4,128,128]{2,1,0:T(8,128)(2,1)S(1)}, bf16[4,128,128]{2,1,0:T(8,128)(2,1)S(1)}, u32[]{:S(2)}, u32[]{:S(2)}) collective-permute-start(bf16[4,128,128]{2,1,0:T(8,128)(2,1)S(1)} %get-tuple-element.37), channel_id=1, source_target_pairs={{128,0},{192,64},{1,128},{65,192},{129,1},{193,65},{2,129},{66,193... | collective-permute-start | bytes 393224 | tf_op jit(solution)/shard_map/ppermute | solution.py:84
  31.8 0.0 collective-permute-done.9.shared_ref
  31.9 0.1 collective-permute-start.10
  31.9 0.1 collective-permute-start.11
  32.0 1.4 %collective-permute-start.12 = (bf16[5,2,32,128]{3,2,1,0:T(8,128)(2,1)S(1)}, bf16[5,2,32,128]{3,2,1,0:T(8,128)(2,1)S(1)}, u32[]{:S(2)}, u32[]{:S(2)}) collective-permute-start(bf16[5,2,32,128]{3,2,1,0:T(8,128)(2,1)S(1)} %get-tuple-element.42), channel_id=1, source_target_pairs={{192,0},{0,64},{64,128},{128,192},{193,1},{1,65},{65,129},{129,193... | collective-permute-start | bytes 245768 | tf_op jit(solution)/shard_map/ppermute | solution.py:84
  33.4 2.0 %collective-permute-done.7.refs_4_.refs_3_ = bf16[4,128,128]{2,1,0:T(8,128)(2,1)S(1)} collective-permute-done((bf16[4,128,128]{2,1,0:T(8,128)(2,1)S(1)}, bf16[4,128,128]{2,1,0:T(8,128)(2,1)S(1)}, u32[]{:S(2)}, u32[]{:S(2)}) %collective-permute-start.7) | collective-permute-done | bytes 131104 | tf_op jit(solution)/shard_map/ppermute | solution.py:84
  35.4 3.1 %collective-permute-start.3 = (bf16[6,128,128]{2,1,0:T(8,128)(2,1)S(1)}, bf16[6,128,128]{2,1,0:T(8,128)(2,1)S(1)}, u32[]{:S(2)}, u32[]{:S(2)}) collective-permute-start(bf16[6,128,128]{2,1,0:T(8,128)(2,1)S(1)} %get-tuple-element.32), channel_id=1, source_target_pairs={{20,0},{84,64},{148,128},{212,192},{21,1},{85,65},{149,129},{213,1... | collective-permute-start | bytes 589832 | tf_op jit(solution)/shard_map/ppermute | solution.py:84
  38.5 0.0 collective-permute-done.8.refs_5_.refs_4_
  38.5 3.1 %collective-permute-start.4 = (bf16[6,128,128]{2,1,0:T(8,128)(2,1)S(1)}, bf16[6,128,128]{2,1,0:T(8,128)(2,1)S(1)}, u32[]{:S(2)}, u32[]{:S(2)}) collective-permute-start(bf16[6,128,128]{2,1,0:T(8,128)(2,1)S(1)} %get-tuple-element.33), channel_id=1, source_target_pairs={{44,0},{108,64},{172,128},{236,192},{45,1},{109,65},{173,129},{237... | collective-permute-start | bytes 589832 | tf_op jit(solution)/shard_map/ppermute | solution.py:84
  41.7 0.0 collective-permute-done.10.refs_1_
  41.7 0.0 collective-permute-done.11.refs_2_
  41.7 0.0 collective-permute-done.12.refs_3_
  41.7 4.6 %collective-permute-start.14 = (bf16[10,128,128]{2,1,0:T(8,128)(2,1)S(1)}, bf16[10,128,128]{2,1,0:T(8,128)(2,1)S(1)}, u32[]{:S(2)}, u32[]{:S(2)}) collective-permute-start(bf16[10,128,128]{2,1,0:T(8,128)(2,1)S(1)} %shard_map.32), channel_id=1, source_target_pairs={{40,0},{104,64},{168,128},{232,192},{41,1},{105,65},{169,129},{233... | collective-permute-start | bytes 983048 | tf_op jit(solution)/shard_map/ppermute | solution.py:84
  46.3 0.8 collective-permute-start.13
  47.1 2.5 %collective-permute-done.3.refs_0_.refs_5_ = bf16[6,128,128]{2,1,0:T(8,128)(2,1)S(1)} collective-permute-done((bf16[6,128,128]{2,1,0:T(8,128)(2,1)S(1)}, bf16[6,128,128]{2,1,0:T(8,128)(2,1)S(1)}, u32[]{:S(2)}, u32[]{:S(2)}) %collective-permute-start.3) | collective-permute-done | bytes 196640 | tf_op jit(solution)/shard_map/ppermute | solution.py:84
  49.6 11.9 %collective-permute-done.4.refs_1_.refs_6_ = bf16[6,128,128]{2,1,0:T(8,128)(2,1)S(1)} collective-permute-done((bf16[6,128,128]{2,1,0:T(8,128)(2,1)S(1)}, bf16[6,128,128]{2,1,0:T(8,128)(2,1)S(1)}, u32[]{:S(2)}, u32[]{:S(2)}) %collective-permute-start.4) | collective-permute-done | bytes 196640 | tf_op jit(solution)/shard_map/ppermute | solution.py:84
  61.4 0.1 shard_map.30
  61.5 0.1 collective-permute-start.5
  61.6 5.1 %collective-permute-start.6 = (bf16[17,128,128]{2,1,0:T(8,128)(2,1)S(1)}, bf16[17,128,128]{2,1,0:T(8,128)(2,1)S(1)}, u32[]{:S(2)}, u32[]{:S(2)}) collective-permute-start(bf16[17,128,128]{2,1,0:T(8,128)(2,1)S(1)} %get-tuple-element.35), channel_id=1, source_target_pairs={{64,0},{128,64},{192,128},{1,192},{65,1},{129,65},{193,129},{2,193... | collective-permute-start | bytes 1671176 | tf_op jit(solution)/shard_map/ppermute | solution.py:84
  66.7 0.0 collective-permute-done.14.refs_3_.refs_8_
  66.7 0.0 collective-permute-done.13.refs_2_.refs_7_
  66.7 0.1 shard_map.33
  66.7 0.3 collective-permute-start.15
  67.0 5.1 %collective-permute-start.16 = (bf16[12,128,128]{2,1,0:T(8,128)(2,1)S(1)}, bf16[12,128,128]{2,1,0:T(8,128)(2,1)S(1)}, u32[]{:S(2)}, u32[]{:S(2)}) collective-permute-start(bf16[12,128,128]{2,1,0:T(8,128)(2,1)S(1)} %get-tuple-element.44), channel_id=1, source_target_pairs={{64,0},{128,64},{192,128},{1,192},{65,1},{129,65},{193,129},{2,193... | collective-permute-start | bytes 1179656 | tf_op jit(solution)/shard_map/ppermute | solution.py:84
  72.1 8.1 %collective-permute-done.5.refs_1_ = bf16[17,128,128]{2,1,0:T(8,128)(2,1)S(1)} collective-permute-done((bf16[17,128,128]{2,1,0:T(8,128)(2,1)S(1)}, bf16[17,128,128]{2,1,0:T(8,128)(2,1)S(1)}, u32[]{:S(2)}, u32[]{:S(2)}) %collective-permute-start.5) | collective-permute-done | bytes 557088 | tf_op jit(solution)/shard_map/ppermute | solution.py:84
  80.1 0.0 collective-permute-done.6.refs_2_
  80.1 7.6 %collective-permute-done.15.refs_9_ = bf16[12,128,128]{2,1,0:T(8,128)(2,1)S(1)} collective-permute-done((bf16[12,128,128]{2,1,0:T(8,128)(2,1)S(1)}, bf16[12,128,128]{2,1,0:T(8,128)(2,1)S(1)}, u32[]{:S(2)}, u32[]{:S(2)}) %collective-permute-start.15) | collective-permute-done | bytes 393248 | tf_op jit(solution)/shard_map/ppermute | solution.py:84
  87.7 0.0 collective-permute-done.16.refs_10_
  87.7 5.7 %shard_map.34 = (bf16[13,2,32,128]{3,2,1,0:T(8,128)(2,1)S(1)}, bf16[13,2,32,128]{3,2,1,0:T(8,128)(2,1)S(1)}, bf16[13,2,32,128]{3,2,1,0:T(8,128)(2,1)S(1)}, bf16[13,2,32,128]{3,2,1,0:T(8,128)(2,1)S(1)}) custom-call(s32[1]{0:T(128)} %bitcast.me_ref, s32[8,13]{1,0:T(8,128)S(1)} %bitcast.3, ...), custom_call_target="tpu_custom_call" | custom-call | flops 3758096384 | bytes 4194304 | tf_op jit(solution)/shard_map/pallas_call | solution.py:336
  93.4 0.1 collective-permute-start.17
  93.5 0.1 collective-permute-start.18
  93.6 1.4 %collective-permute-start.19 = (bf16[13,2,32,128]{3,2,1,0:T(8,128)(2,1)S(1)}, bf16[13,2,32,128]{3,2,1,0:T(8,128)(2,1)S(1)}, u32[]{:S(2)}, u32[]{:S(2)}) collective-permute-start(bf16[13,2,32,128]{3,2,1,0:T(8,128)(2,1)S(1)} %get-tuple-element.48), channel_id=1, source_target_pairs={{192,0},{0,64},{64,128},{128,192},{193,1},{1,65},{65,129},{129,193... | collective-permute-start | bytes 638984 | tf_op jit(solution)/shard_map/ppermute | solution.py:84
  95.0 4.3 %collective-permute-done.17.refs_1_ = bf16[13,2,32,128]{3,2,1,0:T(8,128)(2,1)S(1)} collective-permute-done((bf16[13,2,32,128]{3,2,1,0:T(8,128)(2,1)S(1)}, bf16[13,2,32,128]{3,2,1,0:T(8,128)(2,1)S(1)}, u32[]{:S(2)}, u32[]{:S(2)}) %collective-permute-start.17) | collective-permute-done | bytes 213024 | tf_op jit(solution)/shard_map/ppermute | solution.py:84
  99.3 1.6 %collective-permute-done.18.refs_2_ = bf16[13,2,32,128]{3,2,1,0:T(8,128)(2,1)S(1)} collective-permute-done((bf16[13,2,32,128]{3,2,1,0:T(8,128)(2,1)S(1)}, bf16[13,2,32,128]{3,2,1,0:T(8,128)(2,1)S(1)}, u32[]{:S(2)}, u32[]{:S(2)}) %collective-permute-start.18) | collective-permute-done | bytes 213024 | tf_op jit(solution)/shard_map/ppermute | solution.py:84
  100.9 5.9 %collective-permute-done.19.refs_3_ = bf16[13,2,32,128]{3,2,1,0:T(8,128)(2,1)S(1)} collective-permute-done((bf16[13,2,32,128]{3,2,1,0:T(8,128)(2,1)S(1)}, bf16[13,2,32,128]{3,2,1,0:T(8,128)(2,1)S(1)}, u32[]{:S(2)}, u32[]{:S(2)}) %collective-permute-start.19) | collective-permute-done | bytes 213024 | tf_op jit(solution)/shard_map/ppermute | solution.py:84
  106.8 1.0 shard_map.35
  (2 shorter events, 0.1 us)
Async XLA Ops:
  0.0 0.7 copy-start.1
  0.7 1.2 %copy-start = (bf16[13,8,32,128]{3,2,1,0:T(8,128)(2,1)S(1)}, bf16[13,8,32,128]{3,2,1,0:T(8,128)(2,1)}, u32[]{:S(2)}) copy-start(bf16[13,8,32,128]{3,2,1,0:T(8,128)(2,1)} %blocks_ref.1) | copy-start | bytes 2555908
  2.7 29.1 %collective-permute-start.9 = (bf16[5,8,32,128]{3,2,1,0:T(8,128)(2,1)S(1)}, bf16[5,8,32,128]{3,2,1,0:T(8,128)(2,1)S(1)}, u32[]{:S(2)}, u32[]{:S(2)}) collective-permute-start(bf16[5,8,32,128]{3,2,1,0:T(8,128)(2,1)S(1)} %get-tuple-element.38), channel_id=1, source_target_pairs={{4,0},{68,64},{132,128},{196,192},{5,1},{69,65},{133,129},{197,193... | collective-permute-start | bytes 983048 | tf_op jit(solution)/shard_map/ppermute | solution.py:84
  10.6 6.9 %collective-permute-start = (bf16[13,2,32,128]{3,2,1,0:T(8,128)(2,1)S(1)}, bf16[13,2,32,128]{3,2,1,0:T(8,128)(2,1)S(1)}, u32[]{:S(2)}, u32[]{:S(2)}) collective-permute-start(bf16[13,2,32,128]{3,2,1,0:T(8,128)(2,1)S(1)} %get-tuple-element.28), channel_id=1, source_target_pairs={{64,0},{128,64},{192,128},{0,192},{65,1},{129,65},{193,129},{1,193... | collective-permute-start | bytes 638984 | tf_op jit(solution)/shard_map/ppermute | solution.py:84
  13.0 7.1 %collective-permute-start.1 = (bf16[13,2,32,128]{3,2,1,0:T(8,128)(2,1)S(1)}, bf16[13,2,32,128]{3,2,1,0:T(8,128)(2,1)S(1)}, u32[]{:S(2)}, u32[]{:S(2)}) collective-permute-start(bf16[13,2,32,128]{3,2,1,0:T(8,128)(2,1)S(1)} %get-tuple-element.29), channel_id=1, source_target_pairs={{128,0},{192,64},{0,128},{64,192},{129,1},{193,65},{1,129},{65,193... | collective-permute-start | bytes 638984 | tf_op jit(solution)/shard_map/ppermute | solution.py:84
  13.6 12.7 %collective-permute-start.2 = (bf16[13,2,32,128]{3,2,1,0:T(8,128)(2,1)S(1)}, bf16[13,2,32,128]{3,2,1,0:T(8,128)(2,1)S(1)}, u32[]{:S(2)}, u32[]{:S(2)}) collective-permute-start(bf16[13,2,32,128]{3,2,1,0:T(8,128)(2,1)S(1)} %get-tuple-element.30), channel_id=1, source_target_pairs={{192,0},{0,64},{64,128},{128,192},{193,1},{1,65},{65,129},{129,193... | collective-permute-start | bytes 638984 | tf_op jit(solution)/shard_map/ppermute | solution.py:84
  26.4 9.0 %collective-permute-start.7 = (bf16[4,128,128]{2,1,0:T(8,128)(2,1)S(1)}, bf16[4,128,128]{2,1,0:T(8,128)(2,1)S(1)}, u32[]{:S(2)}, u32[]{:S(2)}) collective-permute-start(bf16[4,128,128]{2,1,0:T(8,128)(2,1)S(1)} %get-tuple-element.36), channel_id=1, source_target_pairs={{191,0},{255,64},{0,128},{64,192},{128,1},{192,65},{1,129},{65,193... | collective-permute-start | bytes 393224 | tf_op jit(solution)/shard_map/ppermute | solution.py:84
  27.0 11.5 %collective-permute-start.8 = (bf16[4,128,128]{2,1,0:T(8,128)(2,1)S(1)}, bf16[4,128,128]{2,1,0:T(8,128)(2,1)S(1)}, u32[]{:S(2)}, u32[]{:S(2)}) collective-permute-start(bf16[4,128,128]{2,1,0:T(8,128)(2,1)S(1)} %get-tuple-element.37), channel_id=1, source_target_pairs={{128,0},{192,64},{1,128},{65,192},{129,1},{193,65},{2,129},{66,193... | collective-permute-start | bytes 393224 | tf_op jit(solution)/shard_map/ppermute | solution.py:84
  31.9 9.8 %collective-permute-start.10 = (bf16[5,2,32,128]{3,2,1,0:T(8,128)(2,1)S(1)}, bf16[5,2,32,128]{3,2,1,0:T(8,128)(2,1)S(1)}, u32[]{:S(2)}, u32[]{:S(2)}) collective-permute-start(bf16[5,2,32,128]{3,2,1,0:T(8,128)(2,1)S(1)} %get-tuple-element.40), channel_id=1, source_target_pairs={{64,0},{128,64},{192,128},{0,192},{65,1},{129,65},{193,129},{1,193... | collective-permute-start | bytes 245768 | tf_op jit(solution)/shard_map/ppermute | solution.py:84
  31.9 9.7 %collective-permute-start.11 = (bf16[5,2,32,128]{3,2,1,0:T(8,128)(2,1)S(1)}, bf16[5,2,32,128]{3,2,1,0:T(8,128)(2,1)S(1)}, u32[]{:S(2)}, u32[]{:S(2)}) collective-permute-start(bf16[5,2,32,128]{3,2,1,0:T(8,128)(2,1)S(1)} %get-tuple-element.41), channel_id=1, source_target_pairs={{128,0},{192,64},{0,128},{64,192},{129,1},{193,65},{1,129},{65,193... | collective-permute-start | bytes 245768 | tf_op jit(solution)/shard_map/ppermute | solution.py:84
  32.0 9.6 %collective-permute-start.12 = (bf16[5,2,32,128]{3,2,1,0:T(8,128)(2,1)S(1)}, bf16[5,2,32,128]{3,2,1,0:T(8,128)(2,1)S(1)}, u32[]{:S(2)}, u32[]{:S(2)}) collective-permute-start(bf16[5,2,32,128]{3,2,1,0:T(8,128)(2,1)S(1)} %get-tuple-element.42), channel_id=1, source_target_pairs={{192,0},{0,64},{64,128},{128,192},{193,1},{1,65},{65,129},{129,193... | collective-permute-start | bytes 245768 | tf_op jit(solution)/shard_map/ppermute | solution.py:84
  35.4 14.2 %collective-permute-start.3 = (bf16[6,128,128]{2,1,0:T(8,128)(2,1)S(1)}, bf16[6,128,128]{2,1,0:T(8,128)(2,1)S(1)}, u32[]{:S(2)}, u32[]{:S(2)}) collective-permute-start(bf16[6,128,128]{2,1,0:T(8,128)(2,1)S(1)} %get-tuple-element.32), channel_id=1, source_target_pairs={{20,0},{84,64},{148,128},{212,192},{21,1},{85,65},{149,129},{213,1... | collective-permute-start | bytes 589832 | tf_op jit(solution)/shard_map/ppermute | solution.py:84
  38.5 22.9 %collective-permute-start.4 = (bf16[6,128,128]{2,1,0:T(8,128)(2,1)S(1)}, bf16[6,128,128]{2,1,0:T(8,128)(2,1)S(1)}, u32[]{:S(2)}, u32[]{:S(2)}) collective-permute-start(bf16[6,128,128]{2,1,0:T(8,128)(2,1)S(1)} %get-tuple-element.33), channel_id=1, source_target_pairs={{44,0},{108,64},{172,128},{236,192},{45,1},{109,65},{173,129},{237... | collective-permute-start | bytes 589832 | tf_op jit(solution)/shard_map/ppermute | solution.py:84
  41.7 25.0 %collective-permute-start.14 = (bf16[10,128,128]{2,1,0:T(8,128)(2,1)S(1)}, bf16[10,128,128]{2,1,0:T(8,128)(2,1)S(1)}, u32[]{:S(2)}, u32[]{:S(2)}) collective-permute-start(bf16[10,128,128]{2,1,0:T(8,128)(2,1)S(1)} %shard_map.32), channel_id=1, source_target_pairs={{40,0},{104,64},{168,128},{232,192},{41,1},{105,65},{169,129},{233... | collective-permute-start | bytes 983048 | tf_op jit(solution)/shard_map/ppermute | solution.py:84
  46.3 20.3 %collective-permute-start.13 = (bf16[10,128,128]{2,1,0:T(8,128)(2,1)S(1)}, bf16[10,128,128]{2,1,0:T(8,128)(2,1)S(1)}, u32[]{:S(2)}, u32[]{:S(2)}) collective-permute-start(bf16[10,128,128]{2,1,0:T(8,128)(2,1)S(1)} %shard_map.32), channel_id=1, source_target_pairs={{16,0},{80,64},{144,128},{208,192},{17,1},{81,65},{145,129},{209,1... | collective-permute-start | bytes 983048 | tf_op jit(solution)/shard_map/ppermute | solution.py:84
  61.5 18.6 %collective-permute-start.5 = (bf16[17,128,128]{2,1,0:T(8,128)(2,1)S(1)}, bf16[17,128,128]{2,1,0:T(8,128)(2,1)S(1)}, u32[]{:S(2)}, u32[]{:S(2)}) collective-permute-start(bf16[17,128,128]{2,1,0:T(8,128)(2,1)S(1)} %get-tuple-element.34), channel_id=1, source_target_pairs={{255,0},{0,64},{64,128},{128,192},{192,1},{1,65},{65,129},{129,193... | collective-permute-start | bytes 1671176 | tf_op jit(solution)/shard_map/ppermute | solution.py:84
  61.6 18.5 %collective-permute-start.6 = (bf16[17,128,128]{2,1,0:T(8,128)(2,1)S(1)}, bf16[17,128,128]{2,1,0:T(8,128)(2,1)S(1)}, u32[]{:S(2)}, u32[]{:S(2)}) collective-permute-start(bf16[17,128,128]{2,1,0:T(8,128)(2,1)S(1)} %get-tuple-element.35), channel_id=1, source_target_pairs={{64,0},{128,64},{192,128},{1,192},{65,1},{129,65},{193,129},{2,193... | collective-permute-start | bytes 1671176 | tf_op jit(solution)/shard_map/ppermute | solution.py:84
  66.7 21.0 %collective-permute-start.15 = (bf16[12,128,128]{2,1,0:T(8,128)(2,1)S(1)}, bf16[12,128,128]{2,1,0:T(8,128)(2,1)S(1)}, u32[]{:S(2)}, u32[]{:S(2)}) collective-permute-start(bf16[12,128,128]{2,1,0:T(8,128)(2,1)S(1)} %get-tuple-element.43), channel_id=1, source_target_pairs={{255,0},{0,64},{64,128},{128,192},{192,1},{1,65},{65,129},{129,193... | collective-permute-start | bytes 1179656 | tf_op jit(solution)/shard_map/ppermute | solution.py:84
  67.0 20.7 %collective-permute-start.16 = (bf16[12,128,128]{2,1,0:T(8,128)(2,1)S(1)}, bf16[12,128,128]{2,1,0:T(8,128)(2,1)S(1)}, u32[]{:S(2)}, u32[]{:S(2)}) collective-permute-start(bf16[12,128,128]{2,1,0:T(8,128)(2,1)S(1)} %get-tuple-element.44), channel_id=1, source_target_pairs={{64,0},{128,64},{192,128},{1,192},{65,1},{129,65},{193,129},{2,193... | collective-permute-start | bytes 1179656 | tf_op jit(solution)/shard_map/ppermute | solution.py:84
  93.4 5.9 %collective-permute-start.17 = (bf16[13,2,32,128]{3,2,1,0:T(8,128)(2,1)S(1)}, bf16[13,2,32,128]{3,2,1,0:T(8,128)(2,1)S(1)}, u32[]{:S(2)}, u32[]{:S(2)}) collective-permute-start(bf16[13,2,32,128]{3,2,1,0:T(8,128)(2,1)S(1)} %get-tuple-element.46), channel_id=1, source_target_pairs={{64,0},{128,64},{192,128},{0,192},{65,1},{129,65},{193,129},{1,193... | collective-permute-start | bytes 638984 | tf_op jit(solution)/shard_map/ppermute | solution.py:84
  93.5 7.4 %collective-permute-start.18 = (bf16[13,2,32,128]{3,2,1,0:T(8,128)(2,1)S(1)}, bf16[13,2,32,128]{3,2,1,0:T(8,128)(2,1)S(1)}, u32[]{:S(2)}, u32[]{:S(2)}) collective-permute-start(bf16[13,2,32,128]{3,2,1,0:T(8,128)(2,1)S(1)} %get-tuple-element.47), channel_id=1, source_target_pairs={{128,0},{192,64},{0,128},{64,192},{129,1},{193,65},{1,129},{65,193... | collective-permute-start | bytes 638984 | tf_op jit(solution)/shard_map/ppermute | solution.py:84
  93.6 13.2 %collective-permute-start.19 = (bf16[13,2,32,128]{3,2,1,0:T(8,128)(2,1)S(1)}, bf16[13,2,32,128]{3,2,1,0:T(8,128)(2,1)S(1)}, u32[]{:S(2)}, u32[]{:S(2)}) collective-permute-start(bf16[13,2,32,128]{3,2,1,0:T(8,128)(2,1)S(1)} %get-tuple-element.48), channel_id=1, source_target_pairs={{192,0},{0,64},{64,128},{128,192},{193,1},{1,65},{65,129},{129,193... | collective-permute-start | bytes 638984 | tf_op jit(solution)/shard_map/ppermute | solution.py:84

commit v12 on v9

--- a/solution.py
+++ b/solution.py
@@ -124,7 +124,7 @@
             lambda _: pl.BlockSpec(memory_space=pltpu.VMEM), out_shape
         ),
         scratch_shapes=list(scratch),
-        compiler_params=pltpu.CompilerParams(vmem_limit_bytes=48 << 20),
+        compiler_params=pltpu.CompilerParams(vmem_limit_bytes=24 << 20),
         cost_estimate=pl.CostEstimate(
             flops=flops, bytes_accessed=traffic, transcendentals=0
         ),
@@ -207,49 +207,78 @@
     return found
 
 
-def purify_body(me_ref, presence_ref, *refs):
-    sources, outs = refs[: len(ARRIVE)], refs[len(ARRIVE) : len(ARRIVE) + LAYERS]
-    right_ref, left_ref, result_ref = refs[len(ARRIVE) + LAYERS :]
-    me = me_ref[0]
-    placed = placements()
-    zero = jnp.zeros((BS, BS), jnp.bfloat16)
-    for row in range(16):
-        for column in range(16):
-            where = (pl.ds(row * BS, BS), pl.ds(column * BS, BS))
-            if (row, column) in placed:
-                operand, index = placed[row, column]
-                right_ref[where] = sources[operand][index]
-            else:
-                right_ref[where] = zero
-    targets = {
+NEAR_SOURCES = 5
+
+
+def targets():
+    return {
         (i, SLOT[(i + offset) % NBG]): d
         for i in range(2)
         for d, offset in enumerate(OFFSETS)
     }
+
+
+def fill_right(out_ref, sources, first, rows):
+    placed = placements()
+    for row in rows:
+        for column in range(16):
+            where = (pl.ds((row - rows[0]) * BS, BS), pl.ds(column * BS, BS))
+            if (row, column) in placed:
+                operand, index = placed[row, column]
+                out_ref[where] = sources[operand - first][index]
+            else:
+                out_ref[where] = jnp.zeros((BS, BS), jnp.bfloat16)
+
+
+def fill_left(out_ref, own_ref, columns):
     for i in range(2):
-        for column in range(16):
-            where = (pl.ds(i * BS, BS), pl.ds(column * BS, BS))
-            d = targets.get((i, column))
-            left_ref[where] = zero if d is None else sources[0][d, i]
-
-    def dot(left, right):
-        return jnp.dot(left, right, preferred_element_type=jnp.float32)
-
-    def product(columns):
+        for column in columns:
+            where = (pl.ds(i * BS, BS), pl.ds((column - columns[0]) * BS, BS))
+            d = targets().get((i, column))
+            if d is None:
+                out_ref[where] = jnp.zeros((BS, BS), jnp.bfloat16)
+            else:
+                out_ref[where] = own_ref[d, i]
+
+
+def dot(left, right):
+    return jnp.dot(left, right, preferred_element_type=jnp.float32)
+
+
+def near_product_body(*refs):
+    sources, (right_ref, partial_ref, left_ref) = refs[:NEAR_SOURCES], refs[NEAR_SOURCES:]
+    fill_right(right_ref, sources, 0, range(8))
+    fill_left(left_ref, sources[0], range(8))
+    for column in range(0, 16, 2):
+        wide = pl.ds(column * BS, 2 * BS)
+        partial_ref[:, wide] = dot(left_ref[...], right_ref[:, wide])
+
+
+def purify_body(me_ref, presence_ref, own_ref, right_near_ref, partial_ref, *refs):
+    fars = len(ARRIVE) - NEAR_SOURCES
+    sources, outs = refs[:fars], refs[fars : fars + LAYERS]
+    right_ref, left_ref, result_ref = refs[fars + LAYERS :]
+    me = me_ref[0]
+    fill_right(right_ref, sources, NEAR_SOURCES, range(8, 16))
+    fill_left(left_ref, own_ref, range(16))
+
+    def far_product(columns):
         start = columns[0] * BS
         wide = pl.ds(start, len(columns) * BS)
         if start < NEAR_END:
-            return dot(left_ref[...], right_ref[:, wide])
+            return dot(left_ref[:, NEAR_END:], right_ref[:, wide])
         if start < PLUS_END:
-            return dot(left_ref[:, :PLUS_END], right_ref[:PLUS_END, wide])
-        return dot(left_ref[:, :NEAR_END], right_ref[:NEAR_END, wide]) + dot(
-            left_ref[:, PLUS_END:], right_ref[PLUS_END:, wide]
-        )
+            return dot(left_ref[:, NEAR_END:PLUS_END], right_ref[: PLUS_END - NEAR_END, wide])
+        return dot(left_ref[:, PLUS_END:], right_ref[PLUS_END - NEAR_END :, wide])
+
+    def near_product(columns):
+        wide = pl.ds(columns[0] * BS, len(columns) * BS)
+        return dot(left_ref[:, :NEAR_END], right_near_ref[:, wide])
 
     def each(columns, total, use):
         for at, column in enumerate(columns):
             for i in range(2):
-                d = targets.get((i, column))
+                d = targets().get((i, column))
                 if d is not None:
                     tile = total[i * BS : (i + 1) * BS, at * BS : (at + 1) * BS]
                     use(i, column, d, presence_ref[d, 2 * me + i] != 0, tile)
@@ -261,8 +290,9 @@
         result_ref[d, i] = second
 
     for columns in groups:
-        each(columns, product(columns), keep_second)
-    for (i, column), d in targets.items():
+        partial = partial_ref[:, pl.ds(columns[0] * BS, len(columns) * BS)]
+        each(columns, partial + far_product(columns), keep_second)
+    for (i, column), d in targets().items():
         left_ref[pl.ds(i * BS, BS), pl.ds(column * BS, BS)] = result_ref[d, i]
 
     def keep_result(i, column, d, present, tile):
@@ -271,7 +301,7 @@
         result_ref[d, i] = (3.0 * second - 2.0 * third).astype(jnp.bfloat16)
 
     for columns in groups:
-        each(columns, product(columns), keep_result)
+        each(columns, near_product(columns) + far_product(columns), keep_result)
     for s, out_ref in enumerate(outs):
         other = lax.rem(me - s + LAYERS, LAYERS)
         start = pl.multiple_of(other * (BS // LAYERS), BS // LAYERS)
@@ -332,18 +362,26 @@
         edge_body, packed([EDGE_LOW, EDGE_HIGH]), 0, len(arrived)
     )(*arrived)
     edge_low, edge_high = from_pair(edge_low, -1), from_pair(edge_high, 1)
+    near = [own, low, high, lower, higher]
+    right, partial = call(
+        near_product_body,
+        [bf16(NEAR_END, WIDTH), jax.ShapeDtypeStruct((2 * BS, WIDTH), jnp.float32)],
+        0,
+        len(near),
+        scratch=[pltpu.VMEM((2 * BS, NEAR_END), jnp.bfloat16)],
+    )(*near)
     results = call(
         purify_body,
         [quarter] * LAYERS,
         2,
-        len(ARRIVE),
+        3 + len(ARRIVE) - NEAR_SOURCES,
         scratch=[
-            pltpu.VMEM((WIDTH, WIDTH), jnp.bfloat16),
+            pltpu.VMEM((WIDTH - NEAR_END, WIDTH), jnp.bfloat16),
             pltpu.VMEM((2 * BS, WIDTH), jnp.bfloat16),
             pltpu.VMEM((DIAGS, 2, BS, BS), jnp.bfloat16),
         ],
-        flops=4 * 224 * 2 * BS**3,
-    )(me, presence, own, low, high, lower, higher, *arrived, edge_low, edge_high)
+        flops=4 * 160 * 2 * BS**3,
+    )(me, presence, own, right, partial, *arrived, edge_low, edge_high)
     results = exchanged(results)
     return call(join_body, bf16(DIAGS, 2 * LAYERS, BS // LAYERS, BS), 1, LAYERS)(
         me, *results

time: 103 us -> 101 us (0.981)
  waiting for transfers between devices: 41.4 us -> 39.1 us
    ppermute x20, waiting for transfers between devices: 41.4 us -> 39.1 us  [moved(): return lax.ppermute(x, AXES, route)]
    pallas_call x1 -> x2, Pallas kernels: 5.76 us -> 6.18 us  [the longest x1 4.3 us: per_device(): call(purify_body, [quarter] * LAYERS, 2, 3 + len(ARRIVE) - NEAR_SOURCES,...]
  transfers between devices with their start and end apart: 20 -> 20, of which waited for: 12 -> 12; matrix products, arithmetic and copies ran while one was open for 0% -> 0% of each run, Pallas kernels for 0% -> 2%
where the time goes in v12:
time: 101 us
  starting transfers between devices  51.4 us (51%)
  waiting for transfers between devices  39.1 us (39%)
  Pallas kernels  8.38 us (8%)
  local copies, waits for them, and re-layouts  1.92 us (2%)
    ppermute x20, starting transfers between devices, moved(): return lax.ppermute(x, AXES, route)  51.4 us
    ppermute x20, waiting for transfers between devices, moved(): return lax.ppermute(x, AXES, route)  39.1 us
    pallas_call x1, Pallas kernels, per_device(): call(purify_body, [quarter] * LAYERS, 2, 3 + len(ARRIVE) - NEAR_SOURCES,...  4.3 us
  transfers between devices with their start and end apart: 20, of which 12 were waited for; matrix products, arithmetic and copies ran while one was open for 0% of the time, Pallas kernels for 2%

profile of v12, /device:TPU:56, one launch (start us, length us, event | category | flops | bytes accessed | tf_op | source)
XLA Modules:
  0.0 100.9 jit_solution(13271468854161388144)
XLA Ops:
  0.0 0.8 copy.4.presence_ref
  0.8 0.0 copy-start
  0.8 1.2 %copy-done = bf16[13,8,32,128]{3,2,1,0:T(8,128)(2,1)S(1)} copy-done((bf16[13,8,32,128]{3,2,1,0:T(8,128)(2,1)S(1)}, bf16[13,8,32,128]{3,2,1,0:T(8,128)(2,1)}, u32[]{:S(2)}) %copy-start) | copy-done | bytes 851992
  1.9 0.9 shard_map.28
  2.9 6.4 %collective-permute-start.3 = (bf16[5,8,32,128]{3,2,1,0:T(8,128)(2,1)S(1)}, bf16[5,8,32,128]{3,2,1,0:T(8,128)(2,1)S(1)}, u32[]{:S(2)}, u32[]{:S(2)}) collective-permute-start(bf16[5,8,32,128]{3,2,1,0:T(8,128)(2,1)S(1)} %get-tuple-element.34), channel_id=1, source_target_pairs={{4,0},{68,64},{132,128},{196,192},{5,1},{69,65},{133,129},{197,193... | collective-permute-start | bytes 983048 | tf_op jit(solution)/shard_map/ppermute | solution.py:84
  9.3 2.8 %collective-permute-start = (bf16[13,2,32,128]{3,2,1,0:T(8,128)(2,1)S(1)}, bf16[13,2,32,128]{3,2,1,0:T(8,128)(2,1)S(1)}, u32[]{:S(2)}, u32[]{:S(2)}) collective-permute-start(bf16[13,2,32,128]{3,2,1,0:T(8,128)(2,1)S(1)} %get-tuple-element.30), channel_id=1, source_target_pairs={{64,0},{128,64},{192,128},{0,192},{65,1},{129,65},{193,129},{1,193... | collective-permute-start | bytes 638984 | tf_op jit(solution)/shard_map/ppermute | solution.py:84
  12.0 0.8 collective-permute-start.1
  12.8 0.9 collective-permute-start.2
  13.7 7.1 %collective-permute-done.refs_1_ = bf16[13,2,32,128]{3,2,1,0:T(8,128)(2,1)S(1)} collective-permute-done((bf16[13,2,32,128]{3,2,1,0:T(8,128)(2,1)S(1)}, bf16[13,2,32,128]{3,2,1,0:T(8,128)(2,1)S(1)}, u32[]{:S(2)}, u32[]{:S(2)}) %collective-permute-start) | collective-permute-done | bytes 213024 | tf_op jit(solution)/shard_map/ppermute | solution.py:84
  20.8 0.9 collective-permute-done.1.refs_2_
  21.8 2.8 %collective-permute-done.2.refs_3_ = bf16[13,2,32,128]{3,2,1,0:T(8,128)(2,1)S(1)} collective-permute-done((bf16[13,2,32,128]{3,2,1,0:T(8,128)(2,1)S(1)}, bf16[13,2,32,128]{3,2,1,0:T(8,128)(2,1)S(1)}, u32[]{:S(2)}, u32[]{:S(2)}) %collective-permute-start.2) | collective-permute-done | bytes 213024 | tf_op jit(solution)/shard_map/ppermute | solution.py:84
  24.5 0.1 shard_map.29
  24.6 0.0 collective-permute-done.3.shared_ref
  24.7 2.3 %collective-permute-start.4 = (bf16[5,2,32,128]{3,2,1,0:T(8,128)(2,1)S(1)}, bf16[5,2,32,128]{3,2,1,0:T(8,128)(2,1)S(1)}, u32[]{:S(2)}, u32[]{:S(2)}) collective-permute-start(bf16[5,2,32,128]{3,2,1,0:T(8,128)(2,1)S(1)} %get-tuple-element.36), channel_id=1, source_target_pairs={{64,0},{128,64},{192,128},{0,192},{65,1},{129,65},{193,129},{1,193... | collective-permute-start | bytes 245768 | tf_op jit(solution)/shard_map/ppermute | solution.py:84
  26.9 0.8 collective-permute-start.5
  27.7 0.9 collective-permute-start.6
  28.6 3.3 %collective-permute-start.11 = (bf16[6,128,128]{2,1,0:T(8,128)(2,1)S(1)}, bf16[6,128,128]{2,1,0:T(8,128)(2,1)S(1)}, u32[]{:S(2)}, u32[]{:S(2)}) collective-permute-start(bf16[6,128,128]{2,1,0:T(8,128)(2,1)S(1)} %get-tuple-element.45), channel_id=1, source_target_pairs={{20,0},{84,64},{148,128},{212,192},{21,1},{85,65},{149,129},{213,1... | collective-permute-start | bytes 589832 | tf_op jit(solution)/shard_map/ppermute | solution.py:84
  31.9 2.1 %collective-permute-start.7 = (bf16[4,128,128]{2,1,0:T(8,128)(2,1)S(1)}, bf16[4,128,128]{2,1,0:T(8,128)(2,1)S(1)}, u32[]{:S(2)}, u32[]{:S(2)}) collective-permute-start(bf16[4,128,128]{2,1,0:T(8,128)(2,1)S(1)} %get-tuple-element.39), channel_id=1, source_target_pairs={{191,0},{255,64},{0,128},{64,192},{128,1},{192,65},{1,129},{65,193... | collective-permute-start | bytes 393224 | tf_op jit(solution)/shard_map/ppermute | solution.py:84
  34.0 0.0 collective-permute-done.4.refs_1_
  34.0 0.0 collective-permute-done.5.refs_2_
  34.0 0.0 collective-permute-done.6.refs_3_
  34.1 0.5 collective-permute-start.13
  34.6 4.1 %collective-permute-start.14 = (bf16[10,128,128]{2,1,0:T(8,128)(2,1)S(1)}, bf16[10,128,128]{2,1,0:T(8,128)(2,1)S(1)}, u32[]{:S(2)}, u32[]{:S(2)}) collective-permute-start(bf16[10,128,128]{2,1,0:T(8,128)(2,1)S(1)} %shard_map.31.refs_0_), channel_id=1, source_target_pairs={{40,0},{104,64},{168,128},{232,192},{41,1},{105,65},{169,129},{233... | collective-permute-start | bytes 983048 | tf_op jit(solution)/shard_map/ppermute | solution.py:84
  38.7 2.6 %collective-permute-start.8 = (bf16[4,128,128]{2,1,0:T(8,128)(2,1)S(1)}, bf16[4,128,128]{2,1,0:T(8,128)(2,1)S(1)}, u32[]{:S(2)}, u32[]{:S(2)}) collective-permute-start(bf16[4,128,128]{2,1,0:T(8,128)(2,1)S(1)} %get-tuple-element.40), channel_id=1, source_target_pairs={{128,0},{192,64},{1,128},{65,192},{129,1},{193,65},{2,129},{66,193... | collective-permute-start | bytes 393224 | tf_op jit(solution)/shard_map/ppermute | solution.py:84
  41.3 1.7 %collective-permute-done.7.refs_1_.refs_3_ = bf16[4,128,128]{2,1,0:T(8,128)(2,1)S(1)} collective-permute-done((bf16[4,128,128]{2,1,0:T(8,128)(2,1)S(1)}, bf16[4,128,128]{2,1,0:T(8,128)(2,1)S(1)}, u32[]{:S(2)}, u32[]{:S(2)}) %collective-permute-start.7) | collective-permute-done | bytes 131104 | tf_op jit(solution)/shard_map/ppermute | solution.py:84
  43.0 7.9 %collective-permute-start.12 = (bf16[6,128,128]{2,1,0:T(8,128)(2,1)S(1)}, bf16[6,128,128]{2,1,0:T(8,128)(2,1)S(1)}, u32[]{:S(2)}, u32[]{:S(2)}) collective-permute-start(bf16[6,128,128]{2,1,0:T(8,128)(2,1)S(1)} %get-tuple-element.46), channel_id=1, source_target_pairs={{44,0},{108,64},{172,128},{236,192},{45,1},{109,65},{173,129},{237... | collective-permute-start | bytes 589832 | tf_op jit(solution)/shard_map/ppermute | solution.py:84
  50.9 0.0 collective-permute-done.8.refs_2_.refs_4_
  50.9 0.1 shard_map.32
  51.0 0.1 collective-permute-start.9
  51.1 0.0 collective-permute-done.11.refs_0_
  51.1 4.1 %collective-permute-start.10 = (bf16[17,128,128]{2,1,0:T(8,128)(2,1)S(1)}, bf16[17,128,128]{2,1,0:T(8,128)(2,1)S(1)}, u32[]{:S(2)}, u32[]{:S(2)}) collective-permute-start(bf16[17,128,128]{2,1,0:T(8,128)(2,1)S(1)} %get-tuple-element.42), channel_id=1, source_target_pairs={{64,0},{128,64},{192,128},{1,192},{65,1},{129,65},{193,129},{2,193... | collective-permute-start | bytes 1671176 | tf_op jit(solution)/shard_map/ppermute | solution.py:84
  55.2 4.1 %collective-permute-done.12.refs_1_ = bf16[6,128,128]{2,1,0:T(8,128)(2,1)S(1)} collective-permute-done((bf16[6,128,128]{2,1,0:T(8,128)(2,1)S(1)}, bf16[6,128,128]{2,1,0:T(8,128)(2,1)S(1)}, u32[]{:S(2)}, u32[]{:S(2)}) %collective-permute-start.12) | collective-permute-done | bytes 196640 | tf_op jit(solution)/shard_map/ppermute | solution.py:84
  59.3 0.0 collective-permute-done.13.refs_2_
  59.3 0.0 collective-permute-done.14.refs_3_
  59.3 0.1 shard_map.34
  59.3 5.0 %collective-permute-start.15 = (bf16[12,128,128]{2,1,0:T(8,128)(2,1)S(1)}, bf16[12,128,128]{2,1,0:T(8,128)(2,1)S(1)}, u32[]{:S(2)}, u32[]{:S(2)}) collective-permute-start(bf16[12,128,128]{2,1,0:T(8,128)(2,1)S(1)} %get-tuple-element.47), channel_id=1, source_target_pairs={{255,0},{0,64},{64,128},{128,192},{192,1},{1,65},{65,129},{129,193... | collective-permute-start | bytes 1179656 | tf_op jit(solution)/shard_map/ppermute | solution.py:84
  64.3 0.0 collective-permute-start.16
  64.3 4.7 %collective-permute-done.9.refs_1_ = bf16[17,128,128]{2,1,0:T(8,128)(2,1)S(1)} collective-permute-done((bf16[17,128,128]{2,1,0:T(8,128)(2,1)S(1)}, bf16[17,128,128]{2,1,0:T(8,128)(2,1)S(1)}, u32[]{:S(2)}, u32[]{:S(2)}) %collective-permute-start.9) | collective-permute-done | bytes 557088 | tf_op jit(solution)/shard_map/ppermute | solution.py:84
  69.1 2.4 %collective-permute-done.10.refs_2_ = bf16[17,128,128]{2,1,0:T(8,128)(2,1)S(1)} collective-permute-done((bf16[17,128,128]{2,1,0:T(8,128)(2,1)S(1)}, bf16[17,128,128]{2,1,0:T(8,128)(2,1)S(1)}, u32[]{:S(2)}, u32[]{:S(2)}) %collective-permute-start.10) | collective-permute-done | bytes 557088 | tf_op jit(solution)/shard_map/ppermute | solution.py:84
  71.4 1.9 %shard_map.33 = (bf16[1024,2048]{1,0:T(8,128)(2,1)S(1)}, f32[256,2048]{1,0:T(8,128)S(1)}) custom-call(bf16[13,2,128,128]{3,2,1,0:T(8,128)(2,1)S(1)} %get-tuple-element.33.out_refs_0_.own_ref.refs_0_, bf16[17,128,128]{2,1,0:T(8,128)(2,1)S(1)} %collective-permute-done.9.refs_1_, bf16[17,128,128]{2,1,0:T(8,128)(2,1)S(1)} %collective-permute-done.10.refs_2_, ...), custom_call_target="tpu_custom_call" | custom-call | bytes 4194304 | tf_op jit(solution)/shard_map/pallas_call | solution.py:366
  73.3 2.7 %collective-permute-done.15.refs_4_ = bf16[12,128,128]{2,1,0:T(8,128)(2,1)S(1)} collective-permute-done((bf16[12,128,128]{2,1,0:T(8,128)(2,1)S(1)}, bf16[12,128,128]{2,1,0:T(8,128)(2,1)S(1)}, u32[]{:S(2)}, u32[]{:S(2)}) %collective-permute-start.15) | collective-permute-done | bytes 393248 | tf_op jit(solution)/shard_map/ppermute | solution.py:84
  76.0 1.2 %collective-permute-done.16.refs_5_ = bf16[12,128,128]{2,1,0:T(8,128)(2,1)S(1)} collective-permute-done((bf16[12,128,128]{2,1,0:T(8,128)(2,1)S(1)}, bf16[12,128,128]{2,1,0:T(8,128)(2,1)S(1)}, u32[]{:S(2)}, u32[]{:S(2)}) %collective-permute-start.16) | collective-permute-done | bytes 393248 | tf_op jit(solution)/shard_map/ppermute | solution.py:84
  77.2 4.3 %shard_map.35 = (bf16[13,2,32,128]{3,2,1,0:T(8,128)(2,1)S(1)}, bf16[13,2,32,128]{3,2,1,0:T(8,128)(2,1)S(1)}, bf16[13,2,32,128]{3,2,1,0:T(8,128)(2,1)S(1)}, bf16[13,2,32,128]{3,2,1,0:T(8,128)(2,1)S(1)}) custom-call(s32[1]{0:T(128)} %bitcast.me_ref, s32[13,8]{1,0:T(8,128)S(1)} %copy.4.presence_ref, ...), custom_call_target="tpu_custom_call" | custom-call | flops 2684354560 | bytes 4194304 | tf_op jit(solution)/shard_map/pallas_call | solution.py:373
  81.5 5.9 %collective-permute-start.17 = (bf16[13,2,32,128]{3,2,1,0:T(8,128)(2,1)S(1)}, bf16[13,2,32,128]{3,2,1,0:T(8,128)(2,1)S(1)}, u32[]{:S(2)}, u32[]{:S(2)}) collective-permute-start(bf16[13,2,32,128]{3,2,1,0:T(8,128)(2,1)S(1)} %get-tuple-element.50), channel_id=1, source_target_pairs={{64,0},{128,64},{192,128},{0,192},{65,1},{129,65},{193,129},{1,193... | collective-permute-start | bytes 638984 | tf_op jit(solution)/shard_map/ppermute | solution.py:84
  87.4 0.0 collective-permute-start.18
  87.4 1.0 collective-permute-start.19
  88.3 8.2 %collective-permute-done.17.refs_1_ = bf16[13,2,32,128]{3,2,1,0:T(8,128)(2,1)S(1)} collective-permute-done((bf16[13,2,32,128]{3,2,1,0:T(8,128)(2,1)S(1)}, bf16[13,2,32,128]{3,2,1,0:T(8,128)(2,1)S(1)}, u32[]{:S(2)}, u32[]{:S(2)}) %collective-permute-start.17) | collective-permute-done | bytes 213024 | tf_op jit(solution)/shard_map/ppermute | solution.py:84
  96.5 0.6 collective-permute-done.18.refs_2_
  97.1 2.8 %collective-permute-done.19.refs_3_ = bf16[13,2,32,128]{3,2,1,0:T(8,128)(2,1)S(1)} collective-permute-done((bf16[13,2,32,128]{3,2,1,0:T(8,128)(2,1)S(1)}, bf16[13,2,32,128]{3,2,1,0:T(8,128)(2,1)S(1)}, u32[]{:S(2)}, u32[]{:S(2)}) %collective-permute-start.19) | collective-permute-done | bytes 213024 | tf_op jit(solution)/shard_map/ppermute | solution.py:84
  99.9 1.0 shard_map.36
  (2 shorter events, 0.1 us)
Async XLA Ops:
  0.8 1.2 %copy-start = (bf16[13,8,32,128]{3,2,1,0:T(8,128)(2,1)S(1)}, bf16[13,8,32,128]{3,2,1,0:T(8,128)(2,1)}, u32[]{:S(2)}) copy-start(bf16[13,8,32,128]{3,2,1,0:T(8,128)(2,1)} %blocks_ref.1) | copy-start | bytes 2555908
  2.9 21.8 %collective-permute-start.3 = (bf16[5,8,32,128]{3,2,1,0:T(8,128)(2,1)S(1)}, bf16[5,8,32,128]{3,2,1,0:T(8,128)(2,1)S(1)}, u32[]{:S(2)}, u32[]{:S(2)}) collective-permute-start(bf16[5,8,32,128]{3,2,1,0:T(8,128)(2,1)S(1)} %get-tuple-element.34), channel_id=1, source_target_pairs={{4,0},{68,64},{132,128},{196,192},{5,1},{69,65},{133,129},{197,193... | collective-permute-start | bytes 983048 | tf_op jit(solution)/shard_map/ppermute | solution.py:84
  9.3 11.6 %collective-permute-start = (bf16[13,2,32,128]{3,2,1,0:T(8,128)(2,1)S(1)}, bf16[13,2,32,128]{3,2,1,0:T(8,128)(2,1)S(1)}, u32[]{:S(2)}, u32[]{:S(2)}) collective-permute-start(bf16[13,2,32,128]{3,2,1,0:T(8,128)(2,1)S(1)} %get-tuple-element.30), channel_id=1, source_target_pairs={{64,0},{128,64},{192,128},{0,192},{65,1},{129,65},{193,129},{1,193... | collective-permute-start | bytes 638984 | tf_op jit(solution)/shard_map/ppermute | solution.py:84
  12.0 9.7 %collective-permute-start.1 = (bf16[13,2,32,128]{3,2,1,0:T(8,128)(2,1)S(1)}, bf16[13,2,32,128]{3,2,1,0:T(8,128)(2,1)S(1)}, u32[]{:S(2)}, u32[]{:S(2)}) collective-permute-start(bf16[13,2,32,128]{3,2,1,0:T(8,128)(2,1)S(1)} %get-tuple-element.31), channel_id=1, source_target_pairs={{128,0},{192,64},{0,128},{64,192},{129,1},{193,65},{1,129},{65,193... | collective-permute-start | bytes 638984 | tf_op jit(solution)/shard_map/ppermute | solution.py:84
  12.8 11.7 %collective-permute-start.2 = (bf16[13,2,32,128]{3,2,1,0:T(8,128)(2,1)S(1)}, bf16[13,2,32,128]{3,2,1,0:T(8,128)(2,1)S(1)}, u32[]{:S(2)}, u32[]{:S(2)}) collective-permute-start(bf16[13,2,32,128]{3,2,1,0:T(8,128)(2,1)S(1)} %get-tuple-element.32), channel_id=1, source_target_pairs={{192,0},{0,64},{64,128},{128,192},{193,1},{1,65},{65,129},{129,193... | collective-permute-start | bytes 638984 | tf_op jit(solution)/shard_map/ppermute | solution.py:84
  24.7 9.3 %collective-permute-start.4 = (bf16[5,2,32,128]{3,2,1,0:T(8,128)(2,1)S(1)}, bf16[5,2,32,128]{3,2,1,0:T(8,128)(2,1)S(1)}, u32[]{:S(2)}, u32[]{:S(2)}) collective-permute-start(bf16[5,2,32,128]{3,2,1,0:T(8,128)(2,1)S(1)} %get-tuple-element.36), channel_id=1, source_target_pairs={{64,0},{128,64},{192,128},{0,192},{65,1},{129,65},{193,129},{1,193... | collective-permute-start | bytes 245768 | tf_op jit(solution)/shard_map/ppermute | solution.py:84
  26.9 7.1 %collective-permute-start.5 = (bf16[5,2,32,128]{3,2,1,0:T(8,128)(2,1)S(1)}, bf16[5,2,32,128]{3,2,1,0:T(8,128)(2,1)S(1)}, u32[]{:S(2)}, u32[]{:S(2)}) collective-permute-start(bf16[5,2,32,128]{3,2,1,0:T(8,128)(2,1)S(1)} %get-tuple-element.37), channel_id=1, source_target_pairs={{128,0},{192,64},{0,128},{64,192},{129,1},{193,65},{1,129},{65,193... | collective-permute-start | bytes 245768 | tf_op jit(solution)/shard_map/ppermute | solution.py:84
  27.7 6.3 %collective-permute-start.6 = (bf16[5,2,32,128]{3,2,1,0:T(8,128)(2,1)S(1)}, bf16[5,2,32,128]{3,2,1,0:T(8,128)(2,1)S(1)}, u32[]{:S(2)}, u32[]{:S(2)}) collective-permute-start(bf16[5,2,32,128]{3,2,1,0:T(8,128)(2,1)S(1)} %get-tuple-element.38), channel_id=1, source_target_pairs={{192,0},{0,64},{64,128},{128,192},{193,1},{1,65},{65,129},{129,193... | collective-permute-start | bytes 245768 | tf_op jit(solution)/shard_map/ppermute | solution.py:84
  28.6 22.4 %collective-permute-start.11 = (bf16[6,128,128]{2,1,0:T(8,128)(2,1)S(1)}, bf16[6,128,128]{2,1,0:T(8,128)(2,1)S(1)}, u32[]{:S(2)}, u32[]{:S(2)}) collective-permute-start(bf16[6,128,128]{2,1,0:T(8,128)(2,1)S(1)} %get-tuple-element.45), channel_id=1, source_target_pairs={{20,0},{84,64},{148,128},{212,192},{21,1},{85,65},{149,129},{213,1... | collective-permute-start | bytes 589832 | tf_op jit(solution)/shard_map/ppermute | solution.py:84
  31.9 11.1 %collective-permute-start.7 = (bf16[4,128,128]{2,1,0:T(8,128)(2,1)S(1)}, bf16[4,128,128]{2,1,0:T(8,128)(2,1)S(1)}, u32[]{:S(2)}, u32[]{:S(2)}) collective-permute-start(bf16[4,128,128]{2,1,0:T(8,128)(2,1)S(1)} %get-tuple-element.39), channel_id=1, source_target_pairs={{191,0},{255,64},{0,128},{64,192},{128,1},{192,65},{1,129},{65,193... | collective-permute-start | bytes 393224 | tf_op jit(solution)/shard_map/ppermute | solution.py:84
  34.1 25.2 %collective-permute-start.13 = (bf16[10,128,128]{2,1,0:T(8,128)(2,1)S(1)}, bf16[10,128,128]{2,1,0:T(8,128)(2,1)S(1)}, u32[]{:S(2)}, u32[]{:S(2)}) collective-permute-start(bf16[10,128,128]{2,1,0:T(8,128)(2,1)S(1)} %shard_map.31.refs_0_), channel_id=1, source_target_pairs={{16,0},{80,64},{144,128},{208,192},{17,1},{81,65},{145,129},{209,1... | collective-permute-start | bytes 983048 | tf_op jit(solution)/shard_map/ppermute | solution.py:84
  34.6 24.7 %collective-permute-start.14 = (bf16[10,128,128]{2,1,0:T(8,128)(2,1)S(1)}, bf16[10,128,128]{2,1,0:T(8,128)(2,1)S(1)}, u32[]{:S(2)}, u32[]{:S(2)}) collective-permute-start(bf16[10,128,128]{2,1,0:T(8,128)(2,1)S(1)} %shard_map.31.refs_0_), channel_id=1, source_target_pairs={{40,0},{104,64},{168,128},{232,192},{41,1},{105,65},{169,129},{233... | collective-permute-start | bytes 983048 | tf_op jit(solution)/shard_map/ppermute | solution.py:84
  38.7 12.2 %collective-permute-start.8 = (bf16[4,128,128]{2,1,0:T(8,128)(2,1)S(1)}, bf16[4,128,128]{2,1,0:T(8,128)(2,1)S(1)}, u32[]{:S(2)}, u32[]{:S(2)}) collective-permute-start(bf16[4,128,128]{2,1,0:T(8,128)(2,1)S(1)} %get-tuple-element.40), channel_id=1, source_target_pairs={{128,0},{192,64},{1,128},{65,192},{129,1},{193,65},{2,129},{66,193... | collective-permute-start | bytes 393224 | tf_op jit(solution)/shard_map/ppermute | solution.py:84
  43.0 16.3 %collective-permute-start.12 = (bf16[6,128,128]{2,1,0:T(8,128)(2,1)S(1)}, bf16[6,128,128]{2,1,0:T(8,128)(2,1)S(1)}, u32[]{:S(2)}, u32[]{:S(2)}) collective-permute-start(bf16[6,128,128]{2,1,0:T(8,128)(2,1)S(1)} %get-tuple-element.46), channel_id=1, source_target_pairs={{44,0},{108,64},{172,128},{236,192},{45,1},{109,65},{173,129},{237... | collective-permute-start | bytes 589832 | tf_op jit(solution)/shard_map/ppermute | solution.py:84
  51.0 18.1 %collective-permute-start.9 = (bf16[17,128,128]{2,1,0:T(8,128)(2,1)S(1)}, bf16[17,128,128]{2,1,0:T(8,128)(2,1)S(1)}, u32[]{:S(2)}, u32[]{:S(2)}) collective-permute-start(bf16[17,128,128]{2,1,0:T(8,128)(2,1)S(1)} %get-tuple-element.41), channel_id=1, source_target_pairs={{255,0},{0,64},{64,128},{128,192},{192,1},{1,65},{65,129},{129,193... | collective-permute-start | bytes 1671176 | tf_op jit(solution)/shard_map/ppermute | solution.py:84
  51.1 20.4 %collective-permute-start.10 = (bf16[17,128,128]{2,1,0:T(8,128)(2,1)S(1)}, bf16[17,128,128]{2,1,0:T(8,128)(2,1)S(1)}, u32[]{:S(2)}, u32[]{:S(2)}) collective-permute-start(bf16[17,128,128]{2,1,0:T(8,128)(2,1)S(1)} %get-tuple-element.42), channel_id=1, source_target_pairs={{64,0},{128,64},{192,128},{1,192},{65,1},{129,65},{193,129},{2,193... | collective-permute-start | bytes 1671176 | tf_op jit(solution)/shard_map/ppermute | solution.py:84
  59.3 16.6 %collective-permute-start.15 = (bf16[12,128,128]{2,1,0:T(8,128)(2,1)S(1)}, bf16[12,128,128]{2,1,0:T(8,128)(2,1)S(1)}, u32[]{:S(2)}, u32[]{:S(2)}) collective-permute-start(bf16[12,128,128]{2,1,0:T(8,128)(2,1)S(1)} %get-tuple-element.47), channel_id=1, source_target_pairs={{255,0},{0,64},{64,128},{128,192},{192,1},{1,65},{65,129},{129,193... | collective-permute-start | bytes 1179656 | tf_op jit(solution)/shard_map/ppermute | solution.py:84
  64.3 12.9 %collective-permute-start.16 = (bf16[12,128,128]{2,1,0:T(8,128)(2,1)S(1)}, bf16[12,128,128]{2,1,0:T(8,128)(2,1)S(1)}, u32[]{:S(2)}, u32[]{:S(2)}) collective-permute-start(bf16[12,128,128]{2,1,0:T(8,128)(2,1)S(1)} %get-tuple-element.48), channel_id=1, source_target_pairs={{64,0},{128,64},{192,128},{1,192},{65,1},{129,65},{193,129},{2,193... | collective-permute-start | bytes 1179656 | tf_op jit(solution)/shard_map/ppermute | solution.py:84
  81.5 15.0 %collective-permute-start.17 = (bf16[13,2,32,128]{3,2,1,0:T(8,128)(2,1)S(1)}, bf16[13,2,32,128]{3,2,1,0:T(8,128)(2,1)S(1)}, u32[]{:S(2)}, u32[]{:S(2)}) collective-permute-start(bf16[13,2,32,128]{3,2,1,0:T(8,128)(2,1)S(1)} %get-tuple-element.50), channel_id=1, source_target_pairs={{64,0},{128,64},{192,128},{0,192},{65,1},{129,65},{193,129},{1,193... | collective-permute-start | bytes 638984 | tf_op jit(solution)/shard_map/ppermute | solution.py:84
  87.4 9.7 %collective-permute-start.18 = (bf16[13,2,32,128]{3,2,1,0:T(8,128)(2,1)S(1)}, bf16[13,2,32,128]{3,2,1,0:T(8,128)(2,1)S(1)}, u32[]{:S(2)}, u32[]{:S(2)}) collective-permute-start(bf16[13,2,32,128]{3,2,1,0:T(8,128)(2,1)S(1)} %get-tuple-element.51), channel_id=1, source_target_pairs={{128,0},{192,64},{0,128},{64,192},{129,1},{193,65},{1,129},{65,193... | collective-permute-start | bytes 638984 | tf_op jit(solution)/shard_map/ppermute | solution.py:84
  87.4 12.5 %collective-permute-start.19 = (bf16[13,2,32,128]{3,2,1,0:T(8,128)(2,1)S(1)}, bf16[13,2,32,128]{3,2,1,0:T(8,128)(2,1)S(1)}, u32[]{:S(2)}, u32[]{:S(2)}) collective-permute-start(bf16[13,2,32,128]{3,2,1,0:T(8,128)(2,1)S(1)} %get-tuple-element.52), channel_id=1, source_target_pairs={{192,0},{0,64},{64,128},{128,192},{193,1},{1,65},{65,129},{129,193... | collective-permute-start | bytes 638984 | tf_op jit(solution)/shard_map/ppermute | solution.py:84

commit v13 on v12

--- a/solution.py
+++ b/solution.py
@@ -177,7 +177,7 @@
 
 
 def fan_body(me_ref, *refs):
-    pieces, out_ref = refs[:LAYERS], refs[LAYERS]
+    pieces, out_ref = refs[:LAYERS], refs[-1]
     for s, piece in enumerate(pieces):
         other = lax.rem(me_ref[0] + s, LAYERS)
         rows = pl.ds(pl.multiple_of(other * (BS // LAYERS), BS // LAYERS), BS // LAYERS)
@@ -351,10 +351,10 @@
     some = [shared, own]
     some = call(resplit_body, [shared_quarter] * LAYERS, 1, len(some))(me, *some)
     some = exchanged(some)
-    band = call(fan_body, packed([FAN])[0], 1, LAYERS)(me, *some)
+    band = call(fan_body, packed([FAN])[0], 1, LAYERS + 1)(me, *some, higher)
     plus_band, minus_band = far_across(band, FAR_PAIRS), far_across(band, -FAR_PAIRS)
     before = [own, band]
-    before += [lower, higher]
+    before += [lower]
     low, high = call(near_body, packed(NEAR[:2]), 0, len(before))(*before)
     low, high = from_pair(low, -1), from_pair(high, 1)
     arrived = [plus_far, minus_far, plus_band, minus_band]

time: 101 us -> 100 us (0.990)
  the two profiles are of different devices: /device:TPU:56 before, /device:TPU:1 now
where the time goes in v13:
time: 100 us; the launch traced here: 99.9 us
  waiting for transfers between devices  48.5 us (48%)
  starting transfers between devices  41 us (41%)
  Pallas kernels  8.39 us (8%)
  local copies, waits for them, and re-layouts  1.92 us (2%)
    ppermute x20, waiting for transfers between devices, moved(): return lax.ppermute(x, AXES, route)  48.5 us
    ppermute x20, starting transfers between devices, moved(): return lax.ppermute(x, AXES, route)  41 us
    pallas_call x1, Pallas kernels, per_device(): call(purify_body, [quarter] * LAYERS, 2, 3 + len(ARRIVE) - NEAR_SOURCES,...  4.32 us
  transfers between devices with their start and end apart: 20, of which 9 were waited for; matrix products, arithmetic and copies ran while one was open for 0% of the time, Pallas kernels for 2%

profile of v13, /device:TPU:1, one launch (start us, length us, event | category | flops | bytes accessed | tf_op | source)
XLA Modules:
  0.0 99.9 jit_solution(699659587387268834)
XLA Ops:
  0.0 0.8 copy.4.presence_ref
  0.8 0.0 copy-start
  0.8 1.2 %copy-done = bf16[13,8,32,128]{3,2,1,0:T(8,128)(2,1)S(1)} copy-done((bf16[13,8,32,128]{3,2,1,0:T(8,128)(2,1)S(1)}, bf16[13,8,32,128]{3,2,1,0:T(8,128)(2,1)}, u32[]{:S(2)}) %copy-start) | copy-done | bytes 851992
  1.9 0.9 shard_map.28
  2.9 7.8 %collective-permute-start.3 = (bf16[5,8,32,128]{3,2,1,0:T(8,128)(2,1)S(1)}, bf16[5,8,32,128]{3,2,1,0:T(8,128)(2,1)S(1)}, u32[]{:S(2)}, u32[]{:S(2)}) collective-permute-start(bf16[5,8,32,128]{3,2,1,0:T(8,128)(2,1)S(1)} %get-tuple-element.34), channel_id=1, source_target_pairs={{4,0},{68,64},{132,128},{196,192},{5,1},{69,65},{133,129},{197,193... | collective-permute-start | bytes 983048 | tf_op jit(solution)/shard_map/ppermute | solution.py:84
  10.7 2.5 %collective-permute-start = (bf16[13,2,32,128]{3,2,1,0:T(8,128)(2,1)S(1)}, bf16[13,2,32,128]{3,2,1,0:T(8,128)(2,1)S(1)}, u32[]{:S(2)}, u32[]{:S(2)}) collective-permute-start(bf16[13,2,32,128]{3,2,1,0:T(8,128)(2,1)S(1)} %get-tuple-element.30), channel_id=1, source_target_pairs={{64,0},{128,64},{192,128},{0,192},{65,1},{129,65},{193,129},{1,193... | collective-permute-start | bytes 638984 | tf_op jit(solution)/shard_map/ppermute | solution.py:84
  13.2 0.5 collective-permute-start.1
  13.7 0.6 collective-permute-start.2
  14.3 3.3 %collective-permute-done.refs_1_ = bf16[13,2,32,128]{3,2,1,0:T(8,128)(2,1)S(1)} collective-permute-done((bf16[13,2,32,128]{3,2,1,0:T(8,128)(2,1)S(1)}, bf16[13,2,32,128]{3,2,1,0:T(8,128)(2,1)S(1)}, u32[]{:S(2)}, u32[]{:S(2)}) %collective-permute-start) | collective-permute-done | bytes 213024 | tf_op jit(solution)/shard_map/ppermute | solution.py:84
  17.6 2.7 %collective-permute-done.1.refs_2_ = bf16[13,2,32,128]{3,2,1,0:T(8,128)(2,1)S(1)} collective-permute-done((bf16[13,2,32,128]{3,2,1,0:T(8,128)(2,1)S(1)}, bf16[13,2,32,128]{3,2,1,0:T(8,128)(2,1)S(1)}, u32[]{:S(2)}, u32[]{:S(2)}) %collective-permute-start.1) | collective-permute-done | bytes 213024 | tf_op jit(solution)/shard_map/ppermute | solution.py:84
  20.2 6.2 %collective-permute-done.2.refs_3_ = bf16[13,2,32,128]{3,2,1,0:T(8,128)(2,1)S(1)} collective-permute-done((bf16[13,2,32,128]{3,2,1,0:T(8,128)(2,1)S(1)}, bf16[13,2,32,128]{3,2,1,0:T(8,128)(2,1)S(1)}, u32[]{:S(2)}, u32[]{:S(2)}) %collective-permute-start.2) | collective-permute-done | bytes 213024 | tf_op jit(solution)/shard_map/ppermute | solution.py:84
  26.4 0.1 shard_map.29
  26.5 0.5 collective-permute-start.7
  27.1 0.0 collective-permute-done.3.shared_ref
  27.1 0.1 collective-permute-start.4
  27.2 2.6 %collective-permute-start.5 = (bf16[5,2,32,128]{3,2,1,0:T(8,128)(2,1)S(1)}, bf16[5,2,32,128]{3,2,1,0:T(8,128)(2,1)S(1)}, u32[]{:S(2)}, u32[]{:S(2)}) collective-permute-start(bf16[5,2,32,128]{3,2,1,0:T(8,128)(2,1)S(1)} %get-tuple-element.37), channel_id=1, source_target_pairs={{128,0},{192,64},{0,128},{64,192},{129,1},{193,65},{1,129},{65,193... | collective-permute-start | bytes 245768 | tf_op jit(solution)/shard_map/ppermute | solution.py:84
  29.8 0.8 collective-permute-start.6
  30.6 7.4 %collective-permute-start.11 = (bf16[6,128,128]{2,1,0:T(8,128)(2,1)S(1)}, bf16[6,128,128]{2,1,0:T(8,128)(2,1)S(1)}, u32[]{:S(2)}, u32[]{:S(2)}) collective-permute-start(bf16[6,128,128]{2,1,0:T(8,128)(2,1)S(1)} %get-tuple-element.45), channel_id=1, source_target_pairs={{20,0},{84,64},{148,128},{212,192},{21,1},{85,65},{149,129},{213,1... | collective-permute-start | bytes 589832 | tf_op jit(solution)/shard_map/ppermute | solution.py:84
  38.0 0.0 collective-permute-done.7.refs_4_
  38.0 0.0 collective-permute-done.4.refs_1_
  38.0 0.0 collective-permute-done.5.refs_2_
  38.0 0.0 collective-permute-done.6.refs_3_
  38.1 1.5 %collective-permute-start.13 = (bf16[10,128,128]{2,1,0:T(8,128)(2,1)S(1)}, bf16[10,128,128]{2,1,0:T(8,128)(2,1)S(1)}, u32[]{:S(2)}, u32[]{:S(2)}) collective-permute-start(bf16[10,128,128]{2,1,0:T(8,128)(2,1)S(1)} %shard_map.31.refs_0_), channel_id=1, source_target_pairs={{16,0},{80,64},{144,128},{208,192},{17,1},{81,65},{145,129},{209,1... | collective-permute-start | bytes 983048 | tf_op jit(solution)/shard_map/ppermute | solution.py:84
  39.5 1.4 %collective-permute-start.14 = (bf16[10,128,128]{2,1,0:T(8,128)(2,1)S(1)}, bf16[10,128,128]{2,1,0:T(8,128)(2,1)S(1)}, u32[]{:S(2)}, u32[]{:S(2)}) collective-permute-start(bf16[10,128,128]{2,1,0:T(8,128)(2,1)S(1)} %shard_map.31.refs_0_), channel_id=1, source_target_pairs={{40,0},{104,64},{168,128},{232,192},{41,1},{105,65},{169,129},{233... | collective-permute-start | bytes 983048 | tf_op jit(solution)/shard_map/ppermute | solution.py:84
  40.9 1.4 %collective-permute-start.8 = (bf16[4,128,128]{2,1,0:T(8,128)(2,1)S(1)}, bf16[4,128,128]{2,1,0:T(8,128)(2,1)S(1)}, u32[]{:S(2)}, u32[]{:S(2)}) collective-permute-start(bf16[4,128,128]{2,1,0:T(8,128)(2,1)S(1)} %get-tuple-element.40), channel_id=1, source_target_pairs={{191,0},{255,64},{0,128},{64,192},{128,1},{192,65},{1,129},{65,193... | collective-permute-start | bytes 393224 | tf_op jit(solution)/shard_map/ppermute | solution.py:84
  42.3 1.8 %collective-permute-start.12 = (bf16[6,128,128]{2,1,0:T(8,128)(2,1)S(1)}, bf16[6,128,128]{2,1,0:T(8,128)(2,1)S(1)}, u32[]{:S(2)}, u32[]{:S(2)}) collective-permute-start(bf16[6,128,128]{2,1,0:T(8,128)(2,1)S(1)} %get-tuple-element.46), channel_id=1, source_target_pairs={{44,0},{108,64},{172,128},{236,192},{45,1},{109,65},{173,129},{237... | collective-permute-start | bytes 589832 | tf_op jit(solution)/shard_map/ppermute | solution.py:84
  44.1 8.2 %collective-permute-done.8.refs_1_.refs_3_ = bf16[4,128,128]{2,1,0:T(8,128)(2,1)S(1)} collective-permute-done((bf16[4,128,128]{2,1,0:T(8,128)(2,1)S(1)}, bf16[4,128,128]{2,1,0:T(8,128)(2,1)S(1)}, u32[]{:S(2)}, u32[]{:S(2)}) %collective-permute-start.8) | collective-permute-done | bytes 131104 | tf_op jit(solution)/shard_map/ppermute | solution.py:84
  52.4 0.1 shard_map.32
  52.4 0.3 collective-permute-start.9
  52.8 0.0 collective-permute-done.11.refs_0_
  52.8 4.8 %collective-permute-start.10 = (bf16[17,128,128]{2,1,0:T(8,128)(2,1)S(1)}, bf16[17,128,128]{2,1,0:T(8,128)(2,1)S(1)}, u32[]{:S(2)}, u32[]{:S(2)}) collective-permute-start(bf16[17,128,128]{2,1,0:T(8,128)(2,1)S(1)} %get-tuple-element.42), channel_id=1, source_target_pairs={{64,0},{128,64},{192,128},{1,192},{65,1},{129,65},{193,129},{2,193... | collective-permute-start | bytes 1671176 | tf_op jit(solution)/shard_map/ppermute | solution.py:84
  57.6 0.0 collective-permute-done.12.refs_1_
  57.6 0.0 collective-permute-done.13.refs_2_
  57.6 0.0 collective-permute-done.14.refs_3_
  57.6 0.1 shard_map.34
  57.7 3.7 %collective-permute-start.15 = (bf16[12,128,128]{2,1,0:T(8,128)(2,1)S(1)}, bf16[12,128,128]{2,1,0:T(8,128)(2,1)S(1)}, u32[]{:S(2)}, u32[]{:S(2)}) collective-permute-start(bf16[12,128,128]{2,1,0:T(8,128)(2,1)S(1)} %get-tuple-element.47), channel_id=1, source_target_pairs={{255,0},{0,64},{64,128},{128,192},{192,1},{1,65},{65,129},{129,193... | collective-permute-start | bytes 1179656 | tf_op jit(solution)/shard_map/ppermute | solution.py:84
  61.3 1.6 %collective-permute-start.16 = (bf16[12,128,128]{2,1,0:T(8,128)(2,1)S(1)}, bf16[12,128,128]{2,1,0:T(8,128)(2,1)S(1)}, u32[]{:S(2)}, u32[]{:S(2)}) collective-permute-start(bf16[12,128,128]{2,1,0:T(8,128)(2,1)S(1)} %get-tuple-element.48), channel_id=1, source_target_pairs={{64,0},{128,64},{192,128},{1,192},{65,1},{129,65},{193,129},{2,193... | collective-permute-start | bytes 1179656 | tf_op jit(solution)/shard_map/ppermute | solution.py:84
  63.0 9.1 %collective-permute-done.9.refs_1_ = bf16[17,128,128]{2,1,0:T(8,128)(2,1)S(1)} collective-permute-done((bf16[17,128,128]{2,1,0:T(8,128)(2,1)S(1)}, bf16[17,128,128]{2,1,0:T(8,128)(2,1)S(1)}, u32[]{:S(2)}, u32[]{:S(2)}) %collective-permute-start.9) | collective-permute-done | bytes 557088 | tf_op jit(solution)/shard_map/ppermute | solution.py:84
  72.0 0.0 collective-permute-done.10.refs_2_
  72.0 1.9 %shard_map.33 = (bf16[1024,2048]{1,0:T(8,128)(2,1)S(1)}, f32[256,2048]{1,0:T(8,128)S(1)}) custom-call(bf16[13,2,128,128]{3,2,1,0:T(8,128)(2,1)S(1)} %get-tuple-element.33.out_refs_0_.own_ref.refs_0_, bf16[17,128,128]{2,1,0:T(8,128)(2,1)S(1)} %collective-permute-done.9.refs_1_, bf16[17,128,128]{2,1,0:T(8,128)(2,1)S(1)} %collective-permute-done.10.refs_2_, ...), custom_call_target="tpu_custom_call" | custom-call | bytes 4194304 | tf_op jit(solution)/shard_map/pallas_call | solution.py:366
  73.9 6.5 %collective-permute-done.15.refs_4_ = bf16[12,128,128]{2,1,0:T(8,128)(2,1)S(1)} collective-permute-done((bf16[12,128,128]{2,1,0:T(8,128)(2,1)S(1)}, bf16[12,128,128]{2,1,0:T(8,128)(2,1)S(1)}, u32[]{:S(2)}, u32[]{:S(2)}) %collective-permute-start.15) | collective-permute-done | bytes 393248 | tf_op jit(solution)/shard_map/ppermute | solution.py:84
  80.5 0.0 collective-permute-done.16.refs_5_
  80.5 4.3 %shard_map.35 = (bf16[13,2,32,128]{3,2,1,0:T(8,128)(2,1)S(1)}, bf16[13,2,32,128]{3,2,1,0:T(8,128)(2,1)S(1)}, bf16[13,2,32,128]{3,2,1,0:T(8,128)(2,1)S(1)}, bf16[13,2,32,128]{3,2,1,0:T(8,128)(2,1)S(1)}) custom-call(s32[1]{0:T(128)} %bitcast.me_ref, s32[13,8]{1,0:T(8,128)S(1)} %copy.4.presence_ref, ...), custom_call_target="tpu_custom_call" | custom-call | flops 2684354560 | bytes 4194304 | tf_op jit(solution)/shard_map/pallas_call | solution.py:373
  84.8 0.9 collective-permute-start.17
  85.7 0.0 collective-permute-start.18
  85.7 0.7 collective-permute-start.19
  86.4 3.9 %collective-permute-done.17.refs_1_ = bf16[13,2,32,128]{3,2,1,0:T(8,128)(2,1)S(1)} collective-permute-done((bf16[13,2,32,128]{3,2,1,0:T(8,128)(2,1)S(1)}, bf16[13,2,32,128]{3,2,1,0:T(8,128)(2,1)S(1)}, u32[]{:S(2)}, u32[]{:S(2)}) %collective-permute-start.17) | collective-permute-done | bytes 213024 | tf_op jit(solution)/shard_map/ppermute | solution.py:84
  90.3 3.0 %collective-permute-done.18.refs_2_ = bf16[13,2,32,128]{3,2,1,0:T(8,128)(2,1)S(1)} collective-permute-done((bf16[13,2,32,128]{3,2,1,0:T(8,128)(2,1)S(1)}, bf16[13,2,32,128]{3,2,1,0:T(8,128)(2,1)S(1)}, u32[]{:S(2)}, u32[]{:S(2)}) %collective-permute-start.18) | collective-permute-done | bytes 213024 | tf_op jit(solution)/shard_map/ppermute | solution.py:84
  93.2 5.7 %collective-permute-done.19.refs_3_ = bf16[13,2,32,128]{3,2,1,0:T(8,128)(2,1)S(1)} collective-permute-done((bf16[13,2,32,128]{3,2,1,0:T(8,128)(2,1)S(1)}, bf16[13,2,32,128]{3,2,1,0:T(8,128)(2,1)S(1)}, u32[]{:S(2)}, u32[]{:S(2)}) %collective-permute-start.19) | collective-permute-done | bytes 213024 | tf_op jit(solution)/shard_map/ppermute | solution.py:84
  99.0 1.0 shard_map.36
  (2 shorter events, 0.1 us)
Async XLA Ops:
  0.8 1.2 %copy-start = (bf16[13,8,32,128]{3,2,1,0:T(8,128)(2,1)S(1)}, bf16[13,8,32,128]{3,2,1,0:T(8,128)(2,1)}, u32[]{:S(2)}) copy-start(bf16[13,8,32,128]{3,2,1,0:T(8,128)(2,1)} %blocks_ref.1) | copy-start | bytes 2555908
  2.9 24.2 %collective-permute-start.3 = (bf16[5,8,32,128]{3,2,1,0:T(8,128)(2,1)S(1)}, bf16[5,8,32,128]{3,2,1,0:T(8,128)(2,1)S(1)}, u32[]{:S(2)}, u32[]{:S(2)}) collective-permute-start(bf16[5,8,32,128]{3,2,1,0:T(8,128)(2,1)S(1)} %get-tuple-element.34), channel_id=1, source_target_pairs={{4,0},{68,64},{132,128},{196,192},{5,1},{69,65},{133,129},{197,193... | collective-permute-start | bytes 983048 | tf_op jit(solution)/shard_map/ppermute | solution.py:84
  10.7 6.9 %collective-permute-start = (bf16[13,2,32,128]{3,2,1,0:T(8,128)(2,1)S(1)}, bf16[13,2,32,128]{3,2,1,0:T(8,128)(2,1)S(1)}, u32[]{:S(2)}, u32[]{:S(2)}) collective-permute-start(bf16[13,2,32,128]{3,2,1,0:T(8,128)(2,1)S(1)} %get-tuple-element.30), channel_id=1, source_target_pairs={{64,0},{128,64},{192,128},{0,192},{65,1},{129,65},{193,129},{1,193... | collective-permute-start | bytes 638984 | tf_op jit(solution)/shard_map/ppermute | solution.py:84
  13.2 7.1 %collective-permute-start.1 = (bf16[13,2,32,128]{3,2,1,0:T(8,128)(2,1)S(1)}, bf16[13,2,32,128]{3,2,1,0:T(8,128)(2,1)S(1)}, u32[]{:S(2)}, u32[]{:S(2)}) collective-permute-start(bf16[13,2,32,128]{3,2,1,0:T(8,128)(2,1)S(1)} %get-tuple-element.31), channel_id=1, source_target_pairs={{128,0},{192,64},{0,128},{64,192},{129,1},{193,65},{1,129},{65,193... | collective-permute-start | bytes 638984 | tf_op jit(solution)/shard_map/ppermute | solution.py:84
  13.7 12.7 %collective-permute-start.2 = (bf16[13,2,32,128]{3,2,1,0:T(8,128)(2,1)S(1)}, bf16[13,2,32,128]{3,2,1,0:T(8,128)(2,1)S(1)}, u32[]{:S(2)}, u32[]{:S(2)}) collective-permute-start(bf16[13,2,32,128]{3,2,1,0:T(8,128)(2,1)S(1)} %get-tuple-element.32), channel_id=1, source_target_pairs={{192,0},{0,64},{64,128},{128,192},{193,1},{1,65},{65,129},{129,193... | collective-permute-start | bytes 638984 | tf_op jit(solution)/shard_map/ppermute | solution.py:84
  26.5 11.5 %collective-permute-start.7 = (bf16[4,128,128]{2,1,0:T(8,128)(2,1)S(1)}, bf16[4,128,128]{2,1,0:T(8,128)(2,1)S(1)}, u32[]{:S(2)}, u32[]{:S(2)}) collective-permute-start(bf16[4,128,128]{2,1,0:T(8,128)(2,1)S(1)} %get-tuple-element.39), channel_id=1, source_target_pairs={{128,0},{192,64},{1,128},{65,192},{129,1},{193,65},{2,129},{66,193... | collective-permute-start | bytes 393224 | tf_op jit(solution)/shard_map/ppermute | solution.py:84
  27.1 10.9 %collective-permute-start.4 = (bf16[5,2,32,128]{3,2,1,0:T(8,128)(2,1)S(1)}, bf16[5,2,32,128]{3,2,1,0:T(8,128)(2,1)S(1)}, u32[]{:S(2)}, u32[]{:S(2)}) collective-permute-start(bf16[5,2,32,128]{3,2,1,0:T(8,128)(2,1)S(1)} %get-tuple-element.36), channel_id=1, source_target_pairs={{64,0},{128,64},{192,128},{0,192},{65,1},{129,65},{193,129},{1,193... | collective-permute-start | bytes 245768 | tf_op jit(solution)/shard_map/ppermute | solution.py:84
  27.2 10.8 %collective-permute-start.5 = (bf16[5,2,32,128]{3,2,1,0:T(8,128)(2,1)S(1)}, bf16[5,2,32,128]{3,2,1,0:T(8,128)(2,1)S(1)}, u32[]{:S(2)}, u32[]{:S(2)}) collective-permute-start(bf16[5,2,32,128]{3,2,1,0:T(8,128)(2,1)S(1)} %get-tuple-element.37), channel_id=1, source_target_pairs={{128,0},{192,64},{0,128},{64,192},{129,1},{193,65},{1,129},{65,193... | collective-permute-start | bytes 245768 | tf_op jit(solution)/shard_map/ppermute | solution.py:84
  29.8 8.2 %collective-permute-start.6 = (bf16[5,2,32,128]{3,2,1,0:T(8,128)(2,1)S(1)}, bf16[5,2,32,128]{3,2,1,0:T(8,128)(2,1)S(1)}, u32[]{:S(2)}, u32[]{:S(2)}) collective-permute-start(bf16[5,2,32,128]{3,2,1,0:T(8,128)(2,1)S(1)} %get-tuple-element.38), channel_id=1, source_target_pairs={{192,0},{0,64},{64,128},{128,192},{193,1},{1,65},{65,129},{129,193... | collective-permute-start | bytes 245768 | tf_op jit(solution)/shard_map/ppermute | solution.py:84
  30.6 22.2 %collective-permute-start.11 = (bf16[6,128,128]{2,1,0:T(8,128)(2,1)S(1)}, bf16[6,128,128]{2,1,0:T(8,128)(2,1)S(1)}, u32[]{:S(2)}, u32[]{:S(2)}) collective-permute-start(bf16[6,128,128]{2,1,0:T(8,128)(2,1)S(1)} %get-tuple-element.45), channel_id=1, source_target_pairs={{20,0},{84,64},{148,128},{212,192},{21,1},{85,65},{149,129},{213,1... | collective-permute-start | bytes 589832 | tf_op jit(solution)/shard_map/ppermute | solution.py:84
  38.1 19.5 %collective-permute-start.13 = (bf16[10,128,128]{2,1,0:T(8,128)(2,1)S(1)}, bf16[10,128,128]{2,1,0:T(8,128)(2,1)S(1)}, u32[]{:S(2)}, u32[]{:S(2)}) collective-permute-start(bf16[10,128,128]{2,1,0:T(8,128)(2,1)S(1)} %shard_map.31.refs_0_), channel_id=1, source_target_pairs={{16,0},{80,64},{144,128},{208,192},{17,1},{81,65},{145,129},{209,1... | collective-permute-start | bytes 983048 | tf_op jit(solution)/shard_map/ppermute | solution.py:84
  39.5 18.0 %collective-permute-start.14 = (bf16[10,128,128]{2,1,0:T(8,128)(2,1)S(1)}, bf16[10,128,128]{2,1,0:T(8,128)(2,1)S(1)}, u32[]{:S(2)}, u32[]{:S(2)}) collective-permute-start(bf16[10,128,128]{2,1,0:T(8,128)(2,1)S(1)} %shard_map.31.refs_0_), channel_id=1, source_target_pairs={{40,0},{104,64},{168,128},{232,192},{41,1},{105,65},{169,129},{233... | collective-permute-start | bytes 983048 | tf_op jit(solution)/shard_map/ppermute | solution.py:84
  40.9 11.4 %collective-permute-start.8 = (bf16[4,128,128]{2,1,0:T(8,128)(2,1)S(1)}, bf16[4,128,128]{2,1,0:T(8,128)(2,1)S(1)}, u32[]{:S(2)}, u32[]{:S(2)}) collective-permute-start(bf16[4,128,128]{2,1,0:T(8,128)(2,1)S(1)} %get-tuple-element.40), channel_id=1, source_target_pairs={{191,0},{255,64},{0,128},{64,192},{128,1},{192,65},{1,129},{65,193... | collective-permute-start | bytes 393224 | tf_op jit(solution)/shard_map/ppermute | solution.py:84
  42.3 15.3 %collective-permute-start.12 = (bf16[6,128,128]{2,1,0:T(8,128)(2,1)S(1)}, bf16[6,128,128]{2,1,0:T(8,128)(2,1)S(1)}, u32[]{:S(2)}, u32[]{:S(2)}) collective-permute-start(bf16[6,128,128]{2,1,0:T(8,128)(2,1)S(1)} %get-tuple-element.46), channel_id=1, source_target_pairs={{44,0},{108,64},{172,128},{236,192},{45,1},{109,65},{173,129},{237... | collective-permute-start | bytes 589832 | tf_op jit(solution)/shard_map/ppermute | solution.py:84
  52.4 19.6 %collective-permute-start.9 = (bf16[17,128,128]{2,1,0:T(8,128)(2,1)S(1)}, bf16[17,128,128]{2,1,0:T(8,128)(2,1)S(1)}, u32[]{:S(2)}, u32[]{:S(2)}) collective-permute-start(bf16[17,128,128]{2,1,0:T(8,128)(2,1)S(1)} %get-tuple-element.41), channel_id=1, source_target_pairs={{255,0},{0,64},{64,128},{128,192},{192,1},{1,65},{65,129},{129,193... | collective-permute-start | bytes 1671176 | tf_op jit(solution)/shard_map/ppermute | solution.py:84
  52.8 19.3 %collective-permute-start.10 = (bf16[17,128,128]{2,1,0:T(8,128)(2,1)S(1)}, bf16[17,128,128]{2,1,0:T(8,128)(2,1)S(1)}, u32[]{:S(2)}, u32[]{:S(2)}) collective-permute-start(bf16[17,128,128]{2,1,0:T(8,128)(2,1)S(1)} %get-tuple-element.42), channel_id=1, source_target_pairs={{64,0},{128,64},{192,128},{1,192},{65,1},{129,65},{193,129},{2,193... | collective-permute-start | bytes 1671176 | tf_op jit(solution)/shard_map/ppermute | solution.py:84
  57.7 22.8 %collective-permute-start.15 = (bf16[12,128,128]{2,1,0:T(8,128)(2,1)S(1)}, bf16[12,128,128]{2,1,0:T(8,128)(2,1)S(1)}, u32[]{:S(2)}, u32[]{:S(2)}) collective-permute-start(bf16[12,128,128]{2,1,0:T(8,128)(2,1)S(1)} %get-tuple-element.47), channel_id=1, source_target_pairs={{255,0},{0,64},{64,128},{128,192},{192,1},{1,65},{65,129},{129,193... | collective-permute-start | bytes 1179656 | tf_op jit(solution)/shard_map/ppermute | solution.py:84
  61.3 19.1 %collective-permute-start.16 = (bf16[12,128,128]{2,1,0:T(8,128)(2,1)S(1)}, bf16[12,128,128]{2,1,0:T(8,128)(2,1)S(1)}, u32[]{:S(2)}, u32[]{:S(2)}) collective-permute-start(bf16[12,128,128]{2,1,0:T(8,128)(2,1)S(1)} %get-tuple-element.48), channel_id=1, source_target_pairs={{64,0},{128,64},{192,128},{1,192},{65,1},{129,65},{193,129},{2,193... | collective-permute-start | bytes 1179656 | tf_op jit(solution)/shard_map/ppermute | solution.py:84
  84.8 5.5 %collective-permute-start.17 = (bf16[13,2,32,128]{3,2,1,0:T(8,128)(2,1)S(1)}, bf16[13,2,32,128]{3,2,1,0:T(8,128)(2,1)S(1)}, u32[]{:S(2)}, u32[]{:S(2)}) collective-permute-start(bf16[13,2,32,128]{3,2,1,0:T(8,128)(2,1)S(1)} %get-tuple-element.50), channel_id=1, source_target_pairs={{64,0},{128,64},{192,128},{0,192},{65,1},{129,65},{193,129},{1,193... | collective-permute-start | bytes 638984 | tf_op jit(solution)/shard_map/ppermute | solution.py:84
  85.7 7.5 %collective-permute-start.18 = (bf16[13,2,32,128]{3,2,1,0:T(8,128)(2,1)S(1)}, bf16[13,2,32,128]{3,2,1,0:T(8,128)(2,1)S(1)}, u32[]{:S(2)}, u32[]{:S(2)}) collective-permute-start(bf16[13,2,32,128]{3,2,1,0:T(8,128)(2,1)S(1)} %get-tuple-element.51), channel_id=1, source_target_pairs={{128,0},{192,64},{0,128},{64,192},{129,1},{193,65},{1,129},{65,193... | collective-permute-start | bytes 638984 | tf_op jit(solution)/shard_map/ppermute | solution.py:84
  85.7 13.2 %collective-permute-start.19 = (bf16[13,2,32,128]{3,2,1,0:T(8,128)(2,1)S(1)}, bf16[13,2,32,128]{3,2,1,0:T(8,128)(2,1)S(1)}, u32[]{:S(2)}, u32[]{:S(2)}) collective-permute-start(bf16[13,2,32,128]{3,2,1,0:T(8,128)(2,1)S(1)} %get-tuple-element.52), channel_id=1, source_target_pairs={{192,0},{0,64},{64,128},{128,192},{193,1},{1,65},{65,129},{129,193... | collective-permute-start | bytes 638984 | tf_op jit(solution)/shard_map/ppermute | solution.py:84

commit v14 on v13

--- a/solution.py
+++ b/solution.py
@@ -273,7 +273,9 @@
 
     def near_product(columns):
         wide = pl.ds(columns[0] * BS, len(columns) * BS)
-        return dot(left_ref[:, :NEAR_END], right_near_ref[:, wide])
+        first = 2 * BS if columns[0] in (6, 10, 14) else 0
+        last = NEAR_END - 2 * BS if columns[0] in (0, 8, 12) else NEAR_END
+        return dot(left_ref[:, first:last], right_near_ref[first:last, wide])
 
     def each(columns, total, use):
         for at, column in enumerate(columns):

time: 100 us -> 99.9 us (level)
  no operation moved by 1% of the time
where the time goes in v14:
time: 99.9 us; the launch traced here: 99.7 us
  waiting for transfers between devices  48.5 us (49%)
  starting transfers between devices  41 us (41%)
  Pallas kernels  8.2 us (8%)
  local copies, waits for them, and re-layouts  1.92 us (2%)
    ppermute x20, waiting for transfers between devices, moved(): return lax.ppermute(x, AXES, route)  48.5 us
    ppermute x20, starting transfers between devices, moved(): return lax.ppermute(x, AXES, route)  41 us
    pallas_call x1, Pallas kernels, per_device(): call(purify_body, [quarter] * LAYERS, 2, 3 + len(ARRIVE) - NEAR_SOURCES,...  4.13 us
  transfers between devices with their start and end apart: 20, of which 9 were waited for; matrix products, arithmetic and copies ran while one was open for 0% of the time, Pallas kernels for 2%

profile of v14, /device:TPU:1, one launch (start us, length us, event | category | flops | bytes accessed | tf_op | source)
XLA Modules:
  0.0 99.7 jit_solution(17063866713848922978)
XLA Ops:
  0.0 0.8 copy.4.presence_ref
  0.8 0.0 copy-start
  0.8 1.2 %copy-done = bf16[13,8,32,128]{3,2,1,0:T(8,128)(2,1)S(1)} copy-done((bf16[13,8,32,128]{3,2,1,0:T(8,128)(2,1)S(1)}, bf16[13,8,32,128]{3,2,1,0:T(8,128)(2,1)}, u32[]{:S(2)}) %copy-start) | copy-done | bytes 851992
  1.9 0.9 shard_map.28
  2.9 7.8 %collective-permute-start.3 = (bf16[5,8,32,128]{3,2,1,0:T(8,128)(2,1)S(1)}, bf16[5,8,32,128]{3,2,1,0:T(8,128)(2,1)S(1)}, u32[]{:S(2)}, u32[]{:S(2)}) collective-permute-start(bf16[5,8,32,128]{3,2,1,0:T(8,128)(2,1)S(1)} %get-tuple-element.34), channel_id=1, source_target_pairs={{4,0},{68,64},{132,128},{196,192},{5,1},{69,65},{133,129},{197,193... | collective-permute-start | bytes 983048 | tf_op jit(solution)/shard_map/ppermute | solution.py:84
  10.7 2.5 %collective-permute-start = (bf16[13,2,32,128]{3,2,1,0:T(8,128)(2,1)S(1)}, bf16[13,2,32,128]{3,2,1,0:T(8,128)(2,1)S(1)}, u32[]{:S(2)}, u32[]{:S(2)}) collective-permute-start(bf16[13,2,32,128]{3,2,1,0:T(8,128)(2,1)S(1)} %get-tuple-element.30), channel_id=1, source_target_pairs={{64,0},{128,64},{192,128},{0,192},{65,1},{129,65},{193,129},{1,193... | collective-permute-start | bytes 638984 | tf_op jit(solution)/shard_map/ppermute | solution.py:84
  13.2 0.5 collective-permute-start.1
  13.7 0.6 collective-permute-start.2
  14.3 3.3 %collective-permute-done.refs_1_ = bf16[13,2,32,128]{3,2,1,0:T(8,128)(2,1)S(1)} collective-permute-done((bf16[13,2,32,128]{3,2,1,0:T(8,128)(2,1)S(1)}, bf16[13,2,32,128]{3,2,1,0:T(8,128)(2,1)S(1)}, u32[]{:S(2)}, u32[]{:S(2)}) %collective-permute-start) | collective-permute-done | bytes 213024 | tf_op jit(solution)/shard_map/ppermute | solution.py:84
  17.6 2.7 %collective-permute-done.1.refs_2_ = bf16[13,2,32,128]{3,2,1,0:T(8,128)(2,1)S(1)} collective-permute-done((bf16[13,2,32,128]{3,2,1,0:T(8,128)(2,1)S(1)}, bf16[13,2,32,128]{3,2,1,0:T(8,128)(2,1)S(1)}, u32[]{:S(2)}, u32[]{:S(2)}) %collective-permute-start.1) | collective-permute-done | bytes 213024 | tf_op jit(solution)/shard_map/ppermute | solution.py:84
  20.2 6.2 %collective-permute-done.2.refs_3_ = bf16[13,2,32,128]{3,2,1,0:T(8,128)(2,1)S(1)} collective-permute-done((bf16[13,2,32,128]{3,2,1,0:T(8,128)(2,1)S(1)}, bf16[13,2,32,128]{3,2,1,0:T(8,128)(2,1)S(1)}, u32[]{:S(2)}, u32[]{:S(2)}) %collective-permute-start.2) | collective-permute-done | bytes 213024 | tf_op jit(solution)/shard_map/ppermute | solution.py:84
  26.4 0.1 shard_map.29
  26.5 0.5 collective-permute-start.7
  27.1 0.0 collective-permute-done.3.shared_ref
  27.1 0.1 collective-permute-start.4
  27.2 2.6 %collective-permute-start.5 = (bf16[5,2,32,128]{3,2,1,0:T(8,128)(2,1)S(1)}, bf16[5,2,32,128]{3,2,1,0:T(8,128)(2,1)S(1)}, u32[]{:S(2)}, u32[]{:S(2)}) collective-permute-start(bf16[5,2,32,128]{3,2,1,0:T(8,128)(2,1)S(1)} %get-tuple-element.37), channel_id=1, source_target_pairs={{128,0},{192,64},{0,128},{64,192},{129,1},{193,65},{1,129},{65,193... | collective-permute-start | bytes 245768 | tf_op jit(solution)/shard_map/ppermute | solution.py:84
  29.8 0.8 collective-permute-start.6
  30.6 7.4 %collective-permute-start.11 = (bf16[6,128,128]{2,1,0:T(8,128)(2,1)S(1)}, bf16[6,128,128]{2,1,0:T(8,128)(2,1)S(1)}, u32[]{:S(2)}, u32[]{:S(2)}) collective-permute-start(bf16[6,128,128]{2,1,0:T(8,128)(2,1)S(1)} %get-tuple-element.45), channel_id=1, source_target_pairs={{20,0},{84,64},{148,128},{212,192},{21,1},{85,65},{149,129},{213,1... | collective-permute-start | bytes 589832 | tf_op jit(solution)/shard_map/ppermute | solution.py:84
  38.0 0.0 collective-permute-done.7.refs_4_
  38.0 0.0 collective-permute-done.4.refs_1_
  38.0 0.0 collective-permute-done.5.refs_2_
  38.0 0.0 collective-permute-done.6.refs_3_
  38.1 1.5 %collective-permute-start.13 = (bf16[10,128,128]{2,1,0:T(8,128)(2,1)S(1)}, bf16[10,128,128]{2,1,0:T(8,128)(2,1)S(1)}, u32[]{:S(2)}, u32[]{:S(2)}) collective-permute-start(bf16[10,128,128]{2,1,0:T(8,128)(2,1)S(1)} %shard_map.31.refs_0_), channel_id=1, source_target_pairs={{16,0},{80,64},{144,128},{208,192},{17,1},{81,65},{145,129},{209,1... | collective-permute-start | bytes 983048 | tf_op jit(solution)/shard_map/ppermute | solution.py:84
  39.5 1.4 %collective-permute-start.14 = (bf16[10,128,128]{2,1,0:T(8,128)(2,1)S(1)}, bf16[10,128,128]{2,1,0:T(8,128)(2,1)S(1)}, u32[]{:S(2)}, u32[]{:S(2)}) collective-permute-start(bf16[10,128,128]{2,1,0:T(8,128)(2,1)S(1)} %shard_map.31.refs_0_), channel_id=1, source_target_pairs={{40,0},{104,64},{168,128},{232,192},{41,1},{105,65},{169,129},{233... | collective-permute-start | bytes 983048 | tf_op jit(solution)/shard_map/ppermute | solution.py:84
  40.9 1.4 %collective-permute-start.8 = (bf16[4,128,128]{2,1,0:T(8,128)(2,1)S(1)}, bf16[4,128,128]{2,1,0:T(8,128)(2,1)S(1)}, u32[]{:S(2)}, u32[]{:S(2)}) collective-permute-start(bf16[4,128,128]{2,1,0:T(8,128)(2,1)S(1)} %get-tuple-element.40), channel_id=1, source_target_pairs={{191,0},{255,64},{0,128},{64,192},{128,1},{192,65},{1,129},{65,193... | collective-permute-start | bytes 393224 | tf_op jit(solution)/shard_map/ppermute | solution.py:84
  42.3 1.8 %collective-permute-start.12 = (bf16[6,128,128]{2,1,0:T(8,128)(2,1)S(1)}, bf16[6,128,128]{2,1,0:T(8,128)(2,1)S(1)}, u32[]{:S(2)}, u32[]{:S(2)}) collective-permute-start(bf16[6,128,128]{2,1,0:T(8,128)(2,1)S(1)} %get-tuple-element.46), channel_id=1, source_target_pairs={{44,0},{108,64},{172,128},{236,192},{45,1},{109,65},{173,129},{237... | collective-permute-start | bytes 589832 | tf_op jit(solution)/shard_map/ppermute | solution.py:84
  44.1 8.2 %collective-permute-done.8.refs_1_.refs_3_ = bf16[4,128,128]{2,1,0:T(8,128)(2,1)S(1)} collective-permute-done((bf16[4,128,128]{2,1,0:T(8,128)(2,1)S(1)}, bf16[4,128,128]{2,1,0:T(8,128)(2,1)S(1)}, u32[]{:S(2)}, u32[]{:S(2)}) %collective-permute-start.8) | collective-permute-done | bytes 131104 | tf_op jit(solution)/shard_map/ppermute | solution.py:84
  52.4 0.1 shard_map.32
  52.4 0.3 collective-permute-start.9
  52.8 0.0 collective-permute-done.11.refs_0_
  52.8 4.8 %collective-permute-start.10 = (bf16[17,128,128]{2,1,0:T(8,128)(2,1)S(1)}, bf16[17,128,128]{2,1,0:T(8,128)(2,1)S(1)}, u32[]{:S(2)}, u32[]{:S(2)}) collective-permute-start(bf16[17,128,128]{2,1,0:T(8,128)(2,1)S(1)} %get-tuple-element.42), channel_id=1, source_target_pairs={{64,0},{128,64},{192,128},{1,192},{65,1},{129,65},{193,129},{2,193... | collective-permute-start | bytes 1671176 | tf_op jit(solution)/shard_map/ppermute | solution.py:84
  57.6 0.0 collective-permute-done.12.refs_1_
  57.6 0.0 collective-permute-done.13.refs_2_
  57.6 0.0 collective-permute-done.14.refs_3_
  57.6 0.1 shard_map.34
  57.7 3.7 %collective-permute-start.15 = (bf16[12,128,128]{2,1,0:T(8,128)(2,1)S(1)}, bf16[12,128,128]{2,1,0:T(8,128)(2,1)S(1)}, u32[]{:S(2)}, u32[]{:S(2)}) collective-permute-start(bf16[12,128,128]{2,1,0:T(8,128)(2,1)S(1)} %get-tuple-element.47), channel_id=1, source_target_pairs={{255,0},{0,64},{64,128},{128,192},{192,1},{1,65},{65,129},{129,193... | collective-permute-start | bytes 1179656 | tf_op jit(solution)/shard_map/ppermute | solution.py:84
  61.3 1.6 %collective-permute-start.16 = (bf16[12,128,128]{2,1,0:T(8,128)(2,1)S(1)}, bf16[12,128,128]{2,1,0:T(8,128)(2,1)S(1)}, u32[]{:S(2)}, u32[]{:S(2)}) collective-permute-start(bf16[12,128,128]{2,1,0:T(8,128)(2,1)S(1)} %get-tuple-element.48), channel_id=1, source_target_pairs={{64,0},{128,64},{192,128},{1,192},{65,1},{129,65},{193,129},{2,193... | collective-permute-start | bytes 1179656 | tf_op jit(solution)/shard_map/ppermute | solution.py:84
  63.0 9.1 %collective-permute-done.9.refs_1_ = bf16[17,128,128]{2,1,0:T(8,128)(2,1)S(1)} collective-permute-done((bf16[17,128,128]{2,1,0:T(8,128)(2,1)S(1)}, bf16[17,128,128]{2,1,0:T(8,128)(2,1)S(1)}, u32[]{:S(2)}, u32[]{:S(2)}) %collective-permute-start.9) | collective-permute-done | bytes 557088 | tf_op jit(solution)/shard_map/ppermute | solution.py:84
  72.0 0.0 collective-permute-done.10.refs_2_
  72.0 1.9 %shard_map.33 = (bf16[1024,2048]{1,0:T(8,128)(2,1)S(1)}, f32[256,2048]{1,0:T(8,128)S(1)}) custom-call(bf16[13,2,128,128]{3,2,1,0:T(8,128)(2,1)S(1)} %get-tuple-element.33.out_refs_0_.own_ref.refs_0_, bf16[17,128,128]{2,1,0:T(8,128)(2,1)S(1)} %collective-permute-done.9.refs_1_, bf16[17,128,128]{2,1,0:T(8,128)(2,1)S(1)} %collective-permute-done.10.refs_2_, ...), custom_call_target="tpu_custom_call" | custom-call | bytes 4194304 | tf_op jit(solution)/shard_map/pallas_call | solution.py:368
  73.9 6.5 %collective-permute-done.15.refs_4_ = bf16[12,128,128]{2,1,0:T(8,128)(2,1)S(1)} collective-permute-done((bf16[12,128,128]{2,1,0:T(8,128)(2,1)S(1)}, bf16[12,128,128]{2,1,0:T(8,128)(2,1)S(1)}, u32[]{:S(2)}, u32[]{:S(2)}) %collective-permute-start.15) | collective-permute-done | bytes 393248 | tf_op jit(solution)/shard_map/ppermute | solution.py:84
  80.5 0.0 collective-permute-done.16.refs_5_
  80.5 4.1 %shard_map.35 = (bf16[13,2,32,128]{3,2,1,0:T(8,128)(2,1)S(1)}, bf16[13,2,32,128]{3,2,1,0:T(8,128)(2,1)S(1)}, bf16[13,2,32,128]{3,2,1,0:T(8,128)(2,1)S(1)}, bf16[13,2,32,128]{3,2,1,0:T(8,128)(2,1)S(1)}) custom-call(s32[1]{0:T(128)} %bitcast.me_ref, s32[13,8]{1,0:T(8,128)S(1)} %copy.4.presence_ref, ...), custom_call_target="tpu_custom_call" | custom-call | flops 2684354560 | bytes 4194304 | tf_op jit(solution)/shard_map/pallas_call | solution.py:375
  84.6 0.9 collective-permute-start.17
  85.5 0.0 collective-permute-start.18
  85.5 0.7 collective-permute-start.19
  86.2 3.9 %collective-permute-done.17.refs_1_ = bf16[13,2,32,128]{3,2,1,0:T(8,128)(2,1)S(1)} collective-permute-done((bf16[13,2,32,128]{3,2,1,0:T(8,128)(2,1)S(1)}, bf16[13,2,32,128]{3,2,1,0:T(8,128)(2,1)S(1)}, u32[]{:S(2)}, u32[]{:S(2)}) %collective-permute-start.17) | collective-permute-done | bytes 213024 | tf_op jit(solution)/shard_map/ppermute | solution.py:84
  90.1 2.9 %collective-permute-done.18.refs_2_ = bf16[13,2,32,128]{3,2,1,0:T(8,128)(2,1)S(1)} collective-permute-done((bf16[13,2,32,128]{3,2,1,0:T(8,128)(2,1)S(1)}, bf16[13,2,32,128]{3,2,1,0:T(8,128)(2,1)S(1)}, u32[]{:S(2)}, u32[]{:S(2)}) %collective-permute-start.18) | collective-permute-done | bytes 213024 | tf_op jit(solution)/shard_map/ppermute | solution.py:84
  93.0 5.7 %collective-permute-done.19.refs_3_ = bf16[13,2,32,128]{3,2,1,0:T(8,128)(2,1)S(1)} collective-permute-done((bf16[13,2,32,128]{3,2,1,0:T(8,128)(2,1)S(1)}, bf16[13,2,32,128]{3,2,1,0:T(8,128)(2,1)S(1)}, u32[]{:S(2)}, u32[]{:S(2)}) %collective-permute-start.19) | collective-permute-done | bytes 213024 | tf_op jit(solution)/shard_map/ppermute | solution.py:84
  98.8 1.0 shard_map.36
  (2 shorter events, 0.1 us)
Async XLA Ops:
  0.8 1.2 %copy-start = (bf16[13,8,32,128]{3,2,1,0:T(8,128)(2,1)S(1)}, bf16[13,8,32,128]{3,2,1,0:T(8,128)(2,1)}, u32[]{:S(2)}) copy-start(bf16[13,8,32,128]{3,2,1,0:T(8,128)(2,1)} %blocks_ref.1) | copy-start | bytes 2555908
  2.9 24.2 %collective-permute-start.3 = (bf16[5,8,32,128]{3,2,1,0:T(8,128)(2,1)S(1)}, bf16[5,8,32,128]{3,2,1,0:T(8,128)(2,1)S(1)}, u32[]{:S(2)}, u32[]{:S(2)}) collective-permute-start(bf16[5,8,32,128]{3,2,1,0:T(8,128)(2,1)S(1)} %get-tuple-element.34), channel_id=1, source_target_pairs={{4,0},{68,64},{132,128},{196,192},{5,1},{69,65},{133,129},{197,193... | collective-permute-start | bytes 983048 | tf_op jit(solution)/shard_map/ppermute | solution.py:84
  10.7 6.9 %collective-permute-start = (bf16[13,2,32,128]{3,2,1,0:T(8,128)(2,1)S(1)}, bf16[13,2,32,128]{3,2,1,0:T(8,128)(2,1)S(1)}, u32[]{:S(2)}, u32[]{:S(2)}) collective-permute-start(bf16[13,2,32,128]{3,2,1,0:T(8,128)(2,1)S(1)} %get-tuple-element.30), channel_id=1, source_target_pairs={{64,0},{128,64},{192,128},{0,192},{65,1},{129,65},{193,129},{1,193... | collective-permute-start | bytes 638984 | tf_op jit(solution)/shard_map/ppermute | solution.py:84
  13.2 7.1 %collective-permute-start.1 = (bf16[13,2,32,128]{3,2,1,0:T(8,128)(2,1)S(1)}, bf16[13,2,32,128]{3,2,1,0:T(8,128)(2,1)S(1)}, u32[]{:S(2)}, u32[]{:S(2)}) collective-permute-start(bf16[13,2,32,128]{3,2,1,0:T(8,128)(2,1)S(1)} %get-tuple-element.31), channel_id=1, source_target_pairs={{128,0},{192,64},{0,128},{64,192},{129,1},{193,65},{1,129},{65,193... | collective-permute-start | bytes 638984 | tf_op jit(solution)/shard_map/ppermute | solution.py:84
  13.7 12.7 %collective-permute-start.2 = (bf16[13,2,32,128]{3,2,1,0:T(8,128)(2,1)S(1)}, bf16[13,2,32,128]{3,2,1,0:T(8,128)(2,1)S(1)}, u32[]{:S(2)}, u32[]{:S(2)}) collective-permute-start(bf16[13,2,32,128]{3,2,1,0:T(8,128)(2,1)S(1)} %get-tuple-element.32), channel_id=1, source_target_pairs={{192,0},{0,64},{64,128},{128,192},{193,1},{1,65},{65,129},{129,193... | collective-permute-start | bytes 638984 | tf_op jit(solution)/shard_map/ppermute | solution.py:84
  26.5 11.5 %collective-permute-start.7 = (bf16[4,128,128]{2,1,0:T(8,128)(2,1)S(1)}, bf16[4,128,128]{2,1,0:T(8,128)(2,1)S(1)}, u32[]{:S(2)}, u32[]{:S(2)}) collective-permute-start(bf16[4,128,128]{2,1,0:T(8,128)(2,1)S(1)} %get-tuple-element.39), channel_id=1, source_target_pairs={{128,0},{192,64},{1,128},{65,192},{129,1},{193,65},{2,129},{66,193... | collective-permute-start | bytes 393224 | tf_op jit(solution)/shard_map/ppermute | solution.py:84
  27.1 10.9 %collective-permute-start.4 = (bf16[5,2,32,128]{3,2,1,0:T(8,128)(2,1)S(1)}, bf16[5,2,32,128]{3,2,1,0:T(8,128)(2,1)S(1)}, u32[]{:S(2)}, u32[]{:S(2)}) collective-permute-start(bf16[5,2,32,128]{3,2,1,0:T(8,128)(2,1)S(1)} %get-tuple-element.36), channel_id=1, source_target_pairs={{64,0},{128,64},{192,128},{0,192},{65,1},{129,65},{193,129},{1,193... | collective-permute-start | bytes 245768 | tf_op jit(solution)/shard_map/ppermute | solution.py:84
  27.2 10.8 %collective-permute-start.5 = (bf16[5,2,32,128]{3,2,1,0:T(8,128)(2,1)S(1)}, bf16[5,2,32,128]{3,2,1,0:T(8,128)(2,1)S(1)}, u32[]{:S(2)}, u32[]{:S(2)}) collective-permute-start(bf16[5,2,32,128]{3,2,1,0:T(8,128)(2,1)S(1)} %get-tuple-element.37), channel_id=1, source_target_pairs={{128,0},{192,64},{0,128},{64,192},{129,1},{193,65},{1,129},{65,193... | collective-permute-start | bytes 245768 | tf_op jit(solution)/shard_map/ppermute | solution.py:84
  29.8 8.2 %collective-permute-start.6 = (bf16[5,2,32,128]{3,2,1,0:T(8,128)(2,1)S(1)}, bf16[5,2,32,128]{3,2,1,0:T(8,128)(2,1)S(1)}, u32[]{:S(2)}, u32[]{:S(2)}) collective-permute-start(bf16[5,2,32,128]{3,2,1,0:T(8,128)(2,1)S(1)} %get-tuple-element.38), channel_id=1, source_target_pairs={{192,0},{0,64},{64,128},{128,192},{193,1},{1,65},{65,129},{129,193... | collective-permute-start | bytes 245768 | tf_op jit(solution)/shard_map/ppermute | solution.py:84
  30.6 22.2 %collective-permute-start.11 = (bf16[6,128,128]{2,1,0:T(8,128)(2,1)S(1)}, bf16[6,128,128]{2,1,0:T(8,128)(2,1)S(1)}, u32[]{:S(2)}, u32[]{:S(2)}) collective-permute-start(bf16[6,128,128]{2,1,0:T(8,128)(2,1)S(1)} %get-tuple-element.45), channel_id=1, source_target_pairs={{20,0},{84,64},{148,128},{212,192},{21,1},{85,65},{149,129},{213,1... | collective-permute-start | bytes 589832 | tf_op jit(solution)/shard_map/ppermute | solution.py:84
  38.1 19.5 %collective-permute-start.13 = (bf16[10,128,128]{2,1,0:T(8,128)(2,1)S(1)}, bf16[10,128,128]{2,1,0:T(8,128)(2,1)S(1)}, u32[]{:S(2)}, u32[]{:S(2)}) collective-permute-start(bf16[10,128,128]{2,1,0:T(8,128)(2,1)S(1)} %shard_map.31.refs_0_), channel_id=1, source_target_pairs={{16,0},{80,64},{144,128},{208,192},{17,1},{81,65},{145,129},{209,1... | collective-permute-start | bytes 983048 | tf_op jit(solution)/shard_map/ppermute | solution.py:84
  39.5 18.0 %collective-permute-start.14 = (bf16[10,128,128]{2,1,0:T(8,128)(2,1)S(1)}, bf16[10,128,128]{2,1,0:T(8,128)(2,1)S(1)}, u32[]{:S(2)}, u32[]{:S(2)}) collective-permute-start(bf16[10,128,128]{2,1,0:T(8,128)(2,1)S(1)} %shard_map.31.refs_0_), channel_id=1, source_target_pairs={{40,0},{104,64},{168,128},{232,192},{41,1},{105,65},{169,129},{233... | collective-permute-start | bytes 983048 | tf_op jit(solution)/shard_map/ppermute | solution.py:84
  40.9 11.4 %collective-permute-start.8 = (bf16[4,128,128]{2,1,0:T(8,128)(2,1)S(1)}, bf16[4,128,128]{2,1,0:T(8,128)(2,1)S(1)}, u32[]{:S(2)}, u32[]{:S(2)}) collective-permute-start(bf16[4,128,128]{2,1,0:T(8,128)(2,1)S(1)} %get-tuple-element.40), channel_id=1, source_target_pairs={{191,0},{255,64},{0,128},{64,192},{128,1},{192,65},{1,129},{65,193... | collective-permute-start | bytes 393224 | tf_op jit(solution)/shard_map/ppermute | solution.py:84
  42.3 15.3 %collective-permute-start.12 = (bf16[6,128,128]{2,1,0:T(8,128)(2,1)S(1)}, bf16[6,128,128]{2,1,0:T(8,128)(2,1)S(1)}, u32[]{:S(2)}, u32[]{:S(2)}) collective-permute-start(bf16[6,128,128]{2,1,0:T(8,128)(2,1)S(1)} %get-tuple-element.46), channel_id=1, source_target_pairs={{44,0},{108,64},{172,128},{236,192},{45,1},{109,65},{173,129},{237... | collective-permute-start | bytes 589832 | tf_op jit(solution)/shard_map/ppermute | solution.py:84
  52.4 19.6 %collective-permute-start.9 = (bf16[17,128,128]{2,1,0:T(8,128)(2,1)S(1)}, bf16[17,128,128]{2,1,0:T(8,128)(2,1)S(1)}, u32[]{:S(2)}, u32[]{:S(2)}) collective-permute-start(bf16[17,128,128]{2,1,0:T(8,128)(2,1)S(1)} %get-tuple-element.41), channel_id=1, source_target_pairs={{255,0},{0,64},{64,128},{128,192},{192,1},{1,65},{65,129},{129,193... | collective-permute-start | bytes 1671176 | tf_op jit(solution)/shard_map/ppermute | solution.py:84
  52.8 19.3 %collective-permute-start.10 = (bf16[17,128,128]{2,1,0:T(8,128)(2,1)S(1)}, bf16[17,128,128]{2,1,0:T(8,128)(2,1)S(1)}, u32[]{:S(2)}, u32[]{:S(2)}) collective-permute-start(bf16[17,128,128]{2,1,0:T(8,128)(2,1)S(1)} %get-tuple-element.42), channel_id=1, source_target_pairs={{64,0},{128,64},{192,128},{1,192},{65,1},{129,65},{193,129},{2,193... | collective-permute-start | bytes 1671176 | tf_op jit(solution)/shard_map/ppermute | solution.py:84
  57.7 22.8 %collective-permute-start.15 = (bf16[12,128,128]{2,1,0:T(8,128)(2,1)S(1)}, bf16[12,128,128]{2,1,0:T(8,128)(2,1)S(1)}, u32[]{:S(2)}, u32[]{:S(2)}) collective-permute-start(bf16[12,128,128]{2,1,0:T(8,128)(2,1)S(1)} %get-tuple-element.47), channel_id=1, source_target_pairs={{255,0},{0,64},{64,128},{128,192},{192,1},{1,65},{65,129},{129,193... | collective-permute-start | bytes 1179656 | tf_op jit(solution)/shard_map/ppermute | solution.py:84
  61.3 19.1 %collective-permute-start.16 = (bf16[12,128,128]{2,1,0:T(8,128)(2,1)S(1)}, bf16[12,128,128]{2,1,0:T(8,128)(2,1)S(1)}, u32[]{:S(2)}, u32[]{:S(2)}) collective-permute-start(bf16[12,128,128]{2,1,0:T(8,128)(2,1)S(1)} %get-tuple-element.48), channel_id=1, source_target_pairs={{64,0},{128,64},{192,128},{1,192},{65,1},{129,65},{193,129},{2,193... | collective-permute-start | bytes 1179656 | tf_op jit(solution)/shard_map/ppermute | solution.py:84
  84.6 5.5 %collective-permute-start.17 = (bf16[13,2,32,128]{3,2,1,0:T(8,128)(2,1)S(1)}, bf16[13,2,32,128]{3,2,1,0:T(8,128)(2,1)S(1)}, u32[]{:S(2)}, u32[]{:S(2)}) collective-permute-start(bf16[13,2,32,128]{3,2,1,0:T(8,128)(2,1)S(1)} %get-tuple-element.50), channel_id=1, source_target_pairs={{64,0},{128,64},{192,128},{0,192},{65,1},{129,65},{193,129},{1,193... | collective-permute-start | bytes 638984 | tf_op jit(solution)/shard_map/ppermute | solution.py:84
  85.5 7.5 %collective-permute-start.18 = (bf16[13,2,32,128]{3,2,1,0:T(8,128)(2,1)S(1)}, bf16[13,2,32,128]{3,2,1,0:T(8,128)(2,1)S(1)}, u32[]{:S(2)}, u32[]{:S(2)}) collective-permute-start(bf16[13,2,32,128]{3,2,1,0:T(8,128)(2,1)S(1)} %get-tuple-element.51), channel_id=1, source_target_pairs={{128,0},{192,64},{0,128},{64,192},{129,1},{193,65},{1,129},{65,193... | collective-permute-start | bytes 638984 | tf_op jit(solution)/shard_map/ppermute | solution.py:84
  85.5 13.2 %collective-permute-start.19 = (bf16[13,2,32,128]{3,2,1,0:T(8,128)(2,1)S(1)}, bf16[13,2,32,128]{3,2,1,0:T(8,128)(2,1)S(1)}, u32[]{:S(2)}, u32[]{:S(2)}) collective-permute-start(bf16[13,2,32,128]{3,2,1,0:T(8,128)(2,1)S(1)} %get-tuple-element.52), channel_id=1, source_target_pairs={{192,0},{0,64},{64,128},{128,192},{193,1},{1,65},{65,129},{129,193... | collective-permute-start | bytes 638984 | tf_op jit(solution)/shard_map/ppermute | solution.py:84
